TPU v7x, 32 devices: a whole 2x2x4 slice. The times are simulated.
32 devices in a mesh: layer: 4 (over y, x), feat: 8 (over z, core).
Axes of the slice: x: 2, y: 2, z: 4, core: 2. Of those that a mesh axis runs over, the one named last changes fastest.
Arguments:
- activations: bfloat16 [4, 1024, 8192], P(None, None, ('layer', 'feat')), may hold values from -6 to 6
- active_blocks: int32 [4, 1024, 64], P(None, None, ('layer', 'feat')), may hold values from 0 to 1, as said below
- cotangent: bfloat16 [4, 1024, 2048], P(None, 'layer', 'feat'), may hold values from -6 to 6
- decoder: bfloat16 [10, 8192, 2048], P(None, ('layer', 'feat')), may hold values from -0.0625 to 0.0625
Outputs:
- decoder_grad: bfloat16 [10, 8192, 2048], P(None, ('layer', 'feat'))
- feature_grad: bfloat16 [4, 1024, 8192], P(None, None, ('layer', 'feat'))
Inputs may be any that keep to these rules, and one draw needn't show every extreme that they name: `active_blocks`: 1 where the block of 128 features is active for that token at that layer, else 0.
All inputs are finite; a program needn't handle non-finite values.
Results may differ from a plain program's by a relative error of at most 0.001.
Values may be sent and summed in bfloat16 or wider, within the bound.
No kernel may reach another device: no remote copies, remote signals or barrier semaphores. Data moves between devices by JAX's collectives and lax.ppermute only.
A program may use at most 128 MiB of HBM per device.

v0:
```python
import jax
import jax.numpy as jnp
from jax import lax
from jax.sharding import PartitionSpec as P


def pair_work(sparse, upstream, weights, layers):
    grads = []
    partial_value = jnp.zeros((layers, sparse.shape[1], sparse.shape[2]), jnp.float32)
    offset = 0
    for target in range(layers):
        count = target + 1
        rows = weights[offset : offset + count]
        grads.append(
            jnp.einsum(
                "stf,td->sfd", sparse[:count], upstream[target], preferred_element_type=jnp.float32
            )
        )
        terms = jnp.einsum(
            "td,sfd->stf", upstream[target], rows, preferred_element_type=jnp.float32
        )
        partial_value = partial_value.at[:count].add(terms)
        offset = offset + count
    return (jnp.concatenate(grads, axis=0), partial_value)


def body(activations, active_blocks, cotangent, decoder):
    width = activations.shape[2] // active_blocks.shape[2]
    layers = activations.shape[0]
    feature_mask = jnp.repeat(active_blocks, width, axis=2).astype(jnp.float32)
    sparse = (activations.astype(jnp.float32) * feature_mask).astype(jnp.bfloat16)
    cot_rows = lax.all_gather(cotangent, "layer", axis=1, tiled=True)
    upstream = lax.all_gather(cot_rows, "feat", axis=2, tiled=True)
    weight_grads, partial_value = pair_work(sparse, upstream, decoder, layers)
    feature_grad = (partial_value * feature_mask).astype(jnp.bfloat16)
    return (weight_grads.astype(jnp.bfloat16), feature_grad)


def solution(mesh):
    in_specs = (
        P(None, None, ("layer", "feat")),
        P(None, None, ("layer", "feat")),
        P(None, "layer", "feat"),
        P(None, ("layer", "feat"), None),
    )
    out_specs = (P(None, ("layer", "feat"), None), P(None, None, ("layer", "feat")))
    return jax.shard_map(body, mesh=mesh, in_specs=in_specs, out_specs=out_specs, check_vma=False)
```

profile of v0, /device:TPU:0, one launch (start us, length us, event | category | flops | bytes accessed | tf_op | source)
XLA Modules:
  0.0 259.0 jit_solution(14028960746892899319)
XLA Ops:
  7.2 0.0 all-gather.3.cloned.1.call-start
  7.2 0.7 all-gather.3.cloned.1.call-update
  7.9 0.0 all-gather.5.cloned.1.call-start
  7.9 39.9 %all-gather.3.cloned.1.call-done = bf16[4,1024,256]{2,1,0:T(8,128)(2,1)} async-done(((bf16[4,256,256]{2,1,0:T(8,128)(2,1)}), bf16[4,1024,256]{2,1,0:T(8,128)(2,1)}) %all-gather.3.cloned.1.call-update) | async-done | bytes 2097168 | tf_op jit(solution)/shard_map/all_gather | solution.py:32
  47.9 0.0 all-gather.5.cloned.1.call-update
  47.9 0.8 convert_element_type.18
  48.7 3.0 %copy.6 = bf16[4,1024,256]{1,2,0:T(8,128)(2,1)S(1)} copy(bf16[4,1024,256]{2,1,0:T(8,128)(2,1)} %param.14) | data formatting | bytes 4194304 | tf_op args[0]
  51.7 1.9 fusion
  53.6 147.7 %all-gather.5.cloned.1.call-done = bf16[4,1024,2048]{2,1,0:T(8,128)(2,1)} async-done(((bf16[4,1024,256]{2,1,0:T(8,128)(2,1)}), bf16[4,1024,2048]{2,1,0:T(8,128)(2,1)}) %all-gather.5.cloned.1.call-update) | async-done | bytes 16777232 | tf_op jit(solution)/shard_map/all_gather | solution.py:33
  201.3 3.8 %fusion.15 = f32[1,1024,256]{1,2,0:T(8,128)S(1)} fusion(bf16[4,1024,2048]{2,1,0:T(8,128)(2,1)} %all-gather.5.cloned.1.call-done, bf16[10,256,2048]{2,1,0:T(8,128)(2,1)} %param.17), kind=kOutput, calls=%fused_computation.26 | convolution fusion | flops 1073741824 | bytes 6291456 | tf_op jit(solution)/shard_map/td,sfd->stf/dot_general | solution.py:19
  205.1 0.0 slice-start
  205.1 0.5 scatter-add.10
  205.7 0.0 slice-start.1
  205.7 0.0 slice-start.2
  205.7 5.6 %fusion.14 = f32[4,1024,256]{1,2,0:T(8,128)S(1)} fusion(f32[4,1024,256]{1,2,0:T(8,128)S(1)} %scatter-add.10, bf16[10,256,2048]{2,1,0:T(8,128)(2,1)} %param.17, bf16[4,1024,2048]{2,1,0:T(8,128)(2,1)} %all-gather.5.cloned.1.call-done), kind=kOutput, calls=%fused_computation.25 | convolution fusion | flops 2148007936 | bytes 18874368 | tf_op jit(solution)/shard_map/td,sfd->stf/dot_general | solution.py:19
  211.3 0.0 slice-done
  211.3 0.0 slice-done.1
  211.3 0.0 slice-done.2
  211.3 5.5 %fusion.10 = f32[4,1024,256]{1,2,0:T(8,128)S(1)} fusion(f32[4,1024,256]{1,2,0:T(8,128)S(1)} %fusion.14, bf16[10,256,2048]{2,1,0:T(8,128)(2,1)S(1)} %bitcast.71, bf16[4,1024,2048]{2,1,0:T(8,128)(2,1)} %all-gather.5.cloned.1.call-done), kind=kOutput, calls=%fused_computation.20 | convolution fusion | flops 3222011904 | bytes 20971520 | tf_op jit(solution)/shard_map/td,sfd->stf/dot_general | solution.py:19
  216.8 7.0 %fusion.1 = bf16[4,1024,256]{1,2,0:T(8,128)(2,1)S(1)} fusion(f32[4,1024,256]{1,2,0:T(8,128)S(1)} %fusion.10, f32[4,1024,2]{1,2,0:T(2,128)S(1)} %convert_element_type.18, bf16[10,256,2048]{2,1,0:T(8,128)(2,1)S(1)} %bitcast.71, bf16[4,1024,2048]{2,1,0:T(8,128)(2,1)} %all-gather.5.cloned.1.call-done), kind=kOutput, calls=%fused_computation.4 | convolution fusion | flops 4298113024 | bytes 21004288 | tf_op jit(solution)/shard_map/td,sfd->stf/dot_general | solution.py:19
  223.8 2.6 copy.7
  226.4 0.0 copy-start
  226.4 0.0 slice-start.3
  226.4 0.0 slice-start.4
  226.4 0.0 slice-start.5
  226.4 7.5 %convolution_convert_fusion = bf16[4,256,2048]{2,1,0:T(8,128)(2,1)S(1)} fusion(bf16[4,1024,256]{1,2,0:T(8,128)(2,1)} %fusion, bf16[4,1024,2048]{2,1,0:T(8,128)(2,1)} %all-gather.5.cloned.1.call-done), kind=kOutput, calls=%fused_computation.10 | convolution fusion | flops 4297064448 | bytes 10485760 | tf_op jit(solution)/shard_map/stf,td->sfd/dot_general | solution.py:15
  233.9 0.0 copy-done
  233.9 0.0 slice-start.6
  233.9 6.2 %fusion.9 = bf16[3,256,2048]{2,1,0:T(8,128)(2,1)S(1)} fusion(bf16[4,1024,256]{1,2,0:T(8,128)(2,1)S(1)} %copy-done, bf16[4,1024,2048]{2,1,0:T(8,128)(2,1)} %all-gather.5.cloned.1.call-done), kind=kOutput, calls=%fused_computation.18 | convolution fusion | flops 3222798336 | bytes 9437184 | tf_op jit(solution)/shard_map/stf,td->sfd/dot_general | solution.py:15
  240.0 0.0 slice-done.3
  240.1 0.0 slice-done.4
  240.1 0.0 slice-done.5
  240.1 0.0 slice-done.6
  240.1 2.4 fusion.11
  242.5 1.3 fusion.13
  243.7 8.4 %pad_maximum_fusion = bf16[10,256,2048]{2,1,0:T(8,128)(2,1)} fusion(bf16[4,256,2048]{2,1,0:T(8,128)(2,1)S(1)} %convolution_convert_fusion, bf16[3,256,2048]{2,1,0:T(8,128)(2,1)S(1)} %fusion.9, bf16[2,256,2048]{2,1,0:T(8,128)(2,1)S(1)} %fusion.11, bf16[1,256,2048]{2,1,0:T(8,128)(2,1)S(1)} %fusion.13), kind=kLoop, calls=%fused_computation | loop fusion | flops 15728640 | bytes 20971520 | tf_op jit(solution)/shard_map/concatenate | solution.py:24
  (2 shorter events, 0.0 us)
Async XLA Ops:
  7.2 40.7 %all-gather.3.cloned.1.call-start = ((), (), s32[]{:S(2)}) async-start(), calls=%async_computation | async-start | bytes 2621440 | tf_op jit(solution)/shard_map/all_gather | solution.py:32
  7.9 193.4 %all-gather.5.cloned.1.call-start = ((), (), s32[]{:S(2)}) async-start(), calls=%async_computation.1 | async-start | bytes 18874368 | tf_op jit(solution)/shard_map/all_gather | solution.py:33
  205.1 6.2 %slice-start = ((s8[10485760]{0:T(1024)(128)(4,1)}), s8[4194304]{0:T(1024)(128)(4,1)S(1)}, s32[]{:S(2)}) async-start(s8[10485760]{0:T(1024)(128)(4,1)} %bitcast.70), calls=%async_computation.2 | async-start | bytes 8388608
  205.7 5.7 %slice-start.1 = ((s8[10485760]{0:T(1024)(128)(4,1)}), s8[4194304]{0:T(1024)(128)(4,1)S(1)}, s32[]{:S(2)}) async-start(s8[10485760]{0:T(1024)(128)(4,1)} %bitcast.70), calls=%async_computation.3 | async-start | bytes 8388608
  205.7 5.7 %slice-start.2 = ((s8[10485760]{0:T(1024)(128)(4,1)}), s8[2097152]{0:T(1024)(128)(4,1)S(1)}, s32[]{:S(2)}) async-start(s8[10485760]{0:T(1024)(128)(4,1)} %bitcast.70), calls=%async_computation.4 | async-start | bytes 4194304
  226.4 7.5 %copy-start = (bf16[4,1024,256]{1,2,0:T(8,128)(2,1)S(1)}, bf16[4,1024,256]{1,2,0:T(8,128)(2,1)}, u32[]{:S(2)}) copy-start(bf16[4,1024,256]{1,2,0:T(8,128)(2,1)} %fusion) | copy-start | bytes 6291460
  226.4 13.7 %slice-start.3 = ((s8[16777216]{0:T(1024)(128)(4,1)}), s8[4194304]{0:T(1024)(128)(4,1)S(1)}, s32[]{:S(2)}) async-start(s8[16777216]{0:T(1024)(128)(4,1)} %bitcast.72), calls=%async_computation.5 | async-start | bytes 8388608
  226.4 13.7 %slice-start.4 = ((s8[16777216]{0:T(1024)(128)(4,1)}), s8[4194304]{0:T(1024)(128)(4,1)S(1)}, s32[]{:S(2)}) async-start(s8[16777216]{0:T(1024)(128)(4,1)} %bitcast.72), calls=%async_computation.6 | async-start | bytes 8388608
  226.4 13.7 %slice-start.5 = ((s8[16777216]{0:T(1024)(128)(4,1)}), s8[4194304]{0:T(1024)(128)(4,1)S(1)}, s32[]{:S(2)}) async-start(s8[16777216]{0:T(1024)(128)(4,1)} %bitcast.72), calls=%async_computation.7 | async-start | bytes 8388608
  233.9 6.2 %slice-start.6 = ((s8[16777216]{0:T(1024)(128)(4,1)}), s8[4194304]{0:T(1024)(128)(4,1)S(1)}, s32[]{:S(2)}) async-start(s8[16777216]{0:T(1024)(128)(4,1)} %bitcast.72), calls=%async_computation.8 | async-start | bytes 8388608
Sparse Core Ops, SparseCore 0:
  9.8 38.0 all-gather.2
  49.5 151.8 all-gather.4
where the time goes:
time: 259 us
  waiting for transfers between devices  188 us (73%)
  matrix products  39.1 us (15%)
  between operations  14.2 us (5%)
  other arithmetic  11 us (4%)
  local copies, waits for them, and re-layouts  6.11 us (2%)
    all_gather x1, waiting for transfers between devices, body(): upstream = lax.all_gather(cot_rows, 'feat', axis=2, tiled=True)  148 us
    all_gather x1, waiting for transfers between devices, body(): cot_rows = lax.all_gather(cotangent, 'layer', axis=1, tiled=True)  39.9 us
    dot_general x4, matrix products, pair_work(): jnp.einsum('td,sfd->stf', upstream[target], rows, preferred_element_type=...  21.9 us
    dot_general x4, matrix products, pair_work(): jnp.einsum('stf,td->sfd', sparse[:count], upstream[target], preferred_ele...  17.3 us
    concatenate x1, other arithmetic, pair_work(): return (jnp.concatenate(grads, axis=0), partial_value)  8.37 us
    unnamed x18, local copies, waits for them, and re-layouts  5.6 us
  transfers between devices with their start and end apart: 2, of which 2 were waited for; matrix products, arithmetic and copies ran while one was open for 2% of the time, Pallas kernels for 0%

commit v1 on v0

v1 whole, which is shorter than its diff:
```python
import jax
import jax.numpy as jnp
from jax import lax
from jax.sharding import PartitionSpec as P


def body(activations, active_blocks, cotangent, decoder):
    width = activations.shape[2] // active_blocks.shape[2]
    layers = activations.shape[0]
    feature_mask = jnp.repeat(active_blocks, width, axis=2).astype(jnp.float32)
    sparse = (activations.astype(jnp.float32) * feature_mask).astype(jnp.bfloat16)
    n_layer = lax.axis_size("layer")
    n_feat = lax.axis_size("feat")
    blocks = lax.all_gather(cotangent, ("layer", "feat"), axis=0, tiled=False)
    g, t, d = cotangent.shape
    upstream = blocks.reshape(n_layer, n_feat, g, t, d).transpose(2, 0, 3, 1, 4)
    upstream = upstream.reshape(g, n_layer * t, n_feat * d)
    grads = []
    total = jnp.zeros((layers, sparse.shape[1], sparse.shape[2]), jnp.float32)
    offset = 0
    for target in range(layers):
        count = target + 1
        rows = decoder[offset : offset + count]
        grads.append(
            jnp.einsum("stf,td->sfd", sparse[:count], upstream[target], preferred_element_type=jnp.float32).astype(jnp.bfloat16)
        )
        total = total.at[:count].add(
            jnp.einsum("td,sfd->stf", upstream[target], rows, preferred_element_type=jnp.float32)
        )
        offset = offset + count
    return jnp.concatenate(grads, axis=0), (total * feature_mask).astype(jnp.bfloat16)


def solution(mesh):
    in_specs = (
        P(None, None, ("layer", "feat")),
        P(None, None, ("layer", "feat")),
        P(None, "layer", "feat"),
        P(None, ("layer", "feat"), None),
    )
    out_specs = (P(None, ("layer", "feat"), None), P(None, None, ("layer", "feat")))
    return jax.shard_map(body, mesh=mesh, in_specs=in_specs, out_specs=out_specs, check_vma=False)
```

time: 259 us -> 235 us (0.907)
  waiting for transfers between devices: 188 us -> 116 us
  local copies, waits for them, and re-layouts: 6.11 us -> 57.2 us
  matrix products: 39.1 us -> 36.2 us
    all_gather x2 -> x1, waiting for transfers between devices: 188 us -> 115 us  [body(): blocks = lax.all_gather(cotangent, ('layer', 'feat'), axis=0, tiled=False)]
    squeeze x0 -> x3, local copies, waits for them, and re-layouts: none -> 22.3 us  [body(): upstream[target]]
    reshape x0 -> x1, local copies, waits for them, and re-layouts: none -> 15.8 us  [body(): upstream = blocks.reshape(n_layer, n_feat, g, t, d).transpose(2, 0, 3, 1, 4)]
    unnamed x18 -> x21, local copies, waits for them, and re-layouts: 5.6 us -> 12.4 us
    slice x0 -> x1, local copies, waits for them, and re-layouts: none -> 6.06 us  [body(): upstream[target]]
    dot_general x8, matrix products: 39.1 us -> 36.2 us  [the longest x4 21.6 us: body(): jnp.einsum('stf,td->sfd', sparse[:count], upstream[target], preferred_ele...]
  transfers between devices with their start and end apart: 2 -> 1, of which waited for: 2 -> 1; matrix products, arithmetic and copies ran while one was open for 2% -> 2% of each run, Pallas kernels for 0% -> 0%
where the time goes in v1:
time: 235 us; the launch traced here: 234 us
  waiting for transfers between devices  116 us (49%)
  local copies, waits for them, and re-layouts  57.2 us (24%)
  matrix products  36.2 us (15%)
  between operations  14.2 us (6%)
  other arithmetic  11 us (5%)
    all_gather x1, waiting for transfers between devices, body(): blocks = lax.all_gather(cotangent, ('layer', 'feat'), axis=0, tiled=False)  115 us
    squeeze x3, local copies, waits for them, and re-layouts, body(): upstream[target]  22.3 us
    dot_general x4, matrix products, body(): jnp.einsum('stf,td->sfd', sparse[:count], upstream[target], preferred_ele...  21.6 us
    reshape x1, local copies, waits for them, and re-layouts, body(): upstream = blocks.reshape(n_layer, n_feat, g, t, d).transpose(2, 0, 3, 1, 4)  15.8 us
    dot_general x4, matrix products, body(): jnp.einsum('td,sfd->stf', upstream[target], rows, preferred_element_type=...  14.6 us
    unnamed x21, local copies, waits for them, and re-layouts  12.4 us
    concatenate x1, other arithmetic, body(): jnp.concatenate(grads, axis=0)  8.29 us
    slice x1, local copies, waits for them, and re-layouts, body(): upstream[target]  6.06 us
  transfers between devices with their start and end apart: 1, of which 1 were waited for; matrix products, arithmetic and copies ran while one was open for 2% of the time, Pallas kernels for 0%

profile of v1, /device:TPU:0, one launch (start us, length us, event | category | flops | bytes accessed | tf_op | source)
XLA Modules:
  0.0 234.3 jit_solution(6825670065235281905)
XLA Ops:
  7.2 0.0 all-gather.3.cloned.1.call-start
  7.2 0.7 all-gather.3.cloned.1.call-update
  7.9 0.8 convert_element_type.32
  8.7 3.0 %copy.9 = bf16[4,1024,256]{1,2,0:T(8,128)(2,1)S(1)} copy(bf16[4,1024,256]{2,1,0:T(8,128)(2,1)} %param.14) | data formatting | bytes 4194304 | tf_op args[0]
  11.7 1.9 fusion
  13.6 115.1 %all-gather.3.cloned.1.call-done = bf16[128,256,256]{2,1,0:T(8,128)(2,1)} async-done(((bf16[4,256,256]{2,1,0:T(8,128)(2,1)}), bf16[128,256,256]{2,1,0:T(8,128)(2,1)}) %all-gather.3.cloned.1.call-update) | async-done | bytes 16777232 | tf_op jit(solution)/shard_map/all_gather | solution.py:14
  128.6 15.8 %copy.14 = bf16[4,8,4,256,256]{4,1,3,0,2:T(8,128)(2,1)S(1)} copy(bf16[4,8,4,256,256]{4,3,2,1,0:T(8,128)(2,1)} %bitcast.57) | data formatting | bytes 33554432 | tf_op jit(solution)/shard_map/reshape | solution.py:16
  144.5 6.1 %fusion.7 = (bf16[1,4,256,8,256]{4,3,2,1,0:T(8,128)(2,1)}, bf16[1,4,256,8,256]{4,3,2,1,0:T(8,128)(2,1)}, bf16[1,4,256,8,256]{4,3,2,1,0:T(8,128)(2,1)}, bf16[1,4,256,8,256]{4,3,2,1,0:T(8,128)(2,1)}) fusion(bf16[4,4,256,8,256]{4,3,2,1,0:T(8,128)(2,1)S(1)} %bitcast.56), kind=kLoop, calls=%fused_computation.20 | loop fusion | bytes 33554432 | tf_op jit(solution)/shard_map/slice | solution.py:25
  150.6 3.7 %copy.12 = bf16[128,8,8,256]{3,1,2,0:T(8,128)(2,1)S(1)} copy(bf16[128,8,8,256]{3,2,1,0:T(8,128)(2,1)} %bitcast.58) | data formatting | bytes 8388608
  154.2 0.0 copy-start.4
  154.3 2.7 %convolution_bitcast_fusion = f32[1,1024,256]{1,2,0:T(8,128)S(1)} fusion(bf16[1024,2048]{1,0:T(8,128)(2,1)S(1)} %bitcast.61, bf16[10,256,2048]{2,1,0:T(8,128)(2,1)} %param.17), kind=kOutput, calls=%fused_computation.16 | convolution fusion | flops 1073741824 | bytes 6291456 | tf_op jit(solution)/shard_map/td,sfd->stf/dot_general | solution.py:28
  156.9 0.0 copy-done.4
  156.9 2.3 fusion.3
  159.2 7.4 %reshape.160 = bf16[1024,2048,1]{1,0,2:T(8,128)(2,1)} reshape(bf16[1,4,256,8,256]{4,3,2,1,0:T(8,128)(2,1)} %get-tuple-element.63) | data formatting | bytes 8388608 | tf_op jit(solution)/shard_map/squeeze | solution.py:25
  166.6 7.4 %reshape.159 = bf16[1024,2048,1]{1,0,2:T(8,128)(2,1)} reshape(bf16[1,4,256,8,256]{4,3,2,1,0:T(8,128)(2,1)} %get-tuple-element.64) | data formatting | bytes 8388608 | tf_op jit(solution)/shard_map/squeeze | solution.py:25
  174.0 6.9 %convolution_convert_fusion.1 = bf16[3,256,2048]{2,1,0:T(8,128)(2,1)} fusion(bf16[4,1024,256]{1,2,0:T(8,128)(2,1)S(1)} %copy-done.4, bf16[1024,2048,1]{1,0,2:T(8,128)(2,1)} %reshape.159), kind=kOutput, calls=%fused_computation.8 | convolution fusion | flops 3222798336 | bytes 9437184 | tf_op jit(solution)/shard_map/stf,td->sfd/dot_general | solution.py:25
  180.9 0.0 slice-start
  180.9 7.6 %reshape.158 = bf16[1024,2048,1]{1,0,2:T(8,128)(2,1)} reshape(bf16[1,4,256,8,256]{4,3,2,1,0:T(8,128)(2,1)} %get-tuple-element.65) | data formatting | bytes 8388608 | tf_op jit(solution)/shard_map/squeeze | solution.py:25
  188.4 0.0 slice-start.1
  188.4 0.0 slice-start.2
  188.4 6.3 %convolution_convert_fusion.2 = bf16[2,256,2048]{2,1,0:T(8,128)(2,1)} fusion(bf16[4,1024,256]{1,2,0:T(8,128)(2,1)} %fusion, bf16[1024,2048,1]{1,0,2:T(8,128)(2,1)} %reshape.158), kind=kOutput, calls=%fused_computation.11 | convolution fusion | flops 2148532224 | bytes 8388608 | tf_op jit(solution)/shard_map/stf,td->sfd/dot_general | solution.py:25
  194.7 0.0 copy-start.2
  194.7 0.5 scatter-add.10
  195.2 0.0 slice-done
  195.3 0.0 slice-done.1
  195.3 0.0 slice-done.2
  195.3 1.6 copy-done.2
  196.9 0.0 copy-start.1
  196.9 2.5 %fusion.4 = f32[4,1024,256]{1,2,0:T(8,128)S(1)} fusion(f32[4,1024,256]{1,2,0:T(8,128)S(1)} %scatter-add.10, bf16[10,256,2048]{2,1,0:T(8,128)(2,1)S(1)} %bitcast.60, bf16[1024,2048,1]{1,0,2:T(8,128)(2,1)S(1)} %copy-done.2), kind=kOutput, calls=%fused_computation.15 | convolution fusion | flops 2148007936 | bytes 18874368 | tf_op jit(solution)/shard_map/td,sfd->stf/dot_general | solution.py:28
  199.5 0.0 copy-done.1
  199.5 0.0 copy-start
  199.5 0.0 copy-start.5
  199.5 3.7 %fusion.2 = f32[4,1024,256]{1,2,0:T(8,128)S(1)} fusion(f32[4,1024,256]{1,2,0:T(8,128)S(1)} %fusion.4, bf16[10,256,2048]{2,1,0:T(8,128)(2,1)S(1)} %bitcast.60, bf16[1024,2048,1]{1,0,2:T(8,128)(2,1)S(1)} %copy-done.1), kind=kOutput, calls=%fused_computation.10 | convolution fusion | flops 3222011904 | bytes 20971520 | tf_op jit(solution)/shard_map/td,sfd->stf/dot_general | solution.py:28
  203.2 0.0 copy-done
  203.2 0.0 copy-done.5
  203.2 6.1 %convolution_convert_fusion = bf16[4,256,2048]{2,1,0:T(8,128)(2,1)} fusion(bf16[4,1024,256]{1,2,0:T(8,128)(2,1)S(1)} %copy-done.5, bf16[1024,2048,1]{1,0,2:T(8,128)(2,1)S(1)} %copy-done), kind=kOutput, calls=%fused_computation.7 | convolution fusion | flops 4297064448 | bytes 10485760 | tf_op jit(solution)/shard_map/stf,td->sfd/dot_general | solution.py:25
  209.3 5.7 %fusion.1 = bf16[4,1024,256]{1,2,0:T(8,128)(2,1)} fusion(f32[4,1024,256]{1,2,0:T(8,128)S(1)} %fusion.2, bf16[10,256,2048]{2,1,0:T(8,128)(2,1)S(1)} %bitcast.60, bf16[1024,2048,1]{1,0,2:T(8,128)(2,1)S(1)} %copy-done, f32[4,1024,2]{1,2,0:T(2,128)S(1)} %convert_element_type.32), kind=kOutput, calls=%fused_computation.5 | convolution fusion | flops 4298113024 | bytes 21004288 | tf_op jit(solution)/shard_map/td,sfd->stf/dot_general | solution.py:28
  215.0 0.0 copy-start.3
  215.0 4.1 %copy.11 = bf16[4,1024,256]{2,1,0:T(8,128)(2,1)} copy(bf16[4,1024,256]{1,2,0:T(8,128)(2,1)} %fusion.1) | data formatting | bytes 4194304
  219.1 0.0 copy-done.3
  219.1 8.3 %pad_maximum_fusion = bf16[10,256,2048]{2,1,0:T(8,128)(2,1)} fusion(bf16[4,256,2048]{2,1,0:T(8,128)(2,1)} %convolution_convert_fusion, bf16[3,256,2048]{2,1,0:T(8,128)(2,1)S(1)} %copy-done.3, bf16[2,256,2048]{2,1,0:T(8,128)(2,1)} %convolution_convert_fusion.2, bf16[1,256,2048]{2,1,0:T(8,128)(2,1)} %fusion.3), kind=kLoop, calls=%fused_computation.1 | loop fusion | flops 15728640 | bytes 20971520 | tf_op jit(solution)/shard_map/concatenate | solution.py:31
  (1 shorter events, 0.0 us)
Async XLA Ops:
  7.2 121.5 %all-gather.3.cloned.1.call-start = ((), (), s32[]{:S(2)}) async-start(), calls=%async_computation | async-start | bytes 17301504 | tf_op jit(solution)/shard_map/all_gather | solution.py:14
  154.2 2.7 %copy-start.4 = (bf16[4,1024,256]{1,2,0:T(8,128)(2,1)S(1)}, bf16[4,1024,256]{1,2,0:T(8,128)(2,1)}, u32[]{:S(2)}) copy-start(bf16[4,1024,256]{1,2,0:T(8,128)(2,1)} %fusion) | copy-start | bytes 6291460
  180.9 14.4 %slice-start = ((s8[10485760]{0:T(1024)(128)(4,1)}), s8[2097152]{0:T(1024)(128)(4,1)S(1)}, s32[]{:S(2)}) async-start(s8[10485760]{0:T(1024)(128)(4,1)} %bitcast.59), calls=%async_computation.1 | async-start | bytes 4194304
  188.4 6.8 %slice-start.1 = ((s8[10485760]{0:T(1024)(128)(4,1)}), s8[4194304]{0:T(1024)(128)(4,1)S(1)}, s32[]{:S(2)}) async-start(s8[10485760]{0:T(1024)(128)(4,1)} %bitcast.59), calls=%async_computation.2 | async-start | bytes 8388608
  188.4 6.8 %slice-start.2 = ((s8[10485760]{0:T(1024)(128)(4,1)}), s8[4194304]{0:T(1024)(128)(4,1)S(1)}, s32[]{:S(2)}) async-start(s8[10485760]{0:T(1024)(128)(4,1)} %bitcast.59), calls=%async_computation.3 | async-start | bytes 8388608
  194.7 2.2 copy-start.2
  196.9 2.5 %copy-start.1 = (bf16[1024,2048,1]{1,0,2:T(8,128)(2,1)S(1)}, bf16[1024,2048,1]{1,0,2:T(8,128)(2,1)}, u32[]{:S(2)}) copy-start(bf16[1024,2048,1]{1,0,2:T(8,128)(2,1)} %reshape.159) | copy-start | bytes 12582916
  199.5 3.7 %copy-start = (bf16[1024,2048,1]{1,0,2:T(8,128)(2,1)S(1)}, bf16[1024,2048,1]{1,0,2:T(8,128)(2,1)}, u32[]{:S(2)}) copy-start(bf16[1024,2048,1]{1,0,2:T(8,128)(2,1)} %reshape.160) | copy-start | bytes 12582916
  199.5 3.7 %copy-start.5 = (bf16[4,1024,256]{1,2,0:T(8,128)(2,1)S(1)}, bf16[4,1024,256]{1,2,0:T(8,128)(2,1)}, u32[]{:S(2)}) copy-start(bf16[4,1024,256]{1,2,0:T(8,128)(2,1)} %fusion) | copy-start | bytes 6291460
  215.0 4.1 %copy-start.3 = (bf16[3,256,2048]{2,1,0:T(8,128)(2,1)S(1)}, bf16[3,256,2048]{2,1,0:T(8,128)(2,1)}, u32[]{:S(2)}) copy-start(bf16[3,256,2048]{2,1,0:T(8,128)(2,1)} %convolution_convert_fusion.1) | copy-start | bytes 9437188
Sparse Core Ops, SparseCore 0:
  11.0 117.5 all-gather.2

commit v2 on v1

v2 whole, which is shorter than its diff:
```python
import functools

import jax
import jax.numpy as jnp
from jax import lax
from jax.experimental import pallas as pl
from jax.experimental.pallas import tpu as pltpu
from jax.sharding import PartitionSpec as P

CORES = 2


def plane_order(planes):
    return [
        sorted(range(planes), key=lambda p: (abs(p - z), p != (z ^ 1))) for z in range(planes)
    ]


def line_groups(order):
    groups = {}
    for z, row in enumerate(order):
        for r in range(1, len(row)):
            step = 1 if row[r] > z else -1
            held = order[z + step].index(row[r])
            key = (abs(row[r] - z), r, held)
            groups.setdefault(key, []).append((z + step, z))
    return [(r, held, groups[(dist, r, held)]) for dist, r, held in sorted(groups)]


class Gather:
    def __init__(self, block, n_layer, n_feat):
        self.n_layer, self.n_feat = n_layer, n_feat
        self.planes = n_feat // CORES
        self.targets = block.shape[0]
        self.order = plane_order(self.planes)
        self.plane = lax.axis_index("feat") // CORES
        groups = line_groups(self.order)
        self.pieces = {(0, 0): [(0, block)]}
        self.along_line(groups, 0, range(1, self.planes))
        far = [0] + ([self.planes - 1] if self.planes > 1 else [])
        near = [r for r in range(self.planes) if r not in far]
        singles = [j for j in range(1, n_layer) if j & (j - 1) == 0]
        others = [j for j in range(1, n_layer) if j & (j - 1) != 0]
        for r in range(self.planes):
            for j in singles:
                self.pieces[(r, j)] = self.across(self.pieces[(r, 0)], j)
            if r in far:
                for j in others:
                    self.diagonal(r, j)
        for j in others:
            self.along_line(groups, j, near)
        self.other = {
            key: [(g, self.swap(x)) for g, x in parts] for key, parts in self.pieces.items()
        }

    def permute(self, x, pairs):
        flat = []
        for (l0, f0), (l1, f1) in pairs:
            flat.append((l0 * self.n_feat + f0, l1 * self.n_feat + f1))
        return lax.ppermute(x, ("layer", "feat"), sorted(flat))

    def swap(self, x):
        return self.permute(
            x,
            [((l, f), (l, f ^ 1)) for l in range(self.n_layer) for f in range(self.n_feat)],
        )

    def across_one(self, x, bit):
        return self.permute(
            x,
            [((l, f), (l ^ bit, f)) for l in range(self.n_layer) for f in range(self.n_feat)],
        )

    def across(self, parts, bit):
        return [(g, self.across_one(x, bit)) for g, x in parts]

    def diagonal(self, r, j):
        bits = [1 << b for b in range(j.bit_length()) if j >> b & 1]
        if len(bits) == 2 and self.targets % 2 == 0:
            half = self.targets // 2
            out = []
            for at, bit in enumerate(bits):
                (_, x), = self.pieces[(r, j ^ bit)]
                part = lax.slice_in_dim(x, at * half, (at + 1) * half, axis=0)
                out.append((at * half, self.across_one(part, bit)))
            self.pieces[(r, j)] = out
        else:
            self.pieces[(r, j)] = self.across(self.pieces[(r, j ^ bits[0])], bits[0])

    def along_line(self, groups, j, rounds):
        for r, held, moves in groups:
            if r not in rounds:
                continue
            pairs = [
                ((l, a * CORES + c), (l, b * CORES + c))
                for l in range(self.n_layer)
                for a, b in moves
                for c in range(CORES)
            ]
            got = [(g, self.permute(x, pairs)) for g, x in self.pieces[(held, j)]]
            if (r, j) in self.pieces:
                here = functools.reduce(jnp.logical_or, [self.plane == b for _, b in moves])
                got = [
                    (g, jnp.where(here, new, old))
                    for (g, new), (_, old) in zip(got, self.pieces[(r, j)])
                ]
            self.pieces[(r, j)] = got


def round_kernel(layout, layers, first, last, meta, sparse, decoder, *refs):
    n_parts = len(layout)
    refs = list(refs)
    mask = refs.pop(0) if last else None
    acc_in = None if first else refs.pop(0)
    parts = [refs[:n_parts], refs[n_parts : 2 * n_parts]]
    refs = refs[2 * n_parts :]
    if not first:
        refs.pop(0)
    grad, acc_out = refs[:2]
    up_v, sparse_v, dec_v, acc_v, grad_v, feat_v, part_sem, in_sem, out_sem = refs[2:]
    tokens, wide = parts[0][0].shape[1:]
    pairs = decoder.shape[0]

    def columns(k):
        return pl.ds(pl.multiple_of(meta[k] * wide, wide), wide)

    def load_parts(k):
        out = []
        for i, (j, g, count) in enumerate(layout):
            rows = pl.ds(pl.multiple_of(meta[2 + j] * tokens, tokens), tokens)
            out.append(
                pltpu.make_async_copy(
                    parts[k][i], up_v.at[k, pl.ds(g, count), rows, :], part_sem.at[k, i]
                )
            )
        return out

    part_copies = [load_parts(0), load_parts(1)]
    dec_copies = [
        pltpu.make_async_copy(decoder.at[:, :, columns(k)], dec_v.at[k], in_sem.at[k]) for k in range(2)
    ]
    sparse_copy = pltpu.make_async_copy(sparse, sparse_v, in_sem.at[2])
    sparse_copy.start()
    for c in part_copies[0]:
        c.start()
    dec_copies[0].start()
    acc_copy = None
    if not first:
        acc_copy = pltpu.make_async_copy(acc_in, acc_v, in_sem.at[3])
        acc_copy.start()
    for c in part_copies[1]:
        c.start()
    dec_copies[1].start()
    mask_copy = None
    if last:
        mask_copy = pltpu.make_async_copy(mask, feat_v, in_sem.at[4])
        mask_copy.start()
    outs = []

    def grads(k):
        for target in range(layers):
            base = target * (target + 1) // 2

            @pl.loop(0, target + 1)
            def _(source):
                grad_v[k, base + source] = jnp.dot(
                    sparse_v[source], up_v[k, target], preferred_element_type=jnp.float32
                ).astype(jnp.bfloat16)

        out = pltpu.make_async_copy(grad_v.at[k], grad.at[:, :, columns(k)], out_sem.at[k])
        out.start()
        outs.append(out)

    def features(k, final):
        for source in range(layers):
            if k == 0 and first:
                acc_v[source] = jnp.zeros(acc_v.shape[1:], jnp.float32)

            @pl.loop(source, layers)
            def _(target):
                pair = target * (target + 1) // 2 + source
                acc_v[source] += lax.dot_general(
                    up_v[k, target],
                    dec_v[k, pair],
                    (((1,), (1,)), ((), ())),
                    preferred_element_type=jnp.float32,
                )

            if final:
                if last:
                    feat_v[source] = (acc_v[source] * feat_v[source].astype(jnp.float32)).astype(
                        jnp.bfloat16
                    )
                out = pltpu.make_async_copy(
                    (feat_v if last else acc_v).at[source], acc_out.at[source], out_sem.at[2 + source]
                )
                out.start()
                outs.append(out)

    sparse_copy.wait()
    for c in part_copies[0]:
        c.wait()
    grads(0)
    dec_copies[0].wait()
    if acc_copy is not None:
        acc_copy.wait()
    features(0, False)
    for c in part_copies[1]:
        c.wait()
    grads(1)
    dec_copies[1].wait()
    if mask_copy is not None:
        mask_copy.wait()
    features(1, True)
    for out in outs:
        out.wait()


def run_round(meta, sparse, decoder, mask, acc, grad, mine, theirs, last):
    first = acc is None
    layers, width, tokens = sparse.shape
    layout = [(j, g, x.shape[0]) for j, part in mine for g, x in part]
    arrays = [x for _, part in mine for _, x in part] + [x for _, part in theirs for _, x in part]
    wide = arrays[0].shape[2]
    pairs = decoder.shape[0]
    operands = [meta, sparse, decoder]
    if last:
        operands.append(mask)
    if not first:
        operands.append(acc)
    operands += arrays
    aliases = {}
    if not first:
        aliases[len(operands)] = 0
        operands.append(grad)
    specs = [pl.BlockSpec(memory_space=pltpu.SMEM)] + [pl.BlockSpec(memory_space=pl.ANY)] * (
        len(operands) - 1
    )
    flops = 2 * 2 * 2 * pairs * width * tokens * wide
    return pl.pallas_call(
        functools.partial(round_kernel, layout, layers, first, last),
        out_shape=(
            jax.ShapeDtypeStruct(decoder.shape, jnp.bfloat16),
            jax.ShapeDtypeStruct((layers, tokens, width), jnp.bfloat16 if last else jnp.float32),
        ),
        in_specs=specs,
        out_specs=(pl.BlockSpec(memory_space=pl.ANY), pl.BlockSpec(memory_space=pl.ANY)),
        scratch_shapes=[
            pltpu.VMEM((2, layers, tokens, wide), jnp.bfloat16),
            pltpu.VMEM((layers, width, tokens), jnp.bfloat16),
            pltpu.VMEM((2, pairs, width, wide), jnp.bfloat16),
            pltpu.VMEM((layers, tokens, width), jnp.float32),
            pltpu.VMEM((2, pairs, width, wide), jnp.bfloat16),
            pltpu.VMEM((layers, tokens, width), jnp.bfloat16),
            pltpu.SemaphoreType.DMA((2, len(layout))),
            pltpu.SemaphoreType.DMA((5,)),
            pltpu.SemaphoreType.DMA((2 + layers,)),
        ],
        input_output_aliases=aliases,
        cost_estimate=pl.CostEstimate(flops=flops, bytes_accessed=20 * 2**20, transcendentals=0),
        compiler_params=pltpu.CompilerParams(vmem_limit_bytes=40 * 2**20),
    )(*operands)


def body(n_layer, n_feat, activations, active_blocks, cotangent, decoder):
    width = activations.shape[2] // active_blocks.shape[2]
    feature_mask = jnp.repeat(active_blocks, width, axis=2).astype(jnp.bfloat16)
    sparse = jnp.swapaxes(activations * feature_mask, 1, 2)
    blocks = Gather(cotangent, n_layer, n_feat)
    core = lax.axis_index("feat") % CORES
    rows = [lax.axis_index("layer") ^ j for j in range(n_layer)]
    acc = grad = None
    for r in range(blocks.planes):
        plane = jnp.asarray([row[r] for row in blocks.order], jnp.int32)[blocks.plane]
        meta = jnp.stack([plane * CORES + core, plane * CORES + 1 - core] + rows).astype(jnp.int32)
        mine = [(j, blocks.pieces[(r, j)]) for j in range(n_layer)]
        theirs = [(j, blocks.other[(r, j)]) for j in range(n_layer)]
        grad, acc = run_round(
            meta, sparse, decoder, feature_mask, acc, grad, mine, theirs, r == blocks.planes - 1
        )
    return grad, acc


def solution(mesh):
    in_specs = (
        P(None, None, ("layer", "feat")),
        P(None, None, ("layer", "feat")),
        P(None, "layer", "feat"),
        P(None, ("layer", "feat"), None),
    )
    out_specs = (P(None, ("layer", "feat"), None), P(None, None, ("layer", "feat")))
    work = functools.partial(body, mesh.shape["layer"], mesh.shape["feat"])
    return jax.shard_map(work, mesh=mesh, in_specs=in_specs, out_specs=out_specs, check_vma=False)
```

time: 235 us -> 186 us (0.79)
  waiting for transfers between devices: 116 us -> 41.5 us
  Pallas kernels: 0 us -> 63.1 us
  matrix products: 36.2 us -> 0 us
  starting transfers between devices: 0.04 us -> 33.9 us
  local copies, waits for them, and re-layouts: 57.2 us -> 36.8 us
  between operations: 14.2 us -> 3.28 us
  other arithmetic: 11 us -> 6.49 us
    all_gather x1 -> x0, waiting for transfers between devices: 115 us -> none  [body(): blocks = lax.all_gather(cotangent, ('layer', 'feat'), axis=0, tiled=False)]
    pallas_call x0 -> x4, Pallas kernels: none -> 63.1 us  [run_round(): pl.pallas_call(functools.partial(round_kernel, layout, layers, first, las...]
    ppermute x0 -> x43, waiting for transfers between devices: none -> 41.5 us  [permute(): return lax.ppermute(x, ('layer', 'feat'), sorted(flat))]
    dot_general x8 -> x0, matrix products: 36.2 us -> none  [the longest x4 21.6 us: body(): jnp.einsum('stf,td->sfd', sparse[:count], upstream[target], preferred_ele...]
    ppermute x0 -> x43, starting transfers between devices: none -> 33.9 us  [permute(): return lax.ppermute(x, ('layer', 'feat'), sorted(flat))]
    squeeze x3 -> x0, local copies, waits for them, and re-layouts: 22.3 us -> none  [body(): upstream[target]]
    reshape x1 -> x0, local copies, waits for them, and re-layouts: 15.8 us -> none  [body(): upstream = blocks.reshape(n_layer, n_feat, g, t, d).transpose(2, 0, 3, 1, 4)]
    concatenate x1 -> x0, other arithmetic: 8.29 us -> none  [body(): jnp.concatenate(grads, axis=0)]
  transfers between devices with their start and end apart: 1 -> 43, of which waited for: 1 -> 12; matrix products, arithmetic and copies ran while one was open for 2% -> 14% of each run, Pallas kernels for 0% -> 25%
where the time goes in v2:
time: 186 us; the launch traced here: 185 us
  Pallas kernels  63.1 us (34%)
  waiting for transfers between devices  41.5 us (22%)
  local copies, waits for them, and re-layouts  36.8 us (20%)
  starting transfers between devices  33.9 us (18%)
  other arithmetic  6.49 us (3%)
  between operations  3.28 us (2%)
    pallas_call x4, Pallas kernels, run_round(): pl.pallas_call(functools.partial(round_kernel, layout, layers, first, las...  63.1 us
    ppermute x43, waiting for transfers between devices, permute(): return lax.ppermute(x, ('layer', 'feat'), sorted(flat))  41.5 us
    ppermute x43, starting transfers between devices, permute(): return lax.ppermute(x, ('layer', 'feat'), sorted(flat))  33.9 us
    unnamed x74, local copies, waits for them, and re-layouts  18.2 us
    broadcast_in_dim x1, local copies, waits for them, and re-layouts, body(): feature_mask = jnp.repeat(active_blocks, width, axis=2).astype(jnp.bfloat16)  7.49 us
    select_n x4, other arithmetic, along_line(): jnp.where(here, new, old)  4.19 us
  transfers between devices with their start and end apart: 43, of which 12 were waited for; matrix products, arithmetic and copies ran while one was open for 14% of the time, Pallas kernels for 25%

profile of v2, /device:TPU:0, one launch (start us, length us, event | category | flops | bytes accessed | tf_op | source)
XLA Modules:
  0.0 185.0 jit_solution(11044956256168200246)
XLA Ops:
  0.6 3.0 %collective-permute-start = (bf16[4,256,256]{2,1,0:T(8,128)(2,1)}, bf16[4,256,256]{2,1,0:T(8,128)(2,1)S(1)}, u32[]{:S(2)}, u32[]{:S(2)}) collective-permute-start(bf16[4,256,256]{2,1,0:T(8,128)(2,1)} %refs_0_.1), channel_id=1, source_target_pairs={{0,8},{1,9},{2,10},{3,11},{4,12},{5,13},{6,14},{7,15},{8,0},{9,1},... | collective-permute-start | bytes 1572872 | tf_op jit(solution)/shard_map/ppermute | solution.py:60
  3.6 1.5 collective-permute-start.1
  5.2 1.6 collective-permute-start.9
  6.7 1.5 collective-permute-start.19
  8.2 7.6 %collective-permute-done.refs_1_ = bf16[4,256,256]{2,1,0:T(8,128)(2,1)S(1)} collective-permute-done((bf16[4,256,256]{2,1,0:T(8,128)(2,1)}, bf16[4,256,256]{2,1,0:T(8,128)(2,1)S(1)}, u32[]{:S(2)}, u32[]{:S(2)}) %collective-permute-start) | collective-permute-done | bytes 524320 | tf_op jit(solution)/shard_map/ppermute | solution.py:60
  15.8 1.5 collective-permute-done.1.refs_2_
  20.5 1.3 collective-permute-start.10
  21.8 5.6 %collective-permute-done.2.refs_3_ = bf16[2,256,256]{2,1,0:T(8,128)(2,1)} collective-permute-done((bf16[2,256,256]{2,1,0:T(8,128)(2,1)S(1)}, bf16[2,256,256]{2,1,0:T(8,128)(2,1)}, u32[]{:S(2)}, u32[]{:S(2)}) %collective-permute-start.2) | collective-permute-done | bytes 262176 | tf_op jit(solution)/shard_map/ppermute | solution.py:60
  27.7 1.1 collective-permute-start.11
  29.7 1.5 collective-permute-start.32
  32.2 1.3 collective-permute-start.20
  34.4 4.0 %collective-permute-start.12 = (bf16[2,256,256]{2,1,0:T(8,128)(2,1)}, bf16[2,256,256]{2,1,0:T(8,128)(2,1)S(1)}, u32[]{:S(2)}, u32[]{:S(2)}) collective-permute-start(bf16[2,256,256]{2,1,0:T(8,128)(2,1)} %collective-permute-done.2.refs_3_), channel_id=1, source_target_pairs={{0,2},{1,3},{2,0},{3,1},{4,6},{5,7},{6,4},{7,5},{8,10},{9,11},{10,... | collective-permute-start | bytes 786440 | tf_op jit(solution)/shard_map/ppermute | solution.py:60
  38.4 1.3 collective-permute-start.13
  39.7 2.1 %collective-permute-done.11.refs_3_ = bf16[4,256,256]{2,1,0:T(8,128)(2,1)} collective-permute-done((bf16[4,256,256]{2,1,0:T(8,128)(2,1)S(1)}, bf16[4,256,256]{2,1,0:T(8,128)(2,1)}, u32[]{:S(2)}, u32[]{:S(2)}) %collective-permute-start.11) | collective-permute-done | bytes 524320 | tf_op jit(solution)/shard_map/ppermute | solution.py:60
  41.8 1.3 collective-permute-start.33
  44.4 7.5 %broadcast_in_dim.3 = bf16[4,1024,2,128]{3,2,1,0:T(2,128)(2,1)} broadcast(bf16[4,1024,2]{2,1,0:T(8,128)(2,1)S(1)} %copy.13), dimensions={0,1,2} | broadcast | bytes 2113536 | tf_op jit(solution)/shard_map/broadcast_in_dim | solution.py:267
  51.9 3.2 %convert_element_type.6.refs_0_ = bf16[4,1024,256]{2,1,0:T(8,128)(2,1)S(1)} reshape(bf16[4,1024,2,128]{3,2,1,0:T(2,128)(2,1)} %broadcast_in_dim.3) | data formatting | bytes 4194304 | tf_op jit(solution)/shard_map/convert_element_type | solution.py:267
  56.2 4.8 %collective-permute-done.13.refs_5_ = bf16[2,256,256]{2,1,0:T(8,128)(2,1)S(1)} collective-permute-done((bf16[2,256,256]{2,1,0:T(8,128)(2,1)}, bf16[2,256,256]{2,1,0:T(8,128)(2,1)S(1)}, u32[]{:S(2)}, u32[]{:S(2)}) %collective-permute-start.13) | collective-permute-done | bytes 262176 | tf_op jit(solution)/shard_map/ppermute | solution.py:60
  61.8 1.1 broadcast_select_fusion.1.refs_1_
  63.6 1.3 collective-permute-start.24
  64.9 7.3 %collective-permute-done.33 = bf16[4,256,256]{2,1,0:T(8,128)(2,1)} collective-permute-done((bf16[4,256,256]{2,1,0:T(8,128)(2,1)}, bf16[4,256,256]{2,1,0:T(8,128)(2,1)}, u32[]{:S(2)}, u32[]{:S(2)}) %collective-permute-start.33) | collective-permute-done | bytes 524320 | tf_op jit(solution)/shard_map/ppermute | solution.py:60
  72.2 1.3 collective-permute-start.26
  73.5 1.1 broadcast_select_fusion.refs_2_
  75.4 1.4 collective-permute-start.21
  78.0 7.5 %collective-permute-done.24 = bf16[2,256,256]{2,1,0:T(8,128)(2,1)S(1)} collective-permute-done((bf16[2,256,256]{2,1,0:T(8,128)(2,1)S(1)}, bf16[2,256,256]{2,1,0:T(8,128)(2,1)S(1)}, u32[]{:S(2)}, u32[]{:S(2)}) %collective-permute-start.24) | collective-permute-done | bytes 262176 | tf_op jit(solution)/shard_map/ppermute | solution.py:60
  85.5 3.3 %collective-permute-done.26 = bf16[2,256,256]{2,1,0:T(8,128)(2,1)S(1)} collective-permute-done((bf16[2,256,256]{2,1,0:T(8,128)(2,1)S(1)}, bf16[2,256,256]{2,1,0:T(8,128)(2,1)S(1)}, u32[]{:S(2)}, u32[]{:S(2)}) %collective-permute-start.26) | collective-permute-done | bytes 262176 | tf_op jit(solution)/shard_map/ppermute | solution.py:60
  90.8 1.5 multiply_bitcast_fusion
  96.2 3.2 %copy.17.sparse = bf16[4,256,1024]{2,1,0:T(8,128)(2,1)S(1)} copy(bf16[4,256,1024]{1,2,0:T(8,128)(2,1)} %multiply_bitcast_fusion) | data formatting | bytes 4194304 | tf_op jit(solution)/shard_map/transpose | solution.py:268
  99.8 1.0 broadcast_select_fusion.3.refs_4_
  101.4 1.0 broadcast_select_fusion.2.refs_5_
  103.1 1.0 copy-done.15
  104.1 1.0 copy-done.17
  105.1 1.0 copy-done.18
  106.2 1.0 copy-done.20
  107.2 1.0 copy-done.22
  108.3 1.0 copy-done.24
  109.3 0.9 copy-done.26
  110.3 0.9 copy-done.28
  111.2 15.5 %shard_map.95 = (bf16[10,256,2048]{2,1,0:T(8,128)(2,1)}, f32[4,1024,256]{2,1,0:T(8,128)S(1)}) custom-call(s32[6]{0:T(128)S(1)} %stack.75.meta, bf16[4,256,1024]{2,1,0:T(8,128)(2,1)S(1)} %copy.17.sparse, bf16[10,256,2048]{2,1,0:T(8,128)(2,1)} %decoder.7, bf16[4,256,256]{2,1,0:T(8,128)(2,1)S(1)} %copy-done.18, bf16[4,256,256]{2,1,0:T(8,128)(2,1)S(1)} %copy-done.15, ...), custom_call_target="tpu_custom_call" | custom-call | flops 5368709120 | bytes 20971520 | tf_op jit(solution)/shard_map/pallas_call | solution.py:240
  126.7 2.0 %copy-done.2 = f32[4,1024,256]{2,1,0:T(8,128)} copy-done((f32[4,1024,256]{2,1,0:T(8,128)}, f32[4,1024,256]{2,1,0:T(8,128)S(1)}, u32[]{:S(2)}) %copy-start.2) | copy-done | bytes 4194328
  128.7 1.0 slice.18
  129.7 1.0 slice.19
  131.1 1.3 collective-permute-start.36
  132.4 1.6 collective-permute-start.37
  134.6 15.5 %shard_map.96 = (bf16[10,256,2048]{2,1,0:T(8,128)(2,1)}, f32[4,1024,256]{2,1,0:T(8,128)S(1)}) custom-call(s32[6]{0:T(128)S(1)} %stack.72.meta, bf16[4,256,1024]{2,1,0:T(8,128)(2,1)S(1)} %copy.17.sparse, bf16[10,256,2048]{2,1,0:T(8,128)(2,1)} %decoder.7, f32[4,1024,256]{2,1,0:T(8,128)} %copy-done.2, ...), custom_call_target="tpu_custom_call", output_to_operand_aliasing={{0}: (14, {})} | custom-call | flops 5368709120 | bytes 20971520 | tf_op jit(solution)/shard_map/pallas_call | solution.py:240
  150.2 2.0 %copy-done.3 = f32[4,1024,256]{2,1,0:T(8,128)} copy-done((f32[4,1024,256]{2,1,0:T(8,128)}, f32[4,1024,256]{2,1,0:T(8,128)S(1)}, u32[]{:S(2)}) %copy-start.3) | copy-done | bytes 4194328
  152.7 15.7 %shard_map.97 = (bf16[10,256,2048]{2,1,0:T(8,128)(2,1)}, f32[4,1024,256]{2,1,0:T(8,128)S(1)}) custom-call(s32[6]{0:T(128)S(1)} %stack.69.meta, bf16[4,256,1024]{2,1,0:T(8,128)(2,1)S(1)} %copy.17.sparse, bf16[10,256,2048]{2,1,0:T(8,128)(2,1)} %decoder.7, f32[4,1024,256]{2,1,0:T(8,128)} %copy-done.3, ...), custom_call_target="tpu_custom_call", output_to_operand_aliasing={{0}: (14, {})} | custom-call | flops 5368709120 | bytes 20971520 | tf_op jit(solution)/shard_map/pallas_call | solution.py:240
  168.5 16.4 %shard_map.98 = (bf16[10,256,2048]{2,1,0:T(8,128)(2,1)}, bf16[4,1024,256]{2,1,0:T(8,128)(2,1)}) custom-call(s32[6]{0:T(128)S(1)} %stack.66.meta, bf16[4,256,1024]{2,1,0:T(8,128)(2,1)S(1)} %copy.17.sparse, bf16[10,256,2048]{2,1,0:T(8,128)(2,1)} %decoder.7, bf16[4,1024,256]{2,1,0:T(8,128)(2,1)S(1)} %copy-done.1, ...), custom_call_target="tpu_custom_call", output_to_operand_aliasing={{0}: (15, {})} | custom-call | flops 5368709120 | bytes 20971520 | tf_op jit(solution)/shard_map/pallas_call | solution.py:240
  (137 shorter events, 19.2 us)
Async XLA Ops:
  0.6 15.1 %collective-permute-start = (bf16[4,256,256]{2,1,0:T(8,128)(2,1)}, bf16[4,256,256]{2,1,0:T(8,128)(2,1)S(1)}, u32[]{:S(2)}, u32[]{:S(2)}) collective-permute-start(bf16[4,256,256]{2,1,0:T(8,128)(2,1)} %refs_0_.1), channel_id=1, source_target_pairs={{0,8},{1,9},{2,10},{3,11},{4,12},{5,13},{6,14},{7,15},{8,0},{9,1},... | collective-permute-start | bytes 1572872 | tf_op jit(solution)/shard_map/ppermute | solution.py:60
  3.6 13.6 %collective-permute-start.1 = (bf16[4,256,256]{2,1,0:T(8,128)(2,1)}, bf16[4,256,256]{2,1,0:T(8,128)(2,1)S(1)}, u32[]{:S(2)}, u32[]{:S(2)}) collective-permute-start(bf16[4,256,256]{2,1,0:T(8,128)(2,1)} %refs_0_.1), channel_id=1, source_target_pairs={{0,16},{1,17},{2,18},{3,19},{4,20},{5,21},{6,22},{7,23},{8,24},{9,... | collective-permute-start | bytes 1572872 | tf_op jit(solution)/shard_map/ppermute | solution.py:60
  5.2 12.1 %collective-permute-start.4 = (bf16[4,256,256]{2,1,0:T(8,128)(2,1)}, bf16[4,256,256]{2,1,0:T(8,128)(2,1)S(1)}, u32[]{:S(2)}, u32[]{:S(2)}) collective-permute-start(bf16[4,256,256]{2,1,0:T(8,128)(2,1)} %refs_0_.1), channel_id=1, source_target_pairs={{0,1},{1,0},{2,3},{3,2},{4,5},{5,4},{6,7},{7,6},{8,9},{9,8},{10,11... | collective-permute-start | bytes 1572872 | tf_op jit(solution)/shard_map/ppermute | solution.py:60
  5.2 14.5 %collective-permute-start.9 = (bf16[4,256,256]{2,1,0:T(8,128)(2,1)}, bf16[4,256,256]{2,1,0:T(8,128)(2,1)S(1)}, u32[]{:S(2)}, u32[]{:S(2)}) collective-permute-start(bf16[4,256,256]{2,1,0:T(8,128)(2,1)} %refs_0_.1), channel_id=1, source_target_pairs={{0,2},{1,3},{2,0},{3,1},{4,6},{5,7},{6,4},{7,5},{8,10},{9,11},{10,... | collective-permute-start | bytes 1572872 | tf_op jit(solution)/shard_map/ppermute | solution.py:60
  6.7 13.8 %collective-permute-start.19 = (bf16[4,256,256]{2,1,0:T(8,128)(2,1)}, bf16[4,256,256]{2,1,0:T(8,128)(2,1)}, u32[]{:S(2)}, u32[]{:S(2)}) collective-permute-start(bf16[4,256,256]{2,1,0:T(8,128)(2,1)} %refs_0_.1), channel_id=1, source_target_pairs={{2,4},{3,5},{4,2},{5,3},{10,12},{11,13},{12,10},{13,11},{18,20},{1... | collective-permute-start | bytes 1572872 | tf_op jit(solution)/shard_map/ppermute | solution.py:60
  15.8 13.1 %collective-permute-start.5 = (bf16[4,256,256]{2,1,0:T(8,128)(2,1)S(1)}, bf16[4,256,256]{2,1,0:T(8,128)(2,1)S(1)}, u32[]{:S(2)}, u32[]{:S(2)}) collective-permute-start(bf16[4,256,256]{2,1,0:T(8,128)(2,1)S(1)} %collective-permute-done.refs_1_), channel_id=1, source_target_pairs={{0,1},{1,0},{2,3},{3,2},{4,5},{5,4},{6,7},{7,6},{8,9},{9,8},{10,11... | collective-permute-start | bytes 1572872 | tf_op jit(solution)/shard_map/ppermute | solution.py:60
  17.2 13.9 %collective-permute-start.6 = (bf16[4,256,256]{2,1,0:T(8,128)(2,1)S(1)}, bf16[4,256,256]{2,1,0:T(8,128)(2,1)S(1)}, u32[]{:S(2)}, u32[]{:S(2)}) collective-permute-start(bf16[4,256,256]{2,1,0:T(8,128)(2,1)S(1)} %collective-permute-done.1.refs_2_), channel_id=1, source_target_pairs={{0,1},{1,0},{2,3},{3,2},{4,5},{5,4},{6,7},{7,6},{8,9},{9,8},{10,11... | collective-permute-start | bytes 1572872 | tf_op jit(solution)/shard_map/ppermute | solution.py:60
  18.1 9.2 %collective-permute-start.2 = (bf16[2,256,256]{2,1,0:T(8,128)(2,1)S(1)}, bf16[2,256,256]{2,1,0:T(8,128)(2,1)}, u32[]{:S(2)}, u32[]{:S(2)}) collective-permute-start(bf16[2,256,256]{2,1,0:T(8,128)(2,1)S(1)} %slice.16), channel_id=1, source_target_pairs={{0,8},{1,9},{2,10},{3,11},{4,12},{5,13},{6,14},{7,15},{8,0},{9,1},... | collective-permute-start | bytes 786440 | tf_op jit(solution)/shard_map/ppermute | solution.py:60
  19.7 32.2 %copy-start.4 = (bf16[4,256,256]{2,1,0:T(8,128)(2,1)}, bf16[4,256,256]{2,1,0:T(8,128)(2,1)S(1)}, u32[]{:S(2)}) copy-start(bf16[4,256,256]{2,1,0:T(8,128)(2,1)S(1)} %collective-permute-done.9.refs_1_) | copy-start | bytes 1572868
  19.7 8.0 %collective-permute-start.3 = (bf16[2,256,256]{2,1,0:T(8,128)(2,1)S(1)}, bf16[2,256,256]{2,1,0:T(8,128)(2,1)}, u32[]{:S(2)}, u32[]{:S(2)}) collective-permute-start(bf16[2,256,256]{2,1,0:T(8,128)(2,1)S(1)} %slice.17), channel_id=1, source_target_pairs={{0,16},{1,17},{2,18},{3,19},{4,20},{5,21},{6,22},{7,23},{8,24},{9,... | collective-permute-start | bytes 786440 | tf_op jit(solution)/shard_map/ppermute | solution.py:60
  20.5 17.9 %collective-permute-start.10 = (bf16[4,256,256]{2,1,0:T(8,128)(2,1)S(1)}, bf16[4,256,256]{2,1,0:T(8,128)(2,1)}, u32[]{:S(2)}, u32[]{:S(2)}) collective-permute-start(bf16[4,256,256]{2,1,0:T(8,128)(2,1)S(1)} %collective-permute-done.9.refs_1_), channel_id=1, source_target_pairs={{0,8},{1,9},{2,10},{3,11},{4,12},{5,13},{6,14},{7,15},{8,0},{9,1},... | collective-permute-start | bytes 1572872 | tf_op jit(solution)/shard_map/ppermute | solution.py:60
  27.3 4.8 %collective-permute-start.7 = (bf16[2,256,256]{2,1,0:T(8,128)(2,1)}, bf16[2,256,256]{2,1,0:T(8,128)(2,1)S(1)}, u32[]{:S(2)}, u32[]{:S(2)}) collective-permute-start(bf16[2,256,256]{2,1,0:T(8,128)(2,1)} %collective-permute-done.2.refs_3_), channel_id=1, source_target_pairs={{0,1},{1,0},{2,3},{3,2},{4,5},{5,4},{6,7},{7,6},{8,9},{9,8},{10,11... | collective-permute-start | bytes 786440 | tf_op jit(solution)/shard_map/ppermute | solution.py:60
  27.7 14.0 %collective-permute-start.11 = (bf16[4,256,256]{2,1,0:T(8,128)(2,1)S(1)}, bf16[4,256,256]{2,1,0:T(8,128)(2,1)}, u32[]{:S(2)}, u32[]{:S(2)}) collective-permute-start(bf16[4,256,256]{2,1,0:T(8,128)(2,1)S(1)} %collective-permute-done.9.refs_1_), channel_id=1, source_target_pairs={{0,16},{1,17},{2,18},{3,19},{4,20},{5,21},{6,22},{7,23},{8,24},{9,... | collective-permute-start | bytes 1572872 | tf_op jit(solution)/shard_map/ppermute | solution.py:60
  29.7 12.1 %collective-permute-start.32 = (bf16[4,256,256]{2,1,0:T(8,128)(2,1)S(1)}, bf16[4,256,256]{2,1,0:T(8,128)(2,1)}, u32[]{:S(2)}, u32[]{:S(2)}) collective-permute-start(bf16[4,256,256]{2,1,0:T(8,128)(2,1)S(1)} %collective-permute-done.9.refs_1_), channel_id=1, source_target_pairs={{2,4},{3,5},{4,2},{5,3},{10,12},{11,13},{12,10},{13,11},{18,20},{1... | collective-permute-start | bytes 1572872 | tf_op jit(solution)/shard_map/ppermute | solution.py:60
  31.9 1.7 collective-permute-start.8
  32.2 29.6 %collective-permute-start.20 = (bf16[4,256,256]{2,1,0:T(8,128)(2,1)}, bf16[4,256,256]{2,1,0:T(8,128)(2,1)}, u32[]{:S(2)}, u32[]{:S(2)}) collective-permute-start(bf16[4,256,256]{2,1,0:T(8,128)(2,1)} %collective-permute-done.19), channel_id=1, source_target_pairs={{2,0},{3,1},{4,6},{5,7},{10,8},{11,9},{12,14},{13,15},{18,16},{19,... | collective-permute-start | bytes 1572872 | tf_op jit(solution)/shard_map/ppermute | solution.py:60
  34.4 21.1 %collective-permute-start.12 = (bf16[2,256,256]{2,1,0:T(8,128)(2,1)}, bf16[2,256,256]{2,1,0:T(8,128)(2,1)S(1)}, u32[]{:S(2)}, u32[]{:S(2)}) collective-permute-start(bf16[2,256,256]{2,1,0:T(8,128)(2,1)} %collective-permute-done.2.refs_3_), channel_id=1, source_target_pairs={{0,2},{1,3},{2,0},{3,1},{4,6},{5,7},{6,4},{7,5},{8,10},{9,11},{10,... | collective-permute-start | bytes 786440 | tf_op jit(solution)/shard_map/ppermute | solution.py:60
  38.4 22.7 %collective-permute-start.13 = (bf16[2,256,256]{2,1,0:T(8,128)(2,1)}, bf16[2,256,256]{2,1,0:T(8,128)(2,1)S(1)}, u32[]{:S(2)}, u32[]{:S(2)}) collective-permute-start(bf16[2,256,256]{2,1,0:T(8,128)(2,1)} %collective-permute-done.3.refs_4_), channel_id=1, source_target_pairs={{0,2},{1,3},{2,0},{3,1},{4,6},{5,7},{6,4},{7,5},{8,10},{9,11},{10,... | collective-permute-start | bytes 786440 | tf_op jit(solution)/shard_map/ppermute | solution.py:60
  41.8 21.2 %collective-permute-start.14 = (bf16[4,256,256]{2,1,0:T(8,128)(2,1)S(1)}, bf16[4,256,256]{2,1,0:T(8,128)(2,1)}, u32[]{:S(2)}, u32[]{:S(2)}) collective-permute-start(bf16[4,256,256]{2,1,0:T(8,128)(2,1)S(1)} %collective-permute-done.9.refs_1_), channel_id=1, source_target_pairs={{0,1},{1,0},{2,3},{3,2},{4,5},{5,4},{6,7},{7,6},{8,9},{9,8},{10,11... | collective-permute-start | bytes 1572872 | tf_op jit(solution)/shard_map/ppermute | solution.py:60
  41.8 30.4 %collective-permute-start.33 = (bf16[4,256,256]{2,1,0:T(8,128)(2,1)}, bf16[4,256,256]{2,1,0:T(8,128)(2,1)}, u32[]{:S(2)}, u32[]{:S(2)}) collective-permute-start(bf16[4,256,256]{2,1,0:T(8,128)(2,1)} %collective-permute-done.32), channel_id=1, source_target_pairs={{2,0},{3,1},{4,6},{5,7},{10,8},{11,9},{12,14},{13,15},{18,16},{19,... | collective-permute-start | bytes 1572872 | tf_op jit(solution)/shard_map/ppermute | solution.py:60
  55.1 37.3 %copy-start = (bf16[4,1024,256]{2,1,0:T(8,128)(2,1)}, bf16[4,1024,256]{2,1,0:T(8,128)(2,1)S(1)}, u32[]{:S(2)}) copy-start(bf16[4,1024,256]{2,1,0:T(8,128)(2,1)S(1)} %convert_element_type.6.refs_0_) | copy-start | bytes 6291460
  55.1 35.7 %copy-start.29 = (bf16[4,1024,256]{2,1,0:T(8,128)(2,1)S(1)}, bf16[4,1024,256]{2,1,0:T(8,128)(2,1)}, u32[]{:S(2)}) copy-start(bf16[4,1024,256]{2,1,0:T(8,128)(2,1)} %param.8) | copy-start | bytes 6291460
  55.4 8.1 %collective-permute-start.23 = (bf16[2,256,256]{2,1,0:T(8,128)(2,1)}, bf16[2,256,256]{2,1,0:T(8,128)(2,1)S(1)}, u32[]{:S(2)}, u32[]{:S(2)}) collective-permute-start(bf16[2,256,256]{2,1,0:T(8,128)(2,1)} %collective-permute-done.2.refs_3_), channel_id=1, source_target_pairs={{2,4},{3,5},{4,2},{5,3},{10,12},{11,13},{12,10},{13,11},{18,20},{1... | collective-permute-start | bytes 786440 | tf_op jit(solution)/shard_map/ppermute | solution.py:60
  61.1 2.6 %collective-permute-start.25 = (bf16[2,256,256]{2,1,0:T(8,128)(2,1)}, bf16[2,256,256]{2,1,0:T(8,128)(2,1)S(1)}, u32[]{:S(2)}, u32[]{:S(2)}) collective-permute-start(bf16[2,256,256]{2,1,0:T(8,128)(2,1)} %collective-permute-done.3.refs_4_), channel_id=1, source_target_pairs={{2,4},{3,5},{4,2},{5,3},{10,12},{11,13},{12,10},{13,11},{18,20},{1... | collective-permute-start | bytes 786440 | tf_op jit(solution)/shard_map/ppermute | solution.py:60
  61.8 27.1 %collective-permute-start.15 = (bf16[4,256,256]{2,1,0:T(8,128)(2,1)}, bf16[4,256,256]{2,1,0:T(8,128)(2,1)S(1)}, u32[]{:S(2)}, u32[]{:S(2)}) collective-permute-start(bf16[4,256,256]{2,1,0:T(8,128)(2,1)} %collective-permute-done.10.refs_2_), channel_id=1, source_target_pairs={{0,1},{1,0},{2,3},{3,2},{4,5},{5,4},{6,7},{7,6},{8,9},{9,8},{10,11... | collective-permute-start | bytes 1572872 | tf_op jit(solution)/shard_map/ppermute | solution.py:60
  63.0 11.7 %collective-permute-start.17 = (bf16[2,256,256]{2,1,0:T(8,128)(2,1)S(1)}, bf16[2,256,256]{2,1,0:T(8,128)(2,1)S(1)}, u32[]{:S(2)}, u32[]{:S(2)}) collective-permute-start(bf16[2,256,256]{2,1,0:T(8,128)(2,1)S(1)} %collective-permute-done.12.refs_4_), channel_id=1, source_target_pairs={{0,1},{1,0},{2,3},{3,2},{4,5},{5,4},{6,7},{7,6},{8,9},{9,8},{10,11... | collective-permute-start | bytes 786440 | tf_op jit(solution)/shard_map/ppermute | solution.py:60
  63.5 13.2 %collective-permute-start.18 = (bf16[2,256,256]{2,1,0:T(8,128)(2,1)}, bf16[2,256,256]{2,1,0:T(8,128)(2,1)S(1)}, u32[]{:S(2)}, u32[]{:S(2)}) collective-permute-start(bf16[2,256,256]{2,1,0:T(8,128)(2,1)} %copy-done.8), channel_id=1, source_target_pairs={{0,1},{1,0},{2,3},{3,2},{4,5},{5,4},{6,7},{7,6},{8,9},{9,8},{10,11... | collective-permute-start | bytes 786440 | tf_op jit(solution)/shard_map/ppermute | solution.py:60
  63.6 21.9 %collective-permute-start.24 = (bf16[2,256,256]{2,1,0:T(8,128)(2,1)S(1)}, bf16[2,256,256]{2,1,0:T(8,128)(2,1)S(1)}, u32[]{:S(2)}, u32[]{:S(2)}) collective-permute-start(bf16[2,256,256]{2,1,0:T(8,128)(2,1)S(1)} %collective-permute-done.23), channel_id=1, source_target_pairs={{2,0},{3,1},{4,6},{5,7},{10,8},{11,9},{12,14},{13,15},{18,16},{19,... | collective-permute-start | bytes 786440 | tf_op jit(solution)/shard_map/ppermute | solution.py:60
  72.2 16.6 %collective-permute-start.26 = (bf16[2,256,256]{2,1,0:T(8,128)(2,1)S(1)}, bf16[2,256,256]{2,1,0:T(8,128)(2,1)S(1)}, u32[]{:S(2)}, u32[]{:S(2)}) collective-permute-start(bf16[2,256,256]{2,1,0:T(8,128)(2,1)S(1)} %collective-permute-done.25), channel_id=1, source_target_pairs={{2,0},{3,1},{4,6},{5,7},{10,8},{11,9},{12,14},{13,15},{18,16},{19,... | collective-permute-start | bytes 786440 | tf_op jit(solution)/shard_map/ppermute | solution.py:60
  75.4 25.5 %collective-permute-start.21 = (bf16[4,256,256]{2,1,0:T(8,128)(2,1)S(1)}, bf16[4,256,256]{2,1,0:T(8,128)(2,1)}, u32[]{:S(2)}, u32[]{:S(2)}) collective-permute-start(bf16[4,256,256]{2,1,0:T(8,128)(2,1)S(1)} %broadcast_select_fusion.1.refs_1_), channel_id=1, source_target_pairs={{0,8},{1,9},{2,10},{3,11},{4,12},{5,13},{6,14},{7,15},{8,0},{9,1},... | collective-permute-start | bytes 1572872 | tf_op jit(solution)/shard_map/ppermute | solution.py:60
  77.5 23.9 %collective-permute-start.22 = (bf16[4,256,256]{2,1,0:T(8,128)(2,1)S(1)}, bf16[4,256,256]{2,1,0:T(8,128)(2,1)}, u32[]{:S(2)}, u32[]{:S(2)}) collective-permute-start(bf16[4,256,256]{2,1,0:T(8,128)(2,1)S(1)} %broadcast_select_fusion.1.refs_1_), channel_id=1, source_target_pairs={{0,16},{1,17},{2,18},{3,19},{4,20},{5,21},{6,22},{7,23},{8,24},{9,... | collective-permute-start | bytes 1572872 | tf_op jit(solution)/shard_map/ppermute | solution.py:60
  85.5 15.3 %collective-permute-start.16 = (bf16[4,256,256]{2,1,0:T(8,128)(2,1)}, bf16[4,256,256]{2,1,0:T(8,128)(2,1)}, u32[]{:S(2)}, u32[]{:S(2)}) collective-permute-start(bf16[4,256,256]{2,1,0:T(8,128)(2,1)} %collective-permute-done.11.refs_3_), channel_id=1, source_target_pairs={{0,1},{1,0},{2,3},{3,2},{4,5},{5,4},{6,7},{7,6},{8,9},{9,8},{10,11... | collective-permute-start | bytes 1572872 | tf_op jit(solution)/shard_map/ppermute | solution.py:60
  88.8 13.6 %collective-permute-start.34 = (bf16[4,256,256]{2,1,0:T(8,128)(2,1)S(1)}, bf16[4,256,256]{2,1,0:T(8,128)(2,1)}, u32[]{:S(2)}, u32[]{:S(2)}) collective-permute-start(bf16[4,256,256]{2,1,0:T(8,128)(2,1)S(1)} %broadcast_select_fusion.refs_2_), channel_id=1, source_target_pairs={{0,8},{1,9},{2,10},{3,11},{4,12},{5,13},{6,14},{7,15},{8,0},{9,1},... | collective-permute-start | bytes 1572872 | tf_op jit(solution)/shard_map/ppermute | solution.py:60
  90.3 12.6 %collective-permute-start.35 = (bf16[4,256,256]{2,1,0:T(8,128)(2,1)S(1)}, bf16[4,256,256]{2,1,0:T(8,128)(2,1)}, u32[]{:S(2)}, u32[]{:S(2)}) collective-permute-start(bf16[4,256,256]{2,1,0:T(8,128)(2,1)S(1)} %broadcast_select_fusion.refs_2_), channel_id=1, source_target_pairs={{0,16},{1,17},{2,18},{3,19},{4,20},{5,21},{6,22},{7,23},{8,24},{9,... | collective-permute-start | bytes 1572872 | tf_op jit(solution)/shard_map/ppermute | solution.py:60
  100.8 29.9 %collective-permute-start.27 = (bf16[4,256,256]{2,1,0:T(8,128)(2,1)S(1)}, bf16[4,256,256]{2,1,0:T(8,128)(2,1)S(1)}, u32[]{:S(2)}, u32[]{:S(2)}) collective-permute-start(bf16[4,256,256]{2,1,0:T(8,128)(2,1)S(1)} %broadcast_select_fusion.1.refs_1_), channel_id=1, source_target_pairs={{0,1},{1,0},{2,3},{3,2},{4,5},{5,4},{6,7},{7,6},{8,9},{9,8},{10,11... | collective-permute-start | bytes 1572872 | tf_op jit(solution)/shard_map/ppermute | solution.py:60
  100.8 33.2 %collective-permute-start.28 = (bf16[4,256,256]{2,1,0:T(8,128)(2,1)}, bf16[4,256,256]{2,1,0:T(8,128)(2,1)S(1)}, u32[]{:S(2)}, u32[]{:S(2)}) collective-permute-start(bf16[4,256,256]{2,1,0:T(8,128)(2,1)} %collective-permute-done.21.refs_2_), channel_id=1, source_target_pairs={{0,1},{1,0},{2,3},{3,2},{4,5},{5,4},{6,7},{7,6},{8,9},{9,8},{10,11... | collective-permute-start | bytes 1572872 | tf_op jit(solution)/shard_map/ppermute | solution.py:60
  101.3 32.7 %collective-permute-start.29 = (bf16[4,256,256]{2,1,0:T(8,128)(2,1)}, bf16[4,256,256]{2,1,0:T(8,128)(2,1)S(1)}, u32[]{:S(2)}, u32[]{:S(2)}) collective-permute-start(bf16[4,256,256]{2,1,0:T(8,128)(2,1)} %collective-permute-done.22.refs_3_), channel_id=1, source_target_pairs={{0,1},{1,0},{2,3},{3,2},{4,5},{5,4},{6,7},{7,6},{8,9},{9,8},{10,11... | collective-permute-start | bytes 1572872 | tf_op jit(solution)/shard_map/ppermute | solution.py:60
  102.4 32.2 %copy-start.5 = (bf16[4,256,256]{2,1,0:T(8,128)(2,1)S(1)}, bf16[4,256,256]{2,1,0:T(8,128)(2,1)}, u32[]{:S(2)}) copy-start(bf16[4,256,256]{2,1,0:T(8,128)(2,1)} %copy-done.4) | copy-start | bytes 1572868
  102.4 32.1 %copy-start.7 = (bf16[4,256,256]{2,1,0:T(8,128)(2,1)S(1)}, bf16[4,256,256]{2,1,0:T(8,128)(2,1)}, u32[]{:S(2)}) copy-start(bf16[4,256,256]{2,1,0:T(8,128)(2,1)} %copy-done.6) | copy-start | bytes 1572868
  102.5 28.7 %collective-permute-start.30 = (bf16[2,256,256]{2,1,0:T(8,128)(2,1)S(1)}, bf16[2,256,256]{2,1,0:T(8,128)(2,1)S(1)}, u32[]{:S(2)}, u32[]{:S(2)}) collective-permute-start(bf16[2,256,256]{2,1,0:T(8,128)(2,1)S(1)} %broadcast_select_fusion.3.refs_4_), channel_id=1, source_target_pairs={{0,1},{1,0},{2,3},{3,2},{4,5},{5,4},{6,7},{7,6},{8,9},{9,8},{10,11... | collective-permute-start | bytes 786440 | tf_op jit(solution)/shard_map/ppermute | solution.py:60
  103.0 29.4 %collective-permute-start.31 = (bf16[2,256,256]{2,1,0:T(8,128)(2,1)S(1)}, bf16[2,256,256]{2,1,0:T(8,128)(2,1)S(1)}, u32[]{:S(2)}, u32[]{:S(2)}) collective-permute-start(bf16[2,256,256]{2,1,0:T(8,128)(2,1)S(1)} %broadcast_select_fusion.2.refs_5_), channel_id=1, source_target_pairs={{0,1},{1,0},{2,3},{3,2},{4,5},{5,4},{6,7},{7,6},{8,9},{9,8},{10,11... | collective-permute-start | bytes 786440 | tf_op jit(solution)/shard_map/ppermute | solution.py:60
  130.6 37.8 %collective-permute-start.38 = (bf16[4,256,256]{2,1,0:T(8,128)(2,1)S(1)}, bf16[4,256,256]{2,1,0:T(8,128)(2,1)S(1)}, u32[]{:S(2)}, u32[]{:S(2)}) collective-permute-start(bf16[4,256,256]{2,1,0:T(8,128)(2,1)S(1)} %broadcast_select_fusion.refs_2_), channel_id=1, source_target_pairs={{0,1},{1,0},{2,3},{3,2},{4,5},{5,4},{6,7},{7,6},{8,9},{9,8},{10,11... | collective-permute-start | bytes 1572872 | tf_op jit(solution)/shard_map/ppermute | solution.py:60
  131.1 21.0 %collective-permute-start.36 = (bf16[2,256,256]{2,1,0:T(8,128)(2,1)S(1)}, bf16[2,256,256]{2,1,0:T(8,128)(2,1)S(1)}, u32[]{:S(2)}, u32[]{:S(2)}) collective-permute-start(bf16[2,256,256]{2,1,0:T(8,128)(2,1)S(1)} %slice.18), channel_id=1, source_target_pairs={{0,8},{1,9},{2,10},{3,11},{4,12},{5,13},{6,14},{7,15},{8,0},{9,1},... | collective-permute-start | bytes 786440 | tf_op jit(solution)/shard_map/ppermute | solution.py:60
  132.4 19.8 %collective-permute-start.37 = (bf16[2,256,256]{2,1,0:T(8,128)(2,1)S(1)}, bf16[2,256,256]{2,1,0:T(8,128)(2,1)S(1)}, u32[]{:S(2)}, u32[]{:S(2)}) collective-permute-start(bf16[2,256,256]{2,1,0:T(8,128)(2,1)S(1)} %slice.19), channel_id=1, source_target_pairs={{0,16},{1,17},{2,18},{3,19},{4,20},{5,21},{6,22},{7,23},{8,24},{9,... | collective-permute-start | bytes 786440 | tf_op jit(solution)/shard_map/ppermute | solution.py:60
  134.1 34.4 %collective-permute-start.39 = (bf16[4,256,256]{2,1,0:T(8,128)(2,1)}, bf16[4,256,256]{2,1,0:T(8,128)(2,1)S(1)}, u32[]{:S(2)}, u32[]{:S(2)}) collective-permute-start(bf16[4,256,256]{2,1,0:T(8,128)(2,1)} %collective-permute-done.34.refs_3_), channel_id=1, source_target_pairs={{0,1},{1,0},{2,3},{3,2},{4,5},{5,4},{6,7},{7,6},{8,9},{9,8},{10,11... | collective-permute-start | bytes 1572872 | tf_op jit(solution)/shard_map/ppermute | solution.py:60
  134.1 34.4 %collective-permute-start.40 = (bf16[4,256,256]{2,1,0:T(8,128)(2,1)}, bf16[4,256,256]{2,1,0:T(8,128)(2,1)S(1)}, u32[]{:S(2)}, u32[]{:S(2)}) collective-permute-start(bf16[4,256,256]{2,1,0:T(8,128)(2,1)} %collective-permute-done.35.refs_4_), channel_id=1, source_target_pairs={{0,1},{1,0},{2,3},{3,2},{4,5},{5,4},{6,7},{7,6},{8,9},{9,8},{10,11... | collective-permute-start | bytes 1572872 | tf_op jit(solution)/shard_map/ppermute | solution.py:60
  152.1 16.3 %collective-permute-start.41 = (bf16[2,256,256]{2,1,0:T(8,128)(2,1)S(1)}, bf16[2,256,256]{2,1,0:T(8,128)(2,1)S(1)}, u32[]{:S(2)}, u32[]{:S(2)}) collective-permute-start(bf16[2,256,256]{2,1,0:T(8,128)(2,1)S(1)} %collective-permute-done.36.refs_5_), channel_id=1, source_target_pairs={{0,1},{1,0},{2,3},{3,2},{4,5},{5,4},{6,7},{7,6},{8,9},{9,8},{10,11... | collective-permute-start | bytes 786440 | tf_op jit(solution)/shard_map/ppermute | solution.py:60
  152.2 16.2 %collective-permute-start.42 = (bf16[2,256,256]{2,1,0:T(8,128)(2,1)S(1)}, bf16[2,256,256]{2,1,0:T(8,128)(2,1)S(1)}, u32[]{:S(2)}, u32[]{:S(2)}) collective-permute-start(bf16[2,256,256]{2,1,0:T(8,128)(2,1)S(1)} %collective-permute-done.37.refs_6_), channel_id=1, source_target_pairs={{0,1},{1,0},{2,3},{3,2},{4,5},{5,4},{6,7},{7,6},{8,9},{9,8},{10,11... | collective-permute-start | bytes 786440 | tf_op jit(solution)/shard_map/ppermute | solution.py:60
  (32 other events, 304.0 us)

commit v3 on v0

v3 whole, which is shorter than its diff:
```python
import functools

import jax
import jax.numpy as jnp
from jax import lax
from jax.experimental import pallas as pl
from jax.experimental.pallas import tpu as pltpu
from jax.sharding import Mesh
from jax.sharding import PartitionSpec as P

CORES = 2


def target_kernel(target, layers, core, sparse, decoder, mask, mine, theirs, *refs):
    refs = list(refs)
    top = target == layers - 1
    acc_in = None if top else refs.pop(0)
    if not top:
        refs = refs[2:]
    grad, feat = refs[:2]
    acc_out = refs[2] if target > 0 else None
    refs = refs[3:] if target > 0 else refs[2:]
    up_v, sparse_v, dec_v, mask_v, acc_v, grad_v, feat_v, up_sem, in_sem, grad_sem, out_sem = refs
    count = target + 1
    base = target * (target + 1) // 2
    n_layer, n_plane, tokens, wide = mine.shape
    width = sparse.shape[1]
    depth = n_plane * CORES * wide
    rows = n_layer * tokens

    def columns(plane, which):
        at = core[0] if which == 0 else 1 - core[0]
        return pl.ds(pl.multiple_of((plane * CORES + at) * wide, wide), wide)

    sparse_copy = pltpu.make_async_copy(sparse.at[pl.ds(0, count)], sparse_v, in_sem.at[0])
    sparse_copy.start()
    ups = []
    for which, ref in enumerate((mine, theirs)):
        for plane in range(n_plane):
            copy = pltpu.make_async_copy(
                ref.at[:, plane], up_v.at[:, :, columns(plane, which)], up_sem.at[which, plane]
            )
            copy.start()
            ups.append((copy, plane, which))
    dec_copy = pltpu.make_async_copy(decoder, dec_v, in_sem.at[1])
    dec_copy.start()
    acc_copy = None
    if not top:
        acc_copy = pltpu.make_async_copy(acc_in.at[pl.ds(0, count)], acc_v, in_sem.at[2])
        acc_copy.start()
    mask_copy = pltpu.make_async_copy(mask.at[target], mask_v, in_sem.at[3])
    mask_copy.start()
    sparse_copy.wait()
    outs = []
    for at, (copy, plane, which) in enumerate(ups):
        copy.wait()
        cols = columns(plane, which)
        grad_v[:, :, cols] = (
            jnp.dot(
                sparse_v[...].reshape(count * width, rows),
                up_v[:, :, cols].reshape(rows, wide),
                preferred_element_type=jnp.float32,
            )
            .astype(jnp.bfloat16)
            .reshape(count, width, wide)
        )
        out = pltpu.make_async_copy(
            grad_v.at[:, :, cols], grad.at[pl.ds(base, count), :, cols], grad_sem.at[at]
        )
        out.start()
        outs.append(out)
    dec_copy.wait()
    mask_copy.wait()
    if acc_copy is not None:
        acc_copy.wait()
    for source in reversed(range(count)):
        total = jnp.dot(
            up_v[...].reshape(rows, depth), dec_v[source], preferred_element_type=jnp.float32
        )
        if not top:
            total = acc_v[source] + total
        if source == target:
            feat_v[...] = (total * mask_v[...].astype(jnp.float32)).astype(jnp.bfloat16)
            out = pltpu.make_async_copy(feat_v, feat.at[source], out_sem.at[source])
        else:
            acc_v[source] = total
            out = pltpu.make_async_copy(acc_v.at[source], acc_out.at[source], out_sem.at[source])
        out.start()
        outs.append(out)
    for out in outs:
        out.wait()


def run_target(target, core, sparse, decoder, pairs, mask, mine, theirs, acc, grad, feat):
    top = acc is None
    layers, width, rows = sparse.shape
    n_layer, n_plane, tokens, wide = mine.shape
    depth = n_plane * CORES * wide
    count = target + 1
    operands = [core, sparse, decoder, mask, mine, theirs]
    aliases = {}
    if not top:
        operands += [acc, grad, feat]
        aliases = {7: 0, 8: 1}
    any_space = pl.BlockSpec(memory_space=pl.ANY)
    out_shape = [
        jax.ShapeDtypeStruct((pairs, width, depth), jnp.bfloat16),
        jax.ShapeDtypeStruct((layers, rows, width), jnp.bfloat16),
    ]
    if target > 0:
        out_shape.append(jax.ShapeDtypeStruct((target, rows, width), jnp.float32))
    flops = 4 * count * width * rows * depth
    outs = pl.pallas_call(
        functools.partial(target_kernel, target, layers),
        out_shape=tuple(out_shape),
        in_specs=[pl.BlockSpec(memory_space=pltpu.SMEM)] + [any_space] * (len(operands) - 1),
        out_specs=tuple([any_space] * len(out_shape)),
        scratch_shapes=[
            pltpu.VMEM((n_layer, tokens, depth), jnp.bfloat16),
            pltpu.VMEM((count, width, rows), jnp.bfloat16),
            pltpu.VMEM((count, depth, width), jnp.bfloat16),
            pltpu.VMEM((rows, width), jnp.bfloat16),
            pltpu.VMEM((count, rows, width), jnp.float32),
            pltpu.VMEM((count, width, depth), jnp.bfloat16),
            pltpu.VMEM((rows, width), jnp.bfloat16),
            pltpu.SemaphoreType.DMA((CORES, n_plane)),
            pltpu.SemaphoreType.DMA((4,)),
            pltpu.SemaphoreType.DMA((CORES * n_plane,)),
            pltpu.SemaphoreType.DMA((count,)),
        ],
        input_output_aliases=aliases,
        cost_estimate=pl.CostEstimate(flops=flops, bytes_accessed=12 * 2**20, transcendentals=0),
        compiler_params=pltpu.CompilerParams(vmem_limit_bytes=44 * 2**20),
    )(*operands)
    return outs if target > 0 else (*outs, None)


def body(activations, active_blocks, cotangent, decoder):
    width = activations.shape[2] // active_blocks.shape[2]
    layers = cotangent.shape[0]
    order = list(reversed(range(layers)))
    blocks = {
        target: lax.all_gather(cotangent[target], ("layer", "plane"), axis=0, tiled=False)
        for target in order
    }
    turned = jnp.repeat(jnp.swapaxes(active_blocks, 1, 2).astype(jnp.bfloat16), width, axis=1)
    sparse = jnp.swapaxes(activations, 1, 2) * turned
    mask = jnp.swapaxes(turned, 1, 2)
    rows = {}
    for target in order:
        base = target * (target + 1) // 2
        rows[target] = jnp.swapaxes(decoder[base : base + target + 1], 1, 2)
    core = lax.axis_index("core").astype(jnp.int32).reshape(1)
    acc = grad = feat = None
    ready = (sparse, mask, [rows[target] for target in order])
    for target in order:
        mine, ready = lax.optimization_barrier((blocks[target], ready))
        if grad is None:
            sparse, mask, turned_rows = ready
            rows = dict(zip(order, turned_rows))
        else:
            grad, feat, acc = ready
        mine = mine.reshape(lax.axis_size("layer"), lax.axis_size("plane"), *mine.shape[1:])
        theirs = lax.ppermute(mine, "core", [(c, c ^ 1) for c in range(CORES)])
        grad, feat, acc = run_target(
            target, core, sparse, rows[target], decoder.shape[0], mask, mine, theirs, acc, grad, feat
        )
        ready = (grad, feat, acc)
    return grad, feat


def solution(mesh):
    n_layer, n_feat = mesh.devices.shape
    fine = Mesh(
        mesh.devices.reshape(n_layer, n_feat // CORES, CORES), ("layer", "plane", "core")
    )
    every = ("layer", "plane", "core")
    in_specs = (
        P(None, None, every),
        P(None, None, every),
        P(None, "layer", ("plane", "core")),
        P(None, every, None),
    )
    out_specs = (P(None, every, None), P(None, None, every))
    return jax.shard_map(body, mesh=fine, in_specs=in_specs, out_specs=out_specs, check_vma=False)
```

time: 259 us -> 285 us (1.10)
  local copies, waits for them, and re-layouts: 6.11 us -> 68.3 us
  Pallas kernels: 0 us -> 46.7 us
  matrix products: 39.1 us -> 0 us
  waiting for transfers between devices: 188 us -> 151 us
  other arithmetic: 11 us -> 3.14 us
    all_gather x2 -> x4, waiting for transfers between devices: 188 us -> 137 us  [body(): lax.all_gather(cotangent[target], ('layer', 'plane'), axis=0, tiled=False)]
    pallas_call x0 -> x4, Pallas kernels: none -> 46.7 us  [run_target(): pl.pallas_call(functools.partial(target_kernel, target, layers), out_shap...]
    dot_general x8 -> x0, matrix products: 39.1 us -> none  [the longest x4 21.9 us: pair_work(): jnp.einsum('td,sfd->stf', upstream[target], rows, preferred_element_type=...]
    unnamed x18 -> x34, local copies, waits for them, and re-layouts: 5.6 us -> 37 us
    slice x0 -> x5, local copies, waits for them, and re-layouts: none -> 16.2 us  [the longest x4 14.3 us: body(): rows[target] = jnp.swapaxes(decoder[base:base + target + 1], 1, 2)]
    ppermute x0 -> x4, waiting for transfers between devices: none -> 13.5 us  [body(): theirs = lax.ppermute(mine, 'core', [(c, c ^ 1) for c in range(CORES)])]
    concatenate x1 -> x0, other arithmetic: 8.37 us -> none  [pair_work(): return (jnp.concatenate(grads, axis=0), partial_value)]
    broadcast_in_dim x0 -> x1, local copies, waits for them, and re-layouts: none -> 7.49 us  [body(): jnp.repeat(jnp.swapaxes(active_blocks, 1, 2).astype(jnp.bfloat16), width,...]
  transfers between devices with their start and end apart: 2 -> 8, of which waited for: 2 -> 8; matrix products, arithmetic and copies ran while one was open for 2% -> 17% of each run, Pallas kernels for 0% -> 14%
where the time goes in v3:
time: 285 us; the launch traced here: 284 us
  waiting for transfers between devices  151 us (53%)
  local copies, waits for them, and re-layouts  68.3 us (24%)
  Pallas kernels  46.7 us (16%)
  between operations  13.9 us (5%)
  other arithmetic  3.14 us (1%)
    all_gather x4, waiting for transfers between devices, body(): lax.all_gather(cotangent[target], ('layer', 'plane'), axis=0, tiled=False)  137 us
    pallas_call x4, Pallas kernels, run_target(): pl.pallas_call(functools.partial(target_kernel, target, layers), out_shap...  46.7 us
    unnamed x34, local copies, waits for them, and re-layouts  37 us
    slice x4, local copies, waits for them, and re-layouts, body(): rows[target] = jnp.swapaxes(decoder[base:base + target + 1], 1, 2)  14.3 us
    ppermute x4, waiting for transfers between devices, body(): theirs = lax.ppermute(mine, 'core', [(c, c ^ 1) for c in range(CORES)])  13.5 us
    broadcast_in_dim x1, local copies, waits for them, and re-layouts, body(): jnp.repeat(jnp.swapaxes(active_blocks, 1, 2).astype(jnp.bfloat16), width,...  7.49 us
  transfers between devices with their start and end apart: 8, of which 8 were waited for; matrix products, arithmetic and copies ran while one was open for 17% of the time, Pallas kernels for 14%

profile of v3, /device:TPU:0, one launch (start us, length us, event | category | flops | bytes accessed | tf_op | source)
XLA Modules:
  0.0 283.7 jit_solution(686043960360395520)
XLA Ops:
  7.2 0.0 all-gather.5.cloned.1.call-start
  7.2 1.9 fusion
  9.1 0.0 all-gather.5.cloned.1.call-update
  9.1 0.0 all-gather.11.cloned.1.call-start
  9.2 0.7 all-gather.11.cloned.1.call-update
  9.9 0.0 all-gather.9.cloned.1.call-start
  9.9 4.8 %slice.25 = bf16[4,256,2048]{2,1,0:T(8,128)(2,1)} slice(bf16[10,256,2048]{2,1,0:T(8,128)(2,1)} %param.7), slice={[6:10], [0:256], [0:2048]} | slice | bytes 8388608 | tf_op jit(solution)/shard_map/slice | solution.py:152
  14.7 4.1 %slice.26 = bf16[3,256,2048]{2,1,0:T(8,128)(2,1)} slice(bf16[10,256,2048]{2,1,0:T(8,128)(2,1)} %param.7), slice={[3:6], [0:256], [0:2048]} | slice | bytes 6291456 | tf_op jit(solution)/shard_map/slice | solution.py:152
  18.8 3.1 %slice.27 = bf16[2,256,2048]{2,1,0:T(8,128)(2,1)} slice(bf16[10,256,2048]{2,1,0:T(8,128)(2,1)} %param.7), slice={[1:3], [0:256], [0:2048]} | slice | bytes 4194304 | tf_op jit(solution)/shard_map/slice | solution.py:152
  21.9 2.3 slice.28
  24.3 0.5 copy.21
  24.8 7.5 %broadcast_in_dim.3 = bf16[4,2,128,1024]{2,1,3,0:T(2,128)(2,1)} broadcast(bf16[4,2,1024]{1,2,0:T(8,128)(2,1)S(1)} %copy.21), dimensions={0,1,3} | broadcast | bytes 2113536 | tf_op jit(solution)/shard_map/broadcast_in_dim | solution.py:146
  32.3 3.2 %reshape.23 = bf16[4,256,1024]{1,2,0:T(8,128)(2,1)S(1)} reshape(bf16[4,2,128,1024]{2,1,3,0:T(2,128)(2,1)} %broadcast_in_dim.3) | data formatting | bytes 4194304 | tf_op jit(solution)/shard_map/reshape | solution.py:146
  35.5 6.2 %copy.30 = bf16[4,256,2048]{1,2,0:T(8,128)(2,1)} copy(bf16[4,256,2048]{2,1,0:T(8,128)(2,1)} %slice.25) | data formatting | bytes 8388608
  41.7 4.7 %copy.31 = bf16[3,256,2048]{1,2,0:T(8,128)(2,1)} copy(bf16[3,256,2048]{2,1,0:T(8,128)(2,1)} %slice.26) | data formatting | bytes 6291456
  46.3 4.0 %copy.32 = bf16[2,256,2048]{1,2,0:T(8,128)(2,1)} copy(bf16[2,256,2048]{2,1,0:T(8,128)(2,1)} %slice.27) | data formatting | bytes 4194304
  50.3 1.5 copy.33
  51.8 3.1 %bitcast_multiply_fusion = bf16[4,256,1024]{1,2,0:T(8,128)(2,1)} fusion(bf16[4,256,1024]{1,2,0:T(8,128)(2,1)S(1)} %reshape.23, bf16[4,1024,256]{2,1,0:T(8,128)(2,1)} %param.4), kind=kLoop, calls=%fused_computation | loop fusion | flops 1048576 | bytes 6291456 | tf_op jit(solution)/shard_map/mul | solution.py:147
  54.9 19.4 %all-gather.5.cloned.1.call-done = bf16[16,256,256]{2,1,0:T(8,128)(2,1)} async-done(((bf16[1,256,256]{2,1,0:T(8,128)(2,1)}), bf16[16,256,256]{2,1,0:T(8,128)(2,1)}) %all-gather.5.cloned.1.call-update) | async-done | bytes 2097168 | tf_op jit(solution)/shard_map/all_gather | solution.py:143
  74.3 0.0 all-gather.9.cloned.1.call-update
  74.3 0.2 all-gather.7.cloned.1.call-start
  74.5 4.0 %copy.29.sparse = bf16[4,256,1024]{2,1,0:T(8,128)(2,1)} copy(bf16[4,256,1024]{1,2,0:T(8,128)(2,1)} %bitcast_multiply_fusion) | data formatting | bytes 4194304 | tf_op jit(solution)/shard_map/optimization_barrier | solution.py:157
  78.5 0.3 collective-permute-done.theirs
  78.8 1.6 copy-done
  80.4 1.6 copy-done.11
  82.0 16.5 %shard_map.59 = (bf16[10,256,2048]{2,1,0:T(8,128)(2,1)}, bf16[4,1024,256]{2,1,0:T(8,128)(2,1)}, f32[3,1024,256]{2,1,0:T(8,128)}) custom-call(s32[1]{0:T(128)} %bitcast.core, bf16[4,256,1024]{2,1,0:T(8,128)(2,1)S(1)} %copy-done, bf16[4,2048,256]{2,1,0:T(8,128)(2,1)} %bitcast.31, bf16[4,1024,256]{2,1,0:T(8,128)(2,1)S(1)} %bitcast.16, ...), custom_call_target="tpu_custom_call" | custom-call | flops 8589934592 | bytes 12582912 | tf_op jit(solution)/shard_map/pallas_call | solution.py:113
  98.5 38.0 %all-gather.11.cloned.1.call-done = bf16[16,256,256]{2,1,0:T(8,128)(2,1)} async-done(((bf16[1,256,256]{2,1,0:T(8,128)(2,1)}), bf16[16,256,256]{2,1,0:T(8,128)(2,1)}) %all-gather.11.cloned.1.call-update) | async-done | bytes 2097168 | tf_op jit(solution)/shard_map/all_gather | solution.py:143
  136.5 0.0 all-gather.7.cloned.1.call-update
  136.5 4.5 %collective-permute-done.1.theirs = bf16[4,4,256,256]{3,2,1,0:T(8,128)(2,1)} collective-permute-done((bf16[4,4,256,256]{3,2,1,0:T(8,128)(2,1)}, bf16[4,4,256,256]{3,2,1,0:T(8,128)(2,1)}, u32[]{:S(2)}, u32[]{:S(2)}) %collective-permute-start.1) | collective-permute-done | bytes 2097184 | tf_op jit(solution)/shard_map/ppermute | solution.py:164
  141.0 1.6 copy-done.1
  142.6 1.6 copy-done.5
  144.2 14.5 %shard_map.60 = (bf16[10,256,2048]{2,1,0:T(8,128)(2,1)}, bf16[4,1024,256]{2,1,0:T(8,128)(2,1)}, f32[2,1024,256]{2,1,0:T(8,128)S(1)}) custom-call(s32[1]{0:T(128)} %bitcast.core, bf16[4,256,1024]{2,1,0:T(8,128)(2,1)S(1)} %copy-done.1, bf16[3,2048,256]{2,1,0:T(8,128)(2,1)} %bitcast.30, ...), custom_call_target="tpu_custom_call", output_to_operand_aliasing={{0}: (7, {}), {1}: (8, {})} | custom-call | flops 6442450944 | bytes 12582912 | tf_op jit(solution)/shard_map/pallas_call | solution.py:113
  158.7 1.3 copy-done.8
  160.0 38.7 %all-gather.9.cloned.1.call-done = bf16[16,256,256]{2,1,0:T(8,128)(2,1)} async-done(((bf16[1,256,256]{2,1,0:T(8,128)(2,1)}), bf16[16,256,256]{2,1,0:T(8,128)(2,1)}) %all-gather.9.cloned.1.call-update) | async-done | bytes 2097168 | tf_op jit(solution)/shard_map/all_gather | solution.py:143
  198.7 4.4 %collective-permute-done.2.theirs = bf16[4,4,256,256]{3,2,1,0:T(8,128)(2,1)S(1)} collective-permute-done((bf16[4,4,256,256]{3,2,1,0:T(8,128)(2,1)}, bf16[4,4,256,256]{3,2,1,0:T(8,128)(2,1)S(1)}, u32[]{:S(2)}, u32[]{:S(2)}) %collective-permute-start.2) | collective-permute-done | bytes 2097184 | tf_op jit(solution)/shard_map/ppermute | solution.py:164
  203.1 1.4 copy-done.13
  204.5 1.6 copy-done.2
  206.1 1.6 copy-done.4
  207.7 1.6 copy-done.7
  209.3 9.5 %shard_map.61 = (bf16[10,256,2048]{2,1,0:T(8,128)(2,1)}, bf16[4,1024,256]{2,1,0:T(8,128)(2,1)}, f32[1,1024,256]{2,1,0:T(8,128)S(1)}) custom-call(s32[1]{0:T(128)} %bitcast.core, bf16[4,256,1024]{2,1,0:T(8,128)(2,1)S(1)} %copy-done.2, bf16[2,2048,256]{2,1,0:T(8,128)(2,1)S(1)} %bitcast.20, ...), custom_call_target="tpu_custom_call", output_to_operand_aliasing={{0}: (7, {}), {1}: (8, {})} | custom-call | flops 4294967296 | bytes 12582912 | tf_op jit(solution)/shard_map/pallas_call | solution.py:113
  218.8 1.0 copy-done.9
  219.8 41.0 %all-gather.7.cloned.1.call-done = bf16[16,256,256]{2,1,0:T(8,128)(2,1)} async-done(((bf16[1,256,256]{2,1,0:T(8,128)(2,1)}), bf16[16,256,256]{2,1,0:T(8,128)(2,1)}) %all-gather.7.cloned.1.call-update) | async-done | bytes 2097168 | tf_op jit(solution)/shard_map/all_gather | solution.py:143
  260.8 4.4 %collective-permute-done.3.theirs = bf16[4,4,256,256]{3,2,1,0:T(8,128)(2,1)S(1)} collective-permute-done((bf16[4,4,256,256]{3,2,1,0:T(8,128)(2,1)}, bf16[4,4,256,256]{3,2,1,0:T(8,128)(2,1)S(1)}, u32[]{:S(2)}, u32[]{:S(2)}) %collective-permute-start.3) | collective-permute-done | bytes 2097184 | tf_op jit(solution)/shard_map/ppermute | solution.py:164
  265.2 1.3 copy-done.12
  266.5 1.6 copy-done.3
  268.1 1.6 copy-done.6
  269.7 1.2 copy-done.10
  270.9 6.2 %shard_map.62 = (bf16[10,256,2048]{2,1,0:T(8,128)(2,1)}, bf16[4,1024,256]{2,1,0:T(8,128)(2,1)}) custom-call(s32[1]{0:T(128)} %bitcast.core, bf16[4,256,1024]{2,1,0:T(8,128)(2,1)S(1)} %copy-done.3, bf16[1,2048,256]{2,1,0:T(8,128)(2,1)S(1)} %bitcast.21, bf16[4,1024,256]{2,1,0:T(8,128)(2,1)S(1)} %bitcast.19, ...), custom_call_target="tpu_custom_call", output_to_operand_aliasing={{0}: (7, {}), {1}: (8, {})} | custom-call | flops 2147483648 | bytes 12582912 | tf_op jit(solution)/shard_map/pallas_call | solution.py:113
  (21 shorter events, 0.1 us)
Async XLA Ops:
  7.2 67.1 %all-gather.5.cloned.1.call-start = ((), (), s32[]{:S(2)}) async-start(), calls=%async_computation | async-start | bytes 2228224 | tf_op jit(solution)/shard_map/all_gather | solution.py:143
  9.1 127.4 %all-gather.11.cloned.1.call-start = ((), (), s32[]{:S(2)}) async-start(), calls=%async_computation.3 | async-start | bytes 2228224 | tf_op jit(solution)/shard_map/all_gather | solution.py:143
  9.9 188.8 %all-gather.9.cloned.1.call-start = ((), (), s32[]{:S(2)}) async-start(), calls=%async_computation.2 | async-start | bytes 2228224 | tf_op jit(solution)/shard_map/all_gather | solution.py:143
  21.9 2.3 copy-start.14
  74.3 4.5 %collective-permute-start = (bf16[4,4,256,256]{3,2,1,0:T(8,128)(2,1)}, bf16[4,4,256,256]{3,2,1,0:T(8,128)(2,1)}, u32[]{:S(2)}, u32[]{:S(2)}) collective-permute-start(bf16[4,4,256,256]{3,2,1,0:T(8,128)(2,1)} %bitcast.28), channel_id=1, source_target_pairs={{0,1},{1,0},{2,3},{3,2},{4,5},{5,4},{6,7},{7,6},{8,9},{9,8},{10,11... | collective-permute-start | bytes 6291464 | tf_op jit(solution)/shard_map/ppermute | solution.py:164
  74.3 186.5 %all-gather.7.cloned.1.call-start = ((), (), s32[]{:S(2)}) async-start(), calls=%async_computation.1 | async-start | bytes 2228224 | tf_op jit(solution)/shard_map/all_gather | solution.py:143
  78.8 1.6 copy-start
  80.4 1.6 copy-start.11
  136.5 4.5 %collective-permute-start.1 = (bf16[4,4,256,256]{3,2,1,0:T(8,128)(2,1)}, bf16[4,4,256,256]{3,2,1,0:T(8,128)(2,1)}, u32[]{:S(2)}, u32[]{:S(2)}) collective-permute-start(bf16[4,4,256,256]{3,2,1,0:T(8,128)(2,1)} %bitcast.22), channel_id=1, source_target_pairs={{0,1},{1,0},{2,3},{3,2},{4,5},{5,4},{6,7},{7,6},{8,9},{9,8},{10,11... | collective-permute-start | bytes 6291464 | tf_op jit(solution)/shard_map/ppermute | solution.py:164
  141.0 1.6 copy-start.1
  142.6 1.6 copy-start.5
  158.7 1.3 copy-start.8
  198.7 4.4 %collective-permute-start.2 = (bf16[4,4,256,256]{3,2,1,0:T(8,128)(2,1)}, bf16[4,4,256,256]{3,2,1,0:T(8,128)(2,1)S(1)}, u32[]{:S(2)}, u32[]{:S(2)}) collective-permute-start(bf16[4,4,256,256]{3,2,1,0:T(8,128)(2,1)} %bitcast.26), channel_id=1, source_target_pairs={{0,1},{1,0},{2,3},{3,2},{4,5},{5,4},{6,7},{7,6},{8,9},{9,8},{10,11... | collective-permute-start | bytes 6291464 | tf_op jit(solution)/shard_map/ppermute | solution.py:164
  203.1 1.4 copy-start.13
  204.5 1.6 copy-start.2
  206.1 1.6 copy-start.4
  207.7 1.6 copy-start.7
  218.8 1.0 copy-start.9
  260.8 4.4 %collective-permute-start.3 = (bf16[4,4,256,256]{3,2,1,0:T(8,128)(2,1)}, bf16[4,4,256,256]{3,2,1,0:T(8,128)(2,1)S(1)}, u32[]{:S(2)}, u32[]{:S(2)}) collective-permute-start(bf16[4,4,256,256]{3,2,1,0:T(8,128)(2,1)} %bitcast.24), channel_id=1, source_target_pairs={{0,1},{1,0},{2,3},{3,2},{4,5},{5,4},{6,7},{7,6},{8,9},{9,8},{10,11... | collective-permute-start | bytes 6291464 | tf_op jit(solution)/shard_map/ppermute | solution.py:164
  265.2 1.3 copy-start.12
  266.5 1.6 copy-start.3
  268.1 1.6 copy-start.6
  269.7 1.2 copy-start.10
Sparse Core Ops, SparseCore 0:
  10.8 63.4 all-gather.4
  77.1 59.3 all-gather.10
  139.3 59.3 all-gather.8
  201.4 59.3 all-gather.6

commit v4 on v3

--- a/solution.py
+++ b/solution.py
@@ -5,13 +5,10 @@
 from jax import lax
 from jax.experimental import pallas as pl
 from jax.experimental.pallas import tpu as pltpu
-from jax.sharding import Mesh
 from jax.sharding import PartitionSpec as P
 
-CORES = 2
 
-
-def target_kernel(target, layers, core, sparse, decoder, mask, mine, theirs, *refs):
+def target_kernel(target, layers, sparse, decoder, mask, mine, *refs):
     refs = list(refs)
     top = target == layers - 1
     acc_in = None if top else refs.pop(0)
@@ -23,25 +20,22 @@
     up_v, sparse_v, dec_v, mask_v, acc_v, grad_v, feat_v, up_sem, in_sem, grad_sem, out_sem = refs
     count = target + 1
     base = target * (target + 1) // 2
-    n_layer, n_plane, tokens, wide = mine.shape
+    n_layer, n_feat, tokens, wide = mine.shape
     width = sparse.shape[1]
-    depth = n_plane * CORES * wide
+    depth = n_feat * wide
     rows = n_layer * tokens
 
-    def columns(plane, which):
-        at = core[0] if which == 0 else 1 - core[0]
-        return pl.ds(pl.multiple_of((plane * CORES + at) * wide, wide), wide)
+    def columns(at):
+        return pl.ds(at * wide, wide)
 
     sparse_copy = pltpu.make_async_copy(sparse.at[pl.ds(0, count)], sparse_v, in_sem.at[0])
     sparse_copy.start()
-    ups = []
-    for which, ref in enumerate((mine, theirs)):
-        for plane in range(n_plane):
-            copy = pltpu.make_async_copy(
-                ref.at[:, plane], up_v.at[:, :, columns(plane, which)], up_sem.at[which, plane]
-            )
-            copy.start()
-            ups.append((copy, plane, which))
+    ups = [
+        pltpu.make_async_copy(mine.at[:, at], up_v.at[:, :, columns(at)], up_sem.at[at])
+        for at in range(n_feat)
+    ]
+    for copy in ups:
+        copy.start()
     dec_copy = pltpu.make_async_copy(decoder, dec_v, in_sem.at[1])
     dec_copy.start()
     acc_copy = None
@@ -52,9 +46,9 @@
     mask_copy.start()
     sparse_copy.wait()
     outs = []
-    for at, (copy, plane, which) in enumerate(ups):
+    for at, copy in enumerate(ups):
         copy.wait()
-        cols = columns(plane, which)
+        cols = columns(at)
         grad_v[:, :, cols] = (
             jnp.dot(
                 sparse_v[...].reshape(count * width, rows),
@@ -91,17 +85,17 @@
         out.wait()
 
 
-def run_target(target, core, sparse, decoder, pairs, mask, mine, theirs, acc, grad, feat):
+def run_target(target, sparse, decoder, pairs, mask, mine, acc, grad, feat):
     top = acc is None
     layers, width, rows = sparse.shape
-    n_layer, n_plane, tokens, wide = mine.shape
-    depth = n_plane * CORES * wide
+    n_layer, n_feat, tokens, wide = mine.shape
+    depth = n_feat * wide
     count = target + 1
-    operands = [core, sparse, decoder, mask, mine, theirs]
+    operands = [sparse, decoder, mask, mine]
     aliases = {}
     if not top:
         operands += [acc, grad, feat]
-        aliases = {7: 0, 8: 1}
+        aliases = {5: 0, 6: 1}
     any_space = pl.BlockSpec(memory_space=pl.ANY)
     out_shape = [
         jax.ShapeDtypeStruct((pairs, width, depth), jnp.bfloat16),
@@ -113,7 +107,7 @@
     outs = pl.pallas_call(
         functools.partial(target_kernel, target, layers),
         out_shape=tuple(out_shape),
-        in_specs=[pl.BlockSpec(memory_space=pltpu.SMEM)] + [any_space] * (len(operands) - 1),
+        in_specs=[any_space] * len(operands),
         out_specs=tuple([any_space] * len(out_shape)),
         scratch_shapes=[
             pltpu.VMEM((n_layer, tokens, depth), jnp.bfloat16),
@@ -123,9 +117,9 @@
             pltpu.VMEM((count, rows, width), jnp.float32),
             pltpu.VMEM((count, width, depth), jnp.bfloat16),
             pltpu.VMEM((rows, width), jnp.bfloat16),
-            pltpu.SemaphoreType.DMA((CORES, n_plane)),
+            pltpu.SemaphoreType.DMA((n_feat,)),
             pltpu.SemaphoreType.DMA((4,)),
-            pltpu.SemaphoreType.DMA((CORES * n_plane,)),
+            pltpu.SemaphoreType.DMA((n_feat,)),
             pltpu.SemaphoreType.DMA((count,)),
         ],
         input_output_aliases=aliases,
@@ -140,7 +134,7 @@
     layers = cotangent.shape[0]
     order = list(reversed(range(layers)))
     blocks = {
-        target: lax.all_gather(cotangent[target], ("layer", "plane"), axis=0, tiled=False)
+        target: lax.all_gather(cotangent[target], ("layer", "feat"), axis=0, tiled=False)
         for target in order
     }
     turned = jnp.repeat(jnp.swapaxes(active_blocks, 1, 2).astype(jnp.bfloat16), width, axis=1)
@@ -150,7 +144,6 @@
     for target in order:
         base = target * (target + 1) // 2
         rows[target] = jnp.swapaxes(decoder[base : base + target + 1], 1, 2)
-    core = lax.axis_index("core").astype(jnp.int32).reshape(1)
     acc = grad = feat = None
     ready = (sparse, mask, [rows[target] for target in order])
     for target in order:
@@ -160,26 +153,20 @@
             rows = dict(zip(order, turned_rows))
         else:
             grad, feat, acc = ready
-        mine = mine.reshape(lax.axis_size("layer"), lax.axis_size("plane"), *mine.shape[1:])
-        theirs = lax.ppermute(mine, "core", [(c, c ^ 1) for c in range(CORES)])
+        mine = mine.reshape(lax.axis_size("layer"), lax.axis_size("feat"), *mine.shape[1:])
         grad, feat, acc = run_target(
-            target, core, sparse, rows[target], decoder.shape[0], mask, mine, theirs, acc, grad, feat
+            target, sparse, rows[target], decoder.shape[0], mask, mine, acc, grad, feat
         )
         ready = (grad, feat, acc)
     return grad, feat
 
 
 def solution(mesh):
-    n_layer, n_feat = mesh.devices.shape
-    fine = Mesh(
-        mesh.devices.reshape(n_layer, n_feat // CORES, CORES), ("layer", "plane", "core")
+    in_specs = (
+        P(None, None, ("layer", "feat")),
+        P(None, None, ("layer", "feat")),
+        P(None, "layer", "feat"),
+        P(None, ("layer", "feat"), None),
     )
-    every = ("layer", "plane", "core")
-    in_specs = (
-        P(None, None, every),
-        P(None, None, every),
-        P(None, "layer", ("plane", "core")),
-        P(None, every, None),
-    )
-    out_specs = (P(None, every, None), P(None, None, every))
-    return jax.shard_map(body, mesh=fine, in_specs=in_specs, out_specs=out_specs, check_vma=False)
+    out_specs = (P(None, ("layer", "feat"), None), P(None, None, ("layer", "feat")))
+    return jax.shard_map(body, mesh=mesh, in_specs=in_specs, out_specs=out_specs, check_vma=False)

time: 285 us -> 284 us (level)
  local copies, waits for them, and re-layouts: 68.3 us -> 64.4 us
  Pallas kernels: 46.7 us -> 50.1 us
    ppermute x4 -> x0, waiting for transfers between devices: 13.5 us -> none  [body(): theirs = lax.ppermute(mine, 'core', [(c, c ^ 1) for c in range(CORES)])]
    all_gather x4, waiting for transfers between devices: 137 us -> 149 us  [body(): lax.all_gather(cotangent[target], ('layer', 'feat'), axis=0, tiled=False)]
    unnamed x34 -> x28, local copies, waits for them, and re-layouts: 37 us -> 32.9 us
    pallas_call x4, Pallas kernels: 46.7 us -> 50.1 us  [run_target(): pl.pallas_call(functools.partial(target_kernel, target, layers), out_shap...]
  transfers between devices with their start and end apart: 8 -> 4, of which waited for: 8 -> 4; matrix products, arithmetic and copies ran while one was open for 17% -> 17% of each run, Pallas kernels for 14% -> 15%
where the time goes in v4:
time: 284 us; the launch traced here: 283 us
  waiting for transfers between devices  151 us (53%)
  local copies, waits for them, and re-layouts  64.4 us (23%)
  Pallas kernels  50.1 us (18%)
  between operations  13.9 us (5%)
  other arithmetic  3.14 us (1%)
    all_gather x4, waiting for transfers between devices, body(): lax.all_gather(cotangent[target], ('layer', 'feat'), axis=0, tiled=False)  149 us
    pallas_call x4, Pallas kernels, run_target(): pl.pallas_call(functools.partial(target_kernel, target, layers), out_shap...  50.1 us
    unnamed x28, local copies, waits for them, and re-layouts  32.9 us
    slice x4, local copies, waits for them, and re-layouts, body(): rows[target] = jnp.swapaxes(decoder[base:base + target + 1], 1, 2)  14.4 us
    broadcast_in_dim x1, local copies, waits for them, and re-layouts, body(): jnp.repeat(jnp.swapaxes(active_blocks, 1, 2).astype(jnp.bfloat16), width,...  7.49 us
  transfers between devices with their start and end apart: 4, of which 4 were waited for; matrix products, arithmetic and copies ran while one was open for 17% of the time, Pallas kernels for 15%

profile of v4, /device:TPU:0, one launch (start us, length us, event | category | flops | bytes accessed | tf_op | source)
XLA Modules:
  0.0 282.9 jit_solution(327367964927433873)
XLA Ops:
  7.2 0.0 all-gather.5.cloned.1.call-start
  7.2 1.9 fusion
  9.1 0.0 all-gather.5.cloned.1.call-update
  9.1 0.0 all-gather.11.cloned.1.call-start
  9.2 0.7 all-gather.11.cloned.1.call-update
  9.9 0.0 all-gather.9.cloned.1.call-start
  9.9 0.7 all-gather.9.cloned.1.call-update
  10.6 0.0 all-gather.7.cloned.1.call-start
  10.7 0.5 all-gather.7.cloned.1.call-update
  11.2 4.8 %slice.25 = bf16[4,256,2048]{2,1,0:T(8,128)(2,1)} slice(bf16[10,256,2048]{2,1,0:T(8,128)(2,1)} %param.7), slice={[6:10], [0:256], [0:2048]} | slice | bytes 8388608 | tf_op jit(solution)/shard_map/slice | solution.py:146
  16.0 4.1 %slice.26 = bf16[3,256,2048]{2,1,0:T(8,128)(2,1)} slice(bf16[10,256,2048]{2,1,0:T(8,128)(2,1)} %param.7), slice={[3:6], [0:256], [0:2048]} | slice | bytes 6291456 | tf_op jit(solution)/shard_map/slice | solution.py:146
  20.0 3.3 %slice.27 = bf16[2,256,2048]{2,1,0:T(8,128)(2,1)} slice(bf16[10,256,2048]{2,1,0:T(8,128)(2,1)} %param.7), slice={[1:3], [0:256], [0:2048]} | slice | bytes 4194304 | tf_op jit(solution)/shard_map/slice | solution.py:146
  23.3 0.0 copy-start.11
  23.3 2.3 slice.28
  25.6 0.0 copy-done.11
  25.7 0.5 copy.21
  26.2 7.5 %broadcast_in_dim.3 = bf16[4,2,128,1024]{2,1,3,0:T(2,128)(2,1)} broadcast(bf16[4,2,1024]{1,2,0:T(8,128)(2,1)S(1)} %copy.21), dimensions={0,1,3} | broadcast | bytes 2113536 | tf_op jit(solution)/shard_map/broadcast_in_dim | solution.py:140
  33.7 3.2 %reshape.19 = bf16[4,256,1024]{1,2,0:T(8,128)(2,1)S(1)} reshape(bf16[4,2,128,1024]{2,1,3,0:T(2,128)(2,1)} %broadcast_in_dim.3) | data formatting | bytes 4194304 | tf_op jit(solution)/shard_map/reshape | solution.py:140
  36.8 6.2 %copy.30 = bf16[4,256,2048]{1,2,0:T(8,128)(2,1)} copy(bf16[4,256,2048]{2,1,0:T(8,128)(2,1)} %slice.25) | data formatting | bytes 8388608
  43.0 4.7 %copy.31 = bf16[3,256,2048]{1,2,0:T(8,128)(2,1)} copy(bf16[3,256,2048]{2,1,0:T(8,128)(2,1)} %slice.26) | data formatting | bytes 6291456
  47.7 3.9 %copy.32 = bf16[2,256,2048]{1,2,0:T(8,128)(2,1)} copy(bf16[2,256,2048]{2,1,0:T(8,128)(2,1)} %slice.27) | data formatting | bytes 4194304
  51.6 1.5 copy.33
  53.1 3.1 %bitcast_multiply_fusion = bf16[4,256,1024]{1,2,0:T(8,128)(2,1)} fusion(bf16[4,256,1024]{1,2,0:T(8,128)(2,1)S(1)} %reshape.19, bf16[4,1024,256]{2,1,0:T(8,128)(2,1)} %param.4), kind=kLoop, calls=%fused_computation | loop fusion | flops 1048576 | bytes 6291456 | tf_op jit(solution)/shard_map/mul | solution.py:141
  56.2 19.6 %all-gather.5.cloned.1.call-done = bf16[32,256,256]{2,1,0:T(8,128)(2,1)} async-done(((bf16[1,256,256]{2,1,0:T(8,128)(2,1)}), bf16[32,256,256]{2,1,0:T(8,128)(2,1)}) %all-gather.5.cloned.1.call-update) | async-done | bytes 4194320 | tf_op jit(solution)/shard_map/all_gather | solution.py:137
  75.9 4.0 %copy.29.sparse = bf16[4,256,1024]{2,1,0:T(8,128)(2,1)} copy(bf16[4,256,1024]{1,2,0:T(8,128)(2,1)} %bitcast_multiply_fusion) | data formatting | bytes 4194304 | tf_op jit(solution)/shard_map/optimization_barrier | solution.py:150
  79.9 0.0 copy-start
  79.9 1.6 copy-done
  81.5 18.4 %shard_map.59 = (bf16[10,256,2048]{2,1,0:T(8,128)(2,1)}, bf16[4,1024,256]{2,1,0:T(8,128)(2,1)}, f32[3,1024,256]{2,1,0:T(8,128)S(1)}) custom-call(bf16[4,256,1024]{2,1,0:T(8,128)(2,1)S(1)} %copy-done, bf16[4,2048,256]{2,1,0:T(8,128)(2,1)} %bitcast.22, bf16[4,1024,256]{2,1,0:T(8,128)(2,1)S(1)} %bitcast.15, bf16[4,8,256,256]{3,2,1,0:T(8,128)(2,1)} %bitcast.26), custom_call_target="tpu_custom_call" | custom-call | flops 8589934592 | bytes 12582912 | tf_op jit(solution)/shard_map/pallas_call | solution.py:107
  99.9 0.0 copy-start.6
  99.9 1.6 copy-done.6
  101.6 38.0 %all-gather.11.cloned.1.call-done = bf16[32,256,256]{2,1,0:T(8,128)(2,1)} async-done(((bf16[1,256,256]{2,1,0:T(8,128)(2,1)}), bf16[32,256,256]{2,1,0:T(8,128)(2,1)}) %all-gather.11.cloned.1.call-update) | async-done | bytes 4194320 | tf_op jit(solution)/shard_map/all_gather | solution.py:137
  139.6 0.0 copy-start.1
  139.6 1.6 copy-done.1
  141.2 1.9 copy-done.4
  143.1 14.9 %shard_map.60 = (bf16[10,256,2048]{2,1,0:T(8,128)(2,1)}, bf16[4,1024,256]{2,1,0:T(8,128)(2,1)}, f32[2,1024,256]{2,1,0:T(8,128)S(1)}) custom-call(bf16[4,256,1024]{2,1,0:T(8,128)(2,1)S(1)} %copy-done.1, bf16[3,2048,256]{2,1,0:T(8,128)(2,1)S(1)} %bitcast.19, bf16[4,1024,256]{2,1,0:T(8,128)(2,1)S(1)} %bitcast.16, ...), custom_call_target="tpu_custom_call", output_to_operand_aliasing={{0}: (5, {}), {1}: (6, {})} | custom-call | flops 6442450944 | bytes 12582912 | tf_op jit(solution)/shard_map/pallas_call | solution.py:107
  158.0 0.0 copy-start.7
  158.0 1.4 copy-done.7
  159.4 43.9 %all-gather.9.cloned.1.call-done = bf16[32,256,256]{2,1,0:T(8,128)(2,1)} async-done(((bf16[1,256,256]{2,1,0:T(8,128)(2,1)}), bf16[32,256,256]{2,1,0:T(8,128)(2,1)}) %all-gather.9.cloned.1.call-update) | async-done | bytes 4194320 | tf_op jit(solution)/shard_map/all_gather | solution.py:137
  203.3 1.6 copy-done.2
  204.9 1.6 copy-done.5
  206.5 1.6 copy-done.8
  208.1 10.0 %shard_map.61 = (bf16[10,256,2048]{2,1,0:T(8,128)(2,1)}, bf16[4,1024,256]{2,1,0:T(8,128)(2,1)}, f32[1,1024,256]{2,1,0:T(8,128)S(1)}) custom-call(bf16[4,256,1024]{2,1,0:T(8,128)(2,1)S(1)} %copy-done.2, bf16[2,2048,256]{2,1,0:T(8,128)(2,1)S(1)} %bitcast.20, bf16[4,1024,256]{2,1,0:T(8,128)(2,1)S(1)} %bitcast.17, ...), custom_call_target="tpu_custom_call", output_to_operand_aliasing={{0}: (5, {}), {1}: (6, {})} | custom-call | flops 4294967296 | bytes 12582912 | tf_op jit(solution)/shard_map/pallas_call | solution.py:107
  218.1 0.0 copy-start.9
  218.1 1.0 copy-done.9
  219.1 47.8 %all-gather.7.cloned.1.call-done = bf16[32,256,256]{2,1,0:T(8,128)(2,1)} async-done(((bf16[1,256,256]{2,1,0:T(8,128)(2,1)}), bf16[32,256,256]{2,1,0:T(8,128)(2,1)}) %all-gather.7.cloned.1.call-update) | async-done | bytes 4194320 | tf_op jit(solution)/shard_map/all_gather | solution.py:137
  266.9 1.6 copy-done.3
  268.5 1.2 copy-done.10
  269.7 6.7 %shard_map.62 = (bf16[10,256,2048]{2,1,0:T(8,128)(2,1)}, bf16[4,1024,256]{2,1,0:T(8,128)(2,1)}) custom-call(bf16[4,256,1024]{2,1,0:T(8,128)(2,1)S(1)} %copy-done.3, bf16[1,2048,256]{2,1,0:T(8,128)(2,1)S(1)} %bitcast.21, bf16[4,1024,256]{2,1,0:T(8,128)(2,1)S(1)} %bitcast.18, ...), custom_call_target="tpu_custom_call", output_to_operand_aliasing={{0}: (5, {}), {1}: (6, {})} | custom-call | flops 2147483648 | bytes 12582912 | tf_op jit(solution)/shard_map/pallas_call | solution.py:107
  (7 shorter events, 0.0 us)
Async XLA Ops:
  7.2 68.7 %all-gather.5.cloned.1.call-start = ((), (), s32[]{:S(2)}) async-start(), calls=%async_computation | async-start | bytes 4325376 | tf_op jit(solution)/shard_map/all_gather | solution.py:137
  9.1 130.4 %all-gather.11.cloned.1.call-start = ((), (), s32[]{:S(2)}) async-start(), calls=%async_computation.3 | async-start | bytes 4325376 | tf_op jit(solution)/shard_map/all_gather | solution.py:137
  9.9 193.4 %all-gather.9.cloned.1.call-start = ((), (), s32[]{:S(2)}) async-start(), calls=%async_computation.2 | async-start | bytes 4325376 | tf_op jit(solution)/shard_map/all_gather | solution.py:137
  10.6 256.2 %all-gather.7.cloned.1.call-start = ((), (), s32[]{:S(2)}) async-start(), calls=%async_computation.1 | async-start | bytes 4325376 | tf_op jit(solution)/shard_map/all_gather | solution.py:137
  23.3 2.3 copy-start.11
  79.9 1.6 copy-start
  99.9 1.7 copy-start.6
  139.6 1.6 copy-start.1
  141.2 1.9 copy-start.4
  158.0 1.4 copy-start.7
  203.3 1.6 copy-start.2
  204.9 1.6 copy-start.5
  206.5 1.6 copy-start.8
  218.1 1.0 copy-start.9
  266.9 1.6 copy-start.3
  268.4 1.2 copy-start.10
Sparse Core Ops, SparseCore 0:
  11.0 64.8 all-gather.4
  78.9 60.6 all-gather.10
  142.6 60.6 all-gather.8
  206.2 60.6 all-gather.6

commit v5 on v1

v5 whole, which is shorter than its diff:
```python
import functools

import jax
import jax.numpy as jnp
from jax import lax
from jax.experimental import pallas as pl
from jax.experimental.pallas import tpu as pltpu
from jax.sharding import PartitionSpec as P

CORES = 2
VMEM_LIMIT = 60 * 2**20


def plane_order(planes):
    return [
        sorted(range(planes), key=lambda p: (abs(p - z), p != (z ^ 1))) for z in range(planes)
    ]


def line_groups(order):
    groups = {}
    for z, row in enumerate(order):
        for r in range(1, len(row)):
            step = 1 if row[r] > z else -1
            held = order[z + step].index(row[r])
            groups.setdefault((abs(row[r] - z), r, held), []).append((z + step, z))
    return [(*key, groups[key]) for key in sorted(groups)]


class Gather:
    def __init__(self, block, n_layer, n_feat):
        self.n_layer, self.n_feat = n_layer, n_feat
        self.planes = n_feat // CORES
        self.order = plane_order(self.planes)
        self.plane = lax.axis_index("feat") // CORES
        self.groups = line_groups(self.order)
        self.singles = [j for j in range(1, n_layer) if j & (j - 1) == 0]
        self.others = [j for j in range(1, n_layer) if j & (j - 1) != 0]
        self.pieces = {(0, 0): block}
        self.sent = []
        self.token = None

    def tie(self, x):
        if self.token is None:
            return x
        return lax.optimization_barrier((x, self.token))[0]

    def permute(self, x, pairs):
        flat = [(l0 * self.n_feat + f0, l1 * self.n_feat + f1) for (l0, f0), (l1, f1) in pairs]
        return lax.ppermute(x, ("layer", "feat"), sorted(flat))

    def swap(self, x):
        every = [(l, f) for l in range(self.n_layer) for f in range(self.n_feat)]
        return self.permute(x, [((l, f), (l, f ^ 1)) for l, f in every])

    def across(self, r, j, bit):
        every = [(l, f) for l in range(self.n_layer) for f in range(self.n_feat)]
        x = self.tie(self.pieces[(r, j ^ bit)])
        self.sent.append(x)
        self.pieces[(r, j)] = self.permute(x, [((l, f), (l ^ bit, f)) for l, f in every])

    def straight(self, r):
        for j in self.singles:
            self.across(r, j, j)

    def diagonal(self, r):
        for j in self.others:
            bits = [1 << b for b in range(j.bit_length()) if j >> b & 1]
            self.across(r, j, bits[0] if r == 0 else bits[-1])

    def along_line(self, j, rounds, hops):
        for dist, r, held, moves in self.groups:
            if r not in rounds or dist not in hops:
                continue
            pairs = [
                ((l, a * CORES + c), (l, b * CORES + c))
                for l in range(self.n_layer)
                for a, b in moves
                for c in range(CORES)
            ]
            x = self.tie(self.pieces[(held, j)])
            self.sent.append(x)
            got = self.permute(x, pairs)
            if (r, j) in self.pieces:
                here = functools.reduce(jnp.logical_or, [self.plane == b for _, b in moves])
                got = jnp.where(here, got, self.pieces[(r, j)])
            self.pieces[(r, j)] = got


def prepare_kernel(act, blocks, sparse, mask):
    width, rows = sparse.shape[1:]
    count = blocks.shape[1]
    bits = blocks[0].astype(jnp.float32)
    turned = jnp.concatenate(
        [jnp.broadcast_to(bits[b : b + 1], (width // count, rows)) for b in range(count)], axis=0
    ).astype(jnp.bfloat16)
    sparse[0] = act[0].T * turned
    mask[0] = turned.T


def prepare(activations, active_blocks):
    layers, rows, width = activations.shape
    count = active_blocks.shape[2]

    def block(*shape):
        return pl.BlockSpec((1, *shape), lambda s: (s, 0, 0))

    return pl.pallas_call(
        prepare_kernel,
        grid=(layers,),
        in_specs=[block(rows, width), block(count, rows)],
        out_specs=(block(width, rows), block(rows, width)),
        out_shape=(
            jax.ShapeDtypeStruct((layers, width, rows), jnp.bfloat16),
            jax.ShapeDtypeStruct((layers, rows, width), jnp.bfloat16),
        ),
        cost_estimate=pl.CostEstimate(flops=0, bytes_accessed=6 * layers * rows * width, transcendentals=0),
        compiler_params=pltpu.CompilerParams(vmem_limit_bytes=VMEM_LIMIT),
    )(activations, jnp.swapaxes(active_blocks, 1, 2))


def round_kernel(n_layer, layers, first, last, meta, sparse, decoder, *refs):
    refs = list(refs)
    mask = refs.pop(0) if last else None
    acc_in = None if first else refs.pop(0)
    parts = refs[: CORES * n_layer]
    refs = refs[CORES * n_layer :]
    if not first:
        refs.pop(0)
    grad, acc_out, token = refs[:3]
    up_v, sparse_v, dec_v, acc_v, grad_v, feat_v, up_sem, dec_sem, in_sem, grad_sem, out_sem = refs[3:]
    tokens, wide = parts[0].shape[1:]
    both = CORES * wide
    width = decoder.shape[1]
    rows = n_layer * tokens
    columns = pl.ds(pl.multiple_of(meta[0] * both, both), both)
    token[...] = jnp.zeros_like(token)

    copies = [pltpu.make_async_copy(sparse, sparse_v, in_sem.at[0])]
    ups = {}
    for target in range(layers):
        ups[target] = []
        for i, part in enumerate(parts):
            core = meta[1] if i < n_layer else 1 - meta[1]
            at_rows = pl.ds(pl.multiple_of(meta[2 + i % n_layer] * tokens, tokens), tokens)
            at_cols = pl.ds(pl.multiple_of(target * both + core * wide, wide), wide)
            ups[target].append(
                pltpu.make_async_copy(
                    part.at[target], up_v.at[at_rows, at_cols], up_sem.at[target, i]
                )
            )
    decs = []
    for target in range(layers):
        for source in range(target + 1):
            pair = target * (target + 1) // 2 + source
            decs.append(
                pltpu.make_async_copy(
                    decoder.at[pair, :, columns],
                    dec_v.at[source, :, pl.ds(target * both, both)],
                    dec_sem.at[pair],
                )
            )
    copies[0].start()
    for target in reversed(range(layers)):
        for copy in ups[target]:
            copy.start()
    for copy in decs:
        copy.start()
    acc_copies = []
    if not first:
        for source in range(layers):
            acc_copies.append(
                pltpu.make_async_copy(acc_in.at[source], acc_v.at[source], in_sem.at[2 + source])
            )
            acc_copies[-1].start()
    if last:
        mask_copy = pltpu.make_async_copy(mask, feat_v, in_sem.at[1])
        mask_copy.start()
    copies[0].wait()
    outs = []
    for target in reversed(range(layers)):
        for copy in ups[target]:
            copy.wait()
        count = target + 1
        base = target * (target + 1) // 2
        for core in range(CORES):
            grad_v[pl.ds(base, count), :, core * wide : (core + 1) * wide] = (
                jnp.dot(
                    sparse_v[:count].reshape(count * width, rows),
                    up_v[:, target * both + core * wide : target * both + (core + 1) * wide],
                    preferred_element_type=jnp.float32,
                )
                .astype(jnp.bfloat16)
                .reshape(count, width, wide)
            )
        out = pltpu.make_async_copy(
            grad_v.at[pl.ds(base, count)], grad.at[pl.ds(base, count), :, columns], grad_sem.at[target]
        )
        out.start()
        outs.append(out)
    for copy in decs:
        copy.wait()
    if last:
        mask_copy.wait()
    for source in range(layers):
        total = lax.dot_general(
            up_v[:, source * both :],
            dec_v[source, :, source * both :],
            (((1,), (1,)), ((), ())),
            preferred_element_type=jnp.float32,
        )
        if not first:
            acc_copies[source].wait()
            total = acc_v[source] + total
        if last:
            feat_v[source] = (total * feat_v[source].astype(jnp.float32)).astype(jnp.bfloat16)
        else:
            acc_v[source] = total
        out = pltpu.make_async_copy(
            (feat_v if last else acc_v).at[source], acc_out.at[source], out_sem.at[source]
        )
        out.start()
        outs.append(out)
    for out in outs:
        out.wait()


def run_round(meta, sparse, decoder, mask, acc, grad, mine, theirs, last):
    first = acc is None
    layers, width, rows = sparse.shape
    wide = mine[0].shape[2]
    pairs = decoder.shape[0]
    operands = [meta, sparse, decoder]
    if last:
        operands.append(mask)
    if not first:
        operands.append(acc)
    operands += mine + theirs
    aliases = {}
    if not first:
        aliases[len(operands)] = 0
        operands.append(grad)
    any_space = pl.BlockSpec(memory_space=pl.ANY)
    both = CORES * wide
    return pl.pallas_call(
        functools.partial(round_kernel, len(mine), layers, first, last),
        out_shape=(
            jax.ShapeDtypeStruct(decoder.shape, jnp.bfloat16),
            jax.ShapeDtypeStruct((layers, rows, width), jnp.bfloat16 if last else jnp.float32),
            jax.ShapeDtypeStruct((8, 128), jnp.float32),
        ),
        in_specs=[pl.BlockSpec(memory_space=pltpu.SMEM)] + [any_space] * (len(operands) - 1),
        out_specs=(any_space, any_space, pl.BlockSpec(memory_space=pltpu.VMEM)),
        scratch_shapes=[
            pltpu.VMEM((rows, layers * both), jnp.bfloat16),
            pltpu.VMEM((layers, width, rows), jnp.bfloat16),
            pltpu.VMEM((layers, width, layers * both), jnp.bfloat16),
            pltpu.VMEM((layers, rows, width), jnp.float32),
            pltpu.VMEM((pairs, width, both), jnp.bfloat16),
            pltpu.VMEM((layers, rows, width), jnp.bfloat16),
            pltpu.SemaphoreType.DMA((layers, CORES * len(mine))),
            pltpu.SemaphoreType.DMA((pairs,)),
            pltpu.SemaphoreType.DMA((2 + layers,)),
            pltpu.SemaphoreType.DMA((layers,)),
            pltpu.SemaphoreType.DMA((layers,)),
        ],
        input_output_aliases=aliases,
        cost_estimate=pl.CostEstimate(
            flops=2 * 4 * pairs * width * rows * both, bytes_accessed=20 * 2**20, transcendentals=0
        ),
        compiler_params=pltpu.CompilerParams(vmem_limit_bytes=VMEM_LIMIT),
    )(*operands)


def body(n_layer, n_feat, activations, active_blocks, cotangent, decoder):
    blocks = Gather(cotangent, n_layer, n_feat)
    planes = blocks.planes
    end = planes - 1
    sparse, mask = prepare(activations, active_blocks)
    core = lax.axis_index("feat") % CORES
    rows = [lax.axis_index("layer") ^ j for j in range(n_layer)]
    hops = range(1, planes)
    acc = grad = None
    for r in range(planes):
        blocks.sent = []
        if r == 0:
            blocks.straight(0)
            blocks.along_line(0, range(1, planes), hops)
            for near in range(1, min(3, planes)):
                blocks.straight(near)
            blocks.diagonal(0)
            for j in blocks.others:
                blocks.along_line(j, range(1, end), [1])
        else:
            if r + 2 < planes:
                blocks.straight(r + 2)
            for j in blocks.others:
                blocks.along_line(j, range(1, end), [r + 1])
        if r == max(end - 1, 0) and end > 0:
            blocks.diagonal(end)
        mine = [blocks.pieces[(r, j)] for j in range(n_layer)]
        theirs = [blocks.swap(blocks.tie(x)) for x in mine]
        plane = jnp.asarray([row[r] for row in blocks.order], jnp.int32)[blocks.plane]
        meta = jnp.stack([plane, core] + rows).astype(jnp.int32)
        meta = lax.optimization_barrier((meta, *blocks.sent))[0]
        grad, acc, blocks.token = run_round(
            meta, sparse, decoder, mask, acc, grad, mine, theirs, r == end
        )
    return grad, acc


def solution(mesh):
    in_specs = (
        P(None, None, ("layer", "feat")),
        P(None, None, ("layer", "feat")),
        P(None, "layer", "feat"),
        P(None, ("layer", "feat"), None),
    )
    out_specs = (P(None, ("layer", "feat"), None), P(None, None, ("layer", "feat")))
    work = functools.partial(body, mesh.shape["layer"], mesh.shape["feat"])
    return jax.shard_map(work, mesh=mesh, in_specs=in_specs, out_specs=out_specs, check_vma=False)
```

time: 235 us -> 137 us (0.58)
  waiting for transfers between devices: 116 us -> 32.8 us
  Pallas kernels: 0 us -> 66.6 us
  local copies, waits for them, and re-layouts: 57.2 us -> 6.34 us
  matrix products: 36.2 us -> 0 us
  starting transfers between devices: 0.04 us -> 29.4 us
  between operations: 14.2 us -> 1.1 us
  other arithmetic: 11 us -> 0.17 us
    all_gather x1 -> x0, waiting for transfers between devices: 115 us -> none  [body(): blocks = lax.all_gather(cotangent, ('layer', 'feat'), axis=0, tiled=False)]
    pallas_call x0 -> x5, Pallas kernels: none -> 66.6 us  [the longest x4 62 us: run_round(): pl.pallas_call(functools.partial(round_kernel, len(mine), layers, first,...]
    dot_general x8 -> x0, matrix products: 36.2 us -> none  [the longest x4 21.6 us: body(): jnp.einsum('stf,td->sfd', sparse[:count], upstream[target], preferred_ele...]
    ppermute x0 -> x34, waiting for transfers between devices: none -> 32.8 us  [permute(): return lax.ppermute(x, ('layer', 'feat'), sorted(flat))]
    ppermute x0 -> x34, starting transfers between devices: none -> 29.4 us  [permute(): return lax.ppermute(x, ('layer', 'feat'), sorted(flat))]
    squeeze x3 -> x0, local copies, waits for them, and re-layouts: 22.3 us -> none  [body(): upstream[target]]
    reshape x1 -> x0, local copies, waits for them, and re-layouts: 15.8 us -> none  [body(): upstream = blocks.reshape(n_layer, n_feat, g, t, d).transpose(2, 0, 3, 1, 4)]
    unnamed x21 -> x26, local copies, waits for them, and re-layouts: 12.4 us -> 0.06 us
  transfers between devices with their start and end apart: 1 -> 34, of which waited for: 1 -> 11; matrix products, arithmetic and copies ran while one was open for 2% -> 5% of each run, Pallas kernels for 0% -> 37%
where the time goes in v5:
time: 137 us; the launch traced here: 136 us
  Pallas kernels  66.6 us (49%)
  waiting for transfers between devices  32.8 us (24%)
  starting transfers between devices  29.4 us (21%)
  local copies, waits for them, and re-layouts  6.34 us (5%)
    pallas_call x4, Pallas kernels, run_round(): pl.pallas_call(functools.partial(round_kernel, len(mine), layers, first,...  62 us
    ppermute x34, waiting for transfers between devices, permute(): return lax.ppermute(x, ('layer', 'feat'), sorted(flat))  32.8 us
    ppermute x34, starting transfers between devices, permute(): return lax.ppermute(x, ('layer', 'feat'), sorted(flat))  29.4 us
    pallas_call x1, Pallas kernels, prepare(): pl.pallas_call(prepare_kernel, grid=(layers,), in_specs=[block(rows, widt...  4.57 us
    another operation x4, local copies, waits for them, and re-layouts, body(): meta = jnp.stack([plane, core] + rows).astype(jnp.int32)  4.46 us
  transfers between devices with their start and end apart: 34, of which 11 were waited for; matrix products, arithmetic and copies ran while one was open for 5% of the time, Pallas kernels for 37%

profile of v5, /device:TPU:0, one launch (start us, length us, event | category | flops | bytes accessed | tf_op | source)
XLA Modules:
  0.0 136.4 jit_solution(10434969671172178704)
XLA Ops:
  0.6 0.7 collective-permute-start.3
  1.3 3.0 %collective-permute-start.5 = (bf16[4,256,256]{2,1,0:T(8,128)(2,1)}, bf16[4,256,256]{2,1,0:T(8,128)(2,1)S(1)}, u32[]{:S(2)}, u32[]{:S(2)}) collective-permute-start(bf16[4,256,256]{2,1,0:T(8,128)(2,1)} %refs_0_.1), channel_id=1, source_target_pairs={{0,16},{1,17},{2,18},{3,19},{4,20},{5,21},{6,22},{7,23},{8,24},{9,... | collective-permute-start | bytes 1572872 | tf_op jit(solution)/shard_map/ppermute | solution.py:50
  4.4 4.4 %collective-permute-start = (bf16[4,256,256]{2,1,0:T(8,128)(2,1)}, bf16[4,256,256]{2,1,0:T(8,128)(2,1)S(1)}, u32[]{:S(2)}, u32[]{:S(2)}) collective-permute-start(bf16[4,256,256]{2,1,0:T(8,128)(2,1)} %refs_0_.1), channel_id=1, source_target_pairs={{0,2},{1,3},{2,0},{3,1},{4,6},{5,7},{6,4},{7,5},{8,10},{9,11},{10,... | collective-permute-start | bytes 1572872 | tf_op jit(solution)/shard_map/ppermute | solution.py:50
  8.7 1.5 %collective-permute-start.7 = (bf16[4,256,256]{2,1,0:T(8,128)(2,1)}, bf16[4,256,256]{2,1,0:T(8,128)(2,1)}, u32[]{:S(2)}, u32[]{:S(2)}) collective-permute-start(bf16[4,256,256]{2,1,0:T(8,128)(2,1)} %refs_0_.1), channel_id=1, source_target_pairs={{0,8},{1,9},{2,10},{3,11},{4,12},{5,13},{6,14},{7,15},{8,0},{9,1},... | collective-permute-start | bytes 1572872 | tf_op jit(solution)/shard_map/ppermute | solution.py:50
  10.2 1.3 collective-permute-start.4
  11.5 5.0 %collective-permute-done.5.refs_2_ = bf16[4,256,256]{2,1,0:T(8,128)(2,1)S(1)} collective-permute-done((bf16[4,256,256]{2,1,0:T(8,128)(2,1)}, bf16[4,256,256]{2,1,0:T(8,128)(2,1)S(1)}, u32[]{:S(2)}, u32[]{:S(2)}) %collective-permute-start.5) | collective-permute-done | bytes 524320 | tf_op jit(solution)/shard_map/ppermute | solution.py:50
  16.5 1.7 %collective-permute-start.6 = (bf16[4,256,256]{2,1,0:T(8,128)(2,1)S(1)}, bf16[4,256,256]{2,1,0:T(8,128)(2,1)}, u32[]{:S(2)}, u32[]{:S(2)}) collective-permute-start(bf16[4,256,256]{2,1,0:T(8,128)(2,1)S(1)} %collective-permute-done.5.refs_2_), channel_id=1, source_target_pairs={{0,8},{1,9},{2,10},{3,11},{4,12},{5,13},{6,14},{7,15},{8,0},{9,1},... | collective-permute-start | bytes 1572872 | tf_op jit(solution)/shard_map/ppermute | solution.py:50
  18.2 2.1 %collective-permute-done.refs_1_ = bf16[4,256,256]{2,1,0:T(8,128)(2,1)S(1)} collective-permute-done((bf16[4,256,256]{2,1,0:T(8,128)(2,1)}, bf16[4,256,256]{2,1,0:T(8,128)(2,1)S(1)}, u32[]{:S(2)}, u32[]{:S(2)}) %collective-permute-start) | collective-permute-done | bytes 524320 | tf_op jit(solution)/shard_map/ppermute | solution.py:50
  20.3 0.7 collective-permute-start.1
  21.1 2.8 %collective-permute-done.7.refs_1_ = bf16[4,256,256]{2,1,0:T(8,128)(2,1)} collective-permute-done((bf16[4,256,256]{2,1,0:T(8,128)(2,1)}, bf16[4,256,256]{2,1,0:T(8,128)(2,1)}, u32[]{:S(2)}, u32[]{:S(2)}) %collective-permute-start.7) | collective-permute-done | bytes 524320 | tf_op jit(solution)/shard_map/ppermute | solution.py:50
  23.9 7.9 %collective-permute-done.4 = bf16[4,256,256]{2,1,0:T(8,128)(2,1)S(1)} collective-permute-done((bf16[4,256,256]{2,1,0:T(8,128)(2,1)S(1)}, bf16[4,256,256]{2,1,0:T(8,128)(2,1)S(1)}, u32[]{:S(2)}, u32[]{:S(2)}) %collective-permute-start.4) | collective-permute-done | bytes 524320 | tf_op jit(solution)/shard_map/ppermute | solution.py:50
  31.8 1.3 collective-permute-done.6.refs_3_
  33.1 4.6 %shard_map.95 = (bf16[4,256,1024]{2,1,0:T(8,128)(2,1)}, bf16[4,1024,256]{2,1,0:T(8,128)(2,1)}) custom-call(bf16[4,1024,256]{2,1,0:T(8,128)(2,1)} %act.1, s32[4,2,1024]{2,1,0:T(2,128)} %bitcast.7), custom_call_target="tpu_custom_call" | custom-call | bytes 6291456 | tf_op jit(solution)/shard_map/pallas_call | solution.py:108
  37.7 0.7 stack.49.meta
  38.4 1.6 %collective-permute-start.14 = (bf16[4,256,256]{2,1,0:T(8,128)(2,1)S(1)}, bf16[4,256,256]{2,1,0:T(8,128)(2,1)}, u32[]{:S(2)}, u32[]{:S(2)}) collective-permute-start(bf16[4,256,256]{2,1,0:T(8,128)(2,1)S(1)} %collective-permute-done.refs_1_), channel_id=1, source_target_pairs={{0,8},{1,9},{2,10},{3,11},{4,12},{5,13},{6,14},{7,15},{8,0},{9,1},... | collective-permute-start | bytes 1572872 | tf_op jit(solution)/shard_map/ppermute | solution.py:50
  40.0 0.8 collective-permute-start.15
  40.7 1.5 %collective-permute-start.16 = (bf16[4,256,256]{2,1,0:T(8,128)(2,1)}, bf16[4,256,256]{2,1,0:T(8,128)(2,1)}, u32[]{:S(2)}, u32[]{:S(2)}) collective-permute-start(bf16[4,256,256]{2,1,0:T(8,128)(2,1)} %collective-permute-done.6.refs_3_), channel_id=1, source_target_pairs={{0,2},{1,3},{2,0},{3,1},{4,6},{5,7},{6,4},{7,5},{8,10},{9,11},{10,... | collective-permute-start | bytes 1572872 | tf_op jit(solution)/shard_map/ppermute | solution.py:50
  42.2 0.7 collective-permute-start.13
  42.9 1.3 collective-permute-start.2
  44.3 13.2 %shard_map.96 = (bf16[10,256,2048]{2,1,0:T(8,128)(2,1)}, f32[4,1024,256]{2,1,0:T(8,128)}, f32[8,128]{1,0:T(8,128)}) custom-call(s32[6]{0:T(128)} %stack.49.meta, bf16[4,256,1024]{2,1,0:T(8,128)(2,1)} %get-tuple-element.33.sparse, bf16[10,256,2048]{2,1,0:T(8,128)(2,1)} %decoder.7, bf16[4,256,256]{2,1,0:T(8,128)(2,1)} %refs_0_.1, ...), custom_call_target="tpu_custom_call" | custom-call | flops 10737418240 | bytes 20971520 | tf_op jit(solution)/shard_map/pallas_call | solution.py:245
  57.6 0.5 collective-permute-start.18
  58.1 0.1 collective-permute-start.19
  58.2 0.4 collective-permute-start.17
  58.6 0.6 dynamic_slice.15
  59.2 1.3 stack.50.meta
  60.5 5.2 %collective-permute-done.2 = bf16[4,256,256]{2,1,0:T(8,128)(2,1)S(1)} collective-permute-done((bf16[4,256,256]{2,1,0:T(8,128)(2,1)S(1)}, bf16[4,256,256]{2,1,0:T(8,128)(2,1)S(1)}, u32[]{:S(2)}, u32[]{:S(2)}) %collective-permute-start.2) | collective-permute-done | bytes 524320 | tf_op jit(solution)/shard_map/ppermute | solution.py:50
  65.7 1.5 %collective-permute-start.22 = (bf16[4,256,256]{2,1,0:T(8,128)(2,1)S(1)}, bf16[4,256,256]{2,1,0:T(8,128)(2,1)}, u32[]{:S(2)}, u32[]{:S(2)}) collective-permute-start(bf16[4,256,256]{2,1,0:T(8,128)(2,1)S(1)} %broadcast_select_fusion.1.refs_1_), channel_id=1, source_target_pairs={{0,16},{1,17},{2,18},{3,19},{4,20},{5,21},{6,22},{7,23},{8,24},{9,... | collective-permute-start | bytes 1572872 | tf_op jit(solution)/shard_map/ppermute | solution.py:50
  67.3 0.6 collective-permute-start.21
  67.9 1.5 %collective-permute-start.23 = (bf16[4,256,256]{2,1,0:T(8,128)(2,1)S(1)}, bf16[4,256,256]{2,1,0:T(8,128)(2,1)S(1)}, u32[]{:S(2)}, u32[]{:S(2)}) collective-permute-start(bf16[4,256,256]{2,1,0:T(8,128)(2,1)S(1)} %collective-permute-done.13), channel_id=1, source_target_pairs={{2,0},{3,1},{4,6},{5,7},{10,8},{11,9},{12,14},{13,15},{18,16},{19,... | collective-permute-start | bytes 1572872 | tf_op jit(solution)/shard_map/ppermute | solution.py:50
  69.4 1.6 %collective-permute-start.12 = (bf16[4,256,256]{2,1,0:T(8,128)(2,1)S(1)}, bf16[4,256,256]{2,1,0:T(8,128)(2,1)S(1)}, u32[]{:S(2)}, u32[]{:S(2)}) collective-permute-start(bf16[4,256,256]{2,1,0:T(8,128)(2,1)S(1)} %broadcast_select_fusion.2.refs_2_), channel_id=1, source_target_pairs={{0,8},{1,9},{2,10},{3,11},{4,12},{5,13},{6,14},{7,15},{8,0},{9,1},... | collective-permute-start | bytes 1572872 | tf_op jit(solution)/shard_map/ppermute | solution.py:50
  71.0 16.3 %shard_map.97 = (bf16[10,256,2048]{2,1,0:T(8,128)(2,1)}, f32[4,1024,256]{2,1,0:T(8,128)}, f32[8,128]{1,0:T(8,128)}) custom-call(s32[6]{0:T(128)} %stack.50.meta, bf16[4,256,1024]{2,1,0:T(8,128)(2,1)} %get-tuple-element.33.sparse, bf16[10,256,2048]{2,1,0:T(8,128)(2,1)} %decoder.7, ...), custom_call_target="tpu_custom_call", output_to_operand_aliasing={{0}: (12, {})} | custom-call | flops 10737418240 | bytes 20971520 | tf_op jit(solution)/shard_map/pallas_call | solution.py:245
  87.4 0.5 collective-permute-start.26
  88.0 0.4 collective-permute-start.24
  88.4 0.7 dynamic_slice.13
  89.1 1.3 stack.48.meta
  90.3 0.9 collective-permute-done.12.refs_3_
  91.2 0.3 collective-permute-start.28
  91.5 1.7 %collective-permute-start.29 = (bf16[4,256,256]{2,1,0:T(8,128)(2,1)S(1)}, bf16[4,256,256]{2,1,0:T(8,128)(2,1)S(1)}, u32[]{:S(2)}, u32[]{:S(2)}) collective-permute-start(bf16[4,256,256]{2,1,0:T(8,128)(2,1)S(1)} %collective-permute-done.12.refs_3_), channel_id=1, source_target_pairs={{0,16},{1,17},{2,18},{3,19},{4,20},{5,21},{6,22},{7,23},{8,24},{9,... | collective-permute-start | bytes 1572872 | tf_op jit(solution)/shard_map/ppermute | solution.py:50
  93.3 16.1 %shard_map.98 = (bf16[10,256,2048]{2,1,0:T(8,128)(2,1)}, f32[4,1024,256]{2,1,0:T(8,128)}, f32[8,128]{1,0:T(8,128)}) custom-call(s32[6]{0:T(128)} %stack.48.meta, bf16[4,256,1024]{2,1,0:T(8,128)(2,1)} %get-tuple-element.33.sparse, bf16[10,256,2048]{2,1,0:T(8,128)(2,1)} %decoder.7, ...), custom_call_target="tpu_custom_call", output_to_operand_aliasing={{0}: (12, {})} | custom-call | flops 10737418240 | bytes 20971520 | tf_op jit(solution)/shard_map/pallas_call | solution.py:245
  109.4 6.1 %collective-permute-done.29.refs_5_ = bf16[4,256,256]{2,1,0:T(8,128)(2,1)S(1)} collective-permute-done((bf16[4,256,256]{2,1,0:T(8,128)(2,1)S(1)}, bf16[4,256,256]{2,1,0:T(8,128)(2,1)S(1)}, u32[]{:S(2)}, u32[]{:S(2)}) %collective-permute-start.29) | collective-permute-done | bytes 524320 | tf_op jit(solution)/shard_map/ppermute | solution.py:50
  115.5 0.5 collective-permute-start.32
  116.1 0.4 collective-permute-start.30
  116.5 0.6 dynamic_slice.12
  117.1 1.3 stack.23.meta
  118.4 0.5 collective-permute-done.32.refs_8_
  118.9 0.1 collective-permute-done.31.refs_7_
  119.0 0.8 collective-permute-done.30.refs_6_
  119.8 16.4 %shard_map.99 = (bf16[10,256,2048]{2,1,0:T(8,128)(2,1)}, bf16[4,1024,256]{2,1,0:T(8,128)(2,1)}, f32[8,128]{1,0:T(8,128)}) custom-call(s32[6]{0:T(128)} %stack.23.meta, bf16[4,256,1024]{2,1,0:T(8,128)(2,1)} %get-tuple-element.33.sparse, bf16[10,256,2048]{2,1,0:T(8,128)(2,1)} %decoder.7, ...), custom_call_target="tpu_custom_call", output_to_operand_aliasing={{0}: (13, {})} | custom-call | flops 10737418240 | bytes 20971520 | tf_op jit(solution)/shard_map/pallas_call | solution.py:245
  (61 shorter events, 0.7 us)
Async XLA Ops:
  0.6 9.6 %collective-permute-start.3 = (bf16[4,256,256]{2,1,0:T(8,128)(2,1)}, bf16[4,256,256]{2,1,0:T(8,128)(2,1)S(1)}, u32[]{:S(2)}, u32[]{:S(2)}) collective-permute-start(bf16[4,256,256]{2,1,0:T(8,128)(2,1)} %refs_0_.1), channel_id=1, source_target_pairs={{2,4},{3,5},{4,2},{5,3},{10,12},{11,13},{12,10},{13,11},{18,20},{1... | collective-permute-start | bytes 1572872 | tf_op jit(solution)/shard_map/ppermute | solution.py:50
  1.3 15.2 %collective-permute-start.5 = (bf16[4,256,256]{2,1,0:T(8,128)(2,1)}, bf16[4,256,256]{2,1,0:T(8,128)(2,1)S(1)}, u32[]{:S(2)}, u32[]{:S(2)}) collective-permute-start(bf16[4,256,256]{2,1,0:T(8,128)(2,1)} %refs_0_.1), channel_id=1, source_target_pairs={{0,16},{1,17},{2,18},{3,19},{4,20},{5,21},{6,22},{7,23},{8,24},{9,... | collective-permute-start | bytes 1572872 | tf_op jit(solution)/shard_map/ppermute | solution.py:50
  4.4 16.0 %collective-permute-start = (bf16[4,256,256]{2,1,0:T(8,128)(2,1)}, bf16[4,256,256]{2,1,0:T(8,128)(2,1)S(1)}, u32[]{:S(2)}, u32[]{:S(2)}) collective-permute-start(bf16[4,256,256]{2,1,0:T(8,128)(2,1)} %refs_0_.1), channel_id=1, source_target_pairs={{0,2},{1,3},{2,0},{3,1},{4,6},{5,7},{6,4},{7,5},{8,10},{9,11},{10,... | collective-permute-start | bytes 1572872 | tf_op jit(solution)/shard_map/ppermute | solution.py:50
  8.7 15.2 %collective-permute-start.7 = (bf16[4,256,256]{2,1,0:T(8,128)(2,1)}, bf16[4,256,256]{2,1,0:T(8,128)(2,1)}, u32[]{:S(2)}, u32[]{:S(2)}) collective-permute-start(bf16[4,256,256]{2,1,0:T(8,128)(2,1)} %refs_0_.1), channel_id=1, source_target_pairs={{0,8},{1,9},{2,10},{3,11},{4,12},{5,13},{6,14},{7,15},{8,0},{9,1},... | collective-permute-start | bytes 1572872 | tf_op jit(solution)/shard_map/ppermute | solution.py:50
  10.2 21.6 %collective-permute-start.4 = (bf16[4,256,256]{2,1,0:T(8,128)(2,1)S(1)}, bf16[4,256,256]{2,1,0:T(8,128)(2,1)S(1)}, u32[]{:S(2)}, u32[]{:S(2)}) collective-permute-start(bf16[4,256,256]{2,1,0:T(8,128)(2,1)S(1)} %collective-permute-done.3), channel_id=1, source_target_pairs={{2,0},{3,1},{4,6},{5,7},{10,8},{11,9},{12,14},{13,15},{18,16},{19,... | collective-permute-start | bytes 1572872 | tf_op jit(solution)/shard_map/ppermute | solution.py:50
  16.5 26.4 %copy-start.4 = (bf16[4,256,256]{2,1,0:T(8,128)(2,1)}, bf16[4,256,256]{2,1,0:T(8,128)(2,1)S(1)}, u32[]{:S(2)}) copy-start(bf16[4,256,256]{2,1,0:T(8,128)(2,1)S(1)} %collective-permute-done.5.refs_2_) | copy-start | bytes 1572868
  16.5 16.6 %collective-permute-start.6 = (bf16[4,256,256]{2,1,0:T(8,128)(2,1)S(1)}, bf16[4,256,256]{2,1,0:T(8,128)(2,1)}, u32[]{:S(2)}, u32[]{:S(2)}) collective-permute-start(bf16[4,256,256]{2,1,0:T(8,128)(2,1)S(1)} %collective-permute-done.5.refs_2_), channel_id=1, source_target_pairs={{0,8},{1,9},{2,10},{3,11},{4,12},{5,13},{6,14},{7,15},{8,0},{9,1},... | collective-permute-start | bytes 1572872 | tf_op jit(solution)/shard_map/ppermute | solution.py:50
  20.3 37.9 %copy-start.3 = (bf16[4,256,256]{2,1,0:T(8,128)(2,1)}, bf16[4,256,256]{2,1,0:T(8,128)(2,1)S(1)}, u32[]{:S(2)}) copy-start(bf16[4,256,256]{2,1,0:T(8,128)(2,1)S(1)} %collective-permute-done.refs_1_) | copy-start | bytes 1572868
  20.3 18.1 %collective-permute-start.1 = (bf16[4,256,256]{2,1,0:T(8,128)(2,1)S(1)}, bf16[4,256,256]{2,1,0:T(8,128)(2,1)S(1)}, u32[]{:S(2)}, u32[]{:S(2)}) collective-permute-start(bf16[4,256,256]{2,1,0:T(8,128)(2,1)S(1)} %collective-permute-done.refs_1_), channel_id=1, source_target_pairs={{2,4},{3,5},{4,2},{5,3},{10,12},{11,13},{12,10},{13,11},{18,20},{1... | collective-permute-start | bytes 1572872 | tf_op jit(solution)/shard_map/ppermute | solution.py:50
  21.0 18.9 %collective-permute-start.8 = (bf16[4,256,256]{2,1,0:T(8,128)(2,1)}, bf16[4,256,256]{2,1,0:T(8,128)(2,1)}, u32[]{:S(2)}, u32[]{:S(2)}) collective-permute-start(bf16[4,256,256]{2,1,0:T(8,128)(2,1)} %refs_0_.1), channel_id=1, source_target_pairs={{0,1},{1,0},{2,3},{3,2},{4,5},{5,4},{6,7},{7,6},{8,9},{9,8},{10,11... | collective-permute-start | bytes 1572872 | tf_op jit(solution)/shard_map/ppermute | solution.py:50
  23.9 16.8 %collective-permute-start.10 = (bf16[4,256,256]{2,1,0:T(8,128)(2,1)S(1)}, bf16[4,256,256]{2,1,0:T(8,128)(2,1)}, u32[]{:S(2)}, u32[]{:S(2)}) collective-permute-start(bf16[4,256,256]{2,1,0:T(8,128)(2,1)S(1)} %collective-permute-done.5.refs_2_), channel_id=1, source_target_pairs={{0,1},{1,0},{2,3},{3,2},{4,5},{5,4},{6,7},{7,6},{8,9},{9,8},{10,11... | collective-permute-start | bytes 1572872 | tf_op jit(solution)/shard_map/ppermute | solution.py:50
  31.8 10.4 %collective-permute-start.9 = (bf16[4,256,256]{2,1,0:T(8,128)(2,1)}, bf16[4,256,256]{2,1,0:T(8,128)(2,1)}, u32[]{:S(2)}, u32[]{:S(2)}) collective-permute-start(bf16[4,256,256]{2,1,0:T(8,128)(2,1)} %collective-permute-done.7.refs_1_), channel_id=1, source_target_pairs={{0,1},{1,0},{2,3},{3,2},{4,5},{5,4},{6,7},{7,6},{8,9},{9,8},{10,11... | collective-permute-start | bytes 1572872 | tf_op jit(solution)/shard_map/ppermute | solution.py:50
  33.1 9.8 %collective-permute-start.11 = (bf16[4,256,256]{2,1,0:T(8,128)(2,1)}, bf16[4,256,256]{2,1,0:T(8,128)(2,1)}, u32[]{:S(2)}, u32[]{:S(2)}) collective-permute-start(bf16[4,256,256]{2,1,0:T(8,128)(2,1)} %collective-permute-done.6.refs_3_), channel_id=1, source_target_pairs={{0,1},{1,0},{2,3},{3,2},{4,5},{5,4},{6,7},{7,6},{8,9},{9,8},{10,11... | collective-permute-start | bytes 1572872 | tf_op jit(solution)/shard_map/ppermute | solution.py:50
  38.4 49.6 %copy-start = (bf16[4,256,256]{2,1,0:T(8,128)(2,1)}, bf16[4,256,256]{2,1,0:T(8,128)(2,1)S(1)}, u32[]{:S(2)}) copy-start(bf16[4,256,256]{2,1,0:T(8,128)(2,1)S(1)} %broadcast_select_fusion.1.refs_1_) | copy-start | bytes 1572868
  38.4 19.2 %collective-permute-start.14 = (bf16[4,256,256]{2,1,0:T(8,128)(2,1)S(1)}, bf16[4,256,256]{2,1,0:T(8,128)(2,1)}, u32[]{:S(2)}, u32[]{:S(2)}) collective-permute-start(bf16[4,256,256]{2,1,0:T(8,128)(2,1)S(1)} %collective-permute-done.refs_1_), channel_id=1, source_target_pairs={{0,8},{1,9},{2,10},{3,11},{4,12},{5,13},{6,14},{7,15},{8,0},{9,1},... | collective-permute-start | bytes 1572872 | tf_op jit(solution)/shard_map/ppermute | solution.py:50
  40.0 18.1 %collective-permute-start.15 = (bf16[4,256,256]{2,1,0:T(8,128)(2,1)S(1)}, bf16[4,256,256]{2,1,0:T(8,128)(2,1)}, u32[]{:S(2)}, u32[]{:S(2)}) collective-permute-start(bf16[4,256,256]{2,1,0:T(8,128)(2,1)S(1)} %collective-permute-done.refs_1_), channel_id=1, source_target_pairs={{0,16},{1,17},{2,18},{3,19},{4,20},{5,21},{6,22},{7,23},{8,24},{9,... | collective-permute-start | bytes 1572872 | tf_op jit(solution)/shard_map/ppermute | solution.py:50
  40.7 16.8 %collective-permute-start.16 = (bf16[4,256,256]{2,1,0:T(8,128)(2,1)}, bf16[4,256,256]{2,1,0:T(8,128)(2,1)}, u32[]{:S(2)}, u32[]{:S(2)}) collective-permute-start(bf16[4,256,256]{2,1,0:T(8,128)(2,1)} %collective-permute-done.6.refs_3_), channel_id=1, source_target_pairs={{0,2},{1,3},{2,0},{3,1},{4,6},{5,7},{6,4},{7,5},{8,10},{9,11},{10,... | collective-permute-start | bytes 1572872 | tf_op jit(solution)/shard_map/ppermute | solution.py:50
  42.2 16.0 %collective-permute-start.13 = (bf16[4,256,256]{2,1,0:T(8,128)(2,1)}, bf16[4,256,256]{2,1,0:T(8,128)(2,1)S(1)}, u32[]{:S(2)}, u32[]{:S(2)}) collective-permute-start(bf16[4,256,256]{2,1,0:T(8,128)(2,1)} %collective-permute-done.6.refs_3_), channel_id=1, source_target_pairs={{2,4},{3,5},{4,2},{5,3},{10,12},{11,13},{12,10},{13,11},{18,20},{1... | collective-permute-start | bytes 1572872 | tf_op jit(solution)/shard_map/ppermute | solution.py:50
  42.9 22.8 %collective-permute-start.2 = (bf16[4,256,256]{2,1,0:T(8,128)(2,1)S(1)}, bf16[4,256,256]{2,1,0:T(8,128)(2,1)S(1)}, u32[]{:S(2)}, u32[]{:S(2)}) collective-permute-start(bf16[4,256,256]{2,1,0:T(8,128)(2,1)S(1)} %collective-permute-done.1), channel_id=1, source_target_pairs={{2,0},{3,1},{4,6},{5,7},{10,8},{11,9},{12,14},{13,15},{18,16},{19,... | collective-permute-start | bytes 1572872 | tf_op jit(solution)/shard_map/ppermute | solution.py:50
  44.2 14.4 %copy-start.12 = (s32[4]{0:T(128)S(1)}, s32[4]{0:T(128)}, u32[]{:S(2)}) copy-start(s32[4]{0:T(128)} %constant.46.clone) | copy-start | bytes 52
  57.5 9.8 %collective-permute-start.20 = (bf16[4,256,256]{2,1,0:T(8,128)(2,1)}, bf16[4,256,256]{2,1,0:T(8,128)(2,1)}, u32[]{:S(2)}, u32[]{:S(2)}) collective-permute-start(bf16[4,256,256]{2,1,0:T(8,128)(2,1)} %collective-permute-done.16.refs_4_), channel_id=1, source_target_pairs={{0,1},{1,0},{2,3},{3,2},{4,5},{5,4},{6,7},{7,6},{8,9},{9,8},{10,11... | collective-permute-start | bytes 1572872 | tf_op jit(solution)/shard_map/ppermute | solution.py:50
  57.6 10.3 %collective-permute-start.18 = (bf16[4,256,256]{2,1,0:T(8,128)(2,1)}, bf16[4,256,256]{2,1,0:T(8,128)(2,1)}, u32[]{:S(2)}, u32[]{:S(2)}) collective-permute-start(bf16[4,256,256]{2,1,0:T(8,128)(2,1)} %collective-permute-done.14.refs_2_), channel_id=1, source_target_pairs={{0,1},{1,0},{2,3},{3,2},{4,5},{5,4},{6,7},{7,6},{8,9},{9,8},{10,11... | collective-permute-start | bytes 1572872 | tf_op jit(solution)/shard_map/ppermute | solution.py:50
  58.1 11.3 %collective-permute-start.19 = (bf16[4,256,256]{2,1,0:T(8,128)(2,1)}, bf16[4,256,256]{2,1,0:T(8,128)(2,1)}, u32[]{:S(2)}, u32[]{:S(2)}) collective-permute-start(bf16[4,256,256]{2,1,0:T(8,128)(2,1)} %collective-permute-done.15.refs_3_), channel_id=1, source_target_pairs={{0,1},{1,0},{2,3},{3,2},{4,5},{5,4},{6,7},{7,6},{8,9},{9,8},{10,11... | collective-permute-start | bytes 1572872 | tf_op jit(solution)/shard_map/ppermute | solution.py:50
  58.2 12.8 %collective-permute-start.17 = (bf16[4,256,256]{2,1,0:T(8,128)(2,1)S(1)}, bf16[4,256,256]{2,1,0:T(8,128)(2,1)}, u32[]{:S(2)}, u32[]{:S(2)}) collective-permute-start(bf16[4,256,256]{2,1,0:T(8,128)(2,1)S(1)} %collective-permute-done.refs_1_), channel_id=1, source_target_pairs={{0,1},{1,0},{2,3},{3,2},{4,5},{5,4},{6,7},{7,6},{8,9},{9,8},{10,11... | collective-permute-start | bytes 1572872 | tf_op jit(solution)/shard_map/ppermute | solution.py:50
  65.7 21.7 %collective-permute-start.22 = (bf16[4,256,256]{2,1,0:T(8,128)(2,1)S(1)}, bf16[4,256,256]{2,1,0:T(8,128)(2,1)}, u32[]{:S(2)}, u32[]{:S(2)}) collective-permute-start(bf16[4,256,256]{2,1,0:T(8,128)(2,1)S(1)} %broadcast_select_fusion.1.refs_1_), channel_id=1, source_target_pairs={{0,16},{1,17},{2,18},{3,19},{4,20},{5,21},{6,22},{7,23},{8,24},{9,... | collective-permute-start | bytes 1572872 | tf_op jit(solution)/shard_map/ppermute | solution.py:50
  67.3 48.8 %copy-start.1 = (bf16[4,256,256]{2,1,0:T(8,128)(2,1)}, bf16[4,256,256]{2,1,0:T(8,128)(2,1)S(1)}, u32[]{:S(2)}) copy-start(bf16[4,256,256]{2,1,0:T(8,128)(2,1)S(1)} %broadcast_select_fusion.2.refs_2_) | copy-start | bytes 1572868
  67.3 20.6 %collective-permute-start.21 = (bf16[4,256,256]{2,1,0:T(8,128)(2,1)S(1)}, bf16[4,256,256]{2,1,0:T(8,128)(2,1)}, u32[]{:S(2)}, u32[]{:S(2)}) collective-permute-start(bf16[4,256,256]{2,1,0:T(8,128)(2,1)S(1)} %broadcast_select_fusion.1.refs_1_), channel_id=1, source_target_pairs={{0,8},{1,9},{2,10},{3,11},{4,12},{5,13},{6,14},{7,15},{8,0},{9,1},... | collective-permute-start | bytes 1572872 | tf_op jit(solution)/shard_map/ppermute | solution.py:50
  67.9 19.3 %collective-permute-start.23 = (bf16[4,256,256]{2,1,0:T(8,128)(2,1)S(1)}, bf16[4,256,256]{2,1,0:T(8,128)(2,1)S(1)}, u32[]{:S(2)}, u32[]{:S(2)}) collective-permute-start(bf16[4,256,256]{2,1,0:T(8,128)(2,1)S(1)} %collective-permute-done.13), channel_id=1, source_target_pairs={{2,0},{3,1},{4,6},{5,7},{10,8},{11,9},{12,14},{13,15},{18,16},{19,... | collective-permute-start | bytes 1572872 | tf_op jit(solution)/shard_map/ppermute | solution.py:50
  69.4 21.8 %collective-permute-start.12 = (bf16[4,256,256]{2,1,0:T(8,128)(2,1)S(1)}, bf16[4,256,256]{2,1,0:T(8,128)(2,1)S(1)}, u32[]{:S(2)}, u32[]{:S(2)}) collective-permute-start(bf16[4,256,256]{2,1,0:T(8,128)(2,1)S(1)} %broadcast_select_fusion.2.refs_2_), channel_id=1, source_target_pairs={{0,8},{1,9},{2,10},{3,11},{4,12},{5,13},{6,14},{7,15},{8,0},{9,1},... | collective-permute-start | bytes 1572872 | tf_op jit(solution)/shard_map/ppermute | solution.py:50
  71.0 17.4 %copy-start.11 = (s32[4]{0:T(128)S(1)}, s32[4]{0:T(128)}, u32[]{:S(2)}) copy-start(s32[4]{0:T(128)} %constant.47.clone) | copy-start | bytes 52
  87.3 6.0 %copy-start.2 = (bf16[4,256,256]{2,1,0:T(8,128)(2,1)}, bf16[4,256,256]{2,1,0:T(8,128)(2,1)S(1)}, u32[]{:S(2)}) copy-start(bf16[4,256,256]{2,1,0:T(8,128)(2,1)S(1)} %broadcast_select_fusion.refs_4_) | copy-start | bytes 1572868
  87.3 4.2 %collective-permute-start.27 = (bf16[4,256,256]{2,1,0:T(8,128)(2,1)S(1)}, bf16[4,256,256]{2,1,0:T(8,128)(2,1)}, u32[]{:S(2)}, u32[]{:S(2)}) collective-permute-start(bf16[4,256,256]{2,1,0:T(8,128)(2,1)S(1)} %broadcast_select_fusion.refs_4_), channel_id=1, source_target_pairs={{0,1},{1,0},{2,3},{3,2},{4,5},{5,4},{6,7},{7,6},{8,9},{9,8},{10,11... | collective-permute-start | bytes 1572872 | tf_op jit(solution)/shard_map/ppermute | solution.py:50
  87.4 5.9 %collective-permute-start.26 = (bf16[4,256,256]{2,1,0:T(8,128)(2,1)}, bf16[4,256,256]{2,1,0:T(8,128)(2,1)}, u32[]{:S(2)}, u32[]{:S(2)}) collective-permute-start(bf16[4,256,256]{2,1,0:T(8,128)(2,1)} %collective-permute-done.22.refs_3_), channel_id=1, source_target_pairs={{0,1},{1,0},{2,3},{3,2},{4,5},{5,4},{6,7},{7,6},{8,9},{9,8},{10,11... | collective-permute-start | bytes 1572872 | tf_op jit(solution)/shard_map/ppermute | solution.py:50
  87.9 5.4 %collective-permute-start.25 = (bf16[4,256,256]{2,1,0:T(8,128)(2,1)}, bf16[4,256,256]{2,1,0:T(8,128)(2,1)}, u32[]{:S(2)}, u32[]{:S(2)}) collective-permute-start(bf16[4,256,256]{2,1,0:T(8,128)(2,1)} %collective-permute-done.21.refs_2_), channel_id=1, source_target_pairs={{0,1},{1,0},{2,3},{3,2},{4,5},{5,4},{6,7},{7,6},{8,9},{9,8},{10,11... | collective-permute-start | bytes 1572872 | tf_op jit(solution)/shard_map/ppermute | solution.py:50
  88.0 5.3 %collective-permute-start.24 = (bf16[4,256,256]{2,1,0:T(8,128)(2,1)S(1)}, bf16[4,256,256]{2,1,0:T(8,128)(2,1)}, u32[]{:S(2)}, u32[]{:S(2)}) collective-permute-start(bf16[4,256,256]{2,1,0:T(8,128)(2,1)S(1)} %broadcast_select_fusion.1.refs_1_), channel_id=1, source_target_pairs={{0,1},{1,0},{2,3},{3,2},{4,5},{5,4},{6,7},{7,6},{8,9},{9,8},{10,11... | collective-permute-start | bytes 1572872 | tf_op jit(solution)/shard_map/ppermute | solution.py:50
  91.2 24.7 %copy-start.5 = (bf16[4,256,256]{2,1,0:T(8,128)(2,1)}, bf16[4,256,256]{2,1,0:T(8,128)(2,1)S(1)}, u32[]{:S(2)}) copy-start(bf16[4,256,256]{2,1,0:T(8,128)(2,1)S(1)} %collective-permute-done.12.refs_3_) | copy-start | bytes 1572868
  91.2 24.2 %collective-permute-start.28 = (bf16[4,256,256]{2,1,0:T(8,128)(2,1)S(1)}, bf16[4,256,256]{2,1,0:T(8,128)(2,1)S(1)}, u32[]{:S(2)}, u32[]{:S(2)}) collective-permute-start(bf16[4,256,256]{2,1,0:T(8,128)(2,1)S(1)} %broadcast_select_fusion.2.refs_2_), channel_id=1, source_target_pairs={{0,16},{1,17},{2,18},{3,19},{4,20},{5,21},{6,22},{7,23},{8,24},{9,... | collective-permute-start | bytes 1572872 | tf_op jit(solution)/shard_map/ppermute | solution.py:50
  91.5 23.9 %collective-permute-start.29 = (bf16[4,256,256]{2,1,0:T(8,128)(2,1)S(1)}, bf16[4,256,256]{2,1,0:T(8,128)(2,1)S(1)}, u32[]{:S(2)}, u32[]{:S(2)}) collective-permute-start(bf16[4,256,256]{2,1,0:T(8,128)(2,1)S(1)} %collective-permute-done.12.refs_3_), channel_id=1, source_target_pairs={{0,16},{1,17},{2,18},{3,19},{4,20},{5,21},{6,22},{7,23},{8,24},{9,... | collective-permute-start | bytes 1572872 | tf_op jit(solution)/shard_map/ppermute | solution.py:50
  93.3 23.2 %copy-start.10 = (s32[4]{0:T(128)S(1)}, s32[4]{0:T(128)}, u32[]{:S(2)}) copy-start(s32[4]{0:T(128)} %constant.48.clone) | copy-start | bytes 52
  115.5 4.3 %copy-start.7 = (bf16[4,256,256]{2,1,0:T(8,128)(2,1)}, bf16[4,256,256]{2,1,0:T(8,128)(2,1)S(1)}, u32[]{:S(2)}) copy-start(bf16[4,256,256]{2,1,0:T(8,128)(2,1)S(1)} %collective-permute-done.29.refs_5_) | copy-start | bytes 1572868
  115.5 2.9 %collective-permute-start.33 = (bf16[4,256,256]{2,1,0:T(8,128)(2,1)S(1)}, bf16[4,256,256]{2,1,0:T(8,128)(2,1)S(1)}, u32[]{:S(2)}, u32[]{:S(2)}) collective-permute-start(bf16[4,256,256]{2,1,0:T(8,128)(2,1)S(1)} %collective-permute-done.29.refs_5_), channel_id=1, source_target_pairs={{0,1},{1,0},{2,3},{3,2},{4,5},{5,4},{6,7},{7,6},{8,9},{9,8},{10,11... | collective-permute-start | bytes 1572872 | tf_op jit(solution)/shard_map/ppermute | solution.py:50
  115.5 4.3 %copy-start.6 = (bf16[4,256,256]{2,1,0:T(8,128)(2,1)}, bf16[4,256,256]{2,1,0:T(8,128)(2,1)S(1)}, u32[]{:S(2)}) copy-start(bf16[4,256,256]{2,1,0:T(8,128)(2,1)S(1)} %collective-permute-done.28.refs_4_) | copy-start | bytes 1572868
  115.5 3.4 %collective-permute-start.32 = (bf16[4,256,256]{2,1,0:T(8,128)(2,1)S(1)}, bf16[4,256,256]{2,1,0:T(8,128)(2,1)S(1)}, u32[]{:S(2)}, u32[]{:S(2)}) collective-permute-start(bf16[4,256,256]{2,1,0:T(8,128)(2,1)S(1)} %collective-permute-done.28.refs_4_), channel_id=1, source_target_pairs={{0,1},{1,0},{2,3},{3,2},{4,5},{5,4},{6,7},{7,6},{8,9},{9,8},{10,11... | collective-permute-start | bytes 1572872 | tf_op jit(solution)/shard_map/ppermute | solution.py:50
  116.0 3.0 %collective-permute-start.31 = (bf16[4,256,256]{2,1,0:T(8,128)(2,1)S(1)}, bf16[4,256,256]{2,1,0:T(8,128)(2,1)}, u32[]{:S(2)}, u32[]{:S(2)}) collective-permute-start(bf16[4,256,256]{2,1,0:T(8,128)(2,1)S(1)} %collective-permute-done.12.refs_3_), channel_id=1, source_target_pairs={{0,1},{1,0},{2,3},{3,2},{4,5},{5,4},{6,7},{7,6},{8,9},{9,8},{10,11... | collective-permute-start | bytes 1572872 | tf_op jit(solution)/shard_map/ppermute | solution.py:50
  116.1 3.7 %collective-permute-start.30 = (bf16[4,256,256]{2,1,0:T(8,128)(2,1)S(1)}, bf16[4,256,256]{2,1,0:T(8,128)(2,1)}, u32[]{:S(2)}, u32[]{:S(2)}) collective-permute-start(bf16[4,256,256]{2,1,0:T(8,128)(2,1)S(1)} %broadcast_select_fusion.2.refs_2_), channel_id=1, source_target_pairs={{0,1},{1,0},{2,3},{3,2},{4,5},{5,4},{6,7},{7,6},{8,9},{9,8},{10,11... | collective-permute-start | bytes 1572872 | tf_op jit(solution)/shard_map/ppermute | solution.py:50
  118.4 1.4 %copy-start.8 = (bf16[4,256,256]{2,1,0:T(8,128)(2,1)}, bf16[4,256,256]{2,1,0:T(8,128)(2,1)S(1)}, u32[]{:S(2)}) copy-start(bf16[4,256,256]{2,1,0:T(8,128)(2,1)S(1)} %collective-permute-done.33.refs_9_) | copy-start | bytes 1572868
  118.9 0.9 copy-start.9

commit v6 on v5

--- a/solution.py
+++ b/solution.py
@@ -9,6 +9,7 @@
 
 CORES = 2
 VMEM_LIMIT = 60 * 2**20
+CHUNK = 256
 
 
 def plane_order(planes):
@@ -28,7 +29,8 @@
 
 
 class Gather:
-    def __init__(self, block, n_layer, n_feat):
+    def __init__(self, block, sparse, n_layer, n_feat):
+        self.sparse = self.ahead = sparse
         self.n_layer, self.n_feat = n_layer, n_feat
         self.planes = n_feat // CORES
         self.order = plane_order(self.planes)
@@ -37,13 +39,15 @@
         self.singles = [j for j in range(1, n_layer) if j & (j - 1) == 0]
         self.others = [j for j in range(1, n_layer) if j & (j - 1) != 0]
         self.pieces = {(0, 0): block}
-        self.sent = []
         self.token = None
+        self.tokens = []
 
     def tie(self, x):
         if self.token is None:
             return x
-        return lax.optimization_barrier((x, self.token))[0]
+        x, token = lax.optimization_barrier((x, self.token))
+        self.tokens.append(token)
+        return x
 
     def permute(self, x, pairs):
         flat = [(l0 * self.n_feat + f0, l1 * self.n_feat + f1) for (l0, f0), (l1, f1) in pairs]
@@ -56,7 +60,6 @@
     def across(self, r, j, bit):
         every = [(l, f) for l in range(self.n_layer) for f in range(self.n_feat)]
         x = self.tie(self.pieces[(r, j ^ bit)])
-        self.sent.append(x)
         self.pieces[(r, j)] = self.permute(x, [((l, f), (l ^ bit, f)) for l, f in every])
 
     def straight(self, r):
@@ -79,7 +82,9 @@
                 for c in range(CORES)
             ]
             x = self.tie(self.pieces[(held, j)])
-            self.sent.append(x)
+            if dist > 1 and self.ahead is not None:
+                x, self.sparse = lax.optimization_barrier((x, self.ahead))
+                self.ahead = None
             got = self.permute(x, pairs)
             if (r, j) in self.pieces:
                 here = functools.reduce(jnp.logical_or, [self.plane == b for _, b in moves])
@@ -119,7 +124,7 @@
     )(activations, jnp.swapaxes(active_blocks, 1, 2))
 
 
-def round_kernel(n_layer, layers, first, last, meta, sparse, decoder, *refs):
+def round_kernel(n_layer, n_tokens, layers, order, first, last, meta, sparse, decoder, *refs):
     refs = list(refs)
     mask = refs.pop(0) if last else None
     acc_in = None if first else refs.pop(0)
@@ -127,13 +132,17 @@
     refs = refs[CORES * n_layer :]
     if not first:
         refs.pop(0)
+    refs = refs[n_tokens:]
     grad, acc_out, token = refs[:3]
     up_v, sparse_v, dec_v, acc_v, grad_v, feat_v, up_sem, dec_sem, in_sem, grad_sem, out_sem = refs[3:]
     tokens, wide = parts[0].shape[1:]
     both = CORES * wide
     width = decoder.shape[1]
     rows = n_layer * tokens
-    columns = pl.ds(pl.multiple_of(meta[0] * both, both), both)
+    plane = jnp.int32(order[0])
+    for z in range(1, len(order)):
+        plane = jnp.where(meta[0] == z, jnp.int32(order[z]), plane)
+    columns = pl.ds(pl.multiple_of(plane * both, both), both)
     token[...] = jnp.zeros_like(token)
 
     copies = [pltpu.make_async_copy(sparse, sparse_v, in_sem.at[0])]
@@ -142,7 +151,7 @@
         ups[target] = []
         for i, part in enumerate(parts):
             core = meta[1] if i < n_layer else 1 - meta[1]
-            at_rows = pl.ds(pl.multiple_of(meta[2 + i % n_layer] * tokens, tokens), tokens)
+            at_rows = pl.ds(pl.multiple_of((meta[2] ^ (i % n_layer)) * tokens, tokens), tokens)
             at_cols = pl.ds(pl.multiple_of(target * both + core * wide, wide), wide)
             ups[target].append(
                 pltpu.make_async_copy(
@@ -183,16 +192,14 @@
             copy.wait()
         count = target + 1
         base = target * (target + 1) // 2
-        for core in range(CORES):
-            grad_v[pl.ds(base, count), :, core * wide : (core + 1) * wide] = (
-                jnp.dot(
-                    sparse_v[:count].reshape(count * width, rows),
+        for source in range(count):
+            for core in range(CORES):
+                part = pl.ds(core * wide, wide)
+                grad_v[base + source, :, part] = jnp.dot(
+                    sparse_v[source],
                     up_v[:, target * both + core * wide : target * both + (core + 1) * wide],
                     preferred_element_type=jnp.float32,
-                )
-                .astype(jnp.bfloat16)
-                .reshape(count, width, wide)
-            )
+                ).astype(jnp.bfloat16)
         out = pltpu.make_async_copy(
             grad_v.at[pl.ds(base, count)], grad.at[pl.ds(base, count), :, columns], grad_sem.at[target]
         )
@@ -203,19 +210,24 @@
     if last:
         mask_copy.wait()
     for source in range(layers):
-        total = lax.dot_general(
-            up_v[:, source * both :],
-            dec_v[source, :, source * both :],
-            (((1,), (1,)), ((), ())),
-            preferred_element_type=jnp.float32,
-        )
         if not first:
             acc_copies[source].wait()
-            total = acc_v[source] + total
-        if last:
-            feat_v[source] = (total * feat_v[source].astype(jnp.float32)).astype(jnp.bfloat16)
-        else:
-            acc_v[source] = total
+        for at in range(0, rows, CHUNK):
+            total = lax.dot_general(
+                up_v[at : at + CHUNK, source * both :],
+                dec_v[source, :, source * both :],
+                (((1,), (1,)), ((), ())),
+                preferred_element_type=jnp.float32,
+            )
+            part = pl.ds(at, CHUNK)
+            if not first:
+                total = acc_v[source, part] + total
+            if last:
+                feat_v[source, part] = (total * feat_v[source, part].astype(jnp.float32)).astype(
+                    jnp.bfloat16
+                )
+            else:
+                acc_v[source, part] = total
         out = pltpu.make_async_copy(
             (feat_v if last else acc_v).at[source], acc_out.at[source], out_sem.at[source]
         )
@@ -225,7 +237,7 @@
         out.wait()
 
 
-def run_round(meta, sparse, decoder, mask, acc, grad, mine, theirs, last):
+def run_round(order, meta, tokens, sparse, decoder, mask, acc, grad, mine, theirs, last):
     first = acc is None
     layers, width, rows = sparse.shape
     wide = mine[0].shape[2]
@@ -240,10 +252,11 @@
     if not first:
         aliases[len(operands)] = 0
         operands.append(grad)
+    operands += tokens
     any_space = pl.BlockSpec(memory_space=pl.ANY)
     both = CORES * wide
     return pl.pallas_call(
-        functools.partial(round_kernel, len(mine), layers, first, last),
+        functools.partial(round_kernel, len(mine), len(tokens), layers, order, first, last),
         out_shape=(
             jax.ShapeDtypeStruct(decoder.shape, jnp.bfloat16),
             jax.ShapeDtypeStruct((layers, rows, width), jnp.bfloat16 if last else jnp.float32),
@@ -273,16 +286,15 @@
 
 
 def body(n_layer, n_feat, activations, active_blocks, cotangent, decoder):
-    blocks = Gather(cotangent, n_layer, n_feat)
+    sparse, mask = prepare(activations, active_blocks)
+    blocks = Gather(cotangent, sparse, n_layer, n_feat)
     planes = blocks.planes
     end = planes - 1
-    sparse, mask = prepare(activations, active_blocks)
     core = lax.axis_index("feat") % CORES
-    rows = [lax.axis_index("layer") ^ j for j in range(n_layer)]
+    place = jnp.stack([blocks.plane, core, lax.axis_index("layer")]).astype(jnp.int32)
     hops = range(1, planes)
     acc = grad = None
     for r in range(planes):
-        blocks.sent = []
         if r == 0:
             blocks.straight(0)
             blocks.along_line(0, range(1, planes), hops)
@@ -299,13 +311,18 @@
         if r == max(end - 1, 0) and end > 0:
             blocks.diagonal(end)
         mine = [blocks.pieces[(r, j)] for j in range(n_layer)]
-        theirs = [blocks.swap(blocks.tie(x)) for x in mine]
-        plane = jnp.asarray([row[r] for row in blocks.order], jnp.int32)[blocks.plane]
-        meta = jnp.stack([plane, core] + rows).astype(jnp.int32)
-        meta = lax.optimization_barrier((meta, *blocks.sent))[0]
+        theirs = [
+            blocks.swap(blocks.tie(x) if j in blocks.others else x) for j, x in enumerate(mine)
+        ]
+        soon = [(r + 1, j) for j in blocks.singles] if r < end else []
+        soon += [(r + 2, 0)] if r + 2 <= end else []
+        place, *ready = lax.optimization_barrier((place, *[blocks.pieces[at] for at in soon]))
+        blocks.pieces.update(zip(soon, ready))
+        row = [row[r] for row in blocks.order]
         grad, acc, blocks.token = run_round(
-            meta, sparse, decoder, mask, acc, grad, mine, theirs, r == end
+            row, place, blocks.tokens, blocks.sparse, decoder, mask, acc, grad, mine, theirs, r == end
         )
+        blocks.tokens = []
     return grad, acc
 
 

time: 137 us -> 125 us (0.912)
  Pallas kernels: 66.6 us -> 56.7 us
  local copies, waits for them, and re-layouts: 6.34 us -> 3.47 us
    pallas_call x4, Pallas kernels: 62 us -> 52.1 us  [run_round(): pl.pallas_call(functools.partial(round_kernel, len(mine), len(tokens), la...]
    another operation x4 -> x0, local copies, waits for them, and re-layouts: 4.46 us -> none  [body(): meta = jnp.stack([plane, core] + rows).astype(jnp.int32)]
    unnamed x26 -> x38, local copies, waits for them, and re-layouts: 0.06 us -> 3.47 us
    dynamic_slice x3 -> x0, local copies, waits for them, and re-layouts: 1.82 us -> none  [body(): jnp.asarray([row[r] for row in blocks.order], jnp.int32)[blocks.plane]]
  transfers between devices with their start and end apart: 34 -> 34, of which waited for: 11 -> 10; matrix products, arithmetic and copies ran while one was open for 5% -> 1% of each run, Pallas kernels for 37% -> 35%
where the time goes in v6:
time: 125 us; the launch traced here: 124 us
  Pallas kernels  56.7 us (45%)
  waiting for transfers between devices  34.1 us (27%)
  starting transfers between devices  28.2 us (23%)
  local copies, waits for them, and re-layouts  3.47 us (3%)
    pallas_call x4, Pallas kernels, run_round(): pl.pallas_call(functools.partial(round_kernel, len(mine), len(tokens), la...  52.1 us
    ppermute x34, waiting for transfers between devices, permute(): return lax.ppermute(x, ('layer', 'feat'), sorted(flat))  34.1 us
    ppermute x34, starting transfers between devices, permute(): return lax.ppermute(x, ('layer', 'feat'), sorted(flat))  28.2 us
    pallas_call x1, Pallas kernels, prepare(): pl.pallas_call(prepare_kernel, grid=(layers,), in_specs=[block(rows, widt...  4.52 us
    unnamed x38, local copies, waits for them, and re-layouts  3.47 us
  transfers between devices with their start and end apart: 34, of which 10 were waited for; matrix products, arithmetic and copies ran while one was open for 1% of the time, Pallas kernels for 35%

profile of v6, /device:TPU:0, one launch (start us, length us, event | category | flops | bytes accessed | tf_op | source)
XLA Modules:
  0.0 124.4 jit_solution(2533325944212036139)
XLA Ops:
  0.6 0.7 collective-permute-start.3
  1.3 5.9 %collective-permute-start = (bf16[4,256,256]{2,1,0:T(8,128)(2,1)}, bf16[4,256,256]{2,1,0:T(8,128)(2,1)S(1)}, u32[]{:S(2)}, u32[]{:S(2)}) collective-permute-start(bf16[4,256,256]{2,1,0:T(8,128)(2,1)} %refs_0_.1), channel_id=1, source_target_pairs={{0,2},{1,3},{2,0},{3,1},{4,6},{5,7},{6,4},{7,5},{8,10},{9,11},{10,... | collective-permute-start | bytes 1572872 | tf_op jit(solution)/shard_map/ppermute | solution.py:54
  7.2 1.5 %collective-permute-start.10 = (bf16[4,256,256]{2,1,0:T(8,128)(2,1)}, bf16[4,256,256]{2,1,0:T(8,128)(2,1)S(1)}, u32[]{:S(2)}, u32[]{:S(2)}) collective-permute-start(bf16[4,256,256]{2,1,0:T(8,128)(2,1)} %refs_0_.1), channel_id=1, source_target_pairs={{0,16},{1,17},{2,18},{3,19},{4,20},{5,21},{6,22},{7,23},{8,24},{9,... | collective-permute-start | bytes 1572872 | tf_op jit(solution)/shard_map/ppermute | solution.py:54
  8.7 1.5 %collective-permute-start.9 = (bf16[4,256,256]{2,1,0:T(8,128)(2,1)}, bf16[4,256,256]{2,1,0:T(8,128)(2,1)}, u32[]{:S(2)}, u32[]{:S(2)}) collective-permute-start(bf16[4,256,256]{2,1,0:T(8,128)(2,1)} %refs_0_.1), channel_id=1, source_target_pairs={{0,8},{1,9},{2,10},{3,11},{4,12},{5,13},{6,14},{7,15},{8,0},{9,1},... | collective-permute-start | bytes 1572872 | tf_op jit(solution)/shard_map/ppermute | solution.py:54
  10.2 4.5 %shard_map.59 = (bf16[4,256,1024]{2,1,0:T(8,128)(2,1)}, bf16[4,1024,256]{2,1,0:T(8,128)(2,1)}) custom-call(bf16[4,1024,256]{2,1,0:T(8,128)(2,1)} %act.1, s32[4,2,1024]{2,1,0:T(2,128)} %bitcast.4), custom_call_target="tpu_custom_call" | custom-call | bytes 6291456 | tf_op jit(solution)/shard_map/pallas_call | solution.py:113
  14.8 1.3 %collective-permute-start.4 = (bf16[4,256,256]{2,1,0:T(8,128)(2,1)S(1)}, bf16[4,256,256]{2,1,0:T(8,128)(2,1)S(1)}, u32[]{:S(2)}, u32[]{:S(2)}) collective-permute-start(bf16[4,256,256]{2,1,0:T(8,128)(2,1)S(1)} %collective-permute-done.3), channel_id=1, source_target_pairs={{2,0},{3,1},{4,6},{5,7},{10,8},{11,9},{12,14},{13,15},{18,16},{19,... | collective-permute-start | bytes 1572872 | tf_op jit(solution)/shard_map/ppermute | solution.py:54
  16.0 3.0 %collective-permute-done.refs_1_ = bf16[4,256,256]{2,1,0:T(8,128)(2,1)S(1)} collective-permute-done((bf16[4,256,256]{2,1,0:T(8,128)(2,1)}, bf16[4,256,256]{2,1,0:T(8,128)(2,1)S(1)}, u32[]{:S(2)}, u32[]{:S(2)}) %collective-permute-start) | collective-permute-done | bytes 524320 | tf_op jit(solution)/shard_map/ppermute | solution.py:54
  19.1 1.5 %collective-permute-start.1 = (bf16[4,256,256]{2,1,0:T(8,128)(2,1)S(1)}, bf16[4,256,256]{2,1,0:T(8,128)(2,1)S(1)}, u32[]{:S(2)}, u32[]{:S(2)}) collective-permute-start(bf16[4,256,256]{2,1,0:T(8,128)(2,1)S(1)} %collective-permute-done.refs_1_), channel_id=1, source_target_pairs={{0,8},{1,9},{2,10},{3,11},{4,12},{5,13},{6,14},{7,15},{8,0},{9,1},... | collective-permute-start | bytes 1572872 | tf_op jit(solution)/shard_map/ppermute | solution.py:54
  20.6 1.5 %collective-permute-start.2 = (bf16[4,256,256]{2,1,0:T(8,128)(2,1)S(1)}, bf16[4,256,256]{2,1,0:T(8,128)(2,1)}, u32[]{:S(2)}, u32[]{:S(2)}) collective-permute-start(bf16[4,256,256]{2,1,0:T(8,128)(2,1)S(1)} %collective-permute-done.refs_1_), channel_id=1, source_target_pairs={{0,16},{1,17},{2,18},{3,19},{4,20},{5,21},{6,22},{7,23},{8,24},{9,... | collective-permute-start | bytes 1572872 | tf_op jit(solution)/shard_map/ppermute | solution.py:54
  22.1 0.5 collective-permute-start.11
  22.6 0.2 collective-permute-done.9.refs_1_
  22.8 9.0 %collective-permute-done.4 = bf16[4,256,256]{2,1,0:T(8,128)(2,1)S(1)} collective-permute-done((bf16[4,256,256]{2,1,0:T(8,128)(2,1)S(1)}, bf16[4,256,256]{2,1,0:T(8,128)(2,1)S(1)}, u32[]{:S(2)}, u32[]{:S(2)}) %collective-permute-start.4) | collective-permute-done | bytes 524320 | tf_op jit(solution)/shard_map/ppermute | solution.py:54
  31.8 2.1 %collective-permute-done.1.refs_2_ = bf16[4,256,256]{2,1,0:T(8,128)(2,1)S(1)} collective-permute-done((bf16[4,256,256]{2,1,0:T(8,128)(2,1)S(1)}, bf16[4,256,256]{2,1,0:T(8,128)(2,1)S(1)}, u32[]{:S(2)}, u32[]{:S(2)}) %collective-permute-start.1) | collective-permute-done | bytes 524320 | tf_op jit(solution)/shard_map/ppermute | solution.py:54
  34.0 0.7 collective-permute-start.7
  34.7 9.7 %collective-permute-done.11.refs_3_ = bf16[4,256,256]{2,1,0:T(8,128)(2,1)} collective-permute-done((bf16[4,256,256]{2,1,0:T(8,128)(2,1)S(1)}, bf16[4,256,256]{2,1,0:T(8,128)(2,1)}, u32[]{:S(2)}, u32[]{:S(2)}) %collective-permute-start.11) | collective-permute-done | bytes 524320 | tf_op jit(solution)/shard_map/ppermute | solution.py:54
  44.3 0.6 pad_add_fusion.meta
  45.1 1.6 %collective-permute-start.5 = (bf16[4,256,256]{2,1,0:T(8,128)(2,1)S(1)}, bf16[4,256,256]{2,1,0:T(8,128)(2,1)S(1)}, u32[]{:S(2)}, u32[]{:S(2)}) collective-permute-start(bf16[4,256,256]{2,1,0:T(8,128)(2,1)S(1)} %broadcast_select_fusion.2.refs_1_), channel_id=1, source_target_pairs={{0,8},{1,9},{2,10},{3,11},{4,12},{5,13},{6,14},{7,15},{8,0},{9,1},... | collective-permute-start | bytes 1572872 | tf_op jit(solution)/shard_map/ppermute | solution.py:54
  46.6 0.5 collective-permute-start.6
  47.1 1.7 %collective-permute-start.18 = (bf16[4,256,256]{2,1,0:T(8,128)(2,1)}, bf16[4,256,256]{2,1,0:T(8,128)(2,1)}, u32[]{:S(2)}, u32[]{:S(2)}) collective-permute-start(bf16[4,256,256]{2,1,0:T(8,128)(2,1)} %collective-permute-done.11.refs_3_), channel_id=1, source_target_pairs={{0,2},{1,3},{2,0},{3,1},{4,6},{5,7},{6,4},{7,5},{8,10},{9,11},{10,... | collective-permute-start | bytes 1572872 | tf_op jit(solution)/shard_map/ppermute | solution.py:54
  48.9 0.7 collective-permute-start.23
  49.6 1.3 %collective-permute-start.8 = (bf16[4,256,256]{2,1,0:T(8,128)(2,1)S(1)}, bf16[4,256,256]{2,1,0:T(8,128)(2,1)S(1)}, u32[]{:S(2)}, u32[]{:S(2)}) collective-permute-start(bf16[4,256,256]{2,1,0:T(8,128)(2,1)S(1)} %collective-permute-done.7), channel_id=1, source_target_pairs={{2,0},{3,1},{4,6},{5,7},{10,8},{11,9},{12,14},{13,15},{18,16},{19,... | collective-permute-start | bytes 1572872 | tf_op jit(solution)/shard_map/ppermute | solution.py:54
  50.9 13.0 %shard_map.60 = (bf16[10,256,2048]{2,1,0:T(8,128)(2,1)}, f32[4,1024,256]{2,1,0:T(8,128)}, f32[8,128]{1,0:T(8,128)}) custom-call(s32[3]{0:T(128)} %pad_add_fusion.meta, bf16[4,256,1024]{2,1,0:T(8,128)(2,1)} %get-tuple-element.44.sparse, bf16[10,256,2048]{2,1,0:T(8,128)(2,1)} %decoder.7, bf16[4,256,256]{2,1,0:T(8,128)(2,1)} %refs_0_.1, ...), custom_call_target="tpu_custom_call" | custom-call | flops 10737418240 | bytes 20971520 | tf_op jit(solution)/shard_map/pallas_call | solution.py:258
  64.0 0.5 collective-permute-start.20
  64.5 7.8 %collective-permute-done.8 = bf16[4,256,256]{2,1,0:T(8,128)(2,1)S(1)} collective-permute-done((bf16[4,256,256]{2,1,0:T(8,128)(2,1)S(1)}, bf16[4,256,256]{2,1,0:T(8,128)(2,1)S(1)}, u32[]{:S(2)}, u32[]{:S(2)}) %collective-permute-start.8) | collective-permute-done | bytes 524320 | tf_op jit(solution)/shard_map/ppermute | solution.py:54
  72.4 0.8 copy-done.5
  73.2 0.5 collective-permute-start.22
  73.8 0.1 collective-permute-start.25
  73.9 0.6 collective-permute-start.16
  74.5 1.5 %collective-permute-start.17 = (bf16[4,256,256]{2,1,0:T(8,128)(2,1)S(1)}, bf16[4,256,256]{2,1,0:T(8,128)(2,1)S(1)}, u32[]{:S(2)}, u32[]{:S(2)}) collective-permute-start(bf16[4,256,256]{2,1,0:T(8,128)(2,1)S(1)} %broadcast_select_fusion.1.refs_2_), channel_id=1, source_target_pairs={{0,16},{1,17},{2,18},{3,19},{4,20},{5,21},{6,22},{7,23},{8,24},{9,... | collective-permute-start | bytes 1572872 | tf_op jit(solution)/shard_map/ppermute | solution.py:54
  76.0 1.5 %collective-permute-start.24 = (bf16[4,256,256]{2,1,0:T(8,128)(2,1)S(1)}, bf16[4,256,256]{2,1,0:T(8,128)(2,1)S(1)}, u32[]{:S(2)}, u32[]{:S(2)}) collective-permute-start(bf16[4,256,256]{2,1,0:T(8,128)(2,1)S(1)} %collective-permute-done.23), channel_id=1, source_target_pairs={{2,0},{3,1},{4,6},{5,7},{10,8},{11,9},{12,14},{13,15},{18,16},{19,... | collective-permute-start | bytes 1572872 | tf_op jit(solution)/shard_map/ppermute | solution.py:54
  77.5 0.8 copy-done.16
  78.3 13.0 %shard_map.61 = (bf16[10,256,2048]{2,1,0:T(8,128)(2,1)}, f32[4,1024,256]{2,1,0:T(8,128)}, f32[8,128]{1,0:T(8,128)}) custom-call(s32[3]{0:T(128)} %pad_add_fusion.meta, bf16[4,256,1024]{2,1,0:T(8,128)(2,1)} %get-tuple-element.44.sparse, bf16[10,256,2048]{2,1,0:T(8,128)(2,1)} %decoder.7, ...), custom_call_target="tpu_custom_call", output_to_operand_aliasing={{0}: (12, {})} | custom-call | flops 10737418240 | bytes 20971520 | tf_op jit(solution)/shard_map/pallas_call | solution.py:258
  91.3 0.3 collective-permute-done.24
  91.6 0.3 collective-permute-start.27
  92.0 0.3 collective-permute-start.28
  92.3 0.4 collective-permute-start.30
  92.6 0.8 collective-permute-start.29
  93.5 0.2 collective-permute-start.31
  93.6 0.1 collective-permute-done.27.refs_7_
  93.7 0.3 collective-permute-start.32
  94.0 0.2 collective-permute-done.28.refs_8_
  94.3 0.3 copy-done.15
  94.5 0.8 copy-done.17
  95.3 13.1 %shard_map.62 = (bf16[10,256,2048]{2,1,0:T(8,128)(2,1)}, f32[4,1024,256]{2,1,0:T(8,128)}, f32[8,128]{1,0:T(8,128)}) custom-call(s32[3]{0:T(128)} %pad_add_fusion.meta, bf16[4,256,1024]{2,1,0:T(8,128)(2,1)} %get-tuple-element.44.sparse, bf16[10,256,2048]{2,1,0:T(8,128)(2,1)} %decoder.7, ...), custom_call_target="tpu_custom_call", output_to_operand_aliasing={{0}: (12, {})} | custom-call | flops 10737418240 | bytes 20971520 | tf_op jit(solution)/shard_map/pallas_call | solution.py:258
  108.5 0.4 collective-permute-start.33
  108.9 1.6 %collective-permute-done.33.refs_9_ = bf16[4,256,256]{2,1,0:T(8,128)(2,1)S(1)} collective-permute-done((bf16[4,256,256]{2,1,0:T(8,128)(2,1)S(1)}, bf16[4,256,256]{2,1,0:T(8,128)(2,1)S(1)}, u32[]{:S(2)}, u32[]{:S(2)}) %collective-permute-start.33) | collective-permute-done | bytes 524320 | tf_op jit(solution)/shard_map/ppermute | solution.py:54
  110.5 0.8 copy-done.18
  111.2 13.0 %shard_map.63 = (bf16[10,256,2048]{2,1,0:T(8,128)(2,1)}, bf16[4,1024,256]{2,1,0:T(8,128)(2,1)}, f32[8,128]{1,0:T(8,128)}) custom-call(s32[3]{0:T(128)} %pad_add_fusion.meta, bf16[4,256,1024]{2,1,0:T(8,128)(2,1)} %get-tuple-element.44.sparse, bf16[10,256,2048]{2,1,0:T(8,128)(2,1)} %decoder.7, ...), custom_call_target="tpu_custom_call", output_to_operand_aliasing={{0}: (13, {})} | custom-call | flops 10737418240 | bytes 20971520 | tf_op jit(solution)/shard_map/pallas_call | solution.py:258
  (67 shorter events, 0.4 us)
Async XLA Ops:
  0.6 14.1 %collective-permute-start.3 = (bf16[4,256,256]{2,1,0:T(8,128)(2,1)}, bf16[4,256,256]{2,1,0:T(8,128)(2,1)S(1)}, u32[]{:S(2)}, u32[]{:S(2)}) collective-permute-start(bf16[4,256,256]{2,1,0:T(8,128)(2,1)} %refs_0_.1), channel_id=1, source_target_pairs={{2,4},{3,5},{4,2},{5,3},{10,12},{11,13},{12,10},{13,11},{18,20},{1... | collective-permute-start | bytes 1572872 | tf_op jit(solution)/shard_map/ppermute | solution.py:54
  1.3 17.7 %collective-permute-start = (bf16[4,256,256]{2,1,0:T(8,128)(2,1)}, bf16[4,256,256]{2,1,0:T(8,128)(2,1)S(1)}, u32[]{:S(2)}, u32[]{:S(2)}) collective-permute-start(bf16[4,256,256]{2,1,0:T(8,128)(2,1)} %refs_0_.1), channel_id=1, source_target_pairs={{0,2},{1,3},{2,0},{3,1},{4,6},{5,7},{6,4},{7,5},{8,10},{9,11},{10,... | collective-permute-start | bytes 1572872 | tf_op jit(solution)/shard_map/ppermute | solution.py:54
  7.2 14.9 %collective-permute-start.10 = (bf16[4,256,256]{2,1,0:T(8,128)(2,1)}, bf16[4,256,256]{2,1,0:T(8,128)(2,1)S(1)}, u32[]{:S(2)}, u32[]{:S(2)}) collective-permute-start(bf16[4,256,256]{2,1,0:T(8,128)(2,1)} %refs_0_.1), channel_id=1, source_target_pairs={{0,16},{1,17},{2,18},{3,19},{4,20},{5,21},{6,22},{7,23},{8,24},{9,... | collective-permute-start | bytes 1572872 | tf_op jit(solution)/shard_map/ppermute | solution.py:54
  8.7 14.1 %collective-permute-start.9 = (bf16[4,256,256]{2,1,0:T(8,128)(2,1)}, bf16[4,256,256]{2,1,0:T(8,128)(2,1)}, u32[]{:S(2)}, u32[]{:S(2)}) collective-permute-start(bf16[4,256,256]{2,1,0:T(8,128)(2,1)} %refs_0_.1), channel_id=1, source_target_pairs={{0,8},{1,9},{2,10},{3,11},{4,12},{5,13},{6,14},{7,15},{8,0},{9,1},... | collective-permute-start | bytes 1572872 | tf_op jit(solution)/shard_map/ppermute | solution.py:54
  14.8 17.1 %collective-permute-start.4 = (bf16[4,256,256]{2,1,0:T(8,128)(2,1)S(1)}, bf16[4,256,256]{2,1,0:T(8,128)(2,1)S(1)}, u32[]{:S(2)}, u32[]{:S(2)}) collective-permute-start(bf16[4,256,256]{2,1,0:T(8,128)(2,1)S(1)} %collective-permute-done.3), channel_id=1, source_target_pairs={{2,0},{3,1},{4,6},{5,7},{10,8},{11,9},{12,14},{13,15},{18,16},{19,... | collective-permute-start | bytes 1572872 | tf_op jit(solution)/shard_map/ppermute | solution.py:54
  19.1 44.9 %copy-start.3 = (bf16[4,256,256]{2,1,0:T(8,128)(2,1)}, bf16[4,256,256]{2,1,0:T(8,128)(2,1)S(1)}, u32[]{:S(2)}) copy-start(bf16[4,256,256]{2,1,0:T(8,128)(2,1)S(1)} %collective-permute-done.refs_1_) | copy-start | bytes 1572868
  19.1 14.9 %collective-permute-start.1 = (bf16[4,256,256]{2,1,0:T(8,128)(2,1)S(1)}, bf16[4,256,256]{2,1,0:T(8,128)(2,1)S(1)}, u32[]{:S(2)}, u32[]{:S(2)}) collective-permute-start(bf16[4,256,256]{2,1,0:T(8,128)(2,1)S(1)} %collective-permute-done.refs_1_), channel_id=1, source_target_pairs={{0,8},{1,9},{2,10},{3,11},{4,12},{5,13},{6,14},{7,15},{8,0},{9,1},... | collective-permute-start | bytes 1572872 | tf_op jit(solution)/shard_map/ppermute | solution.py:54
  20.6 13.4 %collective-permute-start.2 = (bf16[4,256,256]{2,1,0:T(8,128)(2,1)S(1)}, bf16[4,256,256]{2,1,0:T(8,128)(2,1)}, u32[]{:S(2)}, u32[]{:S(2)}) collective-permute-start(bf16[4,256,256]{2,1,0:T(8,128)(2,1)S(1)} %collective-permute-done.refs_1_), channel_id=1, source_target_pairs={{0,16},{1,17},{2,18},{3,19},{4,20},{5,21},{6,22},{7,23},{8,24},{9,... | collective-permute-start | bytes 1572872 | tf_op jit(solution)/shard_map/ppermute | solution.py:54
  22.1 27.5 %copy-start.6 = (bf16[4,256,256]{2,1,0:T(8,128)(2,1)}, bf16[4,256,256]{2,1,0:T(8,128)(2,1)S(1)}, u32[]{:S(2)}) copy-start(bf16[4,256,256]{2,1,0:T(8,128)(2,1)S(1)} %collective-permute-done.10.refs_2_) | copy-start | bytes 1572868
  22.1 22.3 %collective-permute-start.11 = (bf16[4,256,256]{2,1,0:T(8,128)(2,1)S(1)}, bf16[4,256,256]{2,1,0:T(8,128)(2,1)}, u32[]{:S(2)}, u32[]{:S(2)}) collective-permute-start(bf16[4,256,256]{2,1,0:T(8,128)(2,1)S(1)} %collective-permute-done.10.refs_2_), channel_id=1, source_target_pairs={{0,8},{1,9},{2,10},{3,11},{4,12},{5,13},{6,14},{7,15},{8,0},{9,1},... | collective-permute-start | bytes 1572872 | tf_op jit(solution)/shard_map/ppermute | solution.py:54
  22.8 22.2 %collective-permute-start.12 = (bf16[4,256,256]{2,1,0:T(8,128)(2,1)}, bf16[4,256,256]{2,1,0:T(8,128)(2,1)}, u32[]{:S(2)}, u32[]{:S(2)}) collective-permute-start(bf16[4,256,256]{2,1,0:T(8,128)(2,1)} %refs_0_.1), channel_id=1, source_target_pairs={{0,1},{1,0},{2,3},{3,2},{4,5},{5,4},{6,7},{7,6},{8,9},{9,8},{10,11... | collective-permute-start | bytes 1572872 | tf_op jit(solution)/shard_map/ppermute | solution.py:54
  31.8 14.8 %collective-permute-start.14 = (bf16[4,256,256]{2,1,0:T(8,128)(2,1)S(1)}, bf16[4,256,256]{2,1,0:T(8,128)(2,1)}, u32[]{:S(2)}, u32[]{:S(2)}) collective-permute-start(bf16[4,256,256]{2,1,0:T(8,128)(2,1)S(1)} %collective-permute-done.10.refs_2_), channel_id=1, source_target_pairs={{0,1},{1,0},{2,3},{3,2},{4,5},{5,4},{6,7},{7,6},{8,9},{9,8},{10,11... | collective-permute-start | bytes 1572872 | tf_op jit(solution)/shard_map/ppermute | solution.py:54
  34.0 30.1 %copy-start.4 = (bf16[4,256,256]{2,1,0:T(8,128)(2,1)}, bf16[4,256,256]{2,1,0:T(8,128)(2,1)S(1)}, u32[]{:S(2)}) copy-start(bf16[4,256,256]{2,1,0:T(8,128)(2,1)S(1)} %collective-permute-done.1.refs_2_) | copy-start | bytes 1572868
  34.0 13.2 %collective-permute-start.13 = (bf16[4,256,256]{2,1,0:T(8,128)(2,1)}, bf16[4,256,256]{2,1,0:T(8,128)(2,1)}, u32[]{:S(2)}, u32[]{:S(2)}) collective-permute-start(bf16[4,256,256]{2,1,0:T(8,128)(2,1)} %collective-permute-done.9.refs_1_), channel_id=1, source_target_pairs={{0,1},{1,0},{2,3},{3,2},{4,5},{5,4},{6,7},{7,6},{8,9},{9,8},{10,11... | collective-permute-start | bytes 1572872 | tf_op jit(solution)/shard_map/ppermute | solution.py:54
  34.0 14.9 %collective-permute-start.7 = (bf16[4,256,256]{2,1,0:T(8,128)(2,1)S(1)}, bf16[4,256,256]{2,1,0:T(8,128)(2,1)S(1)}, u32[]{:S(2)}, u32[]{:S(2)}) collective-permute-start(bf16[4,256,256]{2,1,0:T(8,128)(2,1)S(1)} %collective-permute-done.refs_1_), channel_id=1, source_target_pairs={{2,4},{3,5},{4,2},{5,3},{10,12},{11,13},{12,10},{13,11},{18,20},{1... | collective-permute-start | bytes 1572872 | tf_op jit(solution)/shard_map/ppermute | solution.py:54
  44.3 5.2 %collective-permute-start.15 = (bf16[4,256,256]{2,1,0:T(8,128)(2,1)}, bf16[4,256,256]{2,1,0:T(8,128)(2,1)}, u32[]{:S(2)}, u32[]{:S(2)}) collective-permute-start(bf16[4,256,256]{2,1,0:T(8,128)(2,1)} %collective-permute-done.11.refs_3_), channel_id=1, source_target_pairs={{0,1},{1,0},{2,3},{3,2},{4,5},{5,4},{6,7},{7,6},{8,9},{9,8},{10,11... | collective-permute-start | bytes 1572872 | tf_op jit(solution)/shard_map/ppermute | solution.py:54
  45.0 28.7 %copy-start = (bf16[4,256,256]{2,1,0:T(8,128)(2,1)}, bf16[4,256,256]{2,1,0:T(8,128)(2,1)S(1)}, u32[]{:S(2)}) copy-start(bf16[4,256,256]{2,1,0:T(8,128)(2,1)S(1)} %broadcast_select_fusion.2.refs_1_) | copy-start | bytes 1572868
  45.1 27.3 %collective-permute-start.5 = (bf16[4,256,256]{2,1,0:T(8,128)(2,1)S(1)}, bf16[4,256,256]{2,1,0:T(8,128)(2,1)S(1)}, u32[]{:S(2)}, u32[]{:S(2)}) collective-permute-start(bf16[4,256,256]{2,1,0:T(8,128)(2,1)S(1)} %broadcast_select_fusion.2.refs_1_), channel_id=1, source_target_pairs={{0,8},{1,9},{2,10},{3,11},{4,12},{5,13},{6,14},{7,15},{8,0},{9,1},... | collective-permute-start | bytes 1572872 | tf_op jit(solution)/shard_map/ppermute | solution.py:54
  46.6 27.1 %collective-permute-start.6 = (bf16[4,256,256]{2,1,0:T(8,128)(2,1)S(1)}, bf16[4,256,256]{2,1,0:T(8,128)(2,1)}, u32[]{:S(2)}, u32[]{:S(2)}) collective-permute-start(bf16[4,256,256]{2,1,0:T(8,128)(2,1)S(1)} %broadcast_select_fusion.2.refs_1_), channel_id=1, source_target_pairs={{0,16},{1,17},{2,18},{3,19},{4,20},{5,21},{6,22},{7,23},{8,24},{9,... | collective-permute-start | bytes 1572872 | tf_op jit(solution)/shard_map/ppermute | solution.py:54
  47.1 16.8 %collective-permute-start.18 = (bf16[4,256,256]{2,1,0:T(8,128)(2,1)}, bf16[4,256,256]{2,1,0:T(8,128)(2,1)}, u32[]{:S(2)}, u32[]{:S(2)}) collective-permute-start(bf16[4,256,256]{2,1,0:T(8,128)(2,1)} %collective-permute-done.11.refs_3_), channel_id=1, source_target_pairs={{0,2},{1,3},{2,0},{3,1},{4,6},{5,7},{6,4},{7,5},{8,10},{9,11},{10,... | collective-permute-start | bytes 1572872 | tf_op jit(solution)/shard_map/ppermute | solution.py:54
  48.9 15.1 %collective-permute-start.23 = (bf16[4,256,256]{2,1,0:T(8,128)(2,1)}, bf16[4,256,256]{2,1,0:T(8,128)(2,1)S(1)}, u32[]{:S(2)}, u32[]{:S(2)}) collective-permute-start(bf16[4,256,256]{2,1,0:T(8,128)(2,1)} %collective-permute-done.11.refs_3_), channel_id=1, source_target_pairs={{2,4},{3,5},{4,2},{5,3},{10,12},{11,13},{12,10},{13,11},{18,20},{1... | collective-permute-start | bytes 1572872 | tf_op jit(solution)/shard_map/ppermute | solution.py:54
  49.6 22.8 %collective-permute-start.8 = (bf16[4,256,256]{2,1,0:T(8,128)(2,1)S(1)}, bf16[4,256,256]{2,1,0:T(8,128)(2,1)S(1)}, u32[]{:S(2)}, u32[]{:S(2)}) collective-permute-start(bf16[4,256,256]{2,1,0:T(8,128)(2,1)S(1)} %collective-permute-done.7), channel_id=1, source_target_pairs={{2,0},{3,1},{4,6},{5,7},{10,8},{11,9},{12,14},{13,15},{18,16},{19,... | collective-permute-start | bytes 1572872 | tf_op jit(solution)/shard_map/ppermute | solution.py:54
  63.9 9.9 %collective-permute-start.19 = (bf16[4,256,256]{2,1,0:T(8,128)(2,1)S(1)}, bf16[4,256,256]{2,1,0:T(8,128)(2,1)S(1)}, u32[]{:S(2)}, u32[]{:S(2)}) collective-permute-start(bf16[4,256,256]{2,1,0:T(8,128)(2,1)S(1)} %collective-permute-done.refs_1_), channel_id=1, source_target_pairs={{0,1},{1,0},{2,3},{3,2},{4,5},{5,4},{6,7},{7,6},{8,9},{9,8},{10,11... | collective-permute-start | bytes 1572872 | tf_op jit(solution)/shard_map/ppermute | solution.py:54
  64.0 10.4 %collective-permute-start.20 = (bf16[4,256,256]{2,1,0:T(8,128)(2,1)S(1)}, bf16[4,256,256]{2,1,0:T(8,128)(2,1)S(1)}, u32[]{:S(2)}, u32[]{:S(2)}) collective-permute-start(bf16[4,256,256]{2,1,0:T(8,128)(2,1)S(1)} %collective-permute-done.1.refs_2_), channel_id=1, source_target_pairs={{0,1},{1,0},{2,3},{3,2},{4,5},{5,4},{6,7},{7,6},{8,9},{9,8},{10,11... | collective-permute-start | bytes 1572872 | tf_op jit(solution)/shard_map/ppermute | solution.py:54
  72.4 3.6 %collective-permute-start.21 = (bf16[4,256,256]{2,1,0:T(8,128)(2,1)}, bf16[4,256,256]{2,1,0:T(8,128)(2,1)S(1)}, u32[]{:S(2)}, u32[]{:S(2)}) collective-permute-start(bf16[4,256,256]{2,1,0:T(8,128)(2,1)} %collective-permute-done.2.refs_3_), channel_id=1, source_target_pairs={{0,1},{1,0},{2,3},{3,2},{4,5},{5,4},{6,7},{7,6},{8,9},{9,8},{10,11... | collective-permute-start | bytes 1572872 | tf_op jit(solution)/shard_map/ppermute | solution.py:54
  73.2 4.3 %collective-permute-start.22 = (bf16[4,256,256]{2,1,0:T(8,128)(2,1)}, bf16[4,256,256]{2,1,0:T(8,128)(2,1)S(1)}, u32[]{:S(2)}, u32[]{:S(2)}) collective-permute-start(bf16[4,256,256]{2,1,0:T(8,128)(2,1)} %collective-permute-done.18.refs_4_), channel_id=1, source_target_pairs={{0,1},{1,0},{2,3},{3,2},{4,5},{5,4},{6,7},{7,6},{8,9},{9,8},{10,11... | collective-permute-start | bytes 1572872 | tf_op jit(solution)/shard_map/ppermute | solution.py:54
  73.7 18.5 %copy-start.1 = (bf16[4,256,256]{2,1,0:T(8,128)(2,1)}, bf16[4,256,256]{2,1,0:T(8,128)(2,1)S(1)}, u32[]{:S(2)}) copy-start(bf16[4,256,256]{2,1,0:T(8,128)(2,1)S(1)} %broadcast_select_fusion.1.refs_2_) | copy-start | bytes 1572868
  73.8 18.9 %collective-permute-start.25 = (bf16[4,256,256]{2,1,0:T(8,128)(2,1)S(1)}, bf16[4,256,256]{2,1,0:T(8,128)(2,1)}, u32[]{:S(2)}, u32[]{:S(2)}) collective-permute-start(bf16[4,256,256]{2,1,0:T(8,128)(2,1)S(1)} %broadcast_select_fusion.2.refs_1_), channel_id=1, source_target_pairs={{0,1},{1,0},{2,3},{3,2},{4,5},{5,4},{6,7},{7,6},{8,9},{9,8},{10,11... | collective-permute-start | bytes 1572872 | tf_op jit(solution)/shard_map/ppermute | solution.py:54
  73.8 2.1 %copy-start.9 = (bf16[4,256,256]{2,1,0:T(8,128)(2,1)}, bf16[4,256,256]{2,1,0:T(8,128)(2,1)S(1)}, u32[]{:S(2)}) copy-start(bf16[4,256,256]{2,1,0:T(8,128)(2,1)S(1)} %collective-permute-done.19.refs_5_) | copy-start | bytes 1572868
  73.9 18.1 %collective-permute-start.16 = (bf16[4,256,256]{2,1,0:T(8,128)(2,1)S(1)}, bf16[4,256,256]{2,1,0:T(8,128)(2,1)S(1)}, u32[]{:S(2)}, u32[]{:S(2)}) collective-permute-start(bf16[4,256,256]{2,1,0:T(8,128)(2,1)S(1)} %broadcast_select_fusion.1.refs_2_), channel_id=1, source_target_pairs={{0,8},{1,9},{2,10},{3,11},{4,12},{5,13},{6,14},{7,15},{8,0},{9,1},... | collective-permute-start | bytes 1572872 | tf_op jit(solution)/shard_map/ppermute | solution.py:54
  74.5 1.5 %copy-start.11 = (bf16[4,256,256]{2,1,0:T(8,128)(2,1)}, bf16[4,256,256]{2,1,0:T(8,128)(2,1)S(1)}, u32[]{:S(2)}) copy-start(bf16[4,256,256]{2,1,0:T(8,128)(2,1)S(1)} %collective-permute-done.20.refs_6_) | copy-start | bytes 1572868
  74.5 17.8 %collective-permute-start.17 = (bf16[4,256,256]{2,1,0:T(8,128)(2,1)S(1)}, bf16[4,256,256]{2,1,0:T(8,128)(2,1)S(1)}, u32[]{:S(2)}, u32[]{:S(2)}) collective-permute-start(bf16[4,256,256]{2,1,0:T(8,128)(2,1)S(1)} %broadcast_select_fusion.1.refs_2_), channel_id=1, source_target_pairs={{0,16},{1,17},{2,18},{3,19},{4,20},{5,21},{6,22},{7,23},{8,24},{9,... | collective-permute-start | bytes 1572872 | tf_op jit(solution)/shard_map/ppermute | solution.py:54
  76.0 1.5 %copy-start.13 = (bf16[4,256,256]{2,1,0:T(8,128)(2,1)}, bf16[4,256,256]{2,1,0:T(8,128)(2,1)S(1)}, u32[]{:S(2)}) copy-start(bf16[4,256,256]{2,1,0:T(8,128)(2,1)S(1)} %collective-permute-done.21.refs_7_) | copy-start | bytes 1572868
  76.0 15.6 %collective-permute-start.24 = (bf16[4,256,256]{2,1,0:T(8,128)(2,1)S(1)}, bf16[4,256,256]{2,1,0:T(8,128)(2,1)S(1)}, u32[]{:S(2)}, u32[]{:S(2)}) collective-permute-start(bf16[4,256,256]{2,1,0:T(8,128)(2,1)S(1)} %collective-permute-done.23), channel_id=1, source_target_pairs={{2,0},{3,1},{4,6},{5,7},{10,8},{11,9},{12,14},{13,15},{18,16},{19,... | collective-permute-start | bytes 1572872 | tf_op jit(solution)/shard_map/ppermute | solution.py:54
  78.3 15.2 %collective-permute-start.26 = (bf16[4,256,256]{2,1,0:T(8,128)(2,1)}, bf16[4,256,256]{2,1,0:T(8,128)(2,1)}, u32[]{:S(2)}, u32[]{:S(2)}) collective-permute-start(bf16[4,256,256]{2,1,0:T(8,128)(2,1)} %copy-done.5), channel_id=1, source_target_pairs={{0,1},{1,0},{2,3},{3,2},{4,5},{5,4},{6,7},{7,6},{8,9},{9,8},{10,11... | collective-permute-start | bytes 1572872 | tf_op jit(solution)/shard_map/ppermute | solution.py:54
  91.6 2.1 %collective-permute-start.27 = (bf16[4,256,256]{2,1,0:T(8,128)(2,1)}, bf16[4,256,256]{2,1,0:T(8,128)(2,1)S(1)}, u32[]{:S(2)}, u32[]{:S(2)}) collective-permute-start(bf16[4,256,256]{2,1,0:T(8,128)(2,1)} %collective-permute-done.6.refs_3_), channel_id=1, source_target_pairs={{0,1},{1,0},{2,3},{3,2},{4,5},{5,4},{6,7},{7,6},{8,9},{9,8},{10,11... | collective-permute-start | bytes 1572872 | tf_op jit(solution)/shard_map/ppermute | solution.py:54
  92.0 3.3 %copy-start.2 = (bf16[4,256,256]{2,1,0:T(8,128)(2,1)}, bf16[4,256,256]{2,1,0:T(8,128)(2,1)S(1)}, u32[]{:S(2)}) copy-start(bf16[4,256,256]{2,1,0:T(8,128)(2,1)S(1)} %broadcast_select_fusion.refs_4_) | copy-start | bytes 1572868
  92.0 16.4 %copy-start.7 = (bf16[4,256,256]{2,1,0:T(8,128)(2,1)}, bf16[4,256,256]{2,1,0:T(8,128)(2,1)S(1)}, u32[]{:S(2)}) copy-start(bf16[4,256,256]{2,1,0:T(8,128)(2,1)S(1)} %collective-permute-done.16.refs_3_) | copy-start | bytes 1572868
  92.0 2.3 %collective-permute-start.28 = (bf16[4,256,256]{2,1,0:T(8,128)(2,1)S(1)}, bf16[4,256,256]{2,1,0:T(8,128)(2,1)S(1)}, u32[]{:S(2)}, u32[]{:S(2)}) collective-permute-start(bf16[4,256,256]{2,1,0:T(8,128)(2,1)S(1)} %broadcast_select_fusion.refs_4_), channel_id=1, source_target_pairs={{0,1},{1,0},{2,3},{3,2},{4,5},{5,4},{6,7},{7,6},{8,9},{9,8},{10,11... | collective-permute-start | bytes 1572872 | tf_op jit(solution)/shard_map/ppermute | solution.py:54
  92.3 16.2 %copy-start.8 = (bf16[4,256,256]{2,1,0:T(8,128)(2,1)}, bf16[4,256,256]{2,1,0:T(8,128)(2,1)S(1)}, u32[]{:S(2)}) copy-start(bf16[4,256,256]{2,1,0:T(8,128)(2,1)S(1)} %collective-permute-done.17.refs_4_) | copy-start | bytes 1572868
  92.3 16.6 %collective-permute-start.30 = (bf16[4,256,256]{2,1,0:T(8,128)(2,1)S(1)}, bf16[4,256,256]{2,1,0:T(8,128)(2,1)S(1)}, u32[]{:S(2)}, u32[]{:S(2)}) collective-permute-start(bf16[4,256,256]{2,1,0:T(8,128)(2,1)S(1)} %broadcast_select_fusion.1.refs_2_), channel_id=1, source_target_pairs={{0,1},{1,0},{2,3},{3,2},{4,5},{5,4},{6,7},{7,6},{8,9},{9,8},{10,11... | collective-permute-start | bytes 1572872 | tf_op jit(solution)/shard_map/ppermute | solution.py:54
  92.6 15.8 %collective-permute-start.29 = (bf16[4,256,256]{2,1,0:T(8,128)(2,1)S(1)}, bf16[4,256,256]{2,1,0:T(8,128)(2,1)S(1)}, u32[]{:S(2)}, u32[]{:S(2)}) collective-permute-start(bf16[4,256,256]{2,1,0:T(8,128)(2,1)S(1)} %collective-permute-done.16.refs_3_), channel_id=1, source_target_pairs={{0,16},{1,17},{2,18},{3,19},{4,20},{5,21},{6,22},{7,23},{8,24},{9,... | collective-permute-start | bytes 1572872 | tf_op jit(solution)/shard_map/ppermute | solution.py:54
  93.5 15.4 %collective-permute-start.31 = (bf16[4,256,256]{2,1,0:T(8,128)(2,1)S(1)}, bf16[4,256,256]{2,1,0:T(8,128)(2,1)S(1)}, u32[]{:S(2)}, u32[]{:S(2)}) collective-permute-start(bf16[4,256,256]{2,1,0:T(8,128)(2,1)S(1)} %collective-permute-done.16.refs_3_), channel_id=1, source_target_pairs={{0,1},{1,0},{2,3},{3,2},{4,5},{5,4},{6,7},{7,6},{8,9},{9,8},{10,11... | collective-permute-start | bytes 1572872 | tf_op jit(solution)/shard_map/ppermute | solution.py:54
  93.7 15.2 %collective-permute-start.32 = (bf16[4,256,256]{2,1,0:T(8,128)(2,1)S(1)}, bf16[4,256,256]{2,1,0:T(8,128)(2,1)}, u32[]{:S(2)}, u32[]{:S(2)}) collective-permute-start(bf16[4,256,256]{2,1,0:T(8,128)(2,1)S(1)} %collective-permute-done.17.refs_4_), channel_id=1, source_target_pairs={{0,1},{1,0},{2,3},{3,2},{4,5},{5,4},{6,7},{7,6},{8,9},{9,8},{10,11... | collective-permute-start | bytes 1572872 | tf_op jit(solution)/shard_map/ppermute | solution.py:54
  108.5 2.0 %copy-start.12 = (bf16[4,256,256]{2,1,0:T(8,128)(2,1)}, bf16[4,256,256]{2,1,0:T(8,128)(2,1)S(1)}, u32[]{:S(2)}) copy-start(bf16[4,256,256]{2,1,0:T(8,128)(2,1)S(1)} %collective-permute-done.29.refs_5_) | copy-start | bytes 1572868
  108.5 2.0 %collective-permute-start.33 = (bf16[4,256,256]{2,1,0:T(8,128)(2,1)S(1)}, bf16[4,256,256]{2,1,0:T(8,128)(2,1)S(1)}, u32[]{:S(2)}, u32[]{:S(2)}) collective-permute-start(bf16[4,256,256]{2,1,0:T(8,128)(2,1)S(1)} %collective-permute-done.29.refs_5_), channel_id=1, source_target_pairs={{0,1},{1,0},{2,3},{3,2},{4,5},{5,4},{6,7},{7,6},{8,9},{9,8},{10,11... | collective-permute-start | bytes 1572872 | tf_op jit(solution)/shard_map/ppermute | solution.py:54
  108.9 1.6 %copy-start.10 = (bf16[4,256,256]{2,1,0:T(8,128)(2,1)}, bf16[4,256,256]{2,1,0:T(8,128)(2,1)S(1)}, u32[]{:S(2)}) copy-start(bf16[4,256,256]{2,1,0:T(8,128)(2,1)S(1)} %collective-permute-done.30.refs_6_) | copy-start | bytes 1572868
  108.9 1.6 %copy-start.14 = (bf16[4,256,256]{2,1,0:T(8,128)(2,1)}, bf16[4,256,256]{2,1,0:T(8,128)(2,1)S(1)}, u32[]{:S(2)}) copy-start(bf16[4,256,256]{2,1,0:T(8,128)(2,1)S(1)} %collective-permute-done.31.refs_7_) | copy-start | bytes 1572868
  (5 other events, 4.0 us)

commit v7 on v6

--- a/solution.py
+++ b/solution.py
@@ -39,8 +39,15 @@
         self.singles = [j for j in range(1, n_layer) if j & (j - 1) == 0]
         self.others = [j for j in range(1, n_layer) if j & (j - 1) != 0]
         self.pieces = {(0, 0): block}
+        self.later = {}
         self.token = None
         self.tokens = []
+
+    def piece(self, r, j):
+        if (r, j) in self.later:
+            here, got = self.later.pop((r, j))
+            self.pieces[(r, j)] = jnp.where(here, got, self.pieces[(r, j)])
+        return self.pieces[(r, j)]
 
     def tie(self, x):
         if self.token is None:
@@ -59,7 +66,7 @@
 
     def across(self, r, j, bit):
         every = [(l, f) for l in range(self.n_layer) for f in range(self.n_feat)]
-        x = self.tie(self.pieces[(r, j ^ bit)])
+        x = self.tie(self.piece(r, j ^ bit))
         self.pieces[(r, j)] = self.permute(x, [((l, f), (l ^ bit, f)) for l, f in every])
 
     def straight(self, r):
@@ -81,15 +88,16 @@
                 for a, b in moves
                 for c in range(CORES)
             ]
-            x = self.tie(self.pieces[(held, j)])
+            x = self.tie(self.piece(held, j))
             if dist > 1 and self.ahead is not None:
                 x, self.sparse = lax.optimization_barrier((x, self.ahead))
                 self.ahead = None
             got = self.permute(x, pairs)
             if (r, j) in self.pieces:
                 here = functools.reduce(jnp.logical_or, [self.plane == b for _, b in moves])
-                got = jnp.where(here, got, self.pieces[(r, j)])
-            self.pieces[(r, j)] = got
+                self.later[(r, j)] = (here, got)
+            else:
+                self.pieces[(r, j)] = got
 
 
 def prepare_kernel(act, blocks, sparse, mask):
@@ -193,13 +201,11 @@
         count = target + 1
         base = target * (target + 1) // 2
         for source in range(count):
-            for core in range(CORES):
-                part = pl.ds(core * wide, wide)
-                grad_v[base + source, :, part] = jnp.dot(
-                    sparse_v[source],
-                    up_v[:, target * both + core * wide : target * both + (core + 1) * wide],
-                    preferred_element_type=jnp.float32,
-                ).astype(jnp.bfloat16)
+            grad_v[base + source] = jnp.dot(
+                sparse_v[source],
+                up_v[:, target * both : (target + 1) * both],
+                preferred_element_type=jnp.float32,
+            ).astype(jnp.bfloat16)
         out = pltpu.make_async_copy(
             grad_v.at[pl.ds(base, count)], grad.at[pl.ds(base, count), :, columns], grad_sem.at[target]
         )
@@ -209,30 +215,39 @@
         copy.wait()
     if last:
         mask_copy.wait()
-    for source in range(layers):
+    def transposed_dot(a, b):
+        return lax.dot_general(a, b, (((1,), (1,)), ((), ())), preferred_element_type=jnp.float32)
+
+    for low in range(0, layers, 2):
+        group = list(range(low, min(low + 2, layers)))
+        high = group[-1]
         if not first:
-            acc_copies[source].wait()
+            for source in group:
+                acc_copies[source].wait()
         for at in range(0, rows, CHUNK):
-            total = lax.dot_general(
-                up_v[at : at + CHUNK, source * both :],
-                dec_v[source, :, source * both :],
-                (((1,), (1,)), ((), ())),
-                preferred_element_type=jnp.float32,
-            )
             part = pl.ds(at, CHUNK)
-            if not first:
-                total = acc_v[source, part] + total
-            if last:
-                feat_v[source, part] = (total * feat_v[source, part].astype(jnp.float32)).astype(
-                    jnp.bfloat16
-                )
-            else:
-                acc_v[source, part] = total
-        out = pltpu.make_async_copy(
-            (feat_v if last else acc_v).at[source], acc_out.at[source], out_sem.at[source]
-        )
-        out.start()
-        outs.append(out)
+            totals = transposed_dot(
+                up_v[at : at + CHUNK, high * both :],
+                dec_v[low : high + 1, :, high * both :].reshape(len(group) * width, -1),
+            )
+            for i, source in enumerate(group):
+                total = totals[:, i * width : (i + 1) * width]
+                if source < high:
+                    own = slice(source * both, high * both)
+                    total += transposed_dot(up_v[at : at + CHUNK, own], dec_v[source, :, own])
+                if not first:
+                    total += acc_v[source, part]
+                if last:
+                    total *= feat_v[source, part].astype(jnp.float32)
+                    feat_v[source, part] = total.astype(jnp.bfloat16)
+                else:
+                    acc_v[source, part] = total
+        for source in group:
+            out = pltpu.make_async_copy(
+                (feat_v if last else acc_v).at[source], acc_out.at[source], out_sem.at[source]
+            )
+            out.start()
+            outs.append(out)
     for out in outs:
         out.wait()
 
@@ -310,12 +325,16 @@
                 blocks.along_line(j, range(1, end), [r + 1])
         if r == max(end - 1, 0) and end > 0:
             blocks.diagonal(end)
-        mine = [blocks.pieces[(r, j)] for j in range(n_layer)]
+        mine = [blocks.piece(r, j) for j in range(n_layer)]
         theirs = [
             blocks.swap(blocks.tie(x) if j in blocks.others else x) for j, x in enumerate(mine)
         ]
-        soon = [(r + 1, j) for j in blocks.singles] if r < end else []
-        soon += [(r + 2, 0)] if r + 2 <= end else []
+        soon = [(far, 0) for far in range(r + 1, planes) if far > r + 1 or r == 0]
+        if r == 0 and end > 0:
+            soon += [(1, j) for j in blocks.singles[1:]]
+        if r == end - 1 and r > 0:
+            soon += [(end, j) for j in blocks.singles[:1]]
+        soon = [at for at in soon if at in blocks.pieces]
         place, *ready = lax.optimization_barrier((place, *[blocks.pieces[at] for at in soon]))
         blocks.pieces.update(zip(soon, ready))
         row = [row[r] for row in blocks.order]

time: 125 us -> 127 us (1.016)
  starting transfers between devices: 28.2 us -> 31.4 us
  local copies, waits for them, and re-layouts: 3.47 us -> 1.67 us
    ppermute x34, starting transfers between devices: 28.2 us -> 31.4 us  [permute(): return lax.ppermute(x, ('layer', 'feat'), sorted(flat))]
    unnamed x38 -> x36, local copies, waits for them, and re-layouts: 3.47 us -> 1.67 us
where the time goes in v7:
time: 127 us; the launch traced here: 126 us
  Pallas kernels  56.6 us (45%)
  waiting for transfers between devices  34.7 us (27%)
  starting transfers between devices  31.4 us (25%)
  local copies, waits for them, and re-layouts  1.67 us (1%)
    pallas_call x4, Pallas kernels, run_round(): pl.pallas_call(functools.partial(round_kernel, len(mine), len(tokens), la...  52 us
    ppermute x34, waiting for transfers between devices, permute(): return lax.ppermute(x, ('layer', 'feat'), sorted(flat))  34.7 us
    ppermute x34, starting transfers between devices, permute(): return lax.ppermute(x, ('layer', 'feat'), sorted(flat))  31.4 us
    pallas_call x1, Pallas kernels, prepare(): pl.pallas_call(prepare_kernel, grid=(layers,), in_specs=[block(rows, widt...  4.54 us
  transfers between devices with their start and end apart: 34, of which 10 were waited for; matrix products, arithmetic and copies ran while one was open for 1% of the time, Pallas kernels for 35%

profile of v7, /device:TPU:0, one launch (start us, length us, event | category | flops | bytes accessed | tf_op | source)
XLA Modules:
  0.0 126.3 jit_solution(16091114364926899666)
XLA Ops:
  0.6 0.7 collective-permute-start.1
  1.3 5.9 %collective-permute-start = (bf16[4,256,256]{2,1,0:T(8,128)(2,1)}, bf16[4,256,256]{2,1,0:T(8,128)(2,1)S(1)}, u32[]{:S(2)}, u32[]{:S(2)}) collective-permute-start(bf16[4,256,256]{2,1,0:T(8,128)(2,1)} %refs_0_.1), channel_id=1, source_target_pairs={{0,2},{1,3},{2,0},{3,1},{4,6},{5,7},{6,4},{7,5},{8,10},{9,11},{10,... | collective-permute-start | bytes 1572872 | tf_op jit(solution)/shard_map/ppermute | solution.py:61
  7.2 1.5 %collective-permute-start.7 = (bf16[4,256,256]{2,1,0:T(8,128)(2,1)}, bf16[4,256,256]{2,1,0:T(8,128)(2,1)S(1)}, u32[]{:S(2)}, u32[]{:S(2)}) collective-permute-start(bf16[4,256,256]{2,1,0:T(8,128)(2,1)} %refs_0_.1), channel_id=1, source_target_pairs={{0,16},{1,17},{2,18},{3,19},{4,20},{5,21},{6,22},{7,23},{8,24},{9,... | collective-permute-start | bytes 1572872 | tf_op jit(solution)/shard_map/ppermute | solution.py:61
  8.7 1.5 %collective-permute-start.6 = (bf16[4,256,256]{2,1,0:T(8,128)(2,1)}, bf16[4,256,256]{2,1,0:T(8,128)(2,1)}, u32[]{:S(2)}, u32[]{:S(2)}) collective-permute-start(bf16[4,256,256]{2,1,0:T(8,128)(2,1)} %refs_0_.1), channel_id=1, source_target_pairs={{0,8},{1,9},{2,10},{3,11},{4,12},{5,13},{6,14},{7,15},{8,0},{9,1},... | collective-permute-start | bytes 1572872 | tf_op jit(solution)/shard_map/ppermute | solution.py:61
  10.2 4.5 %shard_map.59 = (bf16[4,256,1024]{2,1,0:T(8,128)(2,1)}, bf16[4,1024,256]{2,1,0:T(8,128)(2,1)}) custom-call(bf16[4,1024,256]{2,1,0:T(8,128)(2,1)} %act.1, s32[4,2,1024]{2,1,0:T(2,128)} %bitcast.4), custom_call_target="tpu_custom_call" | custom-call | bytes 6291456 | tf_op jit(solution)/shard_map/pallas_call | solution.py:121
  14.8 1.3 %collective-permute-start.2 = (bf16[4,256,256]{2,1,0:T(8,128)(2,1)S(1)}, bf16[4,256,256]{2,1,0:T(8,128)(2,1)S(1)}, u32[]{:S(2)}, u32[]{:S(2)}) collective-permute-start(bf16[4,256,256]{2,1,0:T(8,128)(2,1)S(1)} %collective-permute-done.1), channel_id=1, source_target_pairs={{2,0},{3,1},{4,6},{5,7},{10,8},{11,9},{12,14},{13,15},{18,16},{19,... | collective-permute-start | bytes 1572872 | tf_op jit(solution)/shard_map/ppermute | solution.py:61
  16.1 3.0 %collective-permute-done.refs_1_ = bf16[4,256,256]{2,1,0:T(8,128)(2,1)S(1)} collective-permute-done((bf16[4,256,256]{2,1,0:T(8,128)(2,1)}, bf16[4,256,256]{2,1,0:T(8,128)(2,1)S(1)}, u32[]{:S(2)}, u32[]{:S(2)}) %collective-permute-start) | collective-permute-done | bytes 524320 | tf_op jit(solution)/shard_map/ppermute | solution.py:61
  19.1 0.7 collective-permute-start.3
  19.8 0.8 collective-permute-done.7.refs_2_
  20.5 1.5 %collective-permute-start.8 = (bf16[4,256,256]{2,1,0:T(8,128)(2,1)S(1)}, bf16[4,256,256]{2,1,0:T(8,128)(2,1)}, u32[]{:S(2)}, u32[]{:S(2)}) collective-permute-start(bf16[4,256,256]{2,1,0:T(8,128)(2,1)S(1)} %collective-permute-done.7.refs_2_), channel_id=1, source_target_pairs={{0,8},{1,9},{2,10},{3,11},{4,12},{5,13},{6,14},{7,15},{8,0},{9,1},... | collective-permute-start | bytes 1572872 | tf_op jit(solution)/shard_map/ppermute | solution.py:61
  22.0 1.5 %collective-permute-start.4 = (bf16[4,256,256]{2,1,0:T(8,128)(2,1)S(1)}, bf16[4,256,256]{2,1,0:T(8,128)(2,1)S(1)}, u32[]{:S(2)}, u32[]{:S(2)}) collective-permute-start(bf16[4,256,256]{2,1,0:T(8,128)(2,1)S(1)} %collective-permute-done.refs_1_), channel_id=1, source_target_pairs={{0,16},{1,17},{2,18},{3,19},{4,20},{5,21},{6,22},{7,23},{8,24},{9,... | collective-permute-start | bytes 1572872 | tf_op jit(solution)/shard_map/ppermute | solution.py:61
  23.5 8.3 %collective-permute-done.2 = bf16[4,256,256]{2,1,0:T(8,128)(2,1)S(1)} collective-permute-done((bf16[4,256,256]{2,1,0:T(8,128)(2,1)S(1)}, bf16[4,256,256]{2,1,0:T(8,128)(2,1)S(1)}, u32[]{:S(2)}, u32[]{:S(2)}) %collective-permute-start.2) | collective-permute-done | bytes 524320 | tf_op jit(solution)/shard_map/ppermute | solution.py:61
  31.8 0.5 collective-permute-start.10
  32.4 0.8 collective-permute-done.8.refs_3_
  33.1 0.6 pad_add_fusion.meta
  33.7 0.1 broadcast_select_fusion.2.refs_1_
  33.8 0.3 collective-permute-done.4.refs_3_
  34.0 1.3 %collective-permute-start.14 = (bf16[4,256,256]{2,1,0:T(8,128)(2,1)S(1)}, bf16[4,256,256]{2,1,0:T(8,128)(2,1)}, u32[]{:S(2)}, u32[]{:S(2)}) collective-permute-start(bf16[4,256,256]{2,1,0:T(8,128)(2,1)S(1)} %collective-permute-done.refs_1_), channel_id=1, source_target_pairs={{0,8},{1,9},{2,10},{3,11},{4,12},{5,13},{6,14},{7,15},{8,0},{9,1},... | collective-permute-start | bytes 1572872 | tf_op jit(solution)/shard_map/ppermute | solution.py:61
  35.3 0.2 collective-permute-start.16
  35.6 4.0 %collective-permute-start.15 = (bf16[4,256,256]{2,1,0:T(8,128)(2,1)}, bf16[4,256,256]{2,1,0:T(8,128)(2,1)}, u32[]{:S(2)}, u32[]{:S(2)}) collective-permute-start(bf16[4,256,256]{2,1,0:T(8,128)(2,1)} %collective-permute-done.8.refs_3_), channel_id=1, source_target_pairs={{0,2},{1,3},{2,0},{3,1},{4,6},{5,7},{6,4},{7,5},{8,10},{9,11},{10,... | collective-permute-start | bytes 1572872 | tf_op jit(solution)/shard_map/ppermute | solution.py:61
  39.5 0.7 collective-permute-start.20
  40.2 1.3 %collective-permute-start.5 = (bf16[4,256,256]{2,1,0:T(8,128)(2,1)S(1)}, bf16[4,256,256]{2,1,0:T(8,128)(2,1)S(1)}, u32[]{:S(2)}, u32[]{:S(2)}) collective-permute-start(bf16[4,256,256]{2,1,0:T(8,128)(2,1)S(1)} %collective-permute-done.3), channel_id=1, source_target_pairs={{2,0},{3,1},{4,6},{5,7},{10,8},{11,9},{12,14},{13,15},{18,16},{19,... | collective-permute-start | bytes 1572872 | tf_op jit(solution)/shard_map/ppermute | solution.py:61
  41.5 13.3 %shard_map.60 = (bf16[10,256,2048]{2,1,0:T(8,128)(2,1)}, f32[4,1024,256]{2,1,0:T(8,128)}, f32[8,128]{1,0:T(8,128)}) custom-call(s32[3]{0:T(128)} %pad_add_fusion.meta, bf16[4,256,1024]{2,1,0:T(8,128)(2,1)} %get-tuple-element.43.sparse, bf16[10,256,2048]{2,1,0:T(8,128)(2,1)} %decoder.7, bf16[4,256,256]{2,1,0:T(8,128)(2,1)} %refs_0_.1, ...), custom_call_target="tpu_custom_call" | custom-call | flops 10737418240 | bytes 20971520 | tf_op jit(solution)/shard_map/pallas_call | solution.py:273
  54.9 0.1 collective-permute-start.18
  55.0 0.5 collective-permute-start.17
  55.5 7.9 %collective-permute-done.5 = bf16[4,256,256]{2,1,0:T(8,128)(2,1)S(1)} collective-permute-done((bf16[4,256,256]{2,1,0:T(8,128)(2,1)S(1)}, bf16[4,256,256]{2,1,0:T(8,128)(2,1)S(1)}, u32[]{:S(2)}, u32[]{:S(2)}) %collective-permute-start.5) | collective-permute-done | bytes 524320 | tf_op jit(solution)/shard_map/ppermute | solution.py:61
  63.4 0.1 broadcast_select_fusion.1.refs_2_
  63.4 1.0 collective-permute-start.21
  64.4 1.5 %collective-permute-start.22 = (bf16[4,256,256]{2,1,0:T(8,128)(2,1)S(1)}, bf16[4,256,256]{2,1,0:T(8,128)(2,1)}, u32[]{:S(2)}, u32[]{:S(2)}) collective-permute-start(bf16[4,256,256]{2,1,0:T(8,128)(2,1)S(1)} %broadcast_select_fusion.2.refs_1_), channel_id=1, source_target_pairs={{0,16},{1,17},{2,18},{3,19},{4,20},{5,21},{6,22},{7,23},{8,24},{9,... | collective-permute-start | bytes 1572872 | tf_op jit(solution)/shard_map/ppermute | solution.py:61
  65.9 0.1 collective-permute-start.24
  66.0 0.0 copy-start.12
  66.0 1.2 collective-permute-start.13
  67.2 1.5 %collective-permute-start.23 = (bf16[4,256,256]{2,1,0:T(8,128)(2,1)S(1)}, bf16[4,256,256]{2,1,0:T(8,128)(2,1)S(1)}, u32[]{:S(2)}, u32[]{:S(2)}) collective-permute-start(bf16[4,256,256]{2,1,0:T(8,128)(2,1)S(1)} %collective-permute-done.20), channel_id=1, source_target_pairs={{2,0},{3,1},{4,6},{5,7},{10,8},{11,9},{12,14},{13,15},{18,16},{19,... | collective-permute-start | bytes 1572872 | tf_op jit(solution)/shard_map/ppermute | solution.py:61
  68.7 13.0 %shard_map.61 = (bf16[10,256,2048]{2,1,0:T(8,128)(2,1)}, f32[4,1024,256]{2,1,0:T(8,128)}, f32[8,128]{1,0:T(8,128)}) custom-call(s32[3]{0:T(128)} %pad_add_fusion.meta, bf16[4,256,1024]{2,1,0:T(8,128)(2,1)} %get-tuple-element.43.sparse, bf16[10,256,2048]{2,1,0:T(8,128)(2,1)} %decoder.7, ...), custom_call_target="tpu_custom_call", output_to_operand_aliasing={{0}: (12, {})} | custom-call | flops 10737418240 | bytes 20971520 | tf_op jit(solution)/shard_map/pallas_call | solution.py:273
  81.8 0.6 collective-permute-start.28
  82.3 0.8 collective-permute-done.23
  83.1 0.1 broadcast_select_fusion.refs_4_
  83.2 0.0 copy-start.2
  83.2 5.9 %collective-permute-done.13.refs_3_ = bf16[4,256,256]{2,1,0:T(8,128)(2,1)S(1)} collective-permute-done((bf16[4,256,256]{2,1,0:T(8,128)(2,1)S(1)}, bf16[4,256,256]{2,1,0:T(8,128)(2,1)S(1)}, u32[]{:S(2)}, u32[]{:S(2)}) %collective-permute-start.13) | collective-permute-done | bytes 524320 | tf_op jit(solution)/shard_map/ppermute | solution.py:61
  89.1 0.5 collective-permute-start.30
  89.6 1.5 %collective-permute-start.29 = (bf16[4,256,256]{2,1,0:T(8,128)(2,1)S(1)}, bf16[4,256,256]{2,1,0:T(8,128)(2,1)S(1)}, u32[]{:S(2)}, u32[]{:S(2)}) collective-permute-start(bf16[4,256,256]{2,1,0:T(8,128)(2,1)S(1)} %collective-permute-done.13.refs_3_), channel_id=1, source_target_pairs={{0,16},{1,17},{2,18},{3,19},{4,20},{5,21},{6,22},{7,23},{8,24},{9,... | collective-permute-start | bytes 1572872 | tf_op jit(solution)/shard_map/ppermute | solution.py:61
  91.1 5.5 %collective-permute-done.28.refs_4_ = bf16[4,256,256]{2,1,0:T(8,128)(2,1)S(1)} collective-permute-done((bf16[4,256,256]{2,1,0:T(8,128)(2,1)S(1)}, bf16[4,256,256]{2,1,0:T(8,128)(2,1)S(1)}, u32[]{:S(2)}, u32[]{:S(2)}) %collective-permute-start.28) | collective-permute-done | bytes 524320 | tf_op jit(solution)/shard_map/ppermute | solution.py:61
  96.6 0.8 copy-done.16
  97.5 13.0 %shard_map.62 = (bf16[10,256,2048]{2,1,0:T(8,128)(2,1)}, f32[4,1024,256]{2,1,0:T(8,128)}, f32[8,128]{1,0:T(8,128)}) custom-call(s32[3]{0:T(128)} %pad_add_fusion.meta, bf16[4,256,1024]{2,1,0:T(8,128)(2,1)} %get-tuple-element.43.sparse, bf16[10,256,2048]{2,1,0:T(8,128)(2,1)} %decoder.7, ...), custom_call_target="tpu_custom_call", output_to_operand_aliasing={{0}: (12, {})} | custom-call | flops 10737418240 | bytes 20971520 | tf_op jit(solution)/shard_map/pallas_call | solution.py:273
  110.5 0.5 collective-permute-start.33
  111.1 1.5 %collective-permute-done.33.refs_9_ = bf16[4,256,256]{2,1,0:T(8,128)(2,1)S(1)} collective-permute-done((bf16[4,256,256]{2,1,0:T(8,128)(2,1)S(1)}, bf16[4,256,256]{2,1,0:T(8,128)(2,1)S(1)}, u32[]{:S(2)}, u32[]{:S(2)}) %collective-permute-start.33) | collective-permute-done | bytes 524320 | tf_op jit(solution)/shard_map/ppermute | solution.py:61
  112.6 0.8 copy-done.17
  113.4 12.7 %shard_map.63 = (bf16[10,256,2048]{2,1,0:T(8,128)(2,1)}, bf16[4,1024,256]{2,1,0:T(8,128)(2,1)}, f32[8,128]{1,0:T(8,128)}) custom-call(s32[3]{0:T(128)} %pad_add_fusion.meta, bf16[4,256,1024]{2,1,0:T(8,128)(2,1)} %get-tuple-element.43.sparse, bf16[10,256,2048]{2,1,0:T(8,128)(2,1)} %decoder.7, ...), custom_call_target="tpu_custom_call", output_to_operand_aliasing={{0}: (13, {})} | custom-call | flops 10737418240 | bytes 20971520 | tf_op jit(solution)/shard_map/pallas_call | solution.py:273
  (65 shorter events, 0.1 us)
Async XLA Ops:
  0.6 14.1 %collective-permute-start.1 = (bf16[4,256,256]{2,1,0:T(8,128)(2,1)}, bf16[4,256,256]{2,1,0:T(8,128)(2,1)S(1)}, u32[]{:S(2)}, u32[]{:S(2)}) collective-permute-start(bf16[4,256,256]{2,1,0:T(8,128)(2,1)} %refs_0_.1), channel_id=1, source_target_pairs={{2,4},{3,5},{4,2},{5,3},{10,12},{11,13},{12,10},{13,11},{18,20},{1... | collective-permute-start | bytes 1572872 | tf_op jit(solution)/shard_map/ppermute | solution.py:61
  1.3 17.7 %collective-permute-start = (bf16[4,256,256]{2,1,0:T(8,128)(2,1)}, bf16[4,256,256]{2,1,0:T(8,128)(2,1)S(1)}, u32[]{:S(2)}, u32[]{:S(2)}) collective-permute-start(bf16[4,256,256]{2,1,0:T(8,128)(2,1)} %refs_0_.1), channel_id=1, source_target_pairs={{0,2},{1,3},{2,0},{3,1},{4,6},{5,7},{6,4},{7,5},{8,10},{9,11},{10,... | collective-permute-start | bytes 1572872 | tf_op jit(solution)/shard_map/ppermute | solution.py:61
  7.2 13.3 %collective-permute-start.7 = (bf16[4,256,256]{2,1,0:T(8,128)(2,1)}, bf16[4,256,256]{2,1,0:T(8,128)(2,1)S(1)}, u32[]{:S(2)}, u32[]{:S(2)}) collective-permute-start(bf16[4,256,256]{2,1,0:T(8,128)(2,1)} %refs_0_.1), channel_id=1, source_target_pairs={{0,16},{1,17},{2,18},{3,19},{4,20},{5,21},{6,22},{7,23},{8,24},{9,... | collective-permute-start | bytes 1572872 | tf_op jit(solution)/shard_map/ppermute | solution.py:61
  8.7 14.8 %collective-permute-start.6 = (bf16[4,256,256]{2,1,0:T(8,128)(2,1)}, bf16[4,256,256]{2,1,0:T(8,128)(2,1)}, u32[]{:S(2)}, u32[]{:S(2)}) collective-permute-start(bf16[4,256,256]{2,1,0:T(8,128)(2,1)} %refs_0_.1), channel_id=1, source_target_pairs={{0,8},{1,9},{2,10},{3,11},{4,12},{5,13},{6,14},{7,15},{8,0},{9,1},... | collective-permute-start | bytes 1572872 | tf_op jit(solution)/shard_map/ppermute | solution.py:61
  14.8 17.1 %collective-permute-start.2 = (bf16[4,256,256]{2,1,0:T(8,128)(2,1)S(1)}, bf16[4,256,256]{2,1,0:T(8,128)(2,1)S(1)}, u32[]{:S(2)}, u32[]{:S(2)}) collective-permute-start(bf16[4,256,256]{2,1,0:T(8,128)(2,1)S(1)} %collective-permute-done.1), channel_id=1, source_target_pairs={{2,0},{3,1},{4,6},{5,7},{10,8},{11,9},{12,14},{13,15},{18,16},{19,... | collective-permute-start | bytes 1572872 | tf_op jit(solution)/shard_map/ppermute | solution.py:61
  19.1 35.8 %copy-start.3 = (bf16[4,256,256]{2,1,0:T(8,128)(2,1)}, bf16[4,256,256]{2,1,0:T(8,128)(2,1)S(1)}, u32[]{:S(2)}) copy-start(bf16[4,256,256]{2,1,0:T(8,128)(2,1)S(1)} %collective-permute-done.refs_1_) | copy-start | bytes 1572868
  19.1 12.8 %collective-permute-start.3 = (bf16[4,256,256]{2,1,0:T(8,128)(2,1)S(1)}, bf16[4,256,256]{2,1,0:T(8,128)(2,1)S(1)}, u32[]{:S(2)}, u32[]{:S(2)}) collective-permute-start(bf16[4,256,256]{2,1,0:T(8,128)(2,1)S(1)} %collective-permute-done.refs_1_), channel_id=1, source_target_pairs={{2,4},{3,5},{4,2},{5,3},{10,12},{11,13},{12,10},{13,11},{18,20},{1... | collective-permute-start | bytes 1572872 | tf_op jit(solution)/shard_map/ppermute | solution.py:61
  20.5 19.7 %copy-start.5 = (bf16[4,256,256]{2,1,0:T(8,128)(2,1)}, bf16[4,256,256]{2,1,0:T(8,128)(2,1)S(1)}, u32[]{:S(2)}) copy-start(bf16[4,256,256]{2,1,0:T(8,128)(2,1)S(1)} %collective-permute-done.7.refs_2_) | copy-start | bytes 1572868
  20.5 12.6 %collective-permute-start.8 = (bf16[4,256,256]{2,1,0:T(8,128)(2,1)S(1)}, bf16[4,256,256]{2,1,0:T(8,128)(2,1)}, u32[]{:S(2)}, u32[]{:S(2)}) collective-permute-start(bf16[4,256,256]{2,1,0:T(8,128)(2,1)S(1)} %collective-permute-done.7.refs_2_), channel_id=1, source_target_pairs={{0,8},{1,9},{2,10},{3,11},{4,12},{5,13},{6,14},{7,15},{8,0},{9,1},... | collective-permute-start | bytes 1572872 | tf_op jit(solution)/shard_map/ppermute | solution.py:61
  22.0 12.0 %collective-permute-start.4 = (bf16[4,256,256]{2,1,0:T(8,128)(2,1)S(1)}, bf16[4,256,256]{2,1,0:T(8,128)(2,1)S(1)}, u32[]{:S(2)}, u32[]{:S(2)}) collective-permute-start(bf16[4,256,256]{2,1,0:T(8,128)(2,1)S(1)} %collective-permute-done.refs_1_), channel_id=1, source_target_pairs={{0,16},{1,17},{2,18},{3,19},{4,20},{5,21},{6,22},{7,23},{8,24},{9,... | collective-permute-start | bytes 1572872 | tf_op jit(solution)/shard_map/ppermute | solution.py:61
  23.5 11.8 %collective-permute-start.9 = (bf16[4,256,256]{2,1,0:T(8,128)(2,1)}, bf16[4,256,256]{2,1,0:T(8,128)(2,1)}, u32[]{:S(2)}, u32[]{:S(2)}) collective-permute-start(bf16[4,256,256]{2,1,0:T(8,128)(2,1)} %refs_0_.1), channel_id=1, source_target_pairs={{0,1},{1,0},{2,3},{3,2},{4,5},{5,4},{6,7},{7,6},{8,9},{9,8},{10,11... | collective-permute-start | bytes 1572872 | tf_op jit(solution)/shard_map/ppermute | solution.py:61
  31.8 3.7 %collective-permute-start.11 = (bf16[4,256,256]{2,1,0:T(8,128)(2,1)S(1)}, bf16[4,256,256]{2,1,0:T(8,128)(2,1)}, u32[]{:S(2)}, u32[]{:S(2)}) collective-permute-start(bf16[4,256,256]{2,1,0:T(8,128)(2,1)S(1)} %collective-permute-done.7.refs_2_), channel_id=1, source_target_pairs={{0,1},{1,0},{2,3},{3,2},{4,5},{5,4},{6,7},{7,6},{8,9},{9,8},{10,11... | collective-permute-start | bytes 1572872 | tf_op jit(solution)/shard_map/ppermute | solution.py:61
  31.8 7.7 %collective-permute-start.10 = (bf16[4,256,256]{2,1,0:T(8,128)(2,1)}, bf16[4,256,256]{2,1,0:T(8,128)(2,1)}, u32[]{:S(2)}, u32[]{:S(2)}) collective-permute-start(bf16[4,256,256]{2,1,0:T(8,128)(2,1)} %collective-permute-done.6.refs_1_), channel_id=1, source_target_pairs={{0,1},{1,0},{2,3},{3,2},{4,5},{5,4},{6,7},{7,6},{8,9},{9,8},{10,11... | collective-permute-start | bytes 1572872 | tf_op jit(solution)/shard_map/ppermute | solution.py:61
  33.1 7.1 %collective-permute-start.12 = (bf16[4,256,256]{2,1,0:T(8,128)(2,1)}, bf16[4,256,256]{2,1,0:T(8,128)(2,1)}, u32[]{:S(2)}, u32[]{:S(2)}) collective-permute-start(bf16[4,256,256]{2,1,0:T(8,128)(2,1)} %collective-permute-done.8.refs_3_), channel_id=1, source_target_pairs={{0,1},{1,0},{2,3},{3,2},{4,5},{5,4},{6,7},{7,6},{8,9},{9,8},{10,11... | collective-permute-start | bytes 1572872 | tf_op jit(solution)/shard_map/ppermute | solution.py:61
  33.8 32.2 %copy-start = (bf16[4,256,256]{2,1,0:T(8,128)(2,1)}, bf16[4,256,256]{2,1,0:T(8,128)(2,1)S(1)}, u32[]{:S(2)}) copy-start(bf16[4,256,256]{2,1,0:T(8,128)(2,1)S(1)} %broadcast_select_fusion.2.refs_1_) | copy-start | bytes 1572868
  34.0 20.8 %copy-start.4 = (bf16[4,256,256]{2,1,0:T(8,128)(2,1)}, bf16[4,256,256]{2,1,0:T(8,128)(2,1)S(1)}, u32[]{:S(2)}) copy-start(bf16[4,256,256]{2,1,0:T(8,128)(2,1)S(1)} %collective-permute-done.4.refs_3_) | copy-start | bytes 1572868
  34.0 20.8 %collective-permute-start.14 = (bf16[4,256,256]{2,1,0:T(8,128)(2,1)S(1)}, bf16[4,256,256]{2,1,0:T(8,128)(2,1)}, u32[]{:S(2)}, u32[]{:S(2)}) collective-permute-start(bf16[4,256,256]{2,1,0:T(8,128)(2,1)S(1)} %collective-permute-done.refs_1_), channel_id=1, source_target_pairs={{0,8},{1,9},{2,10},{3,11},{4,12},{5,13},{6,14},{7,15},{8,0},{9,1},... | collective-permute-start | bytes 1572872 | tf_op jit(solution)/shard_map/ppermute | solution.py:61
  35.3 29.1 %collective-permute-start.16 = (bf16[4,256,256]{2,1,0:T(8,128)(2,1)S(1)}, bf16[4,256,256]{2,1,0:T(8,128)(2,1)}, u32[]{:S(2)}, u32[]{:S(2)}) collective-permute-start(bf16[4,256,256]{2,1,0:T(8,128)(2,1)S(1)} %collective-permute-done.refs_1_), channel_id=1, source_target_pairs={{0,1},{1,0},{2,3},{3,2},{4,5},{5,4},{6,7},{7,6},{8,9},{9,8},{10,11... | collective-permute-start | bytes 1572872 | tf_op jit(solution)/shard_map/ppermute | solution.py:61
  35.6 19.4 %collective-permute-start.15 = (bf16[4,256,256]{2,1,0:T(8,128)(2,1)}, bf16[4,256,256]{2,1,0:T(8,128)(2,1)}, u32[]{:S(2)}, u32[]{:S(2)}) collective-permute-start(bf16[4,256,256]{2,1,0:T(8,128)(2,1)} %collective-permute-done.8.refs_3_), channel_id=1, source_target_pairs={{0,2},{1,3},{2,0},{3,1},{4,6},{5,7},{6,4},{7,5},{8,10},{9,11},{10,... | collective-permute-start | bytes 1572872 | tf_op jit(solution)/shard_map/ppermute | solution.py:61
  39.5 23.9 %collective-permute-start.20 = (bf16[4,256,256]{2,1,0:T(8,128)(2,1)}, bf16[4,256,256]{2,1,0:T(8,128)(2,1)S(1)}, u32[]{:S(2)}, u32[]{:S(2)}) collective-permute-start(bf16[4,256,256]{2,1,0:T(8,128)(2,1)} %collective-permute-done.8.refs_3_), channel_id=1, source_target_pairs={{2,4},{3,5},{4,2},{5,3},{10,12},{11,13},{12,10},{13,11},{18,20},{1... | collective-permute-start | bytes 1572872 | tf_op jit(solution)/shard_map/ppermute | solution.py:61
  40.2 23.1 %collective-permute-start.5 = (bf16[4,256,256]{2,1,0:T(8,128)(2,1)S(1)}, bf16[4,256,256]{2,1,0:T(8,128)(2,1)S(1)}, u32[]{:S(2)}, u32[]{:S(2)}) collective-permute-start(bf16[4,256,256]{2,1,0:T(8,128)(2,1)S(1)} %collective-permute-done.3), channel_id=1, source_target_pairs={{2,0},{3,1},{4,6},{5,7},{10,8},{11,9},{12,14},{13,15},{18,16},{19,... | collective-permute-start | bytes 1572872 | tf_op jit(solution)/shard_map/ppermute | solution.py:61
  54.9 11.1 %collective-permute-start.18 = (bf16[4,256,256]{2,1,0:T(8,128)(2,1)S(1)}, bf16[4,256,256]{2,1,0:T(8,128)(2,1)S(1)}, u32[]{:S(2)}, u32[]{:S(2)}) collective-permute-start(bf16[4,256,256]{2,1,0:T(8,128)(2,1)S(1)} %collective-permute-done.4.refs_3_), channel_id=1, source_target_pairs={{0,1},{1,0},{2,3},{3,2},{4,5},{5,4},{6,7},{7,6},{8,9},{9,8},{10,11... | collective-permute-start | bytes 1572872 | tf_op jit(solution)/shard_map/ppermute | solution.py:61
  55.0 11.0 %collective-permute-start.17 = (bf16[4,256,256]{2,1,0:T(8,128)(2,1)}, bf16[4,256,256]{2,1,0:T(8,128)(2,1)S(1)}, u32[]{:S(2)}, u32[]{:S(2)}) collective-permute-start(bf16[4,256,256]{2,1,0:T(8,128)(2,1)} %collective-permute-done.14.refs_2_), channel_id=1, source_target_pairs={{0,1},{1,0},{2,3},{3,2},{4,5},{5,4},{6,7},{7,6},{8,9},{9,8},{10,11... | collective-permute-start | bytes 1572872 | tf_op jit(solution)/shard_map/ppermute | solution.py:61
  63.3 3.9 %collective-permute-start.19 = (bf16[4,256,256]{2,1,0:T(8,128)(2,1)}, bf16[4,256,256]{2,1,0:T(8,128)(2,1)S(1)}, u32[]{:S(2)}, u32[]{:S(2)}) collective-permute-start(bf16[4,256,256]{2,1,0:T(8,128)(2,1)} %collective-permute-done.15.refs_4_), channel_id=1, source_target_pairs={{0,1},{1,0},{2,3},{3,2},{4,5},{5,4},{6,7},{7,6},{8,9},{9,8},{10,11... | collective-permute-start | bytes 1572872 | tf_op jit(solution)/shard_map/ppermute | solution.py:61
  63.4 25.7 %copy-start.1 = (bf16[4,256,256]{2,1,0:T(8,128)(2,1)}, bf16[4,256,256]{2,1,0:T(8,128)(2,1)S(1)}, u32[]{:S(2)}) copy-start(bf16[4,256,256]{2,1,0:T(8,128)(2,1)S(1)} %broadcast_select_fusion.1.refs_2_) | copy-start | bytes 1572868
  63.4 18.3 %collective-permute-start.21 = (bf16[4,256,256]{2,1,0:T(8,128)(2,1)S(1)}, bf16[4,256,256]{2,1,0:T(8,128)(2,1)}, u32[]{:S(2)}, u32[]{:S(2)}) collective-permute-start(bf16[4,256,256]{2,1,0:T(8,128)(2,1)S(1)} %broadcast_select_fusion.2.refs_1_), channel_id=1, source_target_pairs={{0,8},{1,9},{2,10},{3,11},{4,12},{5,13},{6,14},{7,15},{8,0},{9,1},... | collective-permute-start | bytes 1572872 | tf_op jit(solution)/shard_map/ppermute | solution.py:61
  64.4 17.9 %collective-permute-start.22 = (bf16[4,256,256]{2,1,0:T(8,128)(2,1)S(1)}, bf16[4,256,256]{2,1,0:T(8,128)(2,1)}, u32[]{:S(2)}, u32[]{:S(2)}) collective-permute-start(bf16[4,256,256]{2,1,0:T(8,128)(2,1)S(1)} %broadcast_select_fusion.2.refs_1_), channel_id=1, source_target_pairs={{0,16},{1,17},{2,18},{3,19},{4,20},{5,21},{6,22},{7,23},{8,24},{9,... | collective-permute-start | bytes 1572872 | tf_op jit(solution)/shard_map/ppermute | solution.py:61
  65.9 23.1 %collective-permute-start.24 = (bf16[4,256,256]{2,1,0:T(8,128)(2,1)S(1)}, bf16[4,256,256]{2,1,0:T(8,128)(2,1)}, u32[]{:S(2)}, u32[]{:S(2)}) collective-permute-start(bf16[4,256,256]{2,1,0:T(8,128)(2,1)S(1)} %broadcast_select_fusion.2.refs_1_), channel_id=1, source_target_pairs={{0,1},{1,0},{2,3},{3,2},{4,5},{5,4},{6,7},{7,6},{8,9},{9,8},{10,11... | collective-permute-start | bytes 1572872 | tf_op jit(solution)/shard_map/ppermute | solution.py:61
  66.0 23.0 %collective-permute-start.13 = (bf16[4,256,256]{2,1,0:T(8,128)(2,1)S(1)}, bf16[4,256,256]{2,1,0:T(8,128)(2,1)S(1)}, u32[]{:S(2)}, u32[]{:S(2)}) collective-permute-start(bf16[4,256,256]{2,1,0:T(8,128)(2,1)S(1)} %broadcast_select_fusion.1.refs_2_), channel_id=1, source_target_pairs={{0,8},{1,9},{2,10},{3,11},{4,12},{5,13},{6,14},{7,15},{8,0},{9,1},... | collective-permute-start | bytes 1572872 | tf_op jit(solution)/shard_map/ppermute | solution.py:61
  67.2 1.5 %copy-start.15 = (bf16[4,256,256]{2,1,0:T(8,128)(2,1)}, bf16[4,256,256]{2,1,0:T(8,128)(2,1)S(1)}, u32[]{:S(2)}) copy-start(bf16[4,256,256]{2,1,0:T(8,128)(2,1)S(1)} %collective-permute-done.19.refs_8_) | copy-start | bytes 1572868
  67.2 15.9 %collective-permute-start.23 = (bf16[4,256,256]{2,1,0:T(8,128)(2,1)S(1)}, bf16[4,256,256]{2,1,0:T(8,128)(2,1)S(1)}, u32[]{:S(2)}, u32[]{:S(2)}) collective-permute-start(bf16[4,256,256]{2,1,0:T(8,128)(2,1)S(1)} %collective-permute-done.20), channel_id=1, source_target_pairs={{2,0},{3,1},{4,6},{5,7},{10,8},{11,9},{12,14},{13,15},{18,16},{19,... | collective-permute-start | bytes 1572872 | tf_op jit(solution)/shard_map/ppermute | solution.py:61
  81.8 14.8 %collective-permute-start.28 = (bf16[4,256,256]{2,1,0:T(8,128)(2,1)S(1)}, bf16[4,256,256]{2,1,0:T(8,128)(2,1)S(1)}, u32[]{:S(2)}, u32[]{:S(2)}) collective-permute-start(bf16[4,256,256]{2,1,0:T(8,128)(2,1)S(1)} %broadcast_select_fusion.1.refs_2_), channel_id=1, source_target_pairs={{0,16},{1,17},{2,18},{3,19},{4,20},{5,21},{6,22},{7,23},{8,24},{9,... | collective-permute-start | bytes 1572872 | tf_op jit(solution)/shard_map/ppermute | solution.py:61
  82.3 7.3 %collective-permute-start.25 = (bf16[4,256,256]{2,1,0:T(8,128)(2,1)}, bf16[4,256,256]{2,1,0:T(8,128)(2,1)S(1)}, u32[]{:S(2)}, u32[]{:S(2)}) collective-permute-start(bf16[4,256,256]{2,1,0:T(8,128)(2,1)} %collective-permute-done.21.refs_2_), channel_id=1, source_target_pairs={{0,1},{1,0},{2,3},{3,2},{4,5},{5,4},{6,7},{7,6},{8,9},{9,8},{10,11... | collective-permute-start | bytes 1572872 | tf_op jit(solution)/shard_map/ppermute | solution.py:61
  83.1 8.0 %collective-permute-start.26 = (bf16[4,256,256]{2,1,0:T(8,128)(2,1)}, bf16[4,256,256]{2,1,0:T(8,128)(2,1)S(1)}, u32[]{:S(2)}, u32[]{:S(2)}) collective-permute-start(bf16[4,256,256]{2,1,0:T(8,128)(2,1)} %collective-permute-done.22.refs_3_), channel_id=1, source_target_pairs={{0,1},{1,0},{2,3},{3,2},{4,5},{5,4},{6,7},{7,6},{8,9},{9,8},{10,11... | collective-permute-start | bytes 1572872 | tf_op jit(solution)/shard_map/ppermute | solution.py:61
  83.2 14.3 %copy-start.2 = (bf16[4,256,256]{2,1,0:T(8,128)(2,1)}, bf16[4,256,256]{2,1,0:T(8,128)(2,1)S(1)}, u32[]{:S(2)}) copy-start(bf16[4,256,256]{2,1,0:T(8,128)(2,1)S(1)} %broadcast_select_fusion.refs_4_) | copy-start | bytes 1572868
  89.1 21.4 %copy-start.6 = (bf16[4,256,256]{2,1,0:T(8,128)(2,1)}, bf16[4,256,256]{2,1,0:T(8,128)(2,1)S(1)}, u32[]{:S(2)}) copy-start(bf16[4,256,256]{2,1,0:T(8,128)(2,1)S(1)} %collective-permute-done.13.refs_3_) | copy-start | bytes 1572868
  89.1 7.5 %collective-permute-start.27 = (bf16[4,256,256]{2,1,0:T(8,128)(2,1)S(1)}, bf16[4,256,256]{2,1,0:T(8,128)(2,1)S(1)}, u32[]{:S(2)}, u32[]{:S(2)}) collective-permute-start(bf16[4,256,256]{2,1,0:T(8,128)(2,1)S(1)} %broadcast_select_fusion.refs_4_), channel_id=1, source_target_pairs={{0,1},{1,0},{2,3},{3,2},{4,5},{5,4},{6,7},{7,6},{8,9},{9,8},{10,11... | collective-permute-start | bytes 1572872 | tf_op jit(solution)/shard_map/ppermute | solution.py:61
  89.1 21.9 %collective-permute-start.30 = (bf16[4,256,256]{2,1,0:T(8,128)(2,1)S(1)}, bf16[4,256,256]{2,1,0:T(8,128)(2,1)S(1)}, u32[]{:S(2)}, u32[]{:S(2)}) collective-permute-start(bf16[4,256,256]{2,1,0:T(8,128)(2,1)S(1)} %broadcast_select_fusion.1.refs_2_), channel_id=1, source_target_pairs={{0,1},{1,0},{2,3},{3,2},{4,5},{5,4},{6,7},{7,6},{8,9},{9,8},{10,11... | collective-permute-start | bytes 1572872 | tf_op jit(solution)/shard_map/ppermute | solution.py:61
  89.6 7.0 %copy-start.11 = (bf16[4,256,256]{2,1,0:T(8,128)(2,1)}, bf16[4,256,256]{2,1,0:T(8,128)(2,1)S(1)}, u32[]{:S(2)}) copy-start(bf16[4,256,256]{2,1,0:T(8,128)(2,1)S(1)} %collective-permute-done.25.refs_6_) | copy-start | bytes 1572868
  89.6 20.9 %collective-permute-start.29 = (bf16[4,256,256]{2,1,0:T(8,128)(2,1)S(1)}, bf16[4,256,256]{2,1,0:T(8,128)(2,1)S(1)}, u32[]{:S(2)}, u32[]{:S(2)}) collective-permute-start(bf16[4,256,256]{2,1,0:T(8,128)(2,1)S(1)} %collective-permute-done.13.refs_3_), channel_id=1, source_target_pairs={{0,16},{1,17},{2,18},{3,19},{4,20},{5,21},{6,22},{7,23},{8,24},{9,... | collective-permute-start | bytes 1572872 | tf_op jit(solution)/shard_map/ppermute | solution.py:61
  91.1 5.5 %copy-start.14 = (bf16[4,256,256]{2,1,0:T(8,128)(2,1)}, bf16[4,256,256]{2,1,0:T(8,128)(2,1)S(1)}, u32[]{:S(2)}) copy-start(bf16[4,256,256]{2,1,0:T(8,128)(2,1)S(1)} %collective-permute-done.26.refs_7_) | copy-start | bytes 1572868
  91.1 19.9 %collective-permute-start.31 = (bf16[4,256,256]{2,1,0:T(8,128)(2,1)S(1)}, bf16[4,256,256]{2,1,0:T(8,128)(2,1)S(1)}, u32[]{:S(2)}, u32[]{:S(2)}) collective-permute-start(bf16[4,256,256]{2,1,0:T(8,128)(2,1)S(1)} %collective-permute-done.13.refs_3_), channel_id=1, source_target_pairs={{0,1},{1,0},{2,3},{3,2},{4,5},{5,4},{6,7},{7,6},{8,9},{9,8},{10,11... | collective-permute-start | bytes 1572872 | tf_op jit(solution)/shard_map/ppermute | solution.py:61
  96.6 13.9 %copy-start.7 = (bf16[4,256,256]{2,1,0:T(8,128)(2,1)}, bf16[4,256,256]{2,1,0:T(8,128)(2,1)S(1)}, u32[]{:S(2)}) copy-start(bf16[4,256,256]{2,1,0:T(8,128)(2,1)S(1)} %collective-permute-done.28.refs_4_) | copy-start | bytes 1572868
  96.6 14.5 %collective-permute-start.32 = (bf16[4,256,256]{2,1,0:T(8,128)(2,1)S(1)}, bf16[4,256,256]{2,1,0:T(8,128)(2,1)}, u32[]{:S(2)}, u32[]{:S(2)}) collective-permute-start(bf16[4,256,256]{2,1,0:T(8,128)(2,1)S(1)} %collective-permute-done.28.refs_4_), channel_id=1, source_target_pairs={{0,1},{1,0},{2,3},{3,2},{4,5},{5,4},{6,7},{7,6},{8,9},{9,8},{10,11... | collective-permute-start | bytes 1572872 | tf_op jit(solution)/shard_map/ppermute | solution.py:61
  110.5 2.1 %copy-start.10 = (bf16[4,256,256]{2,1,0:T(8,128)(2,1)}, bf16[4,256,256]{2,1,0:T(8,128)(2,1)S(1)}, u32[]{:S(2)}) copy-start(bf16[4,256,256]{2,1,0:T(8,128)(2,1)S(1)} %collective-permute-done.29.refs_5_) | copy-start | bytes 1572868
  110.5 2.1 %collective-permute-start.33 = (bf16[4,256,256]{2,1,0:T(8,128)(2,1)S(1)}, bf16[4,256,256]{2,1,0:T(8,128)(2,1)S(1)}, u32[]{:S(2)}, u32[]{:S(2)}) collective-permute-start(bf16[4,256,256]{2,1,0:T(8,128)(2,1)S(1)} %collective-permute-done.29.refs_5_), channel_id=1, source_target_pairs={{0,1},{1,0},{2,3},{3,2},{4,5},{5,4},{6,7},{7,6},{8,9},{9,8},{10,11... | collective-permute-start | bytes 1572872 | tf_op jit(solution)/shard_map/ppermute | solution.py:61
  111.0 1.5 %copy-start.8 = (bf16[4,256,256]{2,1,0:T(8,128)(2,1)}, bf16[4,256,256]{2,1,0:T(8,128)(2,1)S(1)}, u32[]{:S(2)}) copy-start(bf16[4,256,256]{2,1,0:T(8,128)(2,1)S(1)} %collective-permute-done.30.refs_6_) | copy-start | bytes 1572868
  111.0 1.5 %copy-start.13 = (bf16[4,256,256]{2,1,0:T(8,128)(2,1)}, bf16[4,256,256]{2,1,0:T(8,128)(2,1)S(1)}, u32[]{:S(2)}) copy-start(bf16[4,256,256]{2,1,0:T(8,128)(2,1)S(1)} %collective-permute-done.31.refs_7_) | copy-start | bytes 1572868
  (4 other events, 4.1 us)

commit v8 on v7

--- a/solution.py
+++ b/solution.py
@@ -194,47 +194,55 @@
         mask_copy = pltpu.make_async_copy(mask, feat_v, in_sem.at[1])
         mask_copy.start()
     copies[0].wait()
-    outs = []
     for target in reversed(range(layers)):
         for copy in ups[target]:
             copy.wait()
-        count = target + 1
-        base = target * (target + 1) // 2
-        for source in range(count):
-            grad_v[base + source] = jnp.dot(
-                sparse_v[source],
-                up_v[:, target * both : (target + 1) * both],
-                preferred_element_type=jnp.float32,
-            ).astype(jnp.bfloat16)
-        out = pltpu.make_async_copy(
-            grad_v.at[pl.ds(base, count)], grad.at[pl.ds(base, count), :, columns], grad_sem.at[target]
-        )
-        out.start()
-        outs.append(out)
+
+    def grad_copy(pair):
+        return pltpu.make_async_copy(grad_v.at[pair], grad.at[pair, :, columns], grad_sem.at[pair])
+
+    @pl.loop(0, decoder.shape[0])
+    def _(pair):
+        target = sum((pair >= t * (t + 1) // 2).astype(jnp.int32) for t in range(1, layers))
+        source = pair - target * (target + 1) // 2
+        grad_v[pair] = jnp.dot(
+            sparse_v[source],
+            up_v[:, pl.ds(pl.multiple_of(target * both, both), both)],
+            preferred_element_type=jnp.float32,
+        ).astype(jnp.bfloat16)
+        grad_copy(pair).start()
+
     for copy in decs:
+        copy.wait()
+    for copy in acc_copies:
         copy.wait()
     if last:
         mask_copy.wait()
+
     def transposed_dot(a, b):
         return lax.dot_general(a, b, (((1,), (1,)), ((), ())), preferred_element_type=jnp.float32)
 
-    for low in range(0, layers, 2):
-        group = list(range(low, min(low + 2, layers)))
-        high = group[-1]
-        if not first:
-            for source in group:
-                acc_copies[source].wait()
-        for at in range(0, rows, CHUNK):
-            part = pl.ds(at, CHUNK)
+    def acc_copy(at):
+        part = pl.ds(pl.multiple_of(at * CHUNK, CHUNK), CHUNK)
+        return pltpu.make_async_copy(
+            (feat_v if last else acc_v).at[:, part], acc_out.at[:, part], out_sem.at[at]
+        )
+
+    @pl.loop(0, rows // CHUNK)
+    def _(at):
+        part = pl.ds(pl.multiple_of(at * CHUNK, CHUNK), CHUNK)
+        for low in range(0, layers, 2):
+            group = list(range(low, min(low + 2, layers)))
+            high = group[-1]
             totals = transposed_dot(
-                up_v[at : at + CHUNK, high * both :],
+                up_v[part, high * both :],
                 dec_v[low : high + 1, :, high * both :].reshape(len(group) * width, -1),
             )
             for i, source in enumerate(group):
                 total = totals[:, i * width : (i + 1) * width]
                 if source < high:
                     own = slice(source * both, high * both)
-                    total += transposed_dot(up_v[at : at + CHUNK, own], dec_v[source, :, own])
+                    total += transposed_dot(up_v[part, own], dec_v[source, :, own])
                 if not first:
                     total += acc_v[source, part]
                 if last:
@@ -242,14 +250,12 @@
                     feat_v[source, part] = total.astype(jnp.bfloat16)
                 else:
                     acc_v[source, part] = total
-        for source in group:
-            out = pltpu.make_async_copy(
-                (feat_v if last else acc_v).at[source], acc_out.at[source], out_sem.at[source]
-            )
-            out.start()
-            outs.append(out)
-    for out in outs:
-        out.wait()
+        acc_copy(at).start()
+
+    for pair in range(decoder.shape[0]):
+        grad_copy(pair).wait()
+    for at in range(rows // CHUNK):
+        acc_copy(at).wait()
 
 
 def run_round(order, meta, tokens, sparse, decoder, mask, acc, grad, mine, theirs, last):
@@ -289,8 +295,8 @@
             pltpu.SemaphoreType.DMA((layers, CORES * len(mine))),
             pltpu.SemaphoreType.DMA((pairs,)),
             pltpu.SemaphoreType.DMA((2 + layers,)),
-            pltpu.SemaphoreType.DMA((layers,)),
-            pltpu.SemaphoreType.DMA((layers,)),
+            pltpu.SemaphoreType.DMA((pairs,)),
+            pltpu.SemaphoreType.DMA((rows // CHUNK,)),
         ],
         input_output_aliases=aliases,
         cost_estimate=pl.CostEstimate(
@@ -329,11 +335,10 @@
         theirs = [
             blocks.swap(blocks.tie(x) if j in blocks.others else x) for j, x in enumerate(mine)
         ]
-        soon = [(far, 0) for far in range(r + 1, planes) if far > r + 1 or r == 0]
-        if r == 0 and end > 0:
-            soon += [(1, j) for j in blocks.singles[1:]]
-        if r == end - 1 and r > 0:
-            soon += [(end, j) for j in blocks.singles[:1]]
+        if r == 0:
+            soon = [(far, 0) for far in range(1, planes)] + [(1, j) for j in blocks.singles[1:]]
+        else:
+            soon = [(r + 1, j) for j in blocks.singles]
         soon = [at for at in soon if at in blocks.pieces]
         place, *ready = lax.optimization_barrier((place, *[blocks.pieces[at] for at in soon]))
         blocks.pieces.update(zip(soon, ready))

time: 127 us -> 128 us (level)
  waiting for transfers between devices: 34.7 us -> 25.7 us
  Pallas kernels: 56.6 us -> 64.9 us
  local copies, waits for them, and re-layouts: 1.67 us -> 3.2 us
    ppermute x34, waiting for transfers between devices: 34.7 us -> 25.7 us  [permute(): return lax.ppermute(x, ('layer', 'feat'), sorted(flat))]
    pallas_call x4, Pallas kernels: 52 us -> 60.4 us  [run_round(): pl.pallas_call(functools.partial(round_kernel, len(mine), len(tokens), la...]
    unnamed x36 -> x42, local copies, waits for them, and re-layouts: 1.67 us -> 3.2 us
  transfers between devices with their start and end apart: 34 -> 34, of which waited for: 10 -> 10; matrix products, arithmetic and copies ran while one was open for 1% -> 1% of each run, Pallas kernels for 35% -> 39%
where the time goes in v8:
time: 128 us; the launch traced here: 127 us
  Pallas kernels  64.9 us (51%)
  starting transfers between devices  32 us (25%)
  waiting for transfers between devices  25.7 us (20%)
  local copies, waits for them, and re-layouts  3.2 us (2%)
    pallas_call x4, Pallas kernels, run_round(): pl.pallas_call(functools.partial(round_kernel, len(mine), len(tokens), la...  60.4 us
    ppermute x34, starting transfers between devices, permute(): return lax.ppermute(x, ('layer', 'feat'), sorted(flat))  32 us
    ppermute x34, waiting for transfers between devices, permute(): return lax.ppermute(x, ('layer', 'feat'), sorted(flat))  25.7 us
    pallas_call x1, Pallas kernels, prepare(): pl.pallas_call(prepare_kernel, grid=(layers,), in_specs=[block(rows, widt...  4.5 us
    unnamed x42, local copies, waits for them, and re-layouts  3.2 us
  transfers between devices with their start and end apart: 34, of which 10 were waited for; matrix products, arithmetic and copies ran while one was open for 1% of the time, Pallas kernels for 39%

profile of v8, /device:TPU:0, one launch (start us, length us, event | category | flops | bytes accessed | tf_op | source)
XLA Modules:
  0.0 127.5 jit_solution(4024742952088614989)
XLA Ops:
  0.6 0.7 collective-permute-start.1
  1.3 5.9 %collective-permute-start = (bf16[4,256,256]{2,1,0:T(8,128)(2,1)}, bf16[4,256,256]{2,1,0:T(8,128)(2,1)S(1)}, u32[]{:S(2)}, u32[]{:S(2)}) collective-permute-start(bf16[4,256,256]{2,1,0:T(8,128)(2,1)} %refs_0_.1), channel_id=1, source_target_pairs={{0,2},{1,3},{2,0},{3,1},{4,6},{5,7},{6,4},{7,5},{8,10},{9,11},{10,... | collective-permute-start | bytes 1572872 | tf_op jit(solution)/shard_map/ppermute | solution.py:61
  7.2 1.5 %collective-permute-start.9 = (bf16[4,256,256]{2,1,0:T(8,128)(2,1)}, bf16[4,256,256]{2,1,0:T(8,128)(2,1)S(1)}, u32[]{:S(2)}, u32[]{:S(2)}) collective-permute-start(bf16[4,256,256]{2,1,0:T(8,128)(2,1)} %refs_0_.1), channel_id=1, source_target_pairs={{0,16},{1,17},{2,18},{3,19},{4,20},{5,21},{6,22},{7,23},{8,24},{9,... | collective-permute-start | bytes 1572872 | tf_op jit(solution)/shard_map/ppermute | solution.py:61
  8.7 1.5 %collective-permute-start.8 = (bf16[4,256,256]{2,1,0:T(8,128)(2,1)}, bf16[4,256,256]{2,1,0:T(8,128)(2,1)}, u32[]{:S(2)}, u32[]{:S(2)}) collective-permute-start(bf16[4,256,256]{2,1,0:T(8,128)(2,1)} %refs_0_.1), channel_id=1, source_target_pairs={{0,8},{1,9},{2,10},{3,11},{4,12},{5,13},{6,14},{7,15},{8,0},{9,1},... | collective-permute-start | bytes 1572872 | tf_op jit(solution)/shard_map/ppermute | solution.py:61
  10.2 4.5 %shard_map.59 = (bf16[4,256,1024]{2,1,0:T(8,128)(2,1)}, bf16[4,1024,256]{2,1,0:T(8,128)(2,1)}) custom-call(bf16[4,1024,256]{2,1,0:T(8,128)(2,1)} %act.1, s32[4,2,1024]{2,1,0:T(2,128)} %bitcast.4), custom_call_target="tpu_custom_call" | custom-call | bytes 6291456 | tf_op jit(solution)/shard_map/pallas_call | solution.py:121
  14.7 1.3 %collective-permute-start.2 = (bf16[4,256,256]{2,1,0:T(8,128)(2,1)S(1)}, bf16[4,256,256]{2,1,0:T(8,128)(2,1)S(1)}, u32[]{:S(2)}, u32[]{:S(2)}) collective-permute-start(bf16[4,256,256]{2,1,0:T(8,128)(2,1)S(1)} %collective-permute-done.1), channel_id=1, source_target_pairs={{2,0},{3,1},{4,6},{5,7},{10,8},{11,9},{12,14},{13,15},{18,16},{19,... | collective-permute-start | bytes 1572872 | tf_op jit(solution)/shard_map/ppermute | solution.py:61
  16.0 3.0 %collective-permute-done.refs_1_ = bf16[4,256,256]{2,1,0:T(8,128)(2,1)S(1)} collective-permute-done((bf16[4,256,256]{2,1,0:T(8,128)(2,1)}, bf16[4,256,256]{2,1,0:T(8,128)(2,1)S(1)}, u32[]{:S(2)}, u32[]{:S(2)}) %collective-permute-start) | collective-permute-done | bytes 524320 | tf_op jit(solution)/shard_map/ppermute | solution.py:61
  19.1 0.7 collective-permute-start.3
  19.8 0.8 collective-permute-done.9.refs_2_
  20.5 1.5 %collective-permute-start.10 = (bf16[4,256,256]{2,1,0:T(8,128)(2,1)S(1)}, bf16[4,256,256]{2,1,0:T(8,128)(2,1)}, u32[]{:S(2)}, u32[]{:S(2)}) collective-permute-start(bf16[4,256,256]{2,1,0:T(8,128)(2,1)S(1)} %collective-permute-done.9.refs_2_), channel_id=1, source_target_pairs={{0,8},{1,9},{2,10},{3,11},{4,12},{5,13},{6,14},{7,15},{8,0},{9,1},... | collective-permute-start | bytes 1572872 | tf_op jit(solution)/shard_map/ppermute | solution.py:61
  22.0 1.5 %collective-permute-start.4 = (bf16[4,256,256]{2,1,0:T(8,128)(2,1)S(1)}, bf16[4,256,256]{2,1,0:T(8,128)(2,1)S(1)}, u32[]{:S(2)}, u32[]{:S(2)}) collective-permute-start(bf16[4,256,256]{2,1,0:T(8,128)(2,1)S(1)} %collective-permute-done.refs_1_), channel_id=1, source_target_pairs={{0,16},{1,17},{2,18},{3,19},{4,20},{5,21},{6,22},{7,23},{8,24},{9,... | collective-permute-start | bytes 1572872 | tf_op jit(solution)/shard_map/ppermute | solution.py:61
  23.5 8.3 %collective-permute-done.2 = bf16[4,256,256]{2,1,0:T(8,128)(2,1)S(1)} collective-permute-done((bf16[4,256,256]{2,1,0:T(8,128)(2,1)S(1)}, bf16[4,256,256]{2,1,0:T(8,128)(2,1)S(1)}, u32[]{:S(2)}, u32[]{:S(2)}) %collective-permute-start.2) | collective-permute-done | bytes 524320 | tf_op jit(solution)/shard_map/ppermute | solution.py:61
  31.8 0.5 collective-permute-start.12
  32.4 0.8 collective-permute-done.10.refs_3_
  33.1 0.6 pad_add_fusion.meta
  33.8 0.3 collective-permute-done.4.refs_3_
  34.0 1.3 %collective-permute-start.17 = (bf16[4,256,256]{2,1,0:T(8,128)(2,1)S(1)}, bf16[4,256,256]{2,1,0:T(8,128)(2,1)}, u32[]{:S(2)}, u32[]{:S(2)}) collective-permute-start(bf16[4,256,256]{2,1,0:T(8,128)(2,1)S(1)} %collective-permute-done.refs_1_), channel_id=1, source_target_pairs={{0,8},{1,9},{2,10},{3,11},{4,12},{5,13},{6,14},{7,15},{8,0},{9,1},... | collective-permute-start | bytes 1572872 | tf_op jit(solution)/shard_map/ppermute | solution.py:61
  35.4 0.7 collective-permute-start.5
  36.1 4.1 %collective-permute-start.18 = (bf16[4,256,256]{2,1,0:T(8,128)(2,1)}, bf16[4,256,256]{2,1,0:T(8,128)(2,1)}, u32[]{:S(2)}, u32[]{:S(2)}) collective-permute-start(bf16[4,256,256]{2,1,0:T(8,128)(2,1)} %collective-permute-done.10.refs_3_), channel_id=1, source_target_pairs={{0,2},{1,3},{2,0},{3,1},{4,6},{5,7},{6,4},{7,5},{8,10},{9,11},{10,... | collective-permute-start | bytes 1572872 | tf_op jit(solution)/shard_map/ppermute | solution.py:61
  40.2 0.7 collective-permute-start.23
  40.9 1.3 %collective-permute-start.7 = (bf16[4,256,256]{2,1,0:T(8,128)(2,1)S(1)}, bf16[4,256,256]{2,1,0:T(8,128)(2,1)S(1)}, u32[]{:S(2)}, u32[]{:S(2)}) collective-permute-start(bf16[4,256,256]{2,1,0:T(8,128)(2,1)S(1)} %collective-permute-done.3), channel_id=1, source_target_pairs={{2,0},{3,1},{4,6},{5,7},{10,8},{11,9},{12,14},{13,15},{18,16},{19,... | collective-permute-start | bytes 1572872 | tf_op jit(solution)/shard_map/ppermute | solution.py:61
  42.2 14.6 %shard_map.60 = (bf16[10,256,2048]{2,1,0:T(8,128)(2,1)}, f32[4,1024,256]{2,1,0:T(8,128)}, f32[8,128]{1,0:T(8,128)}) custom-call(s32[3]{0:T(128)} %pad_add_fusion.meta, bf16[4,256,1024]{2,1,0:T(8,128)(2,1)} %get-tuple-element.45.sparse, bf16[10,256,2048]{2,1,0:T(8,128)(2,1)} %decoder.7, bf16[4,256,256]{2,1,0:T(8,128)(2,1)} %refs_0_.1, ...), custom_call_target="tpu_custom_call" | custom-call | flops 10737418240 | bytes 20971520 | tf_op jit(solution)/shard_map/pallas_call | solution.py:279
  56.8 1.6 %collective-permute-start.6 = (bf16[4,256,256]{2,1,0:T(8,128)(2,1)S(1)}, bf16[4,256,256]{2,1,0:T(8,128)(2,1)S(1)}, u32[]{:S(2)}, u32[]{:S(2)}) collective-permute-start(bf16[4,256,256]{2,1,0:T(8,128)(2,1)S(1)} %broadcast_select_fusion.2.refs_1_), channel_id=1, source_target_pairs={{0,16},{1,17},{2,18},{3,19},{4,20},{5,21},{6,22},{7,23},{8,24},{9,... | collective-permute-start | bytes 1572872 | tf_op jit(solution)/shard_map/ppermute | solution.py:61
  58.4 0.5 collective-permute-start.21
  58.9 4.4 %collective-permute-done.7 = bf16[4,256,256]{2,1,0:T(8,128)(2,1)S(1)} collective-permute-done((bf16[4,256,256]{2,1,0:T(8,128)(2,1)S(1)}, bf16[4,256,256]{2,1,0:T(8,128)(2,1)S(1)}, u32[]{:S(2)}, u32[]{:S(2)}) %collective-permute-start.7) | collective-permute-done | bytes 524320 | tf_op jit(solution)/shard_map/ppermute | solution.py:61
  63.3 0.8 copy-done.5
  64.1 0.5 collective-permute-start.22
  64.7 5.3 %collective-permute-done.6.refs_3_ = bf16[4,256,256]{2,1,0:T(8,128)(2,1)S(1)} collective-permute-done((bf16[4,256,256]{2,1,0:T(8,128)(2,1)S(1)}, bf16[4,256,256]{2,1,0:T(8,128)(2,1)S(1)}, u32[]{:S(2)}, u32[]{:S(2)}) %collective-permute-start.6) | collective-permute-done | bytes 524320 | tf_op jit(solution)/shard_map/ppermute | solution.py:61
  70.1 1.6 %collective-permute-start.15 = (bf16[4,256,256]{2,1,0:T(8,128)(2,1)S(1)}, bf16[4,256,256]{2,1,0:T(8,128)(2,1)S(1)}, u32[]{:S(2)}, u32[]{:S(2)}) collective-permute-start(bf16[4,256,256]{2,1,0:T(8,128)(2,1)S(1)} %broadcast_select_fusion.1.refs_2_), channel_id=1, source_target_pairs={{0,8},{1,9},{2,10},{3,11},{4,12},{5,13},{6,14},{7,15},{8,0},{9,1},... | collective-permute-start | bytes 1572872 | tf_op jit(solution)/shard_map/ppermute | solution.py:61
  71.6 1.5 %collective-permute-start.16 = (bf16[4,256,256]{2,1,0:T(8,128)(2,1)S(1)}, bf16[4,256,256]{2,1,0:T(8,128)(2,1)}, u32[]{:S(2)}, u32[]{:S(2)}) collective-permute-start(bf16[4,256,256]{2,1,0:T(8,128)(2,1)S(1)} %broadcast_select_fusion.1.refs_2_), channel_id=1, source_target_pairs={{0,16},{1,17},{2,18},{3,19},{4,20},{5,21},{6,22},{7,23},{8,24},{9,... | collective-permute-start | bytes 1572872 | tf_op jit(solution)/shard_map/ppermute | solution.py:61
  73.1 1.3 %collective-permute-start.24 = (bf16[4,256,256]{2,1,0:T(8,128)(2,1)S(1)}, bf16[4,256,256]{2,1,0:T(8,128)(2,1)S(1)}, u32[]{:S(2)}, u32[]{:S(2)}) collective-permute-start(bf16[4,256,256]{2,1,0:T(8,128)(2,1)S(1)} %collective-permute-done.23), channel_id=1, source_target_pairs={{2,0},{3,1},{4,6},{5,7},{10,8},{11,9},{12,14},{13,15},{18,16},{19,... | collective-permute-start | bytes 1572872 | tf_op jit(solution)/shard_map/ppermute | solution.py:61
  74.5 0.1 collective-permute-start.26
  74.6 0.7 copy-done.17
  75.2 15.3 %shard_map.61 = (bf16[10,256,2048]{2,1,0:T(8,128)(2,1)}, f32[4,1024,256]{2,1,0:T(8,128)}, f32[8,128]{1,0:T(8,128)}) custom-call(s32[3]{0:T(128)} %pad_add_fusion.meta, bf16[4,256,1024]{2,1,0:T(8,128)(2,1)} %get-tuple-element.45.sparse, bf16[10,256,2048]{2,1,0:T(8,128)(2,1)} %decoder.7, ...), custom_call_target="tpu_custom_call", output_to_operand_aliasing={{0}: (12, {})} | custom-call | flops 10737418240 | bytes 20971520 | tf_op jit(solution)/shard_map/pallas_call | solution.py:279
  90.6 0.1 collective-permute-start.27
  90.8 0.6 collective-permute-start.28
  91.3 0.1 collective-permute-start.30
  91.4 0.5 collective-permute-start.29
  91.9 0.2 collective-permute-start.31
  92.1 0.5 collective-permute-done.27.refs_7_
  92.6 0.1 collective-permute-start.32
  92.7 0.6 collective-permute-done.28.refs_8_
  93.4 0.8 copy-done.19
  94.2 15.2 %shard_map.62 = (bf16[10,256,2048]{2,1,0:T(8,128)(2,1)}, f32[4,1024,256]{2,1,0:T(8,128)}, f32[8,128]{1,0:T(8,128)}) custom-call(s32[3]{0:T(128)} %pad_add_fusion.meta, bf16[4,256,1024]{2,1,0:T(8,128)(2,1)} %get-tuple-element.45.sparse, bf16[10,256,2048]{2,1,0:T(8,128)(2,1)} %decoder.7, ...), custom_call_target="tpu_custom_call", output_to_operand_aliasing={{0}: (12, {})} | custom-call | flops 10737418240 | bytes 20971520 | tf_op jit(solution)/shard_map/pallas_call | solution.py:279
  109.4 0.2 collective-permute-start.33
  109.6 1.7 %collective-permute-done.33.refs_9_ = bf16[4,256,256]{2,1,0:T(8,128)(2,1)S(1)} collective-permute-done((bf16[4,256,256]{2,1,0:T(8,128)(2,1)S(1)}, bf16[4,256,256]{2,1,0:T(8,128)(2,1)S(1)}, u32[]{:S(2)}, u32[]{:S(2)}) %collective-permute-start.33) | collective-permute-done | bytes 524320 | tf_op jit(solution)/shard_map/ppermute | solution.py:61
  111.4 0.8 copy-done.20
  112.2 15.3 %shard_map.63 = (bf16[10,256,2048]{2,1,0:T(8,128)(2,1)}, bf16[4,1024,256]{2,1,0:T(8,128)(2,1)}, f32[8,128]{1,0:T(8,128)}) custom-call(s32[3]{0:T(128)} %pad_add_fusion.meta, bf16[4,256,1024]{2,1,0:T(8,128)(2,1)} %get-tuple-element.45.sparse, bf16[10,256,2048]{2,1,0:T(8,128)(2,1)} %decoder.7, ...), custom_call_target="tpu_custom_call", output_to_operand_aliasing={{0}: (13, {})} | custom-call | flops 10737418240 | bytes 20971520 | tf_op jit(solution)/shard_map/pallas_call | solution.py:279
  (71 shorter events, 0.4 us)
Async XLA Ops:
  0.6 14.1 %collective-permute-start.1 = (bf16[4,256,256]{2,1,0:T(8,128)(2,1)}, bf16[4,256,256]{2,1,0:T(8,128)(2,1)S(1)}, u32[]{:S(2)}, u32[]{:S(2)}) collective-permute-start(bf16[4,256,256]{2,1,0:T(8,128)(2,1)} %refs_0_.1), channel_id=1, source_target_pairs={{2,4},{3,5},{4,2},{5,3},{10,12},{11,13},{12,10},{13,11},{18,20},{1... | collective-permute-start | bytes 1572872 | tf_op jit(solution)/shard_map/ppermute | solution.py:61
  1.3 17.7 %collective-permute-start = (bf16[4,256,256]{2,1,0:T(8,128)(2,1)}, bf16[4,256,256]{2,1,0:T(8,128)(2,1)S(1)}, u32[]{:S(2)}, u32[]{:S(2)}) collective-permute-start(bf16[4,256,256]{2,1,0:T(8,128)(2,1)} %refs_0_.1), channel_id=1, source_target_pairs={{0,2},{1,3},{2,0},{3,1},{4,6},{5,7},{6,4},{7,5},{8,10},{9,11},{10,... | collective-permute-start | bytes 1572872 | tf_op jit(solution)/shard_map/ppermute | solution.py:61
  7.2 13.3 %collective-permute-start.9 = (bf16[4,256,256]{2,1,0:T(8,128)(2,1)}, bf16[4,256,256]{2,1,0:T(8,128)(2,1)S(1)}, u32[]{:S(2)}, u32[]{:S(2)}) collective-permute-start(bf16[4,256,256]{2,1,0:T(8,128)(2,1)} %refs_0_.1), channel_id=1, source_target_pairs={{0,16},{1,17},{2,18},{3,19},{4,20},{5,21},{6,22},{7,23},{8,24},{9,... | collective-permute-start | bytes 1572872 | tf_op jit(solution)/shard_map/ppermute | solution.py:61
  8.7 14.8 %collective-permute-start.8 = (bf16[4,256,256]{2,1,0:T(8,128)(2,1)}, bf16[4,256,256]{2,1,0:T(8,128)(2,1)}, u32[]{:S(2)}, u32[]{:S(2)}) collective-permute-start(bf16[4,256,256]{2,1,0:T(8,128)(2,1)} %refs_0_.1), channel_id=1, source_target_pairs={{0,8},{1,9},{2,10},{3,11},{4,12},{5,13},{6,14},{7,15},{8,0},{9,1},... | collective-permute-start | bytes 1572872 | tf_op jit(solution)/shard_map/ppermute | solution.py:61
  14.7 17.1 %collective-permute-start.2 = (bf16[4,256,256]{2,1,0:T(8,128)(2,1)S(1)}, bf16[4,256,256]{2,1,0:T(8,128)(2,1)S(1)}, u32[]{:S(2)}, u32[]{:S(2)}) collective-permute-start(bf16[4,256,256]{2,1,0:T(8,128)(2,1)S(1)} %collective-permute-done.1), channel_id=1, source_target_pairs={{2,0},{3,1},{4,6},{5,7},{10,8},{11,9},{12,14},{13,15},{18,16},{19,... | collective-permute-start | bytes 1572872 | tf_op jit(solution)/shard_map/ppermute | solution.py:61
  19.1 39.3 %copy-start.3 = (bf16[4,256,256]{2,1,0:T(8,128)(2,1)}, bf16[4,256,256]{2,1,0:T(8,128)(2,1)S(1)}, u32[]{:S(2)}) copy-start(bf16[4,256,256]{2,1,0:T(8,128)(2,1)S(1)} %collective-permute-done.refs_1_) | copy-start | bytes 1572868
  19.1 12.8 %collective-permute-start.3 = (bf16[4,256,256]{2,1,0:T(8,128)(2,1)S(1)}, bf16[4,256,256]{2,1,0:T(8,128)(2,1)S(1)}, u32[]{:S(2)}, u32[]{:S(2)}) collective-permute-start(bf16[4,256,256]{2,1,0:T(8,128)(2,1)S(1)} %collective-permute-done.refs_1_), channel_id=1, source_target_pairs={{2,4},{3,5},{4,2},{5,3},{10,12},{11,13},{12,10},{13,11},{18,20},{1... | collective-permute-start | bytes 1572872 | tf_op jit(solution)/shard_map/ppermute | solution.py:61
  20.5 20.4 %copy-start.6 = (bf16[4,256,256]{2,1,0:T(8,128)(2,1)}, bf16[4,256,256]{2,1,0:T(8,128)(2,1)S(1)}, u32[]{:S(2)}) copy-start(bf16[4,256,256]{2,1,0:T(8,128)(2,1)S(1)} %collective-permute-done.9.refs_2_) | copy-start | bytes 1572868
  20.5 12.6 %collective-permute-start.10 = (bf16[4,256,256]{2,1,0:T(8,128)(2,1)S(1)}, bf16[4,256,256]{2,1,0:T(8,128)(2,1)}, u32[]{:S(2)}, u32[]{:S(2)}) collective-permute-start(bf16[4,256,256]{2,1,0:T(8,128)(2,1)S(1)} %collective-permute-done.9.refs_2_), channel_id=1, source_target_pairs={{0,8},{1,9},{2,10},{3,11},{4,12},{5,13},{6,14},{7,15},{8,0},{9,1},... | collective-permute-start | bytes 1572872 | tf_op jit(solution)/shard_map/ppermute | solution.py:61
  22.0 12.0 %collective-permute-start.4 = (bf16[4,256,256]{2,1,0:T(8,128)(2,1)S(1)}, bf16[4,256,256]{2,1,0:T(8,128)(2,1)S(1)}, u32[]{:S(2)}, u32[]{:S(2)}) collective-permute-start(bf16[4,256,256]{2,1,0:T(8,128)(2,1)S(1)} %collective-permute-done.refs_1_), channel_id=1, source_target_pairs={{0,16},{1,17},{2,18},{3,19},{4,20},{5,21},{6,22},{7,23},{8,24},{9,... | collective-permute-start | bytes 1572872 | tf_op jit(solution)/shard_map/ppermute | solution.py:61
  23.5 11.8 %collective-permute-start.11 = (bf16[4,256,256]{2,1,0:T(8,128)(2,1)}, bf16[4,256,256]{2,1,0:T(8,128)(2,1)}, u32[]{:S(2)}, u32[]{:S(2)}) collective-permute-start(bf16[4,256,256]{2,1,0:T(8,128)(2,1)} %refs_0_.1), channel_id=1, source_target_pairs={{0,1},{1,0},{2,3},{3,2},{4,5},{5,4},{6,7},{7,6},{8,9},{9,8},{10,11... | collective-permute-start | bytes 1572872 | tf_op jit(solution)/shard_map/ppermute | solution.py:61
  31.8 4.2 %collective-permute-start.13 = (bf16[4,256,256]{2,1,0:T(8,128)(2,1)S(1)}, bf16[4,256,256]{2,1,0:T(8,128)(2,1)}, u32[]{:S(2)}, u32[]{:S(2)}) collective-permute-start(bf16[4,256,256]{2,1,0:T(8,128)(2,1)S(1)} %collective-permute-done.9.refs_2_), channel_id=1, source_target_pairs={{0,1},{1,0},{2,3},{3,2},{4,5},{5,4},{6,7},{7,6},{8,9},{9,8},{10,11... | collective-permute-start | bytes 1572872 | tf_op jit(solution)/shard_map/ppermute | solution.py:61
  31.8 8.4 %collective-permute-start.12 = (bf16[4,256,256]{2,1,0:T(8,128)(2,1)}, bf16[4,256,256]{2,1,0:T(8,128)(2,1)}, u32[]{:S(2)}, u32[]{:S(2)}) collective-permute-start(bf16[4,256,256]{2,1,0:T(8,128)(2,1)} %collective-permute-done.8.refs_1_), channel_id=1, source_target_pairs={{0,1},{1,0},{2,3},{3,2},{4,5},{5,4},{6,7},{7,6},{8,9},{9,8},{10,11... | collective-permute-start | bytes 1572872 | tf_op jit(solution)/shard_map/ppermute | solution.py:61
  33.1 7.8 %collective-permute-start.14 = (bf16[4,256,256]{2,1,0:T(8,128)(2,1)}, bf16[4,256,256]{2,1,0:T(8,128)(2,1)}, u32[]{:S(2)}, u32[]{:S(2)}) collective-permute-start(bf16[4,256,256]{2,1,0:T(8,128)(2,1)} %collective-permute-done.10.refs_3_), channel_id=1, source_target_pairs={{0,1},{1,0},{2,3},{3,2},{4,5},{5,4},{6,7},{7,6},{8,9},{9,8},{10,11... | collective-permute-start | bytes 1572872 | tf_op jit(solution)/shard_map/ppermute | solution.py:61
  33.8 36.3 %copy-start = (bf16[4,256,256]{2,1,0:T(8,128)(2,1)}, bf16[4,256,256]{2,1,0:T(8,128)(2,1)S(1)}, u32[]{:S(2)}) copy-start(bf16[4,256,256]{2,1,0:T(8,128)(2,1)S(1)} %broadcast_select_fusion.2.refs_1_) | copy-start | bytes 1572868
  34.0 24.4 %copy-start.4 = (bf16[4,256,256]{2,1,0:T(8,128)(2,1)}, bf16[4,256,256]{2,1,0:T(8,128)(2,1)S(1)}, u32[]{:S(2)}) copy-start(bf16[4,256,256]{2,1,0:T(8,128)(2,1)S(1)} %collective-permute-done.4.refs_3_) | copy-start | bytes 1572868
  34.0 24.4 %collective-permute-start.17 = (bf16[4,256,256]{2,1,0:T(8,128)(2,1)S(1)}, bf16[4,256,256]{2,1,0:T(8,128)(2,1)}, u32[]{:S(2)}, u32[]{:S(2)}) collective-permute-start(bf16[4,256,256]{2,1,0:T(8,128)(2,1)S(1)} %collective-permute-done.refs_1_), channel_id=1, source_target_pairs={{0,8},{1,9},{2,10},{3,11},{4,12},{5,13},{6,14},{7,15},{8,0},{9,1},... | collective-permute-start | bytes 1572872 | tf_op jit(solution)/shard_map/ppermute | solution.py:61
  35.4 28.0 %collective-permute-start.5 = (bf16[4,256,256]{2,1,0:T(8,128)(2,1)S(1)}, bf16[4,256,256]{2,1,0:T(8,128)(2,1)S(1)}, u32[]{:S(2)}, u32[]{:S(2)}) collective-permute-start(bf16[4,256,256]{2,1,0:T(8,128)(2,1)S(1)} %broadcast_select_fusion.2.refs_1_), channel_id=1, source_target_pairs={{0,8},{1,9},{2,10},{3,11},{4,12},{5,13},{6,14},{7,15},{8,0},{9,1},... | collective-permute-start | bytes 1572872 | tf_op jit(solution)/shard_map/ppermute | solution.py:61
  36.1 20.7 %collective-permute-start.18 = (bf16[4,256,256]{2,1,0:T(8,128)(2,1)}, bf16[4,256,256]{2,1,0:T(8,128)(2,1)}, u32[]{:S(2)}, u32[]{:S(2)}) collective-permute-start(bf16[4,256,256]{2,1,0:T(8,128)(2,1)} %collective-permute-done.10.refs_3_), channel_id=1, source_target_pairs={{0,2},{1,3},{2,0},{3,1},{4,6},{5,7},{6,4},{7,5},{8,10},{9,11},{10,... | collective-permute-start | bytes 1572872 | tf_op jit(solution)/shard_map/ppermute | solution.py:61
  40.2 18.2 %collective-permute-start.23 = (bf16[4,256,256]{2,1,0:T(8,128)(2,1)}, bf16[4,256,256]{2,1,0:T(8,128)(2,1)S(1)}, u32[]{:S(2)}, u32[]{:S(2)}) collective-permute-start(bf16[4,256,256]{2,1,0:T(8,128)(2,1)} %collective-permute-done.10.refs_3_), channel_id=1, source_target_pairs={{2,4},{3,5},{4,2},{5,3},{10,12},{11,13},{12,10},{13,11},{18,20},{1... | collective-permute-start | bytes 1572872 | tf_op jit(solution)/shard_map/ppermute | solution.py:61
  40.9 22.4 %collective-permute-start.7 = (bf16[4,256,256]{2,1,0:T(8,128)(2,1)S(1)}, bf16[4,256,256]{2,1,0:T(8,128)(2,1)S(1)}, u32[]{:S(2)}, u32[]{:S(2)}) collective-permute-start(bf16[4,256,256]{2,1,0:T(8,128)(2,1)S(1)} %collective-permute-done.3), channel_id=1, source_target_pairs={{2,0},{3,1},{4,6},{5,7},{10,8},{11,9},{12,14},{13,15},{18,16},{19,... | collective-permute-start | bytes 1572872 | tf_op jit(solution)/shard_map/ppermute | solution.py:61
  56.8 13.2 %collective-permute-start.6 = (bf16[4,256,256]{2,1,0:T(8,128)(2,1)S(1)}, bf16[4,256,256]{2,1,0:T(8,128)(2,1)S(1)}, u32[]{:S(2)}, u32[]{:S(2)}) collective-permute-start(bf16[4,256,256]{2,1,0:T(8,128)(2,1)S(1)} %broadcast_select_fusion.2.refs_1_), channel_id=1, source_target_pairs={{0,16},{1,17},{2,18},{3,19},{4,20},{5,21},{6,22},{7,23},{8,24},{9,... | collective-permute-start | bytes 1572872 | tf_op jit(solution)/shard_map/ppermute | solution.py:61
  58.4 11.6 %collective-permute-start.19 = (bf16[4,256,256]{2,1,0:T(8,128)(2,1)S(1)}, bf16[4,256,256]{2,1,0:T(8,128)(2,1)S(1)}, u32[]{:S(2)}, u32[]{:S(2)}) collective-permute-start(bf16[4,256,256]{2,1,0:T(8,128)(2,1)S(1)} %collective-permute-done.refs_1_), channel_id=1, source_target_pairs={{0,1},{1,0},{2,3},{3,2},{4,5},{5,4},{6,7},{7,6},{8,9},{9,8},{10,11... | collective-permute-start | bytes 1572872 | tf_op jit(solution)/shard_map/ppermute | solution.py:61
  58.4 13.2 %collective-permute-start.21 = (bf16[4,256,256]{2,1,0:T(8,128)(2,1)S(1)}, bf16[4,256,256]{2,1,0:T(8,128)(2,1)S(1)}, u32[]{:S(2)}, u32[]{:S(2)}) collective-permute-start(bf16[4,256,256]{2,1,0:T(8,128)(2,1)S(1)} %collective-permute-done.4.refs_3_), channel_id=1, source_target_pairs={{0,1},{1,0},{2,3},{3,2},{4,5},{5,4},{6,7},{7,6},{8,9},{9,8},{10,11... | collective-permute-start | bytes 1572872 | tf_op jit(solution)/shard_map/ppermute | solution.py:61
  63.3 9.8 %collective-permute-start.20 = (bf16[4,256,256]{2,1,0:T(8,128)(2,1)}, bf16[4,256,256]{2,1,0:T(8,128)(2,1)S(1)}, u32[]{:S(2)}, u32[]{:S(2)}) collective-permute-start(bf16[4,256,256]{2,1,0:T(8,128)(2,1)} %collective-permute-done.17.refs_2_), channel_id=1, source_target_pairs={{0,1},{1,0},{2,3},{3,2},{4,5},{5,4},{6,7},{7,6},{8,9},{9,8},{10,11... | collective-permute-start | bytes 1572872 | tf_op jit(solution)/shard_map/ppermute | solution.py:61
  64.1 10.3 %collective-permute-start.22 = (bf16[4,256,256]{2,1,0:T(8,128)(2,1)}, bf16[4,256,256]{2,1,0:T(8,128)(2,1)S(1)}, u32[]{:S(2)}, u32[]{:S(2)}) collective-permute-start(bf16[4,256,256]{2,1,0:T(8,128)(2,1)} %collective-permute-done.18.refs_4_), channel_id=1, source_target_pairs={{0,1},{1,0},{2,3},{3,2},{4,5},{5,4},{6,7},{7,6},{8,9},{9,8},{10,11... | collective-permute-start | bytes 1572872 | tf_op jit(solution)/shard_map/ppermute | solution.py:61
  64.7 26.6 %copy-start.1 = (bf16[4,256,256]{2,1,0:T(8,128)(2,1)}, bf16[4,256,256]{2,1,0:T(8,128)(2,1)S(1)}, u32[]{:S(2)}) copy-start(bf16[4,256,256]{2,1,0:T(8,128)(2,1)S(1)} %broadcast_select_fusion.1.refs_2_) | copy-start | bytes 1572868
  70.0 3.1 %copy-start.7 = (bf16[4,256,256]{2,1,0:T(8,128)(2,1)}, bf16[4,256,256]{2,1,0:T(8,128)(2,1)S(1)}, u32[]{:S(2)}) copy-start(bf16[4,256,256]{2,1,0:T(8,128)(2,1)S(1)} %collective-permute-done.6.refs_3_) | copy-start | bytes 1572868
  70.0 21.4 %collective-permute-start.25 = (bf16[4,256,256]{2,1,0:T(8,128)(2,1)S(1)}, bf16[4,256,256]{2,1,0:T(8,128)(2,1)}, u32[]{:S(2)}, u32[]{:S(2)}) collective-permute-start(bf16[4,256,256]{2,1,0:T(8,128)(2,1)S(1)} %broadcast_select_fusion.2.refs_1_), channel_id=1, source_target_pairs={{0,1},{1,0},{2,3},{3,2},{4,5},{5,4},{6,7},{7,6},{8,9},{9,8},{10,11... | collective-permute-start | bytes 1572872 | tf_op jit(solution)/shard_map/ppermute | solution.py:61
  70.0 4.5 %copy-start.10 = (bf16[4,256,256]{2,1,0:T(8,128)(2,1)}, bf16[4,256,256]{2,1,0:T(8,128)(2,1)S(1)}, u32[]{:S(2)}) copy-start(bf16[4,256,256]{2,1,0:T(8,128)(2,1)S(1)} %collective-permute-done.19.refs_5_) | copy-start | bytes 1572868
  70.1 20.7 %collective-permute-start.15 = (bf16[4,256,256]{2,1,0:T(8,128)(2,1)S(1)}, bf16[4,256,256]{2,1,0:T(8,128)(2,1)S(1)}, u32[]{:S(2)}, u32[]{:S(2)}) collective-permute-start(bf16[4,256,256]{2,1,0:T(8,128)(2,1)S(1)} %broadcast_select_fusion.1.refs_2_), channel_id=1, source_target_pairs={{0,8},{1,9},{2,10},{3,11},{4,12},{5,13},{6,14},{7,15},{8,0},{9,1},... | collective-permute-start | bytes 1572872 | tf_op jit(solution)/shard_map/ppermute | solution.py:61
  71.6 2.9 %copy-start.12 = (bf16[4,256,256]{2,1,0:T(8,128)(2,1)}, bf16[4,256,256]{2,1,0:T(8,128)(2,1)S(1)}, u32[]{:S(2)}) copy-start(bf16[4,256,256]{2,1,0:T(8,128)(2,1)S(1)} %collective-permute-done.21.refs_7_) | copy-start | bytes 1572868
  71.6 19.7 %collective-permute-start.16 = (bf16[4,256,256]{2,1,0:T(8,128)(2,1)S(1)}, bf16[4,256,256]{2,1,0:T(8,128)(2,1)}, u32[]{:S(2)}, u32[]{:S(2)}) collective-permute-start(bf16[4,256,256]{2,1,0:T(8,128)(2,1)S(1)} %broadcast_select_fusion.1.refs_2_), channel_id=1, source_target_pairs={{0,16},{1,17},{2,18},{3,19},{4,20},{5,21},{6,22},{7,23},{8,24},{9,... | collective-permute-start | bytes 1572872 | tf_op jit(solution)/shard_map/ppermute | solution.py:61
  73.1 17.4 %collective-permute-start.24 = (bf16[4,256,256]{2,1,0:T(8,128)(2,1)S(1)}, bf16[4,256,256]{2,1,0:T(8,128)(2,1)S(1)}, u32[]{:S(2)}, u32[]{:S(2)}) collective-permute-start(bf16[4,256,256]{2,1,0:T(8,128)(2,1)S(1)} %collective-permute-done.23), channel_id=1, source_target_pairs={{2,0},{3,1},{4,6},{5,7},{10,8},{11,9},{12,14},{13,15},{18,16},{19,... | collective-permute-start | bytes 1572872 | tf_op jit(solution)/shard_map/ppermute | solution.py:61
  74.5 17.5 %collective-permute-start.26 = (bf16[4,256,256]{2,1,0:T(8,128)(2,1)}, bf16[4,256,256]{2,1,0:T(8,128)(2,1)}, u32[]{:S(2)}, u32[]{:S(2)}) collective-permute-start(bf16[4,256,256]{2,1,0:T(8,128)(2,1)} %copy-done.5), channel_id=1, source_target_pairs={{0,1},{1,0},{2,3},{3,2},{4,5},{5,4},{6,7},{7,6},{8,9},{9,8},{10,11... | collective-permute-start | bytes 1572872 | tf_op jit(solution)/shard_map/ppermute | solution.py:61
  75.2 15.3 %copy-start.8 = (bf16[4,256,256]{2,1,0:T(8,128)(2,1)S(1)}, bf16[4,256,256]{2,1,0:T(8,128)(2,1)}, u32[]{:S(2)}) copy-start(bf16[4,256,256]{2,1,0:T(8,128)(2,1)} %copy-done.7) | copy-start | bytes 1572868
  90.6 2.0 %collective-permute-start.27 = (bf16[4,256,256]{2,1,0:T(8,128)(2,1)S(1)}, bf16[4,256,256]{2,1,0:T(8,128)(2,1)S(1)}, u32[]{:S(2)}, u32[]{:S(2)}) collective-permute-start(bf16[4,256,256]{2,1,0:T(8,128)(2,1)S(1)} %copy-done.8), channel_id=1, source_target_pairs={{0,1},{1,0},{2,3},{3,2},{4,5},{5,4},{6,7},{7,6},{8,9},{9,8},{10,11... | collective-permute-start | bytes 1572872 | tf_op jit(solution)/shard_map/ppermute | solution.py:61
  90.7 3.4 %copy-start.2 = (bf16[4,256,256]{2,1,0:T(8,128)(2,1)}, bf16[4,256,256]{2,1,0:T(8,128)(2,1)S(1)}, u32[]{:S(2)}) copy-start(bf16[4,256,256]{2,1,0:T(8,128)(2,1)S(1)} %broadcast_select_fusion.refs_4_) | copy-start | bytes 1572868
  90.8 18.6 %copy-start.9 = (bf16[4,256,256]{2,1,0:T(8,128)(2,1)}, bf16[4,256,256]{2,1,0:T(8,128)(2,1)S(1)}, u32[]{:S(2)}) copy-start(bf16[4,256,256]{2,1,0:T(8,128)(2,1)S(1)} %collective-permute-done.15.refs_3_) | copy-start | bytes 1572868
  90.8 2.5 %collective-permute-start.28 = (bf16[4,256,256]{2,1,0:T(8,128)(2,1)S(1)}, bf16[4,256,256]{2,1,0:T(8,128)(2,1)S(1)}, u32[]{:S(2)}, u32[]{:S(2)}) collective-permute-start(bf16[4,256,256]{2,1,0:T(8,128)(2,1)S(1)} %broadcast_select_fusion.refs_4_), channel_id=1, source_target_pairs={{0,1},{1,0},{2,3},{3,2},{4,5},{5,4},{6,7},{7,6},{8,9},{9,8},{10,11... | collective-permute-start | bytes 1572872 | tf_op jit(solution)/shard_map/ppermute | solution.py:61
  91.3 18.3 %collective-permute-start.30 = (bf16[4,256,256]{2,1,0:T(8,128)(2,1)S(1)}, bf16[4,256,256]{2,1,0:T(8,128)(2,1)S(1)}, u32[]{:S(2)}, u32[]{:S(2)}) collective-permute-start(bf16[4,256,256]{2,1,0:T(8,128)(2,1)S(1)} %broadcast_select_fusion.1.refs_2_), channel_id=1, source_target_pairs={{0,1},{1,0},{2,3},{3,2},{4,5},{5,4},{6,7},{7,6},{8,9},{9,8},{10,11... | collective-permute-start | bytes 1572872 | tf_op jit(solution)/shard_map/ppermute | solution.py:61
  91.4 17.9 %collective-permute-start.29 = (bf16[4,256,256]{2,1,0:T(8,128)(2,1)S(1)}, bf16[4,256,256]{2,1,0:T(8,128)(2,1)S(1)}, u32[]{:S(2)}, u32[]{:S(2)}) collective-permute-start(bf16[4,256,256]{2,1,0:T(8,128)(2,1)S(1)} %collective-permute-done.15.refs_3_), channel_id=1, source_target_pairs={{0,16},{1,17},{2,18},{3,19},{4,20},{5,21},{6,22},{7,23},{8,24},{9,... | collective-permute-start | bytes 1572872 | tf_op jit(solution)/shard_map/ppermute | solution.py:61
  91.9 17.7 %collective-permute-start.31 = (bf16[4,256,256]{2,1,0:T(8,128)(2,1)S(1)}, bf16[4,256,256]{2,1,0:T(8,128)(2,1)S(1)}, u32[]{:S(2)}, u32[]{:S(2)}) collective-permute-start(bf16[4,256,256]{2,1,0:T(8,128)(2,1)S(1)} %collective-permute-done.15.refs_3_), channel_id=1, source_target_pairs={{0,1},{1,0},{2,3},{3,2},{4,5},{5,4},{6,7},{7,6},{8,9},{9,8},{10,11... | collective-permute-start | bytes 1572872 | tf_op jit(solution)/shard_map/ppermute | solution.py:61
  92.6 17.1 %collective-permute-start.32 = (bf16[4,256,256]{2,1,0:T(8,128)(2,1)}, bf16[4,256,256]{2,1,0:T(8,128)(2,1)S(1)}, u32[]{:S(2)}, u32[]{:S(2)}) collective-permute-start(bf16[4,256,256]{2,1,0:T(8,128)(2,1)} %collective-permute-done.16.refs_4_), channel_id=1, source_target_pairs={{0,1},{1,0},{2,3},{3,2},{4,5},{5,4},{6,7},{7,6},{8,9},{9,8},{10,11... | collective-permute-start | bytes 1572872 | tf_op jit(solution)/shard_map/ppermute | solution.py:61
  109.4 2.0 %copy-start.13 = (bf16[4,256,256]{2,1,0:T(8,128)(2,1)}, bf16[4,256,256]{2,1,0:T(8,128)(2,1)S(1)}, u32[]{:S(2)}) copy-start(bf16[4,256,256]{2,1,0:T(8,128)(2,1)S(1)} %collective-permute-done.29.refs_5_) | copy-start | bytes 1572868
  109.4 2.0 %collective-permute-start.33 = (bf16[4,256,256]{2,1,0:T(8,128)(2,1)S(1)}, bf16[4,256,256]{2,1,0:T(8,128)(2,1)S(1)}, u32[]{:S(2)}, u32[]{:S(2)}) collective-permute-start(bf16[4,256,256]{2,1,0:T(8,128)(2,1)S(1)} %collective-permute-done.29.refs_5_), channel_id=1, source_target_pairs={{0,1},{1,0},{2,3},{3,2},{4,5},{5,4},{6,7},{7,6},{8,9},{9,8},{10,11... | collective-permute-start | bytes 1572872 | tf_op jit(solution)/shard_map/ppermute | solution.py:61
  109.6 1.8 %copy-start.11 = (bf16[4,256,256]{2,1,0:T(8,128)(2,1)}, bf16[4,256,256]{2,1,0:T(8,128)(2,1)S(1)}, u32[]{:S(2)}) copy-start(bf16[4,256,256]{2,1,0:T(8,128)(2,1)S(1)} %collective-permute-done.30.refs_6_) | copy-start | bytes 1572868
  109.6 1.8 %copy-start.15 = (bf16[4,256,256]{2,1,0:T(8,128)(2,1)}, bf16[4,256,256]{2,1,0:T(8,128)(2,1)S(1)}, u32[]{:S(2)}) copy-start(bf16[4,256,256]{2,1,0:T(8,128)(2,1)S(1)} %collective-permute-done.31.refs_7_) | copy-start | bytes 1572868
  (7 other events, 7.2 us)

commit v9 on v7

--- a/solution.py
+++ b/solution.py
@@ -327,13 +327,13 @@
             blocks.diagonal(end)
         mine = [blocks.piece(r, j) for j in range(n_layer)]
         theirs = [
-            blocks.swap(blocks.tie(x) if j in blocks.others else x) for j, x in enumerate(mine)
+            blocks.swap(blocks.tie(x) if r > 1 or j in blocks.others else x)
+            for j, x in enumerate(mine)
         ]
-        soon = [(far, 0) for far in range(r + 1, planes) if far > r + 1 or r == 0]
-        if r == 0 and end > 0:
-            soon += [(1, j) for j in blocks.singles[1:]]
-        if r == end - 1 and r > 0:
-            soon += [(end, j) for j in blocks.singles[:1]]
+        if r == 0:
+            soon = [(far, 0) for far in range(1, planes)] + [(1, j) for j in blocks.singles[1:]]
+        else:
+            soon = [(r + 1, j) for j in blocks.singles[: None if r == end - 1 else 1]]
         soon = [at for at in soon if at in blocks.pieces]
         place, *ready = lax.optimization_barrier((place, *[blocks.pieces[at] for at in soon]))
         blocks.pieces.update(zip(soon, ready))

time: 127 us -> 124 us (0.976)
  waiting for transfers between devices: 34.7 us -> 28.6 us
  local copies, waits for them, and re-layouts: 1.67 us -> 3.67 us
    ppermute x34, waiting for transfers between devices: 34.7 us -> 28.6 us  [permute(): return lax.ppermute(x, ('layer', 'feat'), sorted(flat))]
    unnamed x36 -> x42, local copies, waits for them, and re-layouts: 1.67 us -> 3.67 us
  transfers between devices with their start and end apart: 34 -> 34, of which waited for: 10 -> 12; matrix products, arithmetic and copies ran while one was open for 1% -> 1% of each run, Pallas kernels for 35% -> 35%
where the time goes in v9:
time: 124 us; the launch traced here: 123 us
  Pallas kernels  56.4 us (45%)
  starting transfers between devices  32.6 us (26%)
  waiting for transfers between devices  28.6 us (23%)
  local copies, waits for them, and re-layouts  3.67 us (3%)
    pallas_call x4, Pallas kernels, run_round(): pl.pallas_call(functools.partial(round_kernel, len(mine), len(tokens), la...  51.9 us
    ppermute x34, starting transfers between devices, permute(): return lax.ppermute(x, ('layer', 'feat'), sorted(flat))  32.6 us
    ppermute x34, waiting for transfers between devices, permute(): return lax.ppermute(x, ('layer', 'feat'), sorted(flat))  28.6 us
    pallas_call x1, Pallas kernels, prepare(): pl.pallas_call(prepare_kernel, grid=(layers,), in_specs=[block(rows, widt...  4.5 us
    unnamed x42, local copies, waits for them, and re-layouts  3.67 us
  transfers between devices with their start and end apart: 34, of which 12 were waited for; matrix products, arithmetic and copies ran while one was open for 1% of the time, Pallas kernels for 35%

profile of v9, /device:TPU:0, one launch (start us, length us, event | category | flops | bytes accessed | tf_op | source)
XLA Modules:
  0.0 123.3 jit_solution(9518825616993663378)
XLA Ops:
  0.6 0.7 collective-permute-start.1
  1.3 5.9 %collective-permute-start = (bf16[4,256,256]{2,1,0:T(8,128)(2,1)}, bf16[4,256,256]{2,1,0:T(8,128)(2,1)S(1)}, u32[]{:S(2)}, u32[]{:S(2)}) collective-permute-start(bf16[4,256,256]{2,1,0:T(8,128)(2,1)} %refs_0_.1), channel_id=1, source_target_pairs={{0,2},{1,3},{2,0},{3,1},{4,6},{5,7},{6,4},{7,5},{8,10},{9,11},{10,... | collective-permute-start | bytes 1572872 | tf_op jit(solution)/shard_map/ppermute | solution.py:61
  7.2 1.5 %collective-permute-start.8 = (bf16[4,256,256]{2,1,0:T(8,128)(2,1)}, bf16[4,256,256]{2,1,0:T(8,128)(2,1)S(1)}, u32[]{:S(2)}, u32[]{:S(2)}) collective-permute-start(bf16[4,256,256]{2,1,0:T(8,128)(2,1)} %refs_0_.1), channel_id=1, source_target_pairs={{0,16},{1,17},{2,18},{3,19},{4,20},{5,21},{6,22},{7,23},{8,24},{9,... | collective-permute-start | bytes 1572872 | tf_op jit(solution)/shard_map/ppermute | solution.py:61
  8.7 1.5 %collective-permute-start.7 = (bf16[4,256,256]{2,1,0:T(8,128)(2,1)}, bf16[4,256,256]{2,1,0:T(8,128)(2,1)}, u32[]{:S(2)}, u32[]{:S(2)}) collective-permute-start(bf16[4,256,256]{2,1,0:T(8,128)(2,1)} %refs_0_.1), channel_id=1, source_target_pairs={{0,8},{1,9},{2,10},{3,11},{4,12},{5,13},{6,14},{7,15},{8,0},{9,1},... | collective-permute-start | bytes 1572872 | tf_op jit(solution)/shard_map/ppermute | solution.py:61
  10.2 4.5 %shard_map.59 = (bf16[4,256,1024]{2,1,0:T(8,128)(2,1)}, bf16[4,1024,256]{2,1,0:T(8,128)(2,1)}) custom-call(bf16[4,1024,256]{2,1,0:T(8,128)(2,1)} %act.1, s32[4,2,1024]{2,1,0:T(2,128)} %bitcast.4), custom_call_target="tpu_custom_call" | custom-call | bytes 6291456 | tf_op jit(solution)/shard_map/pallas_call | solution.py:121
  14.7 1.3 %collective-permute-start.2 = (bf16[4,256,256]{2,1,0:T(8,128)(2,1)S(1)}, bf16[4,256,256]{2,1,0:T(8,128)(2,1)S(1)}, u32[]{:S(2)}, u32[]{:S(2)}) collective-permute-start(bf16[4,256,256]{2,1,0:T(8,128)(2,1)S(1)} %collective-permute-done.1), channel_id=1, source_target_pairs={{2,0},{3,1},{4,6},{5,7},{10,8},{11,9},{12,14},{13,15},{18,16},{19,... | collective-permute-start | bytes 1572872 | tf_op jit(solution)/shard_map/ppermute | solution.py:61
  16.0 3.0 %collective-permute-done.refs_1_ = bf16[4,256,256]{2,1,0:T(8,128)(2,1)S(1)} collective-permute-done((bf16[4,256,256]{2,1,0:T(8,128)(2,1)}, bf16[4,256,256]{2,1,0:T(8,128)(2,1)S(1)}, u32[]{:S(2)}, u32[]{:S(2)}) %collective-permute-start) | collective-permute-done | bytes 524320 | tf_op jit(solution)/shard_map/ppermute | solution.py:61
  19.1 0.7 collective-permute-start.3
  19.8 0.8 collective-permute-done.8.refs_2_
  20.5 1.5 %collective-permute-start.9 = (bf16[4,256,256]{2,1,0:T(8,128)(2,1)S(1)}, bf16[4,256,256]{2,1,0:T(8,128)(2,1)}, u32[]{:S(2)}, u32[]{:S(2)}) collective-permute-start(bf16[4,256,256]{2,1,0:T(8,128)(2,1)S(1)} %collective-permute-done.8.refs_2_), channel_id=1, source_target_pairs={{0,8},{1,9},{2,10},{3,11},{4,12},{5,13},{6,14},{7,15},{8,0},{9,1},... | collective-permute-start | bytes 1572872 | tf_op jit(solution)/shard_map/ppermute | solution.py:61
  22.0 1.5 %collective-permute-start.4 = (bf16[4,256,256]{2,1,0:T(8,128)(2,1)S(1)}, bf16[4,256,256]{2,1,0:T(8,128)(2,1)S(1)}, u32[]{:S(2)}, u32[]{:S(2)}) collective-permute-start(bf16[4,256,256]{2,1,0:T(8,128)(2,1)S(1)} %collective-permute-done.refs_1_), channel_id=1, source_target_pairs={{0,16},{1,17},{2,18},{3,19},{4,20},{5,21},{6,22},{7,23},{8,24},{9,... | collective-permute-start | bytes 1572872 | tf_op jit(solution)/shard_map/ppermute | solution.py:61
  23.5 8.3 %collective-permute-done.2 = bf16[4,256,256]{2,1,0:T(8,128)(2,1)S(1)} collective-permute-done((bf16[4,256,256]{2,1,0:T(8,128)(2,1)S(1)}, bf16[4,256,256]{2,1,0:T(8,128)(2,1)S(1)}, u32[]{:S(2)}, u32[]{:S(2)}) %collective-permute-start.2) | collective-permute-done | bytes 524320 | tf_op jit(solution)/shard_map/ppermute | solution.py:61
  31.8 0.5 collective-permute-start.11
  32.4 0.8 collective-permute-done.9.refs_3_
  33.1 0.7 pad_add_fusion.meta
  33.8 0.2 collective-permute-done.4.refs_3_
  34.0 1.4 %collective-permute-start.16 = (bf16[4,256,256]{2,1,0:T(8,128)(2,1)S(1)}, bf16[4,256,256]{2,1,0:T(8,128)(2,1)}, u32[]{:S(2)}, u32[]{:S(2)}) collective-permute-start(bf16[4,256,256]{2,1,0:T(8,128)(2,1)S(1)} %collective-permute-done.refs_1_), channel_id=1, source_target_pairs={{0,8},{1,9},{2,10},{3,11},{4,12},{5,13},{6,14},{7,15},{8,0},{9,1},... | collective-permute-start | bytes 1572872 | tf_op jit(solution)/shard_map/ppermute | solution.py:61
  35.4 0.6 collective-permute-start.5
  36.1 4.1 %collective-permute-start.17 = (bf16[4,256,256]{2,1,0:T(8,128)(2,1)}, bf16[4,256,256]{2,1,0:T(8,128)(2,1)}, u32[]{:S(2)}, u32[]{:S(2)}) collective-permute-start(bf16[4,256,256]{2,1,0:T(8,128)(2,1)} %collective-permute-done.9.refs_3_), channel_id=1, source_target_pairs={{0,2},{1,3},{2,0},{3,1},{4,6},{5,7},{6,4},{7,5},{8,10},{9,11},{10,... | collective-permute-start | bytes 1572872 | tf_op jit(solution)/shard_map/ppermute | solution.py:61
  40.2 0.7 collective-permute-start.22
  40.9 1.3 %collective-permute-start.6 = (bf16[4,256,256]{2,1,0:T(8,128)(2,1)S(1)}, bf16[4,256,256]{2,1,0:T(8,128)(2,1)S(1)}, u32[]{:S(2)}, u32[]{:S(2)}) collective-permute-start(bf16[4,256,256]{2,1,0:T(8,128)(2,1)S(1)} %collective-permute-done.3), channel_id=1, source_target_pairs={{2,0},{3,1},{4,6},{5,7},{10,8},{11,9},{12,14},{13,15},{18,16},{19,... | collective-permute-start | bytes 1572872 | tf_op jit(solution)/shard_map/ppermute | solution.py:61
  42.2 13.3 %shard_map.60 = (bf16[10,256,2048]{2,1,0:T(8,128)(2,1)}, f32[4,1024,256]{2,1,0:T(8,128)}, f32[8,128]{1,0:T(8,128)}) custom-call(s32[3]{0:T(128)} %pad_add_fusion.meta, bf16[4,256,1024]{2,1,0:T(8,128)(2,1)} %get-tuple-element.56.sparse, bf16[10,256,2048]{2,1,0:T(8,128)(2,1)} %decoder.7, bf16[4,256,256]{2,1,0:T(8,128)(2,1)} %refs_0_.1, ...), custom_call_target="tpu_custom_call" | custom-call | flops 10737418240 | bytes 20971520 | tf_op jit(solution)/shard_map/pallas_call | solution.py:273
  55.6 0.5 collective-permute-start.20
  56.2 7.2 %collective-permute-done.6 = bf16[4,256,256]{2,1,0:T(8,128)(2,1)S(1)} collective-permute-done((bf16[4,256,256]{2,1,0:T(8,128)(2,1)S(1)}, bf16[4,256,256]{2,1,0:T(8,128)(2,1)S(1)}, u32[]{:S(2)}, u32[]{:S(2)}) %collective-permute-start.6) | collective-permute-done | bytes 524320 | tf_op jit(solution)/shard_map/ppermute | solution.py:61
  63.5 1.6 %collective-permute-start.23 = (bf16[4,256,256]{2,1,0:T(8,128)(2,1)S(1)}, bf16[4,256,256]{2,1,0:T(8,128)(2,1)}, u32[]{:S(2)}, u32[]{:S(2)}) collective-permute-start(bf16[4,256,256]{2,1,0:T(8,128)(2,1)S(1)} %broadcast_select_fusion.2.refs_1_), channel_id=1, source_target_pairs={{0,16},{1,17},{2,18},{3,19},{4,20},{5,21},{6,22},{7,23},{8,24},{9,... | collective-permute-start | bytes 1572872 | tf_op jit(solution)/shard_map/ppermute | solution.py:61
  65.1 1.5 %collective-permute-start.14 = (bf16[4,256,256]{2,1,0:T(8,128)(2,1)S(1)}, bf16[4,256,256]{2,1,0:T(8,128)(2,1)S(1)}, u32[]{:S(2)}, u32[]{:S(2)}) collective-permute-start(bf16[4,256,256]{2,1,0:T(8,128)(2,1)S(1)} %broadcast_select_fusion.1.refs_2_), channel_id=1, source_target_pairs={{0,8},{1,9},{2,10},{3,11},{4,12},{5,13},{6,14},{7,15},{8,0},{9,1},... | collective-permute-start | bytes 1572872 | tf_op jit(solution)/shard_map/ppermute | solution.py:61
  66.6 0.5 collective-permute-start.15
  67.1 0.3 copy-done.10
  67.4 1.5 %collective-permute-start.24 = (bf16[4,256,256]{2,1,0:T(8,128)(2,1)S(1)}, bf16[4,256,256]{2,1,0:T(8,128)(2,1)S(1)}, u32[]{:S(2)}, u32[]{:S(2)}) collective-permute-start(bf16[4,256,256]{2,1,0:T(8,128)(2,1)S(1)} %collective-permute-done.22), channel_id=1, source_target_pairs={{2,0},{3,1},{4,6},{5,7},{10,8},{11,9},{12,14},{13,15},{18,16},{19,... | collective-permute-start | bytes 1572872 | tf_op jit(solution)/shard_map/ppermute | solution.py:61
  68.9 0.8 copy-done.12
  69.6 13.0 %shard_map.61 = (bf16[10,256,2048]{2,1,0:T(8,128)(2,1)}, f32[4,1024,256]{2,1,0:T(8,128)}, f32[8,128]{1,0:T(8,128)}) custom-call(s32[3]{0:T(128)} %pad_add_fusion.meta, bf16[4,256,1024]{2,1,0:T(8,128)(2,1)} %get-tuple-element.56.sparse, bf16[10,256,2048]{2,1,0:T(8,128)(2,1)} %decoder.7, ...), custom_call_target="tpu_custom_call", output_to_operand_aliasing={{0}: (12, {})} | custom-call | flops 10737418240 | bytes 20971520 | tf_op jit(solution)/shard_map/pallas_call | solution.py:273
  82.7 0.4 collective-permute-done.24
  83.2 0.5 collective-permute-start.27
  83.8 0.5 collective-permute-start.25
  84.3 4.9 %collective-permute-done.15.refs_4_ = bf16[4,256,256]{2,1,0:T(8,128)(2,1)S(1)} collective-permute-done((bf16[4,256,256]{2,1,0:T(8,128)(2,1)S(1)}, bf16[4,256,256]{2,1,0:T(8,128)(2,1)S(1)}, u32[]{:S(2)}, u32[]{:S(2)}) %collective-permute-start.15) | collective-permute-done | bytes 524320 | tf_op jit(solution)/shard_map/ppermute | solution.py:61
  89.1 1.5 %collective-permute-start.29 = (bf16[4,256,256]{2,1,0:T(8,128)(2,1)S(1)}, bf16[4,256,256]{2,1,0:T(8,128)(2,1)S(1)}, u32[]{:S(2)}, u32[]{:S(2)}) collective-permute-start(bf16[4,256,256]{2,1,0:T(8,128)(2,1)S(1)} %collective-permute-done.14.refs_3_), channel_id=1, source_target_pairs={{0,16},{1,17},{2,18},{3,19},{4,20},{5,21},{6,22},{7,23},{8,24},{9,... | collective-permute-start | bytes 1572872 | tf_op jit(solution)/shard_map/ppermute | solution.py:61
  90.7 0.9 copy-done.14
  91.6 0.2 copy-done.15
  91.8 0.6 copy-done.18
  92.4 13.0 %shard_map.62 = (bf16[10,256,2048]{2,1,0:T(8,128)(2,1)}, f32[4,1024,256]{2,1,0:T(8,128)}, f32[8,128]{1,0:T(8,128)}) custom-call(s32[3]{0:T(128)} %pad_add_fusion.meta, bf16[4,256,1024]{2,1,0:T(8,128)(2,1)} %get-tuple-element.56.sparse, bf16[10,256,2048]{2,1,0:T(8,128)(2,1)} %decoder.7, ...), custom_call_target="tpu_custom_call", output_to_operand_aliasing={{0}: (12, {})} | custom-call | flops 10737418240 | bytes 20971520 | tf_op jit(solution)/shard_map/pallas_call | solution.py:273
  105.5 0.5 collective-permute-start.32
  106.1 0.4 collective-permute-start.30
  106.5 0.9 collective-permute-done.33.refs_9_
  107.4 0.7 collective-permute-done.32.refs_8_
  108.2 0.7 collective-permute-done.31.refs_7_
  108.9 0.7 collective-permute-done.30.refs_6_
  109.7 0.8 copy-done.20
  110.5 12.7 %shard_map.63 = (bf16[10,256,2048]{2,1,0:T(8,128)(2,1)}, bf16[4,1024,256]{2,1,0:T(8,128)(2,1)}, f32[8,128]{1,0:T(8,128)}) custom-call(s32[3]{0:T(128)} %pad_add_fusion.meta, bf16[4,256,1024]{2,1,0:T(8,128)(2,1)} %get-tuple-element.56.sparse, bf16[10,256,2048]{2,1,0:T(8,128)(2,1)} %decoder.7, ...), custom_call_target="tpu_custom_call", output_to_operand_aliasing={{0}: (13, {})} | custom-call | flops 10737418240 | bytes 20971520 | tf_op jit(solution)/shard_map/pallas_call | solution.py:273
  (71 shorter events, 0.8 us)
Async XLA Ops:
  0.6 14.1 %collective-permute-start.1 = (bf16[4,256,256]{2,1,0:T(8,128)(2,1)}, bf16[4,256,256]{2,1,0:T(8,128)(2,1)S(1)}, u32[]{:S(2)}, u32[]{:S(2)}) collective-permute-start(bf16[4,256,256]{2,1,0:T(8,128)(2,1)} %refs_0_.1), channel_id=1, source_target_pairs={{2,4},{3,5},{4,2},{5,3},{10,12},{11,13},{12,10},{13,11},{18,20},{1... | collective-permute-start | bytes 1572872 | tf_op jit(solution)/shard_map/ppermute | solution.py:61
  1.3 17.7 %collective-permute-start = (bf16[4,256,256]{2,1,0:T(8,128)(2,1)}, bf16[4,256,256]{2,1,0:T(8,128)(2,1)S(1)}, u32[]{:S(2)}, u32[]{:S(2)}) collective-permute-start(bf16[4,256,256]{2,1,0:T(8,128)(2,1)} %refs_0_.1), channel_id=1, source_target_pairs={{0,2},{1,3},{2,0},{3,1},{4,6},{5,7},{6,4},{7,5},{8,10},{9,11},{10,... | collective-permute-start | bytes 1572872 | tf_op jit(solution)/shard_map/ppermute | solution.py:61
  7.2 13.3 %collective-permute-start.8 = (bf16[4,256,256]{2,1,0:T(8,128)(2,1)}, bf16[4,256,256]{2,1,0:T(8,128)(2,1)S(1)}, u32[]{:S(2)}, u32[]{:S(2)}) collective-permute-start(bf16[4,256,256]{2,1,0:T(8,128)(2,1)} %refs_0_.1), channel_id=1, source_target_pairs={{0,16},{1,17},{2,18},{3,19},{4,20},{5,21},{6,22},{7,23},{8,24},{9,... | collective-permute-start | bytes 1572872 | tf_op jit(solution)/shard_map/ppermute | solution.py:61
  8.7 14.8 %collective-permute-start.7 = (bf16[4,256,256]{2,1,0:T(8,128)(2,1)}, bf16[4,256,256]{2,1,0:T(8,128)(2,1)}, u32[]{:S(2)}, u32[]{:S(2)}) collective-permute-start(bf16[4,256,256]{2,1,0:T(8,128)(2,1)} %refs_0_.1), channel_id=1, source_target_pairs={{0,8},{1,9},{2,10},{3,11},{4,12},{5,13},{6,14},{7,15},{8,0},{9,1},... | collective-permute-start | bytes 1572872 | tf_op jit(solution)/shard_map/ppermute | solution.py:61
  14.7 17.1 %collective-permute-start.2 = (bf16[4,256,256]{2,1,0:T(8,128)(2,1)S(1)}, bf16[4,256,256]{2,1,0:T(8,128)(2,1)S(1)}, u32[]{:S(2)}, u32[]{:S(2)}) collective-permute-start(bf16[4,256,256]{2,1,0:T(8,128)(2,1)S(1)} %collective-permute-done.1), channel_id=1, source_target_pairs={{2,0},{3,1},{4,6},{5,7},{10,8},{11,9},{12,14},{13,15},{18,16},{19,... | collective-permute-start | bytes 1572872 | tf_op jit(solution)/shard_map/ppermute | solution.py:61
  19.1 36.4 %copy-start.3 = (bf16[4,256,256]{2,1,0:T(8,128)(2,1)}, bf16[4,256,256]{2,1,0:T(8,128)(2,1)S(1)}, u32[]{:S(2)}) copy-start(bf16[4,256,256]{2,1,0:T(8,128)(2,1)S(1)} %collective-permute-done.refs_1_) | copy-start | bytes 1572868
  19.1 12.8 %collective-permute-start.3 = (bf16[4,256,256]{2,1,0:T(8,128)(2,1)S(1)}, bf16[4,256,256]{2,1,0:T(8,128)(2,1)S(1)}, u32[]{:S(2)}, u32[]{:S(2)}) collective-permute-start(bf16[4,256,256]{2,1,0:T(8,128)(2,1)S(1)} %collective-permute-done.refs_1_), channel_id=1, source_target_pairs={{2,4},{3,5},{4,2},{5,3},{10,12},{11,13},{12,10},{13,11},{18,20},{1... | collective-permute-start | bytes 1572872 | tf_op jit(solution)/shard_map/ppermute | solution.py:61
  20.5 20.4 %copy-start.5 = (bf16[4,256,256]{2,1,0:T(8,128)(2,1)}, bf16[4,256,256]{2,1,0:T(8,128)(2,1)S(1)}, u32[]{:S(2)}) copy-start(bf16[4,256,256]{2,1,0:T(8,128)(2,1)S(1)} %collective-permute-done.8.refs_2_) | copy-start | bytes 1572868
  20.5 12.6 %collective-permute-start.9 = (bf16[4,256,256]{2,1,0:T(8,128)(2,1)S(1)}, bf16[4,256,256]{2,1,0:T(8,128)(2,1)}, u32[]{:S(2)}, u32[]{:S(2)}) collective-permute-start(bf16[4,256,256]{2,1,0:T(8,128)(2,1)S(1)} %collective-permute-done.8.refs_2_), channel_id=1, source_target_pairs={{0,8},{1,9},{2,10},{3,11},{4,12},{5,13},{6,14},{7,15},{8,0},{9,1},... | collective-permute-start | bytes 1572872 | tf_op jit(solution)/shard_map/ppermute | solution.py:61
  22.0 12.0 %collective-permute-start.4 = (bf16[4,256,256]{2,1,0:T(8,128)(2,1)S(1)}, bf16[4,256,256]{2,1,0:T(8,128)(2,1)S(1)}, u32[]{:S(2)}, u32[]{:S(2)}) collective-permute-start(bf16[4,256,256]{2,1,0:T(8,128)(2,1)S(1)} %collective-permute-done.refs_1_), channel_id=1, source_target_pairs={{0,16},{1,17},{2,18},{3,19},{4,20},{5,21},{6,22},{7,23},{8,24},{9,... | collective-permute-start | bytes 1572872 | tf_op jit(solution)/shard_map/ppermute | solution.py:61
  23.5 11.9 %collective-permute-start.10 = (bf16[4,256,256]{2,1,0:T(8,128)(2,1)}, bf16[4,256,256]{2,1,0:T(8,128)(2,1)}, u32[]{:S(2)}, u32[]{:S(2)}) collective-permute-start(bf16[4,256,256]{2,1,0:T(8,128)(2,1)} %refs_0_.1), channel_id=1, source_target_pairs={{0,1},{1,0},{2,3},{3,2},{4,5},{5,4},{6,7},{7,6},{8,9},{9,8},{10,11... | collective-permute-start | bytes 1572872 | tf_op jit(solution)/shard_map/ppermute | solution.py:61
  31.8 4.2 %collective-permute-start.12 = (bf16[4,256,256]{2,1,0:T(8,128)(2,1)S(1)}, bf16[4,256,256]{2,1,0:T(8,128)(2,1)}, u32[]{:S(2)}, u32[]{:S(2)}) collective-permute-start(bf16[4,256,256]{2,1,0:T(8,128)(2,1)S(1)} %collective-permute-done.8.refs_2_), channel_id=1, source_target_pairs={{0,1},{1,0},{2,3},{3,2},{4,5},{5,4},{6,7},{7,6},{8,9},{9,8},{10,11... | collective-permute-start | bytes 1572872 | tf_op jit(solution)/shard_map/ppermute | solution.py:61
  31.8 8.4 %collective-permute-start.11 = (bf16[4,256,256]{2,1,0:T(8,128)(2,1)}, bf16[4,256,256]{2,1,0:T(8,128)(2,1)}, u32[]{:S(2)}, u32[]{:S(2)}) collective-permute-start(bf16[4,256,256]{2,1,0:T(8,128)(2,1)} %collective-permute-done.7.refs_1_), channel_id=1, source_target_pairs={{0,1},{1,0},{2,3},{3,2},{4,5},{5,4},{6,7},{7,6},{8,9},{9,8},{10,11... | collective-permute-start | bytes 1572872 | tf_op jit(solution)/shard_map/ppermute | solution.py:61
  33.1 7.8 %collective-permute-start.13 = (bf16[4,256,256]{2,1,0:T(8,128)(2,1)}, bf16[4,256,256]{2,1,0:T(8,128)(2,1)}, u32[]{:S(2)}, u32[]{:S(2)}) collective-permute-start(bf16[4,256,256]{2,1,0:T(8,128)(2,1)} %collective-permute-done.9.refs_3_), channel_id=1, source_target_pairs={{0,1},{1,0},{2,3},{3,2},{4,5},{5,4},{6,7},{7,6},{8,9},{9,8},{10,11... | collective-permute-start | bytes 1572872 | tf_op jit(solution)/shard_map/ppermute | solution.py:61
  33.8 49.9 %copy-start = (bf16[4,256,256]{2,1,0:T(8,128)(2,1)}, bf16[4,256,256]{2,1,0:T(8,128)(2,1)S(1)}, u32[]{:S(2)}) copy-start(bf16[4,256,256]{2,1,0:T(8,128)(2,1)S(1)} %broadcast_select_fusion.2.refs_1_) | copy-start | bytes 1572868
  34.0 21.6 %copy-start.4 = (bf16[4,256,256]{2,1,0:T(8,128)(2,1)}, bf16[4,256,256]{2,1,0:T(8,128)(2,1)S(1)}, u32[]{:S(2)}) copy-start(bf16[4,256,256]{2,1,0:T(8,128)(2,1)S(1)} %collective-permute-done.4.refs_3_) | copy-start | bytes 1572868
  34.0 21.6 %collective-permute-start.16 = (bf16[4,256,256]{2,1,0:T(8,128)(2,1)S(1)}, bf16[4,256,256]{2,1,0:T(8,128)(2,1)}, u32[]{:S(2)}, u32[]{:S(2)}) collective-permute-start(bf16[4,256,256]{2,1,0:T(8,128)(2,1)S(1)} %collective-permute-done.refs_1_), channel_id=1, source_target_pairs={{0,8},{1,9},{2,10},{3,11},{4,12},{5,13},{6,14},{7,15},{8,0},{9,1},... | collective-permute-start | bytes 1572872 | tf_op jit(solution)/shard_map/ppermute | solution.py:61
  35.4 28.1 %collective-permute-start.5 = (bf16[4,256,256]{2,1,0:T(8,128)(2,1)S(1)}, bf16[4,256,256]{2,1,0:T(8,128)(2,1)}, u32[]{:S(2)}, u32[]{:S(2)}) collective-permute-start(bf16[4,256,256]{2,1,0:T(8,128)(2,1)S(1)} %broadcast_select_fusion.2.refs_1_), channel_id=1, source_target_pairs={{0,8},{1,9},{2,10},{3,11},{4,12},{5,13},{6,14},{7,15},{8,0},{9,1},... | collective-permute-start | bytes 1572872 | tf_op jit(solution)/shard_map/ppermute | solution.py:61
  36.1 19.4 %collective-permute-start.17 = (bf16[4,256,256]{2,1,0:T(8,128)(2,1)}, bf16[4,256,256]{2,1,0:T(8,128)(2,1)}, u32[]{:S(2)}, u32[]{:S(2)}) collective-permute-start(bf16[4,256,256]{2,1,0:T(8,128)(2,1)} %collective-permute-done.9.refs_3_), channel_id=1, source_target_pairs={{0,2},{1,3},{2,0},{3,1},{4,6},{5,7},{6,4},{7,5},{8,10},{9,11},{10,... | collective-permute-start | bytes 1572872 | tf_op jit(solution)/shard_map/ppermute | solution.py:61
  40.2 15.9 %collective-permute-start.22 = (bf16[4,256,256]{2,1,0:T(8,128)(2,1)}, bf16[4,256,256]{2,1,0:T(8,128)(2,1)S(1)}, u32[]{:S(2)}, u32[]{:S(2)}) collective-permute-start(bf16[4,256,256]{2,1,0:T(8,128)(2,1)} %collective-permute-done.9.refs_3_), channel_id=1, source_target_pairs={{2,4},{3,5},{4,2},{5,3},{10,12},{11,13},{12,10},{13,11},{18,20},{1... | collective-permute-start | bytes 1572872 | tf_op jit(solution)/shard_map/ppermute | solution.py:61
  40.9 22.5 %collective-permute-start.6 = (bf16[4,256,256]{2,1,0:T(8,128)(2,1)S(1)}, bf16[4,256,256]{2,1,0:T(8,128)(2,1)S(1)}, u32[]{:S(2)}, u32[]{:S(2)}) collective-permute-start(bf16[4,256,256]{2,1,0:T(8,128)(2,1)S(1)} %collective-permute-done.3), channel_id=1, source_target_pairs={{2,0},{3,1},{4,6},{5,7},{10,8},{11,9},{12,14},{13,15},{18,16},{19,... | collective-permute-start | bytes 1572872 | tf_op jit(solution)/shard_map/ppermute | solution.py:61
  55.5 9.6 %collective-permute-start.18 = (bf16[4,256,256]{2,1,0:T(8,128)(2,1)S(1)}, bf16[4,256,256]{2,1,0:T(8,128)(2,1)S(1)}, u32[]{:S(2)}, u32[]{:S(2)}) collective-permute-start(bf16[4,256,256]{2,1,0:T(8,128)(2,1)S(1)} %collective-permute-done.refs_1_), channel_id=1, source_target_pairs={{0,1},{1,0},{2,3},{3,2},{4,5},{5,4},{6,7},{7,6},{8,9},{9,8},{10,11... | collective-permute-start | bytes 1572872 | tf_op jit(solution)/shard_map/ppermute | solution.py:61
  55.6 11.0 %collective-permute-start.20 = (bf16[4,256,256]{2,1,0:T(8,128)(2,1)S(1)}, bf16[4,256,256]{2,1,0:T(8,128)(2,1)S(1)}, u32[]{:S(2)}, u32[]{:S(2)}) collective-permute-start(bf16[4,256,256]{2,1,0:T(8,128)(2,1)S(1)} %collective-permute-done.4.refs_3_), channel_id=1, source_target_pairs={{0,1},{1,0},{2,3},{3,2},{4,5},{5,4},{6,7},{7,6},{8,9},{9,8},{10,11... | collective-permute-start | bytes 1572872 | tf_op jit(solution)/shard_map/ppermute | solution.py:61
  56.1 11.0 %collective-permute-start.19 = (bf16[4,256,256]{2,1,0:T(8,128)(2,1)}, bf16[4,256,256]{2,1,0:T(8,128)(2,1)S(1)}, u32[]{:S(2)}, u32[]{:S(2)}) collective-permute-start(bf16[4,256,256]{2,1,0:T(8,128)(2,1)} %collective-permute-done.16.refs_2_), channel_id=1, source_target_pairs={{0,1},{1,0},{2,3},{3,2},{4,5},{5,4},{6,7},{7,6},{8,9},{9,8},{10,11... | collective-permute-start | bytes 1572872 | tf_op jit(solution)/shard_map/ppermute | solution.py:61
  63.4 5.5 %collective-permute-start.21 = (bf16[4,256,256]{2,1,0:T(8,128)(2,1)}, bf16[4,256,256]{2,1,0:T(8,128)(2,1)S(1)}, u32[]{:S(2)}, u32[]{:S(2)}) collective-permute-start(bf16[4,256,256]{2,1,0:T(8,128)(2,1)} %collective-permute-done.17.refs_4_), channel_id=1, source_target_pairs={{0,1},{1,0},{2,3},{3,2},{4,5},{5,4},{6,7},{7,6},{8,9},{9,8},{10,11... | collective-permute-start | bytes 1572872 | tf_op jit(solution)/shard_map/ppermute | solution.py:61
  63.5 42.7 %copy-start.1 = (bf16[4,256,256]{2,1,0:T(8,128)(2,1)}, bf16[4,256,256]{2,1,0:T(8,128)(2,1)S(1)}, u32[]{:S(2)}) copy-start(bf16[4,256,256]{2,1,0:T(8,128)(2,1)S(1)} %broadcast_select_fusion.1.refs_2_) | copy-start | bytes 1572868
  63.5 19.7 %collective-permute-start.23 = (bf16[4,256,256]{2,1,0:T(8,128)(2,1)S(1)}, bf16[4,256,256]{2,1,0:T(8,128)(2,1)}, u32[]{:S(2)}, u32[]{:S(2)}) collective-permute-start(bf16[4,256,256]{2,1,0:T(8,128)(2,1)S(1)} %broadcast_select_fusion.2.refs_1_), channel_id=1, source_target_pairs={{0,16},{1,17},{2,18},{3,19},{4,20},{5,21},{6,22},{7,23},{8,24},{9,... | collective-permute-start | bytes 1572872 | tf_op jit(solution)/shard_map/ppermute | solution.py:61
  65.1 2.0 %copy-start.9 = (bf16[4,256,256]{2,1,0:T(8,128)(2,1)}, bf16[4,256,256]{2,1,0:T(8,128)(2,1)S(1)}, u32[]{:S(2)}) copy-start(bf16[4,256,256]{2,1,0:T(8,128)(2,1)S(1)} %collective-permute-done.18.refs_5_) | copy-start | bytes 1572868
  65.1 18.7 %collective-permute-start.14 = (bf16[4,256,256]{2,1,0:T(8,128)(2,1)S(1)}, bf16[4,256,256]{2,1,0:T(8,128)(2,1)S(1)}, u32[]{:S(2)}, u32[]{:S(2)}) collective-permute-start(bf16[4,256,256]{2,1,0:T(8,128)(2,1)S(1)} %broadcast_select_fusion.1.refs_2_), channel_id=1, source_target_pairs={{0,8},{1,9},{2,10},{3,11},{4,12},{5,13},{6,14},{7,15},{8,0},{9,1},... | collective-permute-start | bytes 1572872 | tf_op jit(solution)/shard_map/ppermute | solution.py:61
  66.6 22.5 %collective-permute-start.15 = (bf16[4,256,256]{2,1,0:T(8,128)(2,1)S(1)}, bf16[4,256,256]{2,1,0:T(8,128)(2,1)S(1)}, u32[]{:S(2)}, u32[]{:S(2)}) collective-permute-start(bf16[4,256,256]{2,1,0:T(8,128)(2,1)S(1)} %broadcast_select_fusion.1.refs_2_), channel_id=1, source_target_pairs={{0,16},{1,17},{2,18},{3,19},{4,20},{5,21},{6,22},{7,23},{8,24},{9,... | collective-permute-start | bytes 1572872 | tf_op jit(solution)/shard_map/ppermute | solution.py:61
  67.4 15.7 %collective-permute-start.24 = (bf16[4,256,256]{2,1,0:T(8,128)(2,1)S(1)}, bf16[4,256,256]{2,1,0:T(8,128)(2,1)S(1)}, u32[]{:S(2)}, u32[]{:S(2)}) collective-permute-start(bf16[4,256,256]{2,1,0:T(8,128)(2,1)S(1)} %collective-permute-done.22), channel_id=1, source_target_pairs={{2,0},{3,1},{4,6},{5,7},{10,8},{11,9},{12,14},{13,15},{18,16},{19,... | collective-permute-start | bytes 1572872 | tf_op jit(solution)/shard_map/ppermute | solution.py:61
  83.1 9.3 %copy-start.2 = (bf16[4,256,256]{2,1,0:T(8,128)(2,1)}, bf16[4,256,256]{2,1,0:T(8,128)(2,1)S(1)}, u32[]{:S(2)}) copy-start(bf16[4,256,256]{2,1,0:T(8,128)(2,1)S(1)} %broadcast_select_fusion.refs_4_) | copy-start | bytes 1572868
  83.1 7.5 %collective-permute-start.28 = (bf16[4,256,256]{2,1,0:T(8,128)(2,1)S(1)}, bf16[4,256,256]{2,1,0:T(8,128)(2,1)S(1)}, u32[]{:S(2)}, u32[]{:S(2)}) collective-permute-start(bf16[4,256,256]{2,1,0:T(8,128)(2,1)S(1)} %broadcast_select_fusion.refs_4_), channel_id=1, source_target_pairs={{0,1},{1,0},{2,3},{3,2},{4,5},{5,4},{6,7},{7,6},{8,9},{9,8},{10,11... | collective-permute-start | bytes 1572872 | tf_op jit(solution)/shard_map/ppermute | solution.py:61
  83.2 7.5 %collective-permute-start.27 = (bf16[4,256,256]{2,1,0:T(8,128)(2,1)}, bf16[4,256,256]{2,1,0:T(8,128)(2,1)S(1)}, u32[]{:S(2)}, u32[]{:S(2)}) collective-permute-start(bf16[4,256,256]{2,1,0:T(8,128)(2,1)} %collective-permute-done.23.refs_3_), channel_id=1, source_target_pairs={{0,1},{1,0},{2,3},{3,2},{4,5},{5,4},{6,7},{7,6},{8,9},{9,8},{10,11... | collective-permute-start | bytes 1572872 | tf_op jit(solution)/shard_map/ppermute | solution.py:61
  83.7 7.0 %collective-permute-start.26 = (bf16[4,256,256]{2,1,0:T(8,128)(2,1)}, bf16[4,256,256]{2,1,0:T(8,128)(2,1)S(1)}, u32[]{:S(2)}, u32[]{:S(2)}) collective-permute-start(bf16[4,256,256]{2,1,0:T(8,128)(2,1)} %collective-permute-done.5.refs_2_), channel_id=1, source_target_pairs={{0,1},{1,0},{2,3},{3,2},{4,5},{5,4},{6,7},{7,6},{8,9},{9,8},{10,11... | collective-permute-start | bytes 1572872 | tf_op jit(solution)/shard_map/ppermute | solution.py:61
  83.8 22.3 %copy-start.6 = (bf16[4,256,256]{2,1,0:T(8,128)(2,1)}, bf16[4,256,256]{2,1,0:T(8,128)(2,1)S(1)}, u32[]{:S(2)}) copy-start(bf16[4,256,256]{2,1,0:T(8,128)(2,1)S(1)} %collective-permute-done.14.refs_3_) | copy-start | bytes 1572868
  83.8 6.9 %collective-permute-start.25 = (bf16[4,256,256]{2,1,0:T(8,128)(2,1)S(1)}, bf16[4,256,256]{2,1,0:T(8,128)(2,1)S(1)}, u32[]{:S(2)}, u32[]{:S(2)}) collective-permute-start(bf16[4,256,256]{2,1,0:T(8,128)(2,1)S(1)} %broadcast_select_fusion.2.refs_1_), channel_id=1, source_target_pairs={{0,1},{1,0},{2,3},{3,2},{4,5},{5,4},{6,7},{7,6},{8,9},{9,8},{10,11... | collective-permute-start | bytes 1572872 | tf_op jit(solution)/shard_map/ppermute | solution.py:61
  89.1 16.4 %copy-start.7 = (bf16[4,256,256]{2,1,0:T(8,128)(2,1)}, bf16[4,256,256]{2,1,0:T(8,128)(2,1)S(1)}, u32[]{:S(2)}) copy-start(bf16[4,256,256]{2,1,0:T(8,128)(2,1)S(1)} %collective-permute-done.15.refs_4_) | copy-start | bytes 1572868
  89.1 16.3 %collective-permute-start.29 = (bf16[4,256,256]{2,1,0:T(8,128)(2,1)S(1)}, bf16[4,256,256]{2,1,0:T(8,128)(2,1)S(1)}, u32[]{:S(2)}, u32[]{:S(2)}) collective-permute-start(bf16[4,256,256]{2,1,0:T(8,128)(2,1)S(1)} %collective-permute-done.14.refs_3_), channel_id=1, source_target_pairs={{0,16},{1,17},{2,18},{3,19},{4,20},{5,21},{6,22},{7,23},{8,24},{9,... | collective-permute-start | bytes 1572872 | tf_op jit(solution)/shard_map/ppermute | solution.py:61
  90.6 1.8 %copy-start.13 = (bf16[4,256,256]{2,1,0:T(8,128)(2,1)}, bf16[4,256,256]{2,1,0:T(8,128)(2,1)S(1)}, u32[]{:S(2)}) copy-start(bf16[4,256,256]{2,1,0:T(8,128)(2,1)S(1)} %collective-permute-done.28.refs_8_) | copy-start | bytes 1572868
  105.4 5.0 %copy-start.8 = (bf16[4,256,256]{2,1,0:T(8,128)(2,1)}, bf16[4,256,256]{2,1,0:T(8,128)(2,1)S(1)}, u32[]{:S(2)}) copy-start(bf16[4,256,256]{2,1,0:T(8,128)(2,1)S(1)} %collective-permute-done.29.refs_5_) | copy-start | bytes 1572868
  105.5 2.0 %collective-permute-start.33 = (bf16[4,256,256]{2,1,0:T(8,128)(2,1)S(1)}, bf16[4,256,256]{2,1,0:T(8,128)(2,1)S(1)}, u32[]{:S(2)}, u32[]{:S(2)}) collective-permute-start(bf16[4,256,256]{2,1,0:T(8,128)(2,1)S(1)} %collective-permute-done.29.refs_5_), channel_id=1, source_target_pairs={{0,1},{1,0},{2,3},{3,2},{4,5},{5,4},{6,7},{7,6},{8,9},{9,8},{10,11... | collective-permute-start | bytes 1572872 | tf_op jit(solution)/shard_map/ppermute | solution.py:61
  105.5 2.6 %collective-permute-start.32 = (bf16[4,256,256]{2,1,0:T(8,128)(2,1)S(1)}, bf16[4,256,256]{2,1,0:T(8,128)(2,1)S(1)}, u32[]{:S(2)}, u32[]{:S(2)}) collective-permute-start(bf16[4,256,256]{2,1,0:T(8,128)(2,1)S(1)} %collective-permute-done.15.refs_4_), channel_id=1, source_target_pairs={{0,1},{1,0},{2,3},{3,2},{4,5},{5,4},{6,7},{7,6},{8,9},{9,8},{10,11... | collective-permute-start | bytes 1572872 | tf_op jit(solution)/shard_map/ppermute | solution.py:61
  106.0 2.9 %collective-permute-start.31 = (bf16[4,256,256]{2,1,0:T(8,128)(2,1)S(1)}, bf16[4,256,256]{2,1,0:T(8,128)(2,1)S(1)}, u32[]{:S(2)}, u32[]{:S(2)}) collective-permute-start(bf16[4,256,256]{2,1,0:T(8,128)(2,1)S(1)} %collective-permute-done.14.refs_3_), channel_id=1, source_target_pairs={{0,1},{1,0},{2,3},{3,2},{4,5},{5,4},{6,7},{7,6},{8,9},{9,8},{10,11... | collective-permute-start | bytes 1572872 | tf_op jit(solution)/shard_map/ppermute | solution.py:61
  106.1 3.6 %collective-permute-start.30 = (bf16[4,256,256]{2,1,0:T(8,128)(2,1)S(1)}, bf16[4,256,256]{2,1,0:T(8,128)(2,1)S(1)}, u32[]{:S(2)}, u32[]{:S(2)}) collective-permute-start(bf16[4,256,256]{2,1,0:T(8,128)(2,1)S(1)} %broadcast_select_fusion.1.refs_2_), channel_id=1, source_target_pairs={{0,1},{1,0},{2,3},{3,2},{4,5},{5,4},{6,7},{7,6},{8,9},{9,8},{10,11... | collective-permute-start | bytes 1572872 | tf_op jit(solution)/shard_map/ppermute | solution.py:61
  107.4 3.1 %copy-start.16 = (bf16[4,256,256]{2,1,0:T(8,128)(2,1)}, bf16[4,256,256]{2,1,0:T(8,128)(2,1)S(1)}, u32[]{:S(2)}) copy-start(bf16[4,256,256]{2,1,0:T(8,128)(2,1)S(1)} %collective-permute-done.33.refs_9_) | copy-start | bytes 1572868
  108.2 2.3 %copy-start.17 = (bf16[4,256,256]{2,1,0:T(8,128)(2,1)}, bf16[4,256,256]{2,1,0:T(8,128)(2,1)S(1)}, u32[]{:S(2)}) copy-start(bf16[4,256,256]{2,1,0:T(8,128)(2,1)S(1)} %collective-permute-done.32.refs_8_) | copy-start | bytes 1572868
  108.9 1.6 %copy-start.19 = (bf16[4,256,256]{2,1,0:T(8,128)(2,1)}, bf16[4,256,256]{2,1,0:T(8,128)(2,1)S(1)}, u32[]{:S(2)}) copy-start(bf16[4,256,256]{2,1,0:T(8,128)(2,1)S(1)} %collective-permute-done.31.refs_7_) | copy-start | bytes 1572868
  (7 other events, 6.8 us)

commit v10 on v9

--- a/solution.py
+++ b/solution.py
@@ -76,7 +76,7 @@
     def diagonal(self, r):
         for j in self.others:
             bits = [1 << b for b in range(j.bit_length()) if j >> b & 1]
-            self.across(r, j, bits[0] if r == 0 else bits[-1])
+            self.across(r, j, bits[0] if r < 2 else bits[-1])
 
     def along_line(self, j, rounds, hops):
         for dist, r, held, moves in self.groups:
@@ -316,13 +316,15 @@
             for near in range(1, min(3, planes)):
                 blocks.straight(near)
             blocks.diagonal(0)
+            if end > 1:
+                blocks.diagonal(1)
             for j in blocks.others:
-                blocks.along_line(j, range(1, end), [1])
+                blocks.along_line(j, range(2, end), [1])
         else:
             if r + 2 < planes:
                 blocks.straight(r + 2)
             for j in blocks.others:
-                blocks.along_line(j, range(1, end), [r + 1])
+                blocks.along_line(j, range(2, end), [r + 1])
         if r == max(end - 1, 0) and end > 0:
             blocks.diagonal(end)
         mine = [blocks.piece(r, j) for j in range(n_layer)]
@@ -333,7 +335,7 @@
         if r == 0:
             soon = [(far, 0) for far in range(1, planes)] + [(1, j) for j in blocks.singles[1:]]
         else:
-            soon = [(r + 1, j) for j in blocks.singles[: None if r == end - 1 else 1]]
+            soon = [(r + 1, j) for j in blocks.singles[0 if r == end - 1 else 1 :]]
         soon = [at for at in soon if at in blocks.pieces]
         place, *ready = lax.optimization_barrier((place, *[blocks.pieces[at] for at in soon]))
         blocks.pieces.update(zip(soon, ready))

time: 124 us -> 122 us (0.984); the launches traced: 123 us -> 120 us
  starting transfers between devices: 32.6 us -> 29.7 us
    ppermute x34, starting transfers between devices: 32.6 us -> 29.7 us  [permute(): return lax.ppermute(x, ('layer', 'feat'), sorted(flat))]
  transfers between devices with their start and end apart: 34 -> 34, of which waited for: 12 -> 13; matrix products, arithmetic and copies ran while one was open for 1% -> 1% of each run, Pallas kernels for 35% -> 36%
where the time goes in v10:
time: 122 us; the launch traced here: 120 us
  Pallas kernels  56.4 us (46%)
  starting transfers between devices  29.7 us (24%)
  waiting for transfers between devices  29 us (24%)
  local copies, waits for them, and re-layouts  2.92 us (2%)
    pallas_call x4, Pallas kernels, run_round(): pl.pallas_call(functools.partial(round_kernel, len(mine), len(tokens), la...  51.9 us
    ppermute x34, starting transfers between devices, permute(): return lax.ppermute(x, ('layer', 'feat'), sorted(flat))  29.7 us
    ppermute x34, waiting for transfers between devices, permute(): return lax.ppermute(x, ('layer', 'feat'), sorted(flat))  29 us
    pallas_call x1, Pallas kernels, prepare(): pl.pallas_call(prepare_kernel, grid=(layers,), in_specs=[block(rows, widt...  4.5 us
    unnamed x42, local copies, waits for them, and re-layouts  2.92 us
  transfers between devices with their start and end apart: 34, of which 13 were waited for; matrix products, arithmetic and copies ran while one was open for 1% of the time, Pallas kernels for 36%

profile of v10, /device:TPU:0, one launch (start us, length us, event | category | flops | bytes accessed | tf_op | source)
XLA Modules:
  0.0 120.1 jit_solution(5653355022519713257)
XLA Ops:
  0.6 0.7 collective-permute-start.1
  1.3 5.9 %collective-permute-start = (bf16[4,256,256]{2,1,0:T(8,128)(2,1)}, bf16[4,256,256]{2,1,0:T(8,128)(2,1)S(1)}, u32[]{:S(2)}, u32[]{:S(2)}) collective-permute-start(bf16[4,256,256]{2,1,0:T(8,128)(2,1)} %refs_0_.1), channel_id=1, source_target_pairs={{0,2},{1,3},{2,0},{3,1},{4,6},{5,7},{6,4},{7,5},{8,10},{9,11},{10,... | collective-permute-start | bytes 1572872 | tf_op jit(solution)/shard_map/ppermute | solution.py:61
  7.2 1.5 %collective-permute-start.8 = (bf16[4,256,256]{2,1,0:T(8,128)(2,1)}, bf16[4,256,256]{2,1,0:T(8,128)(2,1)S(1)}, u32[]{:S(2)}, u32[]{:S(2)}) collective-permute-start(bf16[4,256,256]{2,1,0:T(8,128)(2,1)} %refs_0_.1), channel_id=1, source_target_pairs={{0,16},{1,17},{2,18},{3,19},{4,20},{5,21},{6,22},{7,23},{8,24},{9,... | collective-permute-start | bytes 1572872 | tf_op jit(solution)/shard_map/ppermute | solution.py:61
  8.7 1.5 %collective-permute-start.7 = (bf16[4,256,256]{2,1,0:T(8,128)(2,1)}, bf16[4,256,256]{2,1,0:T(8,128)(2,1)}, u32[]{:S(2)}, u32[]{:S(2)}) collective-permute-start(bf16[4,256,256]{2,1,0:T(8,128)(2,1)} %refs_0_.1), channel_id=1, source_target_pairs={{0,8},{1,9},{2,10},{3,11},{4,12},{5,13},{6,14},{7,15},{8,0},{9,1},... | collective-permute-start | bytes 1572872 | tf_op jit(solution)/shard_map/ppermute | solution.py:61
  10.2 4.5 %shard_map.59 = (bf16[4,256,1024]{2,1,0:T(8,128)(2,1)}, bf16[4,1024,256]{2,1,0:T(8,128)(2,1)}) custom-call(bf16[4,1024,256]{2,1,0:T(8,128)(2,1)} %act.1, s32[4,2,1024]{2,1,0:T(2,128)} %bitcast.4), custom_call_target="tpu_custom_call" | custom-call | bytes 6291456 | tf_op jit(solution)/shard_map/pallas_call | solution.py:121
  14.7 1.3 %collective-permute-start.2 = (bf16[4,256,256]{2,1,0:T(8,128)(2,1)S(1)}, bf16[4,256,256]{2,1,0:T(8,128)(2,1)S(1)}, u32[]{:S(2)}, u32[]{:S(2)}) collective-permute-start(bf16[4,256,256]{2,1,0:T(8,128)(2,1)S(1)} %collective-permute-done.1), channel_id=1, source_target_pairs={{2,0},{3,1},{4,6},{5,7},{10,8},{11,9},{12,14},{13,15},{18,16},{19,... | collective-permute-start | bytes 1572872 | tf_op jit(solution)/shard_map/ppermute | solution.py:61
  16.0 3.0 %collective-permute-done.refs_1_ = bf16[4,256,256]{2,1,0:T(8,128)(2,1)S(1)} collective-permute-done((bf16[4,256,256]{2,1,0:T(8,128)(2,1)}, bf16[4,256,256]{2,1,0:T(8,128)(2,1)S(1)}, u32[]{:S(2)}, u32[]{:S(2)}) %collective-permute-start) | collective-permute-done | bytes 524320 | tf_op jit(solution)/shard_map/ppermute | solution.py:61
  19.1 0.7 collective-permute-start.3
  19.8 0.8 collective-permute-done.8.refs_2_
  20.5 1.5 %collective-permute-start.9 = (bf16[4,256,256]{2,1,0:T(8,128)(2,1)S(1)}, bf16[4,256,256]{2,1,0:T(8,128)(2,1)}, u32[]{:S(2)}, u32[]{:S(2)}) collective-permute-start(bf16[4,256,256]{2,1,0:T(8,128)(2,1)S(1)} %collective-permute-done.8.refs_2_), channel_id=1, source_target_pairs={{0,8},{1,9},{2,10},{3,11},{4,12},{5,13},{6,14},{7,15},{8,0},{9,1},... | collective-permute-start | bytes 1572872 | tf_op jit(solution)/shard_map/ppermute | solution.py:61
  22.0 1.5 %collective-permute-start.4 = (bf16[4,256,256]{2,1,0:T(8,128)(2,1)S(1)}, bf16[4,256,256]{2,1,0:T(8,128)(2,1)S(1)}, u32[]{:S(2)}, u32[]{:S(2)}) collective-permute-start(bf16[4,256,256]{2,1,0:T(8,128)(2,1)S(1)} %collective-permute-done.refs_1_), channel_id=1, source_target_pairs={{0,16},{1,17},{2,18},{3,19},{4,20},{5,21},{6,22},{7,23},{8,24},{9,... | collective-permute-start | bytes 1572872 | tf_op jit(solution)/shard_map/ppermute | solution.py:61
  23.5 8.3 %collective-permute-done.2 = bf16[4,256,256]{2,1,0:T(8,128)(2,1)S(1)} collective-permute-done((bf16[4,256,256]{2,1,0:T(8,128)(2,1)S(1)}, bf16[4,256,256]{2,1,0:T(8,128)(2,1)S(1)}, u32[]{:S(2)}, u32[]{:S(2)}) %collective-permute-start.2) | collective-permute-done | bytes 524320 | tf_op jit(solution)/shard_map/ppermute | solution.py:61
  31.8 0.5 collective-permute-start.11
  32.4 0.8 collective-permute-done.9.refs_3_
  33.1 0.7 pad_add_fusion.meta
  34.0 1.4 %collective-permute-start.16 = (bf16[4,256,256]{2,1,0:T(8,128)(2,1)S(1)}, bf16[4,256,256]{2,1,0:T(8,128)(2,1)}, u32[]{:S(2)}, u32[]{:S(2)}) collective-permute-start(bf16[4,256,256]{2,1,0:T(8,128)(2,1)S(1)} %collective-permute-done.refs_1_), channel_id=1, source_target_pairs={{0,8},{1,9},{2,10},{3,11},{4,12},{5,13},{6,14},{7,15},{8,0},{9,1},... | collective-permute-start | bytes 1572872 | tf_op jit(solution)/shard_map/ppermute | solution.py:61
  35.4 1.3 %collective-permute-start.5 = (bf16[4,256,256]{2,1,0:T(8,128)(2,1)S(1)}, bf16[4,256,256]{2,1,0:T(8,128)(2,1)}, u32[]{:S(2)}, u32[]{:S(2)}) collective-permute-start(bf16[4,256,256]{2,1,0:T(8,128)(2,1)S(1)} %broadcast_select_fusion.2.refs_1_), channel_id=1, source_target_pairs={{0,16},{1,17},{2,18},{3,19},{4,20},{5,21},{6,22},{7,23},{8,24},{9,... | collective-permute-start | bytes 1572872 | tf_op jit(solution)/shard_map/ppermute | solution.py:61
  36.8 0.8 collective-permute-start.17
  37.6 0.7 collective-permute-start.22
  38.3 1.3 %collective-permute-start.6 = (bf16[4,256,256]{2,1,0:T(8,128)(2,1)S(1)}, bf16[4,256,256]{2,1,0:T(8,128)(2,1)S(1)}, u32[]{:S(2)}, u32[]{:S(2)}) collective-permute-start(bf16[4,256,256]{2,1,0:T(8,128)(2,1)S(1)} %collective-permute-done.3), channel_id=1, source_target_pairs={{2,0},{3,1},{4,6},{5,7},{10,8},{11,9},{12,14},{13,15},{18,16},{19,... | collective-permute-start | bytes 1572872 | tf_op jit(solution)/shard_map/ppermute | solution.py:61
  39.6 13.3 %shard_map.60 = (bf16[10,256,2048]{2,1,0:T(8,128)(2,1)}, f32[4,1024,256]{2,1,0:T(8,128)}, f32[8,128]{1,0:T(8,128)}) custom-call(s32[3]{0:T(128)} %pad_add_fusion.meta, bf16[4,256,1024]{2,1,0:T(8,128)(2,1)} %get-tuple-element.56.sparse, bf16[10,256,2048]{2,1,0:T(8,128)(2,1)} %decoder.7, bf16[4,256,256]{2,1,0:T(8,128)(2,1)} %refs_0_.1, ...), custom_call_target="tpu_custom_call" | custom-call | flops 10737418240 | bytes 20971520 | tf_op jit(solution)/shard_map/pallas_call | solution.py:273
  52.9 6.8 %collective-permute-done.17.refs_4_ = bf16[4,256,256]{2,1,0:T(8,128)(2,1)} collective-permute-done((bf16[4,256,256]{2,1,0:T(8,128)(2,1)S(1)}, bf16[4,256,256]{2,1,0:T(8,128)(2,1)}, u32[]{:S(2)}, u32[]{:S(2)}) %collective-permute-start.17) | collective-permute-done | bytes 524320 | tf_op jit(solution)/shard_map/ppermute | solution.py:61
  59.6 0.5 collective-permute-start.20
  60.2 0.4 collective-permute-start.21
  60.7 1.5 %collective-permute-start.23 = (bf16[4,256,256]{2,1,0:T(8,128)(2,1)S(1)}, bf16[4,256,256]{2,1,0:T(8,128)(2,1)}, u32[]{:S(2)}, u32[]{:S(2)}) collective-permute-start(bf16[4,256,256]{2,1,0:T(8,128)(2,1)S(1)} %broadcast_select_fusion.2.refs_1_), channel_id=1, source_target_pairs={{0,8},{1,9},{2,10},{3,11},{4,12},{5,13},{6,14},{7,15},{8,0},{9,1},... | collective-permute-start | bytes 1572872 | tf_op jit(solution)/shard_map/ppermute | solution.py:61
  62.3 0.7 collective-permute-start.14
  63.0 1.3 %collective-permute-start.15 = (bf16[4,256,256]{2,1,0:T(8,128)(2,1)S(1)}, bf16[4,256,256]{2,1,0:T(8,128)(2,1)S(1)}, u32[]{:S(2)}, u32[]{:S(2)}) collective-permute-start(bf16[4,256,256]{2,1,0:T(8,128)(2,1)S(1)} %broadcast_select_fusion.1.refs_2_), channel_id=1, source_target_pairs={{0,16},{1,17},{2,18},{3,19},{4,20},{5,21},{6,22},{7,23},{8,24},{9,... | collective-permute-start | bytes 1572872 | tf_op jit(solution)/shard_map/ppermute | solution.py:61
  64.4 1.5 %collective-permute-start.24 = (bf16[4,256,256]{2,1,0:T(8,128)(2,1)S(1)}, bf16[4,256,256]{2,1,0:T(8,128)(2,1)S(1)}, u32[]{:S(2)}, u32[]{:S(2)}) collective-permute-start(bf16[4,256,256]{2,1,0:T(8,128)(2,1)S(1)} %collective-permute-done.22), channel_id=1, source_target_pairs={{2,0},{3,1},{4,6},{5,7},{10,8},{11,9},{12,14},{13,15},{18,16},{19,... | collective-permute-start | bytes 1572872 | tf_op jit(solution)/shard_map/ppermute | solution.py:61
  65.9 0.8 copy-done.12
  66.7 13.0 %shard_map.61 = (bf16[10,256,2048]{2,1,0:T(8,128)(2,1)}, f32[4,1024,256]{2,1,0:T(8,128)}, f32[8,128]{1,0:T(8,128)}) custom-call(s32[3]{0:T(128)} %pad_add_fusion.meta, bf16[4,256,1024]{2,1,0:T(8,128)(2,1)} %get-tuple-element.56.sparse, bf16[10,256,2048]{2,1,0:T(8,128)(2,1)} %decoder.7, ...), custom_call_target="tpu_custom_call", output_to_operand_aliasing={{0}: (12, {})} | custom-call | flops 10737418240 | bytes 20971520 | tf_op jit(solution)/shard_map/pallas_call | solution.py:273
  79.7 2.1 %collective-permute-done.24 = bf16[4,256,256]{2,1,0:T(8,128)(2,1)S(1)} collective-permute-done((bf16[4,256,256]{2,1,0:T(8,128)(2,1)S(1)}, bf16[4,256,256]{2,1,0:T(8,128)(2,1)S(1)}, u32[]{:S(2)}, u32[]{:S(2)}) %collective-permute-start.24) | collective-permute-done | bytes 524320 | tf_op jit(solution)/shard_map/ppermute | solution.py:61
  81.9 0.5 collective-permute-start.27
  82.5 3.5 %collective-permute-done.14.refs_3_ = bf16[4,256,256]{2,1,0:T(8,128)(2,1)S(1)} collective-permute-done((bf16[4,256,256]{2,1,0:T(8,128)(2,1)S(1)}, bf16[4,256,256]{2,1,0:T(8,128)(2,1)S(1)}, u32[]{:S(2)}, u32[]{:S(2)}) %collective-permute-start.14) | collective-permute-done | bytes 524320 | tf_op jit(solution)/shard_map/ppermute | solution.py:61
  86.0 1.4 %collective-permute-start.29 = (bf16[4,256,256]{2,1,0:T(8,128)(2,1)S(1)}, bf16[4,256,256]{2,1,0:T(8,128)(2,1)S(1)}, u32[]{:S(2)}, u32[]{:S(2)}) collective-permute-start(bf16[4,256,256]{2,1,0:T(8,128)(2,1)S(1)} %collective-permute-done.14.refs_3_), channel_id=1, source_target_pairs={{0,16},{1,17},{2,18},{3,19},{4,20},{5,21},{6,22},{7,23},{8,24},{9,... | collective-permute-start | bytes 1572872 | tf_op jit(solution)/shard_map/ppermute | solution.py:61
  87.4 0.5 collective-permute-done.25.refs_5_
  87.9 0.5 copy-done.14
  88.3 0.2 copy-done.15
  88.5 0.6 copy-done.18
  89.1 13.0 %shard_map.62 = (bf16[10,256,2048]{2,1,0:T(8,128)(2,1)}, f32[4,1024,256]{2,1,0:T(8,128)}, f32[8,128]{1,0:T(8,128)}) custom-call(s32[3]{0:T(128)} %pad_add_fusion.meta, bf16[4,256,1024]{2,1,0:T(8,128)(2,1)} %get-tuple-element.56.sparse, bf16[10,256,2048]{2,1,0:T(8,128)(2,1)} %decoder.7, ...), custom_call_target="tpu_custom_call", output_to_operand_aliasing={{0}: (12, {})} | custom-call | flops 10737418240 | bytes 20971520 | tf_op jit(solution)/shard_map/pallas_call | solution.py:273
  102.2 0.2 collective-permute-start.33
  102.4 0.3 collective-permute-start.32
  102.9 0.3 collective-permute-start.30
  103.3 0.9 collective-permute-done.33.refs_9_
  104.1 0.7 collective-permute-done.32.refs_8_
  104.9 0.7 collective-permute-done.31.refs_7_
  105.6 0.7 collective-permute-done.30.refs_6_
  106.4 0.8 copy-done.20
  107.2 12.7 %shard_map.63 = (bf16[10,256,2048]{2,1,0:T(8,128)(2,1)}, bf16[4,1024,256]{2,1,0:T(8,128)(2,1)}, f32[8,128]{1,0:T(8,128)}) custom-call(s32[3]{0:T(128)} %pad_add_fusion.meta, bf16[4,256,1024]{2,1,0:T(8,128)(2,1)} %get-tuple-element.56.sparse, bf16[10,256,2048]{2,1,0:T(8,128)(2,1)} %decoder.7, ...), custom_call_target="tpu_custom_call", output_to_operand_aliasing={{0}: (13, {})} | custom-call | flops 10737418240 | bytes 20971520 | tf_op jit(solution)/shard_map/pallas_call | solution.py:273
  (71 shorter events, 0.9 us)
Async XLA Ops:
  0.6 14.1 %collective-permute-start.1 = (bf16[4,256,256]{2,1,0:T(8,128)(2,1)}, bf16[4,256,256]{2,1,0:T(8,128)(2,1)S(1)}, u32[]{:S(2)}, u32[]{:S(2)}) collective-permute-start(bf16[4,256,256]{2,1,0:T(8,128)(2,1)} %refs_0_.1), channel_id=1, source_target_pairs={{2,4},{3,5},{4,2},{5,3},{10,12},{11,13},{12,10},{13,11},{18,20},{1... | collective-permute-start | bytes 1572872 | tf_op jit(solution)/shard_map/ppermute | solution.py:61
  1.3 17.7 %collective-permute-start = (bf16[4,256,256]{2,1,0:T(8,128)(2,1)}, bf16[4,256,256]{2,1,0:T(8,128)(2,1)S(1)}, u32[]{:S(2)}, u32[]{:S(2)}) collective-permute-start(bf16[4,256,256]{2,1,0:T(8,128)(2,1)} %refs_0_.1), channel_id=1, source_target_pairs={{0,2},{1,3},{2,0},{3,1},{4,6},{5,7},{6,4},{7,5},{8,10},{9,11},{10,... | collective-permute-start | bytes 1572872 | tf_op jit(solution)/shard_map/ppermute | solution.py:61
  7.2 13.3 %collective-permute-start.8 = (bf16[4,256,256]{2,1,0:T(8,128)(2,1)}, bf16[4,256,256]{2,1,0:T(8,128)(2,1)S(1)}, u32[]{:S(2)}, u32[]{:S(2)}) collective-permute-start(bf16[4,256,256]{2,1,0:T(8,128)(2,1)} %refs_0_.1), channel_id=1, source_target_pairs={{0,16},{1,17},{2,18},{3,19},{4,20},{5,21},{6,22},{7,23},{8,24},{9,... | collective-permute-start | bytes 1572872 | tf_op jit(solution)/shard_map/ppermute | solution.py:61
  8.7 14.8 %collective-permute-start.7 = (bf16[4,256,256]{2,1,0:T(8,128)(2,1)}, bf16[4,256,256]{2,1,0:T(8,128)(2,1)}, u32[]{:S(2)}, u32[]{:S(2)}) collective-permute-start(bf16[4,256,256]{2,1,0:T(8,128)(2,1)} %refs_0_.1), channel_id=1, source_target_pairs={{0,8},{1,9},{2,10},{3,11},{4,12},{5,13},{6,14},{7,15},{8,0},{9,1},... | collective-permute-start | bytes 1572872 | tf_op jit(solution)/shard_map/ppermute | solution.py:61
  14.7 17.1 %collective-permute-start.2 = (bf16[4,256,256]{2,1,0:T(8,128)(2,1)S(1)}, bf16[4,256,256]{2,1,0:T(8,128)(2,1)S(1)}, u32[]{:S(2)}, u32[]{:S(2)}) collective-permute-start(bf16[4,256,256]{2,1,0:T(8,128)(2,1)S(1)} %collective-permute-done.1), channel_id=1, source_target_pairs={{2,0},{3,1},{4,6},{5,7},{10,8},{11,9},{12,14},{13,15},{18,16},{19,... | collective-permute-start | bytes 1572872 | tf_op jit(solution)/shard_map/ppermute | solution.py:61
  19.1 40.6 %copy-start.3 = (bf16[4,256,256]{2,1,0:T(8,128)(2,1)}, bf16[4,256,256]{2,1,0:T(8,128)(2,1)S(1)}, u32[]{:S(2)}) copy-start(bf16[4,256,256]{2,1,0:T(8,128)(2,1)S(1)} %collective-permute-done.refs_1_) | copy-start | bytes 1572868
  19.1 12.8 %collective-permute-start.3 = (bf16[4,256,256]{2,1,0:T(8,128)(2,1)S(1)}, bf16[4,256,256]{2,1,0:T(8,128)(2,1)S(1)}, u32[]{:S(2)}, u32[]{:S(2)}) collective-permute-start(bf16[4,256,256]{2,1,0:T(8,128)(2,1)S(1)} %collective-permute-done.refs_1_), channel_id=1, source_target_pairs={{2,4},{3,5},{4,2},{5,3},{10,12},{11,13},{12,10},{13,11},{18,20},{1... | collective-permute-start | bytes 1572872 | tf_op jit(solution)/shard_map/ppermute | solution.py:61
  20.5 17.7 %copy-start.5 = (bf16[4,256,256]{2,1,0:T(8,128)(2,1)}, bf16[4,256,256]{2,1,0:T(8,128)(2,1)S(1)}, u32[]{:S(2)}) copy-start(bf16[4,256,256]{2,1,0:T(8,128)(2,1)S(1)} %collective-permute-done.8.refs_2_) | copy-start | bytes 1572868
  20.5 12.6 %collective-permute-start.9 = (bf16[4,256,256]{2,1,0:T(8,128)(2,1)S(1)}, bf16[4,256,256]{2,1,0:T(8,128)(2,1)}, u32[]{:S(2)}, u32[]{:S(2)}) collective-permute-start(bf16[4,256,256]{2,1,0:T(8,128)(2,1)S(1)} %collective-permute-done.8.refs_2_), channel_id=1, source_target_pairs={{0,8},{1,9},{2,10},{3,11},{4,12},{5,13},{6,14},{7,15},{8,0},{9,1},... | collective-permute-start | bytes 1572872 | tf_op jit(solution)/shard_map/ppermute | solution.py:61
  22.0 12.0 %collective-permute-start.4 = (bf16[4,256,256]{2,1,0:T(8,128)(2,1)S(1)}, bf16[4,256,256]{2,1,0:T(8,128)(2,1)S(1)}, u32[]{:S(2)}, u32[]{:S(2)}) collective-permute-start(bf16[4,256,256]{2,1,0:T(8,128)(2,1)S(1)} %collective-permute-done.refs_1_), channel_id=1, source_target_pairs={{0,16},{1,17},{2,18},{3,19},{4,20},{5,21},{6,22},{7,23},{8,24},{9,... | collective-permute-start | bytes 1572872 | tf_op jit(solution)/shard_map/ppermute | solution.py:61
  23.5 11.9 %collective-permute-start.10 = (bf16[4,256,256]{2,1,0:T(8,128)(2,1)}, bf16[4,256,256]{2,1,0:T(8,128)(2,1)}, u32[]{:S(2)}, u32[]{:S(2)}) collective-permute-start(bf16[4,256,256]{2,1,0:T(8,128)(2,1)} %refs_0_.1), channel_id=1, source_target_pairs={{0,1},{1,0},{2,3},{3,2},{4,5},{5,4},{6,7},{7,6},{8,9},{9,8},{10,11... | collective-permute-start | bytes 1572872 | tf_op jit(solution)/shard_map/ppermute | solution.py:61
  31.8 4.9 %collective-permute-start.12 = (bf16[4,256,256]{2,1,0:T(8,128)(2,1)S(1)}, bf16[4,256,256]{2,1,0:T(8,128)(2,1)}, u32[]{:S(2)}, u32[]{:S(2)}) collective-permute-start(bf16[4,256,256]{2,1,0:T(8,128)(2,1)S(1)} %collective-permute-done.8.refs_2_), channel_id=1, source_target_pairs={{0,1},{1,0},{2,3},{3,2},{4,5},{5,4},{6,7},{7,6},{8,9},{9,8},{10,11... | collective-permute-start | bytes 1572872 | tf_op jit(solution)/shard_map/ppermute | solution.py:61
  31.8 5.7 %collective-permute-start.11 = (bf16[4,256,256]{2,1,0:T(8,128)(2,1)}, bf16[4,256,256]{2,1,0:T(8,128)(2,1)}, u32[]{:S(2)}, u32[]{:S(2)}) collective-permute-start(bf16[4,256,256]{2,1,0:T(8,128)(2,1)} %collective-permute-done.7.refs_1_), channel_id=1, source_target_pairs={{0,1},{1,0},{2,3},{3,2},{4,5},{5,4},{6,7},{7,6},{8,9},{9,8},{10,11... | collective-permute-start | bytes 1572872 | tf_op jit(solution)/shard_map/ppermute | solution.py:61
  33.1 5.2 %collective-permute-start.13 = (bf16[4,256,256]{2,1,0:T(8,128)(2,1)}, bf16[4,256,256]{2,1,0:T(8,128)(2,1)}, u32[]{:S(2)}, u32[]{:S(2)}) collective-permute-start(bf16[4,256,256]{2,1,0:T(8,128)(2,1)} %collective-permute-done.9.refs_3_), channel_id=1, source_target_pairs={{0,1},{1,0},{2,3},{3,2},{4,5},{5,4},{6,7},{7,6},{8,9},{9,8},{10,11... | collective-permute-start | bytes 1572872 | tf_op jit(solution)/shard_map/ppermute | solution.py:61
  33.8 52.1 %copy-start = (bf16[4,256,256]{2,1,0:T(8,128)(2,1)}, bf16[4,256,256]{2,1,0:T(8,128)(2,1)S(1)}, u32[]{:S(2)}) copy-start(bf16[4,256,256]{2,1,0:T(8,128)(2,1)S(1)} %broadcast_select_fusion.2.refs_1_) | copy-start | bytes 1572868
  34.0 25.6 %copy-start.4 = (bf16[4,256,256]{2,1,0:T(8,128)(2,1)}, bf16[4,256,256]{2,1,0:T(8,128)(2,1)S(1)}, u32[]{:S(2)}) copy-start(bf16[4,256,256]{2,1,0:T(8,128)(2,1)S(1)} %collective-permute-done.4.refs_3_) | copy-start | bytes 1572868
  34.0 25.6 %collective-permute-start.16 = (bf16[4,256,256]{2,1,0:T(8,128)(2,1)S(1)}, bf16[4,256,256]{2,1,0:T(8,128)(2,1)}, u32[]{:S(2)}, u32[]{:S(2)}) collective-permute-start(bf16[4,256,256]{2,1,0:T(8,128)(2,1)S(1)} %collective-permute-done.refs_1_), channel_id=1, source_target_pairs={{0,8},{1,9},{2,10},{3,11},{4,12},{5,13},{6,14},{7,15},{8,0},{9,1},... | collective-permute-start | bytes 1572872 | tf_op jit(solution)/shard_map/ppermute | solution.py:61
  35.4 25.3 %collective-permute-start.5 = (bf16[4,256,256]{2,1,0:T(8,128)(2,1)S(1)}, bf16[4,256,256]{2,1,0:T(8,128)(2,1)}, u32[]{:S(2)}, u32[]{:S(2)}) collective-permute-start(bf16[4,256,256]{2,1,0:T(8,128)(2,1)S(1)} %broadcast_select_fusion.2.refs_1_), channel_id=1, source_target_pairs={{0,16},{1,17},{2,18},{3,19},{4,20},{5,21},{6,22},{7,23},{8,24},{9,... | collective-permute-start | bytes 1572872 | tf_op jit(solution)/shard_map/ppermute | solution.py:61
  36.8 22.9 %collective-permute-start.17 = (bf16[4,256,256]{2,1,0:T(8,128)(2,1)S(1)}, bf16[4,256,256]{2,1,0:T(8,128)(2,1)}, u32[]{:S(2)}, u32[]{:S(2)}) collective-permute-start(bf16[4,256,256]{2,1,0:T(8,128)(2,1)S(1)} %collective-permute-done.4.refs_3_), channel_id=1, source_target_pairs={{0,8},{1,9},{2,10},{3,11},{4,12},{5,13},{6,14},{7,15},{8,0},{9,1},... | collective-permute-start | bytes 1572872 | tf_op jit(solution)/shard_map/ppermute | solution.py:61
  37.6 22.6 %collective-permute-start.22 = (bf16[4,256,256]{2,1,0:T(8,128)(2,1)}, bf16[4,256,256]{2,1,0:T(8,128)(2,1)S(1)}, u32[]{:S(2)}, u32[]{:S(2)}) collective-permute-start(bf16[4,256,256]{2,1,0:T(8,128)(2,1)} %collective-permute-done.9.refs_3_), channel_id=1, source_target_pairs={{2,4},{3,5},{4,2},{5,3},{10,12},{11,13},{12,10},{13,11},{18,20},{1... | collective-permute-start | bytes 1572872 | tf_op jit(solution)/shard_map/ppermute | solution.py:61
  38.3 21.9 %collective-permute-start.6 = (bf16[4,256,256]{2,1,0:T(8,128)(2,1)S(1)}, bf16[4,256,256]{2,1,0:T(8,128)(2,1)S(1)}, u32[]{:S(2)}, u32[]{:S(2)}) collective-permute-start(bf16[4,256,256]{2,1,0:T(8,128)(2,1)S(1)} %collective-permute-done.3), channel_id=1, source_target_pairs={{2,0},{3,1},{4,6},{5,7},{10,8},{11,9},{12,14},{13,15},{18,16},{19,... | collective-permute-start | bytes 1572872 | tf_op jit(solution)/shard_map/ppermute | solution.py:61
  59.6 2.6 %collective-permute-start.18 = (bf16[4,256,256]{2,1,0:T(8,128)(2,1)S(1)}, bf16[4,256,256]{2,1,0:T(8,128)(2,1)S(1)}, u32[]{:S(2)}, u32[]{:S(2)}) collective-permute-start(bf16[4,256,256]{2,1,0:T(8,128)(2,1)S(1)} %collective-permute-done.refs_1_), channel_id=1, source_target_pairs={{0,1},{1,0},{2,3},{3,2},{4,5},{5,4},{6,7},{7,6},{8,9},{9,8},{10,11... | collective-permute-start | bytes 1572872 | tf_op jit(solution)/shard_map/ppermute | solution.py:61
  59.6 3.4 %collective-permute-start.20 = (bf16[4,256,256]{2,1,0:T(8,128)(2,1)S(1)}, bf16[4,256,256]{2,1,0:T(8,128)(2,1)S(1)}, u32[]{:S(2)}, u32[]{:S(2)}) collective-permute-start(bf16[4,256,256]{2,1,0:T(8,128)(2,1)S(1)} %collective-permute-done.4.refs_3_), channel_id=1, source_target_pairs={{0,1},{1,0},{2,3},{3,2},{4,5},{5,4},{6,7},{7,6},{8,9},{9,8},{10,11... | collective-permute-start | bytes 1572872 | tf_op jit(solution)/shard_map/ppermute | solution.py:61
  60.1 4.2 %collective-permute-start.19 = (bf16[4,256,256]{2,1,0:T(8,128)(2,1)}, bf16[4,256,256]{2,1,0:T(8,128)(2,1)S(1)}, u32[]{:S(2)}, u32[]{:S(2)}) collective-permute-start(bf16[4,256,256]{2,1,0:T(8,128)(2,1)} %collective-permute-done.16.refs_2_), channel_id=1, source_target_pairs={{0,1},{1,0},{2,3},{3,2},{4,5},{5,4},{6,7},{7,6},{8,9},{9,8},{10,11... | collective-permute-start | bytes 1572872 | tf_op jit(solution)/shard_map/ppermute | solution.py:61
  60.2 5.6 %collective-permute-start.21 = (bf16[4,256,256]{2,1,0:T(8,128)(2,1)}, bf16[4,256,256]{2,1,0:T(8,128)(2,1)S(1)}, u32[]{:S(2)}, u32[]{:S(2)}) collective-permute-start(bf16[4,256,256]{2,1,0:T(8,128)(2,1)} %collective-permute-done.17.refs_4_), channel_id=1, source_target_pairs={{0,1},{1,0},{2,3},{3,2},{4,5},{5,4},{6,7},{7,6},{8,9},{9,8},{10,11... | collective-permute-start | bytes 1572872 | tf_op jit(solution)/shard_map/ppermute | solution.py:61
  60.7 42.2 %copy-start.1 = (bf16[4,256,256]{2,1,0:T(8,128)(2,1)}, bf16[4,256,256]{2,1,0:T(8,128)(2,1)S(1)}, u32[]{:S(2)}) copy-start(bf16[4,256,256]{2,1,0:T(8,128)(2,1)S(1)} %broadcast_select_fusion.1.refs_2_) | copy-start | bytes 1572868
  60.7 21.6 %collective-permute-start.23 = (bf16[4,256,256]{2,1,0:T(8,128)(2,1)S(1)}, bf16[4,256,256]{2,1,0:T(8,128)(2,1)}, u32[]{:S(2)}, u32[]{:S(2)}) collective-permute-start(bf16[4,256,256]{2,1,0:T(8,128)(2,1)S(1)} %broadcast_select_fusion.2.refs_1_), channel_id=1, source_target_pairs={{0,8},{1,9},{2,10},{3,11},{4,12},{5,13},{6,14},{7,15},{8,0},{9,1},... | collective-permute-start | bytes 1572872 | tf_op jit(solution)/shard_map/ppermute | solution.py:61
  62.3 2.1 %copy-start.9 = (bf16[4,256,256]{2,1,0:T(8,128)(2,1)}, bf16[4,256,256]{2,1,0:T(8,128)(2,1)S(1)}, u32[]{:S(2)}) copy-start(bf16[4,256,256]{2,1,0:T(8,128)(2,1)S(1)} %collective-permute-done.18.refs_5_) | copy-start | bytes 1572868
  62.3 23.7 %collective-permute-start.14 = (bf16[4,256,256]{2,1,0:T(8,128)(2,1)S(1)}, bf16[4,256,256]{2,1,0:T(8,128)(2,1)S(1)}, u32[]{:S(2)}, u32[]{:S(2)}) collective-permute-start(bf16[4,256,256]{2,1,0:T(8,128)(2,1)S(1)} %broadcast_select_fusion.1.refs_2_), channel_id=1, source_target_pairs={{0,8},{1,9},{2,10},{3,11},{4,12},{5,13},{6,14},{7,15},{8,0},{9,1},... | collective-permute-start | bytes 1572872 | tf_op jit(solution)/shard_map/ppermute | solution.py:61
  63.0 22.9 %collective-permute-start.15 = (bf16[4,256,256]{2,1,0:T(8,128)(2,1)S(1)}, bf16[4,256,256]{2,1,0:T(8,128)(2,1)S(1)}, u32[]{:S(2)}, u32[]{:S(2)}) collective-permute-start(bf16[4,256,256]{2,1,0:T(8,128)(2,1)S(1)} %broadcast_select_fusion.1.refs_2_), channel_id=1, source_target_pairs={{0,16},{1,17},{2,18},{3,19},{4,20},{5,21},{6,22},{7,23},{8,24},{9,... | collective-permute-start | bytes 1572872 | tf_op jit(solution)/shard_map/ppermute | solution.py:61
  64.4 17.4 %collective-permute-start.24 = (bf16[4,256,256]{2,1,0:T(8,128)(2,1)S(1)}, bf16[4,256,256]{2,1,0:T(8,128)(2,1)S(1)}, u32[]{:S(2)}, u32[]{:S(2)}) collective-permute-start(bf16[4,256,256]{2,1,0:T(8,128)(2,1)S(1)} %collective-permute-done.22), channel_id=1, source_target_pairs={{2,0},{3,1},{4,6},{5,7},{10,8},{11,9},{12,14},{13,15},{18,16},{19,... | collective-permute-start | bytes 1572872 | tf_op jit(solution)/shard_map/ppermute | solution.py:61
  81.8 7.3 %copy-start.2 = (bf16[4,256,256]{2,1,0:T(8,128)(2,1)}, bf16[4,256,256]{2,1,0:T(8,128)(2,1)S(1)}, u32[]{:S(2)}) copy-start(bf16[4,256,256]{2,1,0:T(8,128)(2,1)S(1)} %broadcast_select_fusion.refs_4_) | copy-start | bytes 1572868
  81.8 5.5 %collective-permute-start.28 = (bf16[4,256,256]{2,1,0:T(8,128)(2,1)S(1)}, bf16[4,256,256]{2,1,0:T(8,128)(2,1)S(1)}, u32[]{:S(2)}, u32[]{:S(2)}) collective-permute-start(bf16[4,256,256]{2,1,0:T(8,128)(2,1)S(1)} %broadcast_select_fusion.refs_4_), channel_id=1, source_target_pairs={{0,1},{1,0},{2,3},{3,2},{4,5},{5,4},{6,7},{7,6},{8,9},{9,8},{10,11... | collective-permute-start | bytes 1572872 | tf_op jit(solution)/shard_map/ppermute | solution.py:61
  81.9 5.5 %collective-permute-start.27 = (bf16[4,256,256]{2,1,0:T(8,128)(2,1)}, bf16[4,256,256]{2,1,0:T(8,128)(2,1)S(1)}, u32[]{:S(2)}, u32[]{:S(2)}) collective-permute-start(bf16[4,256,256]{2,1,0:T(8,128)(2,1)} %collective-permute-done.5.refs_3_), channel_id=1, source_target_pairs={{0,1},{1,0},{2,3},{3,2},{4,5},{5,4},{6,7},{7,6},{8,9},{9,8},{10,11... | collective-permute-start | bytes 1572872 | tf_op jit(solution)/shard_map/ppermute | solution.py:61
  82.4 5.0 %collective-permute-start.26 = (bf16[4,256,256]{2,1,0:T(8,128)(2,1)}, bf16[4,256,256]{2,1,0:T(8,128)(2,1)S(1)}, u32[]{:S(2)}, u32[]{:S(2)}) collective-permute-start(bf16[4,256,256]{2,1,0:T(8,128)(2,1)} %collective-permute-done.23.refs_2_), channel_id=1, source_target_pairs={{0,1},{1,0},{2,3},{3,2},{4,5},{5,4},{6,7},{7,6},{8,9},{9,8},{10,11... | collective-permute-start | bytes 1572872 | tf_op jit(solution)/shard_map/ppermute | solution.py:61
  86.0 16.8 %copy-start.6 = (bf16[4,256,256]{2,1,0:T(8,128)(2,1)}, bf16[4,256,256]{2,1,0:T(8,128)(2,1)S(1)}, u32[]{:S(2)}) copy-start(bf16[4,256,256]{2,1,0:T(8,128)(2,1)S(1)} %collective-permute-done.14.refs_3_) | copy-start | bytes 1572868
  86.0 1.9 %collective-permute-start.25 = (bf16[4,256,256]{2,1,0:T(8,128)(2,1)S(1)}, bf16[4,256,256]{2,1,0:T(8,128)(2,1)S(1)}, u32[]{:S(2)}, u32[]{:S(2)}) collective-permute-start(bf16[4,256,256]{2,1,0:T(8,128)(2,1)S(1)} %broadcast_select_fusion.2.refs_1_), channel_id=1, source_target_pairs={{0,1},{1,0},{2,3},{3,2},{4,5},{5,4},{6,7},{7,6},{8,9},{9,8},{10,11... | collective-permute-start | bytes 1572872 | tf_op jit(solution)/shard_map/ppermute | solution.py:61
  86.0 16.4 %copy-start.7 = (bf16[4,256,256]{2,1,0:T(8,128)(2,1)}, bf16[4,256,256]{2,1,0:T(8,128)(2,1)S(1)}, u32[]{:S(2)}) copy-start(bf16[4,256,256]{2,1,0:T(8,128)(2,1)S(1)} %collective-permute-done.15.refs_4_) | copy-start | bytes 1572868
  86.0 16.2 %collective-permute-start.29 = (bf16[4,256,256]{2,1,0:T(8,128)(2,1)S(1)}, bf16[4,256,256]{2,1,0:T(8,128)(2,1)S(1)}, u32[]{:S(2)}, u32[]{:S(2)}) collective-permute-start(bf16[4,256,256]{2,1,0:T(8,128)(2,1)S(1)} %collective-permute-done.14.refs_3_), channel_id=1, source_target_pairs={{0,16},{1,17},{2,18},{3,19},{4,20},{5,21},{6,22},{7,23},{8,24},{9,... | collective-permute-start | bytes 1572872 | tf_op jit(solution)/shard_map/ppermute | solution.py:61
  87.4 1.8 %copy-start.13 = (bf16[4,256,256]{2,1,0:T(8,128)(2,1)}, bf16[4,256,256]{2,1,0:T(8,128)(2,1)S(1)}, u32[]{:S(2)}) copy-start(bf16[4,256,256]{2,1,0:T(8,128)(2,1)S(1)} %collective-permute-done.28.refs_8_) | copy-start | bytes 1572868
  102.2 5.0 %copy-start.8 = (bf16[4,256,256]{2,1,0:T(8,128)(2,1)}, bf16[4,256,256]{2,1,0:T(8,128)(2,1)S(1)}, u32[]{:S(2)}) copy-start(bf16[4,256,256]{2,1,0:T(8,128)(2,1)S(1)} %collective-permute-done.29.refs_5_) | copy-start | bytes 1572868
  102.2 2.0 %collective-permute-start.33 = (bf16[4,256,256]{2,1,0:T(8,128)(2,1)S(1)}, bf16[4,256,256]{2,1,0:T(8,128)(2,1)S(1)}, u32[]{:S(2)}, u32[]{:S(2)}) collective-permute-start(bf16[4,256,256]{2,1,0:T(8,128)(2,1)S(1)} %collective-permute-done.29.refs_5_), channel_id=1, source_target_pairs={{0,1},{1,0},{2,3},{3,2},{4,5},{5,4},{6,7},{7,6},{8,9},{9,8},{10,11... | collective-permute-start | bytes 1572872 | tf_op jit(solution)/shard_map/ppermute | solution.py:61
  102.4 2.5 %collective-permute-start.32 = (bf16[4,256,256]{2,1,0:T(8,128)(2,1)S(1)}, bf16[4,256,256]{2,1,0:T(8,128)(2,1)S(1)}, u32[]{:S(2)}, u32[]{:S(2)}) collective-permute-start(bf16[4,256,256]{2,1,0:T(8,128)(2,1)S(1)} %collective-permute-done.15.refs_4_), channel_id=1, source_target_pairs={{0,1},{1,0},{2,3},{3,2},{4,5},{5,4},{6,7},{7,6},{8,9},{9,8},{10,11... | collective-permute-start | bytes 1572872 | tf_op jit(solution)/shard_map/ppermute | solution.py:61
  102.7 2.9 %collective-permute-start.31 = (bf16[4,256,256]{2,1,0:T(8,128)(2,1)S(1)}, bf16[4,256,256]{2,1,0:T(8,128)(2,1)S(1)}, u32[]{:S(2)}, u32[]{:S(2)}) collective-permute-start(bf16[4,256,256]{2,1,0:T(8,128)(2,1)S(1)} %collective-permute-done.14.refs_3_), channel_id=1, source_target_pairs={{0,1},{1,0},{2,3},{3,2},{4,5},{5,4},{6,7},{7,6},{8,9},{9,8},{10,11... | collective-permute-start | bytes 1572872 | tf_op jit(solution)/shard_map/ppermute | solution.py:61
  102.9 3.5 %collective-permute-start.30 = (bf16[4,256,256]{2,1,0:T(8,128)(2,1)S(1)}, bf16[4,256,256]{2,1,0:T(8,128)(2,1)S(1)}, u32[]{:S(2)}, u32[]{:S(2)}) collective-permute-start(bf16[4,256,256]{2,1,0:T(8,128)(2,1)S(1)} %broadcast_select_fusion.1.refs_2_), channel_id=1, source_target_pairs={{0,1},{1,0},{2,3},{3,2},{4,5},{5,4},{6,7},{7,6},{8,9},{9,8},{10,11... | collective-permute-start | bytes 1572872 | tf_op jit(solution)/shard_map/ppermute | solution.py:61
  104.1 3.1 %copy-start.16 = (bf16[4,256,256]{2,1,0:T(8,128)(2,1)}, bf16[4,256,256]{2,1,0:T(8,128)(2,1)S(1)}, u32[]{:S(2)}) copy-start(bf16[4,256,256]{2,1,0:T(8,128)(2,1)S(1)} %collective-permute-done.33.refs_9_) | copy-start | bytes 1572868
  104.9 2.3 %copy-start.17 = (bf16[4,256,256]{2,1,0:T(8,128)(2,1)}, bf16[4,256,256]{2,1,0:T(8,128)(2,1)S(1)}, u32[]{:S(2)}) copy-start(bf16[4,256,256]{2,1,0:T(8,128)(2,1)S(1)} %collective-permute-done.32.refs_8_) | copy-start | bytes 1572868
  105.6 1.6 %copy-start.19 = (bf16[4,256,256]{2,1,0:T(8,128)(2,1)}, bf16[4,256,256]{2,1,0:T(8,128)(2,1)S(1)}, u32[]{:S(2)}) copy-start(bf16[4,256,256]{2,1,0:T(8,128)(2,1)S(1)} %collective-permute-done.31.refs_7_) | copy-start | bytes 1572868
  (7 other events, 7.3 us)

commit v11 on v10

--- a/solution.py
+++ b/solution.py
@@ -328,10 +328,13 @@
         if r == max(end - 1, 0) and end > 0:
             blocks.diagonal(end)
         mine = [blocks.piece(r, j) for j in range(n_layer)]
-        theirs = [
-            blocks.swap(blocks.tie(x) if r > 1 or j in blocks.others else x)
-            for j, x in enumerate(mine)
-        ]
+        if r == 1 and end > 2:
+            held = [(1, j) for j in blocks.others] + [(end, 0)]
+            ready = lax.optimization_barrier([blocks.piece(*at) for at in held])
+            blocks.pieces.update(zip(held, ready))
+            mine = [blocks.piece(r, j) for j in range(n_layer)]
+        free = [0] + blocks.singles if r in (0, 1, end) else []
+        theirs = [blocks.swap(x if j in free else blocks.tie(x)) for j, x in enumerate(mine)]
         if r == 0:
             soon = [(far, 0) for far in range(1, planes)] + [(1, j) for j in blocks.singles[1:]]
         else:

time: 122 us -> 119 us (0.975)
  waiting for transfers between devices: 29 us -> 27.2 us
    ppermute x34, waiting for transfers between devices: 29 us -> 27.2 us  [permute(): return lax.ppermute(x, ('layer', 'feat'), sorted(flat))]
    unnamed x42 -> x30, local copies, waits for them, and re-layouts: 2.92 us -> 1.92 us
  transfers between devices with their start and end apart: 34 -> 34, of which waited for: 13 -> 10; matrix products, arithmetic and copies ran while one was open for 1% -> 1% of each run, Pallas kernels for 36% -> 37%
where the time goes in v11:
time: 119 us; the launch traced here: 118 us
  Pallas kernels  56.6 us (48%)
  starting transfers between devices  30 us (25%)
  waiting for transfers between devices  27.2 us (23%)
  local copies, waits for them, and re-layouts  1.92 us (2%)
    pallas_call x4, Pallas kernels, run_round(): pl.pallas_call(functools.partial(round_kernel, len(mine), len(tokens), la...  52.1 us
    ppermute x34, starting transfers between devices, permute(): return lax.ppermute(x, ('layer', 'feat'), sorted(flat))  30 us
    ppermute x34, waiting for transfers between devices, permute(): return lax.ppermute(x, ('layer', 'feat'), sorted(flat))  27.2 us
    pallas_call x1, Pallas kernels, prepare(): pl.pallas_call(prepare_kernel, grid=(layers,), in_specs=[block(rows, widt...  4.55 us
  transfers between devices with their start and end apart: 34, of which 10 were waited for; matrix products, arithmetic and copies ran while one was open for 1% of the time, Pallas kernels for 37%

profile of v11, /device:TPU:0, one launch (start us, length us, event | category | flops | bytes accessed | tf_op | source)
XLA Modules:
  0.0 117.7 jit_solution(4621129795478606413)
XLA Ops:
  0.6 0.7 collective-permute-start.1
  1.3 5.9 %collective-permute-start = (bf16[4,256,256]{2,1,0:T(8,128)(2,1)}, bf16[4,256,256]{2,1,0:T(8,128)(2,1)S(1)}, u32[]{:S(2)}, u32[]{:S(2)}) collective-permute-start(bf16[4,256,256]{2,1,0:T(8,128)(2,1)} %refs_0_.1), channel_id=1, source_target_pairs={{0,2},{1,3},{2,0},{3,1},{4,6},{5,7},{6,4},{7,5},{8,10},{9,11},{10,... | collective-permute-start | bytes 1572872 | tf_op jit(solution)/shard_map/ppermute | solution.py:61
  7.2 1.5 %collective-permute-start.8 = (bf16[4,256,256]{2,1,0:T(8,128)(2,1)}, bf16[4,256,256]{2,1,0:T(8,128)(2,1)}, u32[]{:S(2)}, u32[]{:S(2)}) collective-permute-start(bf16[4,256,256]{2,1,0:T(8,128)(2,1)} %refs_0_.1), channel_id=1, source_target_pairs={{0,16},{1,17},{2,18},{3,19},{4,20},{5,21},{6,22},{7,23},{8,24},{9,... | collective-permute-start | bytes 1572872 | tf_op jit(solution)/shard_map/ppermute | solution.py:61
  8.7 1.5 %collective-permute-start.7 = (bf16[4,256,256]{2,1,0:T(8,128)(2,1)}, bf16[4,256,256]{2,1,0:T(8,128)(2,1)}, u32[]{:S(2)}, u32[]{:S(2)}) collective-permute-start(bf16[4,256,256]{2,1,0:T(8,128)(2,1)} %refs_0_.1), channel_id=1, source_target_pairs={{0,8},{1,9},{2,10},{3,11},{4,12},{5,13},{6,14},{7,15},{8,0},{9,1},... | collective-permute-start | bytes 1572872 | tf_op jit(solution)/shard_map/ppermute | solution.py:61
  10.2 4.5 %shard_map.59 = (bf16[4,256,1024]{2,1,0:T(8,128)(2,1)}, bf16[4,1024,256]{2,1,0:T(8,128)(2,1)}) custom-call(bf16[4,1024,256]{2,1,0:T(8,128)(2,1)} %act.1, s32[4,2,1024]{2,1,0:T(2,128)} %bitcast.4), custom_call_target="tpu_custom_call" | custom-call | bytes 6291456 | tf_op jit(solution)/shard_map/pallas_call | solution.py:121
  14.8 1.3 %collective-permute-start.2 = (bf16[4,256,256]{2,1,0:T(8,128)(2,1)S(1)}, bf16[4,256,256]{2,1,0:T(8,128)(2,1)S(1)}, u32[]{:S(2)}, u32[]{:S(2)}) collective-permute-start(bf16[4,256,256]{2,1,0:T(8,128)(2,1)S(1)} %collective-permute-done.1), channel_id=1, source_target_pairs={{2,0},{3,1},{4,6},{5,7},{10,8},{11,9},{12,14},{13,15},{18,16},{19,... | collective-permute-start | bytes 1572872 | tf_op jit(solution)/shard_map/ppermute | solution.py:61
  16.1 3.0 %collective-permute-done.refs_1_ = bf16[4,256,256]{2,1,0:T(8,128)(2,1)S(1)} collective-permute-done((bf16[4,256,256]{2,1,0:T(8,128)(2,1)}, bf16[4,256,256]{2,1,0:T(8,128)(2,1)S(1)}, u32[]{:S(2)}, u32[]{:S(2)}) %collective-permute-start) | collective-permute-done | bytes 524320 | tf_op jit(solution)/shard_map/ppermute | solution.py:61
  19.1 0.7 collective-permute-start.3
  19.8 0.9 collective-permute-done.8.refs_2_
  20.6 1.5 %collective-permute-start.9 = (bf16[4,256,256]{2,1,0:T(8,128)(2,1)}, bf16[4,256,256]{2,1,0:T(8,128)(2,1)}, u32[]{:S(2)}, u32[]{:S(2)}) collective-permute-start(bf16[4,256,256]{2,1,0:T(8,128)(2,1)} %collective-permute-done.8.refs_2_), channel_id=1, source_target_pairs={{0,8},{1,9},{2,10},{3,11},{4,12},{5,13},{6,14},{7,15},{8,0},{9,1},... | collective-permute-start | bytes 1572872 | tf_op jit(solution)/shard_map/ppermute | solution.py:61
  22.1 1.5 %collective-permute-start.4 = (bf16[4,256,256]{2,1,0:T(8,128)(2,1)S(1)}, bf16[4,256,256]{2,1,0:T(8,128)(2,1)S(1)}, u32[]{:S(2)}, u32[]{:S(2)}) collective-permute-start(bf16[4,256,256]{2,1,0:T(8,128)(2,1)S(1)} %collective-permute-done.refs_1_), channel_id=1, source_target_pairs={{0,16},{1,17},{2,18},{3,19},{4,20},{5,21},{6,22},{7,23},{8,24},{9,... | collective-permute-start | bytes 1572872 | tf_op jit(solution)/shard_map/ppermute | solution.py:61
  23.7 8.2 %collective-permute-done.2 = bf16[4,256,256]{2,1,0:T(8,128)(2,1)S(1)} collective-permute-done((bf16[4,256,256]{2,1,0:T(8,128)(2,1)S(1)}, bf16[4,256,256]{2,1,0:T(8,128)(2,1)S(1)}, u32[]{:S(2)}, u32[]{:S(2)}) %collective-permute-start.2) | collective-permute-done | bytes 524320 | tf_op jit(solution)/shard_map/ppermute | solution.py:61
  31.8 0.5 collective-permute-start.11
  32.4 0.8 collective-permute-done.9.refs_3_
  33.1 0.6 pad_add_fusion.meta
  33.7 0.1 broadcast_select_fusion.2.refs_1_
  33.8 0.2 collective-permute-done.4.refs_3_
  34.0 1.3 %collective-permute-start.16 = (bf16[4,256,256]{2,1,0:T(8,128)(2,1)S(1)}, bf16[4,256,256]{2,1,0:T(8,128)(2,1)}, u32[]{:S(2)}, u32[]{:S(2)}) collective-permute-start(bf16[4,256,256]{2,1,0:T(8,128)(2,1)S(1)} %collective-permute-done.refs_1_), channel_id=1, source_target_pairs={{0,8},{1,9},{2,10},{3,11},{4,12},{5,13},{6,14},{7,15},{8,0},{9,1},... | collective-permute-start | bytes 1572872 | tf_op jit(solution)/shard_map/ppermute | solution.py:61
  35.4 1.5 %collective-permute-start.5 = (bf16[4,256,256]{2,1,0:T(8,128)(2,1)S(1)}, bf16[4,256,256]{2,1,0:T(8,128)(2,1)}, u32[]{:S(2)}, u32[]{:S(2)}) collective-permute-start(bf16[4,256,256]{2,1,0:T(8,128)(2,1)S(1)} %broadcast_select_fusion.2.refs_1_), channel_id=1, source_target_pairs={{0,16},{1,17},{2,18},{3,19},{4,20},{5,21},{6,22},{7,23},{8,24},{9,... | collective-permute-start | bytes 1572872 | tf_op jit(solution)/shard_map/ppermute | solution.py:61
  36.9 1.3 %collective-permute-start.6 = (bf16[4,256,256]{2,1,0:T(8,128)(2,1)S(1)}, bf16[4,256,256]{2,1,0:T(8,128)(2,1)S(1)}, u32[]{:S(2)}, u32[]{:S(2)}) collective-permute-start(bf16[4,256,256]{2,1,0:T(8,128)(2,1)S(1)} %collective-permute-done.3), channel_id=1, source_target_pairs={{2,0},{3,1},{4,6},{5,7},{10,8},{11,9},{12,14},{13,15},{18,16},{19,... | collective-permute-start | bytes 1572872 | tf_op jit(solution)/shard_map/ppermute | solution.py:61
  38.2 0.8 collective-permute-start.17
  39.0 0.7 collective-permute-start.22
  39.7 13.3 %shard_map.60 = (bf16[10,256,2048]{2,1,0:T(8,128)(2,1)}, f32[4,1024,256]{2,1,0:T(8,128)}, f32[8,128]{1,0:T(8,128)}) custom-call(s32[3]{0:T(128)} %pad_add_fusion.meta, bf16[4,256,1024]{2,1,0:T(8,128)(2,1)} %get-tuple-element.52.sparse, bf16[10,256,2048]{2,1,0:T(8,128)(2,1)} %decoder.7, bf16[4,256,256]{2,1,0:T(8,128)(2,1)} %refs_0_.1, ...), custom_call_target="tpu_custom_call" | custom-call | flops 10737418240 | bytes 20971520 | tf_op jit(solution)/shard_map/pallas_call | solution.py:273
  53.0 1.4 %collective-permute-done.6 = bf16[4,256,256]{2,1,0:T(8,128)(2,1)S(1)} collective-permute-done((bf16[4,256,256]{2,1,0:T(8,128)(2,1)S(1)}, bf16[4,256,256]{2,1,0:T(8,128)(2,1)S(1)}, u32[]{:S(2)}, u32[]{:S(2)}) %collective-permute-start.6) | collective-permute-done | bytes 524320 | tf_op jit(solution)/shard_map/ppermute | solution.py:61
  54.4 0.6 collective-permute-start.20
  55.0 4.5 %collective-permute-done.17.refs_4_ = bf16[4,256,256]{2,1,0:T(8,128)(2,1)} collective-permute-done((bf16[4,256,256]{2,1,0:T(8,128)(2,1)S(1)}, bf16[4,256,256]{2,1,0:T(8,128)(2,1)}, u32[]{:S(2)}, u32[]{:S(2)}) %collective-permute-start.17) | collective-permute-done | bytes 524320 | tf_op jit(solution)/shard_map/ppermute | solution.py:61
  59.6 0.5 collective-permute-start.21
  60.1 1.5 %collective-permute-start.23 = (bf16[4,256,256]{2,1,0:T(8,128)(2,1)S(1)}, bf16[4,256,256]{2,1,0:T(8,128)(2,1)}, u32[]{:S(2)}, u32[]{:S(2)}) collective-permute-start(bf16[4,256,256]{2,1,0:T(8,128)(2,1)S(1)} %broadcast_select_fusion.2.refs_1_), channel_id=1, source_target_pairs={{0,8},{1,9},{2,10},{3,11},{4,12},{5,13},{6,14},{7,15},{8,0},{9,1},... | collective-permute-start | bytes 1572872 | tf_op jit(solution)/shard_map/ppermute | solution.py:61
  61.6 0.5 collective-permute-start.14
  62.1 1.5 %collective-permute-start.15 = (bf16[4,256,256]{2,1,0:T(8,128)(2,1)S(1)}, bf16[4,256,256]{2,1,0:T(8,128)(2,1)S(1)}, u32[]{:S(2)}, u32[]{:S(2)}) collective-permute-start(bf16[4,256,256]{2,1,0:T(8,128)(2,1)S(1)} %broadcast_select_fusion.1.refs_2_), channel_id=1, source_target_pairs={{0,16},{1,17},{2,18},{3,19},{4,20},{5,21},{6,22},{7,23},{8,24},{9,... | collective-permute-start | bytes 1572872 | tf_op jit(solution)/shard_map/ppermute | solution.py:61
  63.6 1.5 %collective-permute-start.24 = (bf16[4,256,256]{2,1,0:T(8,128)(2,1)S(1)}, bf16[4,256,256]{2,1,0:T(8,128)(2,1)S(1)}, u32[]{:S(2)}, u32[]{:S(2)}) collective-permute-start(bf16[4,256,256]{2,1,0:T(8,128)(2,1)S(1)} %collective-permute-done.22), channel_id=1, source_target_pairs={{2,0},{3,1},{4,6},{5,7},{10,8},{11,9},{12,14},{13,15},{18,16},{19,... | collective-permute-start | bytes 1572872 | tf_op jit(solution)/shard_map/ppermute | solution.py:61
  65.1 13.0 %shard_map.61 = (bf16[10,256,2048]{2,1,0:T(8,128)(2,1)}, f32[4,1024,256]{2,1,0:T(8,128)}, f32[8,128]{1,0:T(8,128)}) custom-call(s32[3]{0:T(128)} %pad_add_fusion.meta, bf16[4,256,1024]{2,1,0:T(8,128)(2,1)} %get-tuple-element.52.sparse, bf16[10,256,2048]{2,1,0:T(8,128)(2,1)} %decoder.7, ...), custom_call_target="tpu_custom_call", output_to_operand_aliasing={{0}: (12, {})} | custom-call | flops 10737418240 | bytes 20971520 | tf_op jit(solution)/shard_map/pallas_call | solution.py:273
  78.1 2.2 %collective-permute-done.24 = bf16[4,256,256]{2,1,0:T(8,128)(2,1)S(1)} collective-permute-done((bf16[4,256,256]{2,1,0:T(8,128)(2,1)S(1)}, bf16[4,256,256]{2,1,0:T(8,128)(2,1)S(1)}, u32[]{:S(2)}, u32[]{:S(2)}) %collective-permute-start.24) | collective-permute-done | bytes 524320 | tf_op jit(solution)/shard_map/ppermute | solution.py:61
  80.4 0.1 collective-permute-start.28
  80.5 0.5 collective-permute-start.27
  81.0 0.1 collective-permute-start.26
  81.1 4.1 %collective-permute-done.14.refs_3_ = bf16[4,256,256]{2,1,0:T(8,128)(2,1)S(1)} collective-permute-done((bf16[4,256,256]{2,1,0:T(8,128)(2,1)S(1)}, bf16[4,256,256]{2,1,0:T(8,128)(2,1)S(1)}, u32[]{:S(2)}, u32[]{:S(2)}) %collective-permute-start.14) | collective-permute-done | bytes 524320 | tf_op jit(solution)/shard_map/ppermute | solution.py:61
  85.3 0.5 collective-permute-start.30
  85.8 1.5 %collective-permute-start.29 = (bf16[4,256,256]{2,1,0:T(8,128)(2,1)S(1)}, bf16[4,256,256]{2,1,0:T(8,128)(2,1)S(1)}, u32[]{:S(2)}, u32[]{:S(2)}) collective-permute-start(bf16[4,256,256]{2,1,0:T(8,128)(2,1)S(1)} %collective-permute-done.14.refs_3_), channel_id=1, source_target_pairs={{0,16},{1,17},{2,18},{3,19},{4,20},{5,21},{6,22},{7,23},{8,24},{9,... | collective-permute-start | bytes 1572872 | tf_op jit(solution)/shard_map/ppermute | solution.py:61
  87.3 0.5 collective-permute-start.32
  87.8 0.3 copy-done.11
  88.1 0.2 copy-done.12
  88.3 0.6 copy-done.13
  88.9 13.0 %shard_map.62 = (bf16[10,256,2048]{2,1,0:T(8,128)(2,1)}, f32[4,1024,256]{2,1,0:T(8,128)}, f32[8,128]{1,0:T(8,128)}) custom-call(s32[3]{0:T(128)} %pad_add_fusion.meta, bf16[4,256,1024]{2,1,0:T(8,128)(2,1)} %get-tuple-element.52.sparse, bf16[10,256,2048]{2,1,0:T(8,128)(2,1)} %decoder.7, ...), custom_call_target="tpu_custom_call", output_to_operand_aliasing={{0}: (12, {})} | custom-call | flops 10737418240 | bytes 20971520 | tf_op jit(solution)/shard_map/pallas_call | solution.py:273
  102.0 0.1 collective-permute-start.33
  102.1 1.9 %collective-permute-done.33.refs_9_ = bf16[4,256,256]{2,1,0:T(8,128)(2,1)S(1)} collective-permute-done((bf16[4,256,256]{2,1,0:T(8,128)(2,1)S(1)}, bf16[4,256,256]{2,1,0:T(8,128)(2,1)S(1)}, u32[]{:S(2)}, u32[]{:S(2)}) %collective-permute-start.33) | collective-permute-done | bytes 524320 | tf_op jit(solution)/shard_map/ppermute | solution.py:61
  104.0 0.8 copy-done.14
  104.8 12.7 %shard_map.63 = (bf16[10,256,2048]{2,1,0:T(8,128)(2,1)}, bf16[4,1024,256]{2,1,0:T(8,128)(2,1)}, f32[8,128]{1,0:T(8,128)}) custom-call(s32[3]{0:T(128)} %pad_add_fusion.meta, bf16[4,256,1024]{2,1,0:T(8,128)(2,1)} %get-tuple-element.52.sparse, bf16[10,256,2048]{2,1,0:T(8,128)(2,1)} %decoder.7, ...), custom_call_target="tpu_custom_call", output_to_operand_aliasing={{0}: (13, {})} | custom-call | flops 10737418240 | bytes 20971520 | tf_op jit(solution)/shard_map/pallas_call | solution.py:273
  (59 shorter events, 0.2 us)
Async XLA Ops:
  0.6 14.1 %collective-permute-start.1 = (bf16[4,256,256]{2,1,0:T(8,128)(2,1)}, bf16[4,256,256]{2,1,0:T(8,128)(2,1)S(1)}, u32[]{:S(2)}, u32[]{:S(2)}) collective-permute-start(bf16[4,256,256]{2,1,0:T(8,128)(2,1)} %refs_0_.1), channel_id=1, source_target_pairs={{2,4},{3,5},{4,2},{5,3},{10,12},{11,13},{12,10},{13,11},{18,20},{1... | collective-permute-start | bytes 1572872 | tf_op jit(solution)/shard_map/ppermute | solution.py:61
  1.3 17.7 %collective-permute-start = (bf16[4,256,256]{2,1,0:T(8,128)(2,1)}, bf16[4,256,256]{2,1,0:T(8,128)(2,1)S(1)}, u32[]{:S(2)}, u32[]{:S(2)}) collective-permute-start(bf16[4,256,256]{2,1,0:T(8,128)(2,1)} %refs_0_.1), channel_id=1, source_target_pairs={{0,2},{1,3},{2,0},{3,1},{4,6},{5,7},{6,4},{7,5},{8,10},{9,11},{10,... | collective-permute-start | bytes 1572872 | tf_op jit(solution)/shard_map/ppermute | solution.py:61
  7.2 13.4 %collective-permute-start.8 = (bf16[4,256,256]{2,1,0:T(8,128)(2,1)}, bf16[4,256,256]{2,1,0:T(8,128)(2,1)}, u32[]{:S(2)}, u32[]{:S(2)}) collective-permute-start(bf16[4,256,256]{2,1,0:T(8,128)(2,1)} %refs_0_.1), channel_id=1, source_target_pairs={{0,16},{1,17},{2,18},{3,19},{4,20},{5,21},{6,22},{7,23},{8,24},{9,... | collective-permute-start | bytes 1572872 | tf_op jit(solution)/shard_map/ppermute | solution.py:61
  8.7 14.9 %collective-permute-start.7 = (bf16[4,256,256]{2,1,0:T(8,128)(2,1)}, bf16[4,256,256]{2,1,0:T(8,128)(2,1)}, u32[]{:S(2)}, u32[]{:S(2)}) collective-permute-start(bf16[4,256,256]{2,1,0:T(8,128)(2,1)} %refs_0_.1), channel_id=1, source_target_pairs={{0,8},{1,9},{2,10},{3,11},{4,12},{5,13},{6,14},{7,15},{8,0},{9,1},... | collective-permute-start | bytes 1572872 | tf_op jit(solution)/shard_map/ppermute | solution.py:61
  14.8 17.1 %collective-permute-start.2 = (bf16[4,256,256]{2,1,0:T(8,128)(2,1)S(1)}, bf16[4,256,256]{2,1,0:T(8,128)(2,1)S(1)}, u32[]{:S(2)}, u32[]{:S(2)}) collective-permute-start(bf16[4,256,256]{2,1,0:T(8,128)(2,1)S(1)} %collective-permute-done.1), channel_id=1, source_target_pairs={{2,0},{3,1},{4,6},{5,7},{10,8},{11,9},{12,14},{13,15},{18,16},{19,... | collective-permute-start | bytes 1572872 | tf_op jit(solution)/shard_map/ppermute | solution.py:61
  19.1 35.3 %copy-start.3 = (bf16[4,256,256]{2,1,0:T(8,128)(2,1)}, bf16[4,256,256]{2,1,0:T(8,128)(2,1)S(1)}, u32[]{:S(2)}) copy-start(bf16[4,256,256]{2,1,0:T(8,128)(2,1)S(1)} %collective-permute-done.refs_1_) | copy-start | bytes 1572868
  19.1 12.8 %collective-permute-start.3 = (bf16[4,256,256]{2,1,0:T(8,128)(2,1)S(1)}, bf16[4,256,256]{2,1,0:T(8,128)(2,1)S(1)}, u32[]{:S(2)}, u32[]{:S(2)}) collective-permute-start(bf16[4,256,256]{2,1,0:T(8,128)(2,1)S(1)} %collective-permute-done.refs_1_), channel_id=1, source_target_pairs={{2,4},{3,5},{4,2},{5,3},{10,12},{11,13},{12,10},{13,11},{18,20},{1... | collective-permute-start | bytes 1572872 | tf_op jit(solution)/shard_map/ppermute | solution.py:61
  20.6 12.5 %collective-permute-start.9 = (bf16[4,256,256]{2,1,0:T(8,128)(2,1)}, bf16[4,256,256]{2,1,0:T(8,128)(2,1)}, u32[]{:S(2)}, u32[]{:S(2)}) collective-permute-start(bf16[4,256,256]{2,1,0:T(8,128)(2,1)} %collective-permute-done.8.refs_2_), channel_id=1, source_target_pairs={{0,8},{1,9},{2,10},{3,11},{4,12},{5,13},{6,14},{7,15},{8,0},{9,1},... | collective-permute-start | bytes 1572872 | tf_op jit(solution)/shard_map/ppermute | solution.py:61
  22.1 11.9 %collective-permute-start.4 = (bf16[4,256,256]{2,1,0:T(8,128)(2,1)S(1)}, bf16[4,256,256]{2,1,0:T(8,128)(2,1)S(1)}, u32[]{:S(2)}, u32[]{:S(2)}) collective-permute-start(bf16[4,256,256]{2,1,0:T(8,128)(2,1)S(1)} %collective-permute-done.refs_1_), channel_id=1, source_target_pairs={{0,16},{1,17},{2,18},{3,19},{4,20},{5,21},{6,22},{7,23},{8,24},{9,... | collective-permute-start | bytes 1572872 | tf_op jit(solution)/shard_map/ppermute | solution.py:61
  23.6 11.7 %collective-permute-start.10 = (bf16[4,256,256]{2,1,0:T(8,128)(2,1)}, bf16[4,256,256]{2,1,0:T(8,128)(2,1)}, u32[]{:S(2)}, u32[]{:S(2)}) collective-permute-start(bf16[4,256,256]{2,1,0:T(8,128)(2,1)} %refs_0_.1), channel_id=1, source_target_pairs={{0,1},{1,0},{2,3},{3,2},{4,5},{5,4},{6,7},{7,6},{8,9},{9,8},{10,11... | collective-permute-start | bytes 1572872 | tf_op jit(solution)/shard_map/ppermute | solution.py:61
  31.8 5.1 %collective-permute-start.12 = (bf16[4,256,256]{2,1,0:T(8,128)(2,1)}, bf16[4,256,256]{2,1,0:T(8,128)(2,1)}, u32[]{:S(2)}, u32[]{:S(2)}) collective-permute-start(bf16[4,256,256]{2,1,0:T(8,128)(2,1)} %collective-permute-done.8.refs_2_), channel_id=1, source_target_pairs={{0,1},{1,0},{2,3},{3,2},{4,5},{5,4},{6,7},{7,6},{8,9},{9,8},{10,11... | collective-permute-start | bytes 1572872 | tf_op jit(solution)/shard_map/ppermute | solution.py:61
  31.8 6.3 %collective-permute-start.11 = (bf16[4,256,256]{2,1,0:T(8,128)(2,1)}, bf16[4,256,256]{2,1,0:T(8,128)(2,1)}, u32[]{:S(2)}, u32[]{:S(2)}) collective-permute-start(bf16[4,256,256]{2,1,0:T(8,128)(2,1)} %collective-permute-done.7.refs_1_), channel_id=1, source_target_pairs={{0,1},{1,0},{2,3},{3,2},{4,5},{5,4},{6,7},{7,6},{8,9},{9,8},{10,11... | collective-permute-start | bytes 1572872 | tf_op jit(solution)/shard_map/ppermute | solution.py:61
  33.1 5.8 %collective-permute-start.13 = (bf16[4,256,256]{2,1,0:T(8,128)(2,1)}, bf16[4,256,256]{2,1,0:T(8,128)(2,1)}, u32[]{:S(2)}, u32[]{:S(2)}) collective-permute-start(bf16[4,256,256]{2,1,0:T(8,128)(2,1)} %collective-permute-done.9.refs_3_), channel_id=1, source_target_pairs={{0,1},{1,0},{2,3},{3,2},{4,5},{5,4},{6,7},{7,6},{8,9},{9,8},{10,11... | collective-permute-start | bytes 1572872 | tf_op jit(solution)/shard_map/ppermute | solution.py:61
  33.8 51.4 %copy-start = (bf16[4,256,256]{2,1,0:T(8,128)(2,1)}, bf16[4,256,256]{2,1,0:T(8,128)(2,1)S(1)}, u32[]{:S(2)}) copy-start(bf16[4,256,256]{2,1,0:T(8,128)(2,1)S(1)} %broadcast_select_fusion.2.refs_1_) | copy-start | bytes 1572868
  34.0 20.4 %copy-start.4 = (bf16[4,256,256]{2,1,0:T(8,128)(2,1)}, bf16[4,256,256]{2,1,0:T(8,128)(2,1)S(1)}, u32[]{:S(2)}) copy-start(bf16[4,256,256]{2,1,0:T(8,128)(2,1)S(1)} %collective-permute-done.4.refs_3_) | copy-start | bytes 1572868
  34.0 20.4 %collective-permute-start.16 = (bf16[4,256,256]{2,1,0:T(8,128)(2,1)S(1)}, bf16[4,256,256]{2,1,0:T(8,128)(2,1)}, u32[]{:S(2)}, u32[]{:S(2)}) collective-permute-start(bf16[4,256,256]{2,1,0:T(8,128)(2,1)S(1)} %collective-permute-done.refs_1_), channel_id=1, source_target_pairs={{0,8},{1,9},{2,10},{3,11},{4,12},{5,13},{6,14},{7,15},{8,0},{9,1},... | collective-permute-start | bytes 1572872 | tf_op jit(solution)/shard_map/ppermute | solution.py:61
  35.4 24.7 %collective-permute-start.5 = (bf16[4,256,256]{2,1,0:T(8,128)(2,1)S(1)}, bf16[4,256,256]{2,1,0:T(8,128)(2,1)}, u32[]{:S(2)}, u32[]{:S(2)}) collective-permute-start(bf16[4,256,256]{2,1,0:T(8,128)(2,1)S(1)} %broadcast_select_fusion.2.refs_1_), channel_id=1, source_target_pairs={{0,16},{1,17},{2,18},{3,19},{4,20},{5,21},{6,22},{7,23},{8,24},{9,... | collective-permute-start | bytes 1572872 | tf_op jit(solution)/shard_map/ppermute | solution.py:61
  36.9 17.4 %collective-permute-start.6 = (bf16[4,256,256]{2,1,0:T(8,128)(2,1)S(1)}, bf16[4,256,256]{2,1,0:T(8,128)(2,1)S(1)}, u32[]{:S(2)}, u32[]{:S(2)}) collective-permute-start(bf16[4,256,256]{2,1,0:T(8,128)(2,1)S(1)} %collective-permute-done.3), channel_id=1, source_target_pairs={{2,0},{3,1},{4,6},{5,7},{10,8},{11,9},{12,14},{13,15},{18,16},{19,... | collective-permute-start | bytes 1572872 | tf_op jit(solution)/shard_map/ppermute | solution.py:61
  38.2 21.4 %collective-permute-start.17 = (bf16[4,256,256]{2,1,0:T(8,128)(2,1)S(1)}, bf16[4,256,256]{2,1,0:T(8,128)(2,1)}, u32[]{:S(2)}, u32[]{:S(2)}) collective-permute-start(bf16[4,256,256]{2,1,0:T(8,128)(2,1)S(1)} %collective-permute-done.4.refs_3_), channel_id=1, source_target_pairs={{0,8},{1,9},{2,10},{3,11},{4,12},{5,13},{6,14},{7,15},{8,0},{9,1},... | collective-permute-start | bytes 1572872 | tf_op jit(solution)/shard_map/ppermute | solution.py:61
  39.0 20.6 %collective-permute-start.22 = (bf16[4,256,256]{2,1,0:T(8,128)(2,1)}, bf16[4,256,256]{2,1,0:T(8,128)(2,1)S(1)}, u32[]{:S(2)}, u32[]{:S(2)}) collective-permute-start(bf16[4,256,256]{2,1,0:T(8,128)(2,1)} %collective-permute-done.9.refs_3_), channel_id=1, source_target_pairs={{2,4},{3,5},{4,2},{5,3},{10,12},{11,13},{12,10},{13,11},{18,20},{1... | collective-permute-start | bytes 1572872 | tf_op jit(solution)/shard_map/ppermute | solution.py:61
  54.3 7.2 %collective-permute-start.18 = (bf16[4,256,256]{2,1,0:T(8,128)(2,1)S(1)}, bf16[4,256,256]{2,1,0:T(8,128)(2,1)S(1)}, u32[]{:S(2)}, u32[]{:S(2)}) collective-permute-start(bf16[4,256,256]{2,1,0:T(8,128)(2,1)S(1)} %collective-permute-done.refs_1_), channel_id=1, source_target_pairs={{0,1},{1,0},{2,3},{3,2},{4,5},{5,4},{6,7},{7,6},{8,9},{9,8},{10,11... | collective-permute-start | bytes 1572872 | tf_op jit(solution)/shard_map/ppermute | solution.py:61
  54.4 30.8 %copy-start.1 = (bf16[4,256,256]{2,1,0:T(8,128)(2,1)}, bf16[4,256,256]{2,1,0:T(8,128)(2,1)S(1)}, u32[]{:S(2)}) copy-start(bf16[4,256,256]{2,1,0:T(8,128)(2,1)S(1)} %broadcast_select_fusion.1.refs_2_) | copy-start | bytes 1572868
  54.4 7.7 %collective-permute-start.20 = (bf16[4,256,256]{2,1,0:T(8,128)(2,1)S(1)}, bf16[4,256,256]{2,1,0:T(8,128)(2,1)S(1)}, u32[]{:S(2)}, u32[]{:S(2)}) collective-permute-start(bf16[4,256,256]{2,1,0:T(8,128)(2,1)S(1)} %collective-permute-done.4.refs_3_), channel_id=1, source_target_pairs={{0,1},{1,0},{2,3},{3,2},{4,5},{5,4},{6,7},{7,6},{8,9},{9,8},{10,11... | collective-permute-start | bytes 1572872 | tf_op jit(solution)/shard_map/ppermute | solution.py:61
  59.6 4.1 %collective-permute-start.19 = (bf16[4,256,256]{2,1,0:T(8,128)(2,1)}, bf16[4,256,256]{2,1,0:T(8,128)(2,1)}, u32[]{:S(2)}, u32[]{:S(2)}) collective-permute-start(bf16[4,256,256]{2,1,0:T(8,128)(2,1)} %collective-permute-done.16.refs_2_), channel_id=1, source_target_pairs={{0,1},{1,0},{2,3},{3,2},{4,5},{5,4},{6,7},{7,6},{8,9},{9,8},{10,11... | collective-permute-start | bytes 1572872 | tf_op jit(solution)/shard_map/ppermute | solution.py:61
  59.6 5.5 %collective-permute-start.21 = (bf16[4,256,256]{2,1,0:T(8,128)(2,1)}, bf16[4,256,256]{2,1,0:T(8,128)(2,1)}, u32[]{:S(2)}, u32[]{:S(2)}) collective-permute-start(bf16[4,256,256]{2,1,0:T(8,128)(2,1)} %collective-permute-done.17.refs_4_), channel_id=1, source_target_pairs={{0,1},{1,0},{2,3},{3,2},{4,5},{5,4},{6,7},{7,6},{8,9},{9,8},{10,11... | collective-permute-start | bytes 1572872 | tf_op jit(solution)/shard_map/ppermute | solution.py:61
  60.1 20.9 %collective-permute-start.23 = (bf16[4,256,256]{2,1,0:T(8,128)(2,1)S(1)}, bf16[4,256,256]{2,1,0:T(8,128)(2,1)}, u32[]{:S(2)}, u32[]{:S(2)}) collective-permute-start(bf16[4,256,256]{2,1,0:T(8,128)(2,1)S(1)} %broadcast_select_fusion.2.refs_1_), channel_id=1, source_target_pairs={{0,8},{1,9},{2,10},{3,11},{4,12},{5,13},{6,14},{7,15},{8,0},{9,1},... | collective-permute-start | bytes 1572872 | tf_op jit(solution)/shard_map/ppermute | solution.py:61
  61.6 2.1 %copy-start.8 = (bf16[4,256,256]{2,1,0:T(8,128)(2,1)}, bf16[4,256,256]{2,1,0:T(8,128)(2,1)S(1)}, u32[]{:S(2)}) copy-start(bf16[4,256,256]{2,1,0:T(8,128)(2,1)S(1)} %collective-permute-done.18.refs_5_) | copy-start | bytes 1572868
  61.6 23.6 %collective-permute-start.14 = (bf16[4,256,256]{2,1,0:T(8,128)(2,1)S(1)}, bf16[4,256,256]{2,1,0:T(8,128)(2,1)S(1)}, u32[]{:S(2)}, u32[]{:S(2)}) collective-permute-start(bf16[4,256,256]{2,1,0:T(8,128)(2,1)S(1)} %broadcast_select_fusion.1.refs_2_), channel_id=1, source_target_pairs={{0,8},{1,9},{2,10},{3,11},{4,12},{5,13},{6,14},{7,15},{8,0},{9,1},... | collective-permute-start | bytes 1572872 | tf_op jit(solution)/shard_map/ppermute | solution.py:61
  62.1 3.0 %copy-start.10 = (bf16[4,256,256]{2,1,0:T(8,128)(2,1)}, bf16[4,256,256]{2,1,0:T(8,128)(2,1)S(1)}, u32[]{:S(2)}) copy-start(bf16[4,256,256]{2,1,0:T(8,128)(2,1)S(1)} %collective-permute-done.20.refs_7_) | copy-start | bytes 1572868
  62.1 23.1 %collective-permute-start.15 = (bf16[4,256,256]{2,1,0:T(8,128)(2,1)S(1)}, bf16[4,256,256]{2,1,0:T(8,128)(2,1)S(1)}, u32[]{:S(2)}, u32[]{:S(2)}) collective-permute-start(bf16[4,256,256]{2,1,0:T(8,128)(2,1)S(1)} %broadcast_select_fusion.1.refs_2_), channel_id=1, source_target_pairs={{0,16},{1,17},{2,18},{3,19},{4,20},{5,21},{6,22},{7,23},{8,24},{9,... | collective-permute-start | bytes 1572872 | tf_op jit(solution)/shard_map/ppermute | solution.py:61
  63.6 16.7 %collective-permute-start.24 = (bf16[4,256,256]{2,1,0:T(8,128)(2,1)S(1)}, bf16[4,256,256]{2,1,0:T(8,128)(2,1)S(1)}, u32[]{:S(2)}, u32[]{:S(2)}) collective-permute-start(bf16[4,256,256]{2,1,0:T(8,128)(2,1)S(1)} %collective-permute-done.22), channel_id=1, source_target_pairs={{2,0},{3,1},{4,6},{5,7},{10,8},{11,9},{12,14},{13,15},{18,16},{19,... | collective-permute-start | bytes 1572872 | tf_op jit(solution)/shard_map/ppermute | solution.py:61
  80.4 8.5 %copy-start.2 = (bf16[4,256,256]{2,1,0:T(8,128)(2,1)}, bf16[4,256,256]{2,1,0:T(8,128)(2,1)S(1)}, u32[]{:S(2)}) copy-start(bf16[4,256,256]{2,1,0:T(8,128)(2,1)S(1)} %broadcast_select_fusion.refs_4_) | copy-start | bytes 1572868
  80.4 5.4 %collective-permute-start.28 = (bf16[4,256,256]{2,1,0:T(8,128)(2,1)S(1)}, bf16[4,256,256]{2,1,0:T(8,128)(2,1)}, u32[]{:S(2)}, u32[]{:S(2)}) collective-permute-start(bf16[4,256,256]{2,1,0:T(8,128)(2,1)S(1)} %broadcast_select_fusion.refs_4_), channel_id=1, source_target_pairs={{0,1},{1,0},{2,3},{3,2},{4,5},{5,4},{6,7},{7,6},{8,9},{9,8},{10,11... | collective-permute-start | bytes 1572872 | tf_op jit(solution)/shard_map/ppermute | solution.py:61
  80.5 6.8 %collective-permute-start.27 = (bf16[4,256,256]{2,1,0:T(8,128)(2,1)}, bf16[4,256,256]{2,1,0:T(8,128)(2,1)S(1)}, u32[]{:S(2)}, u32[]{:S(2)}) collective-permute-start(bf16[4,256,256]{2,1,0:T(8,128)(2,1)} %collective-permute-done.5.refs_3_), channel_id=1, source_target_pairs={{0,1},{1,0},{2,3},{3,2},{4,5},{5,4},{6,7},{7,6},{8,9},{9,8},{10,11... | collective-permute-start | bytes 1572872 | tf_op jit(solution)/shard_map/ppermute | solution.py:61
  81.0 6.3 %collective-permute-start.26 = (bf16[4,256,256]{2,1,0:T(8,128)(2,1)}, bf16[4,256,256]{2,1,0:T(8,128)(2,1)S(1)}, u32[]{:S(2)}, u32[]{:S(2)}) collective-permute-start(bf16[4,256,256]{2,1,0:T(8,128)(2,1)} %collective-permute-done.23.refs_2_), channel_id=1, source_target_pairs={{0,1},{1,0},{2,3},{3,2},{4,5},{5,4},{6,7},{7,6},{8,9},{9,8},{10,11... | collective-permute-start | bytes 1572872 | tf_op jit(solution)/shard_map/ppermute | solution.py:61
  85.2 16.8 %copy-start.5 = (bf16[4,256,256]{2,1,0:T(8,128)(2,1)}, bf16[4,256,256]{2,1,0:T(8,128)(2,1)S(1)}, u32[]{:S(2)}) copy-start(bf16[4,256,256]{2,1,0:T(8,128)(2,1)S(1)} %collective-permute-done.14.refs_3_) | copy-start | bytes 1572868
  85.2 2.6 %collective-permute-start.25 = (bf16[4,256,256]{2,1,0:T(8,128)(2,1)S(1)}, bf16[4,256,256]{2,1,0:T(8,128)(2,1)S(1)}, u32[]{:S(2)}, u32[]{:S(2)}) collective-permute-start(bf16[4,256,256]{2,1,0:T(8,128)(2,1)S(1)} %broadcast_select_fusion.2.refs_1_), channel_id=1, source_target_pairs={{0,1},{1,0},{2,3},{3,2},{4,5},{5,4},{6,7},{7,6},{8,9},{9,8},{10,11... | collective-permute-start | bytes 1572872 | tf_op jit(solution)/shard_map/ppermute | solution.py:61
  85.2 16.7 %copy-start.6 = (bf16[4,256,256]{2,1,0:T(8,128)(2,1)}, bf16[4,256,256]{2,1,0:T(8,128)(2,1)S(1)}, u32[]{:S(2)}) copy-start(bf16[4,256,256]{2,1,0:T(8,128)(2,1)S(1)} %collective-permute-done.15.refs_4_) | copy-start | bytes 1572868
  85.3 16.8 %collective-permute-start.30 = (bf16[4,256,256]{2,1,0:T(8,128)(2,1)S(1)}, bf16[4,256,256]{2,1,0:T(8,128)(2,1)S(1)}, u32[]{:S(2)}, u32[]{:S(2)}) collective-permute-start(bf16[4,256,256]{2,1,0:T(8,128)(2,1)S(1)} %broadcast_select_fusion.1.refs_2_), channel_id=1, source_target_pairs={{0,1},{1,0},{2,3},{3,2},{4,5},{5,4},{6,7},{7,6},{8,9},{9,8},{10,11... | collective-permute-start | bytes 1572872 | tf_op jit(solution)/shard_map/ppermute | solution.py:61
  85.8 16.2 %collective-permute-start.29 = (bf16[4,256,256]{2,1,0:T(8,128)(2,1)S(1)}, bf16[4,256,256]{2,1,0:T(8,128)(2,1)S(1)}, u32[]{:S(2)}, u32[]{:S(2)}) collective-permute-start(bf16[4,256,256]{2,1,0:T(8,128)(2,1)S(1)} %collective-permute-done.14.refs_3_), channel_id=1, source_target_pairs={{0,16},{1,17},{2,18},{3,19},{4,20},{5,21},{6,22},{7,23},{8,24},{9,... | collective-permute-start | bytes 1572872 | tf_op jit(solution)/shard_map/ppermute | solution.py:61
  87.3 0.8 copy-start.11
  87.3 14.8 %collective-permute-start.31 = (bf16[4,256,256]{2,1,0:T(8,128)(2,1)S(1)}, bf16[4,256,256]{2,1,0:T(8,128)(2,1)}, u32[]{:S(2)}, u32[]{:S(2)}) collective-permute-start(bf16[4,256,256]{2,1,0:T(8,128)(2,1)S(1)} %collective-permute-done.14.refs_3_), channel_id=1, source_target_pairs={{0,1},{1,0},{2,3},{3,2},{4,5},{5,4},{6,7},{7,6},{8,9},{9,8},{10,11... | collective-permute-start | bytes 1572872 | tf_op jit(solution)/shard_map/ppermute | solution.py:61
  87.3 0.9 copy-start.12
  87.3 14.8 %collective-permute-start.32 = (bf16[4,256,256]{2,1,0:T(8,128)(2,1)S(1)}, bf16[4,256,256]{2,1,0:T(8,128)(2,1)}, u32[]{:S(2)}, u32[]{:S(2)}) collective-permute-start(bf16[4,256,256]{2,1,0:T(8,128)(2,1)S(1)} %collective-permute-done.15.refs_4_), channel_id=1, source_target_pairs={{0,1},{1,0},{2,3},{3,2},{4,5},{5,4},{6,7},{7,6},{8,9},{9,8},{10,11... | collective-permute-start | bytes 1572872 | tf_op jit(solution)/shard_map/ppermute | solution.py:61
  102.0 2.0 %copy-start.9 = (bf16[4,256,256]{2,1,0:T(8,128)(2,1)}, bf16[4,256,256]{2,1,0:T(8,128)(2,1)S(1)}, u32[]{:S(2)}) copy-start(bf16[4,256,256]{2,1,0:T(8,128)(2,1)S(1)} %collective-permute-done.29.refs_5_) | copy-start | bytes 1572868
  102.0 2.0 %collective-permute-start.33 = (bf16[4,256,256]{2,1,0:T(8,128)(2,1)S(1)}, bf16[4,256,256]{2,1,0:T(8,128)(2,1)S(1)}, u32[]{:S(2)}, u32[]{:S(2)}) collective-permute-start(bf16[4,256,256]{2,1,0:T(8,128)(2,1)S(1)} %collective-permute-done.29.refs_5_), channel_id=1, source_target_pairs={{0,1},{1,0},{2,3},{3,2},{4,5},{5,4},{6,7},{7,6},{8,9},{9,8},{10,11... | collective-permute-start | bytes 1572872 | tf_op jit(solution)/shard_map/ppermute | solution.py:61
  102.1 1.9 %copy-start.7 = (bf16[4,256,256]{2,1,0:T(8,128)(2,1)}, bf16[4,256,256]{2,1,0:T(8,128)(2,1)S(1)}, u32[]{:S(2)}) copy-start(bf16[4,256,256]{2,1,0:T(8,128)(2,1)S(1)} %collective-permute-done.30.refs_6_) | copy-start | bytes 1572868
  104.0 0.8 copy-start.14
  (1 other events, 0.8 us)

commit v12 on v11

--- a/solution.py
+++ b/solution.py
@@ -142,7 +142,8 @@
         refs.pop(0)
     refs = refs[n_tokens:]
     grad, acc_out, token = refs[:3]
-    up_v, sparse_v, dec_v, acc_v, grad_v, feat_v, up_sem, dec_sem, in_sem, grad_sem, out_sem = refs[3:]
+    up_v, sparse_v, dec_v, acc_v, grad_v, feat_v, *sems = refs[3:]
+    up_sem, sparse_sem, dec_sem, in_sem, grad_sem, out_sem = sems
     tokens, wide = parts[0].shape[1:]
     both = CORES * wide
     width = decoder.shape[1]
@@ -153,7 +154,10 @@
     columns = pl.ds(pl.multiple_of(plane * both, both), both)
     token[...] = jnp.zeros_like(token)
 
-    copies = [pltpu.make_async_copy(sparse, sparse_v, in_sem.at[0])]
+    sparse_copies = [
+        pltpu.make_async_copy(sparse.at[source], sparse_v.at[source], sparse_sem.at[source])
+        for source in range(layers)
+    ]
     ups = {}
     for target in range(layers):
         ups[target] = []
@@ -177,8 +181,18 @@
                     dec_sem.at[pair],
                 )
             )
-    copies[0].start()
-    for target in reversed(range(layers)):
+    early = layers - 2 if layers > 1 else 0
+    sparse_copies[0].start()
+    for copy in ups[layers - 1]:
+        copy.start()
+    for copy in sparse_copies[1:]:
+        copy.start()
+    for target in reversed(range(early, layers - 1)):
+        for copy in ups[target]:
+            copy.start()
+    for copy in ups[layers - 1]:
+        copy.wait()
+    for target in reversed(range(early)):
         for copy in ups[target]:
             copy.start()
     for copy in decs:
@@ -187,20 +201,22 @@
     if not first:
         for source in range(layers):
             acc_copies.append(
-                pltpu.make_async_copy(acc_in.at[source], acc_v.at[source], in_sem.at[2 + source])
+                pltpu.make_async_copy(acc_in.at[source], acc_v.at[source], in_sem.at[1 + source])
             )
             acc_copies[-1].start()
     if last:
-        mask_copy = pltpu.make_async_copy(mask, feat_v, in_sem.at[1])
+        mask_copy = pltpu.make_async_copy(mask, feat_v, in_sem.at[0])
         mask_copy.start()
-    copies[0].wait()
     outs = []
     for target in reversed(range(layers)):
-        for copy in ups[target]:
-            copy.wait()
+        if target < layers - 1:
+            for copy in ups[target]:
+                copy.wait()
         count = target + 1
         base = target * (target + 1) // 2
         for source in range(count):
+            if target == layers - 1:
+                sparse_copies[source].wait()
             grad_v[base + source] = jnp.dot(
                 sparse_v[source],
                 up_v[:, target * both : (target + 1) * both],
@@ -287,8 +303,9 @@
             pltpu.VMEM((pairs, width, both), jnp.bfloat16),
             pltpu.VMEM((layers, rows, width), jnp.bfloat16),
             pltpu.SemaphoreType.DMA((layers, CORES * len(mine))),
+            pltpu.SemaphoreType.DMA((layers,)),
             pltpu.SemaphoreType.DMA((pairs,)),
-            pltpu.SemaphoreType.DMA((2 + layers,)),
+            pltpu.SemaphoreType.DMA((1 + layers,)),
             pltpu.SemaphoreType.DMA((layers,)),
             pltpu.SemaphoreType.DMA((layers,)),
         ],

time: 119 us -> 118 us (level)
  Pallas kernels: 56.6 us -> 52.2 us
  waiting for transfers between devices: 27.2 us -> 30 us
    pallas_call x4, Pallas kernels: 52.1 us -> 47.7 us  [run_round(): pl.pallas_call(functools.partial(round_kernel, len(mine), len(tokens), la...]
    ppermute x34, waiting for transfers between devices: 27.2 us -> 30 us  [permute(): return lax.ppermute(x, ('layer', 'feat'), sorted(flat))]
  transfers between devices with their start and end apart: 34 -> 34, of which waited for: 10 -> 10; matrix products, arithmetic and copies ran while one was open for 1% -> 1% of each run, Pallas kernels for 37% -> 34%
where the time goes in v12:
time: 118 us; the launch traced here: 116 us
  Pallas kernels  52.2 us (44%)
  starting transfers between devices  30 us (25%)
  waiting for transfers between devices  30 us (25%)
  local copies, waits for them, and re-layouts  1.92 us (2%)
    pallas_call x4, Pallas kernels, run_round(): pl.pallas_call(functools.partial(round_kernel, len(mine), len(tokens), la...  47.7 us
    ppermute x34, starting transfers between devices, permute(): return lax.ppermute(x, ('layer', 'feat'), sorted(flat))  30 us
    ppermute x34, waiting for transfers between devices, permute(): return lax.ppermute(x, ('layer', 'feat'), sorted(flat))  30 us
    pallas_call x1, Pallas kernels, prepare(): pl.pallas_call(prepare_kernel, grid=(layers,), in_specs=[block(rows, widt...  4.55 us
  transfers between devices with their start and end apart: 34, of which 10 were waited for; matrix products, arithmetic and copies ran while one was open for 1% of the time, Pallas kernels for 34%

profile of v12, /device:TPU:0, one launch (start us, length us, event | category | flops | bytes accessed | tf_op | source)
XLA Modules:
  0.0 116.1 jit_solution(5597162348690036093)
XLA Ops:
  0.6 0.7 collective-permute-start.1
  1.3 5.9 %collective-permute-start = (bf16[4,256,256]{2,1,0:T(8,128)(2,1)}, bf16[4,256,256]{2,1,0:T(8,128)(2,1)S(1)}, u32[]{:S(2)}, u32[]{:S(2)}) collective-permute-start(bf16[4,256,256]{2,1,0:T(8,128)(2,1)} %refs_0_.1), channel_id=1, source_target_pairs={{0,2},{1,3},{2,0},{3,1},{4,6},{5,7},{6,4},{7,5},{8,10},{9,11},{10,... | collective-permute-start | bytes 1572872 | tf_op jit(solution)/shard_map/ppermute | solution.py:61
  7.2 1.5 %collective-permute-start.8 = (bf16[4,256,256]{2,1,0:T(8,128)(2,1)}, bf16[4,256,256]{2,1,0:T(8,128)(2,1)}, u32[]{:S(2)}, u32[]{:S(2)}) collective-permute-start(bf16[4,256,256]{2,1,0:T(8,128)(2,1)} %refs_0_.1), channel_id=1, source_target_pairs={{0,16},{1,17},{2,18},{3,19},{4,20},{5,21},{6,22},{7,23},{8,24},{9,... | collective-permute-start | bytes 1572872 | tf_op jit(solution)/shard_map/ppermute | solution.py:61
  8.7 1.5 %collective-permute-start.7 = (bf16[4,256,256]{2,1,0:T(8,128)(2,1)}, bf16[4,256,256]{2,1,0:T(8,128)(2,1)}, u32[]{:S(2)}, u32[]{:S(2)}) collective-permute-start(bf16[4,256,256]{2,1,0:T(8,128)(2,1)} %refs_0_.1), channel_id=1, source_target_pairs={{0,8},{1,9},{2,10},{3,11},{4,12},{5,13},{6,14},{7,15},{8,0},{9,1},... | collective-permute-start | bytes 1572872 | tf_op jit(solution)/shard_map/ppermute | solution.py:61
  10.2 4.5 %shard_map.59 = (bf16[4,256,1024]{2,1,0:T(8,128)(2,1)}, bf16[4,1024,256]{2,1,0:T(8,128)(2,1)}) custom-call(bf16[4,1024,256]{2,1,0:T(8,128)(2,1)} %act.1, s32[4,2,1024]{2,1,0:T(2,128)} %bitcast.4), custom_call_target="tpu_custom_call" | custom-call | bytes 6291456 | tf_op jit(solution)/shard_map/pallas_call | solution.py:121
  14.8 1.3 %collective-permute-start.2 = (bf16[4,256,256]{2,1,0:T(8,128)(2,1)S(1)}, bf16[4,256,256]{2,1,0:T(8,128)(2,1)S(1)}, u32[]{:S(2)}, u32[]{:S(2)}) collective-permute-start(bf16[4,256,256]{2,1,0:T(8,128)(2,1)S(1)} %collective-permute-done.1), channel_id=1, source_target_pairs={{2,0},{3,1},{4,6},{5,7},{10,8},{11,9},{12,14},{13,15},{18,16},{19,... | collective-permute-start | bytes 1572872 | tf_op jit(solution)/shard_map/ppermute | solution.py:61
  16.1 3.0 %collective-permute-done.refs_1_ = bf16[4,256,256]{2,1,0:T(8,128)(2,1)S(1)} collective-permute-done((bf16[4,256,256]{2,1,0:T(8,128)(2,1)}, bf16[4,256,256]{2,1,0:T(8,128)(2,1)S(1)}, u32[]{:S(2)}, u32[]{:S(2)}) %collective-permute-start) | collective-permute-done | bytes 524320 | tf_op jit(solution)/shard_map/ppermute | solution.py:61
  19.1 0.7 collective-permute-start.3
  19.8 0.9 collective-permute-done.8.refs_2_
  20.6 1.5 %collective-permute-start.9 = (bf16[4,256,256]{2,1,0:T(8,128)(2,1)}, bf16[4,256,256]{2,1,0:T(8,128)(2,1)}, u32[]{:S(2)}, u32[]{:S(2)}) collective-permute-start(bf16[4,256,256]{2,1,0:T(8,128)(2,1)} %collective-permute-done.8.refs_2_), channel_id=1, source_target_pairs={{0,8},{1,9},{2,10},{3,11},{4,12},{5,13},{6,14},{7,15},{8,0},{9,1},... | collective-permute-start | bytes 1572872 | tf_op jit(solution)/shard_map/ppermute | solution.py:61
  22.1 1.5 %collective-permute-start.4 = (bf16[4,256,256]{2,1,0:T(8,128)(2,1)S(1)}, bf16[4,256,256]{2,1,0:T(8,128)(2,1)S(1)}, u32[]{:S(2)}, u32[]{:S(2)}) collective-permute-start(bf16[4,256,256]{2,1,0:T(8,128)(2,1)S(1)} %collective-permute-done.refs_1_), channel_id=1, source_target_pairs={{0,16},{1,17},{2,18},{3,19},{4,20},{5,21},{6,22},{7,23},{8,24},{9,... | collective-permute-start | bytes 1572872 | tf_op jit(solution)/shard_map/ppermute | solution.py:61
  23.7 8.2 %collective-permute-done.2 = bf16[4,256,256]{2,1,0:T(8,128)(2,1)S(1)} collective-permute-done((bf16[4,256,256]{2,1,0:T(8,128)(2,1)S(1)}, bf16[4,256,256]{2,1,0:T(8,128)(2,1)S(1)}, u32[]{:S(2)}, u32[]{:S(2)}) %collective-permute-start.2) | collective-permute-done | bytes 524320 | tf_op jit(solution)/shard_map/ppermute | solution.py:61
  31.8 0.5 collective-permute-start.11
  32.4 0.8 collective-permute-done.9.refs_3_
  33.1 0.6 pad_add_fusion.meta
  33.7 0.1 broadcast_select_fusion.2.refs_1_
  33.8 0.2 collective-permute-done.4.refs_3_
  34.0 1.3 %collective-permute-start.16 = (bf16[4,256,256]{2,1,0:T(8,128)(2,1)S(1)}, bf16[4,256,256]{2,1,0:T(8,128)(2,1)}, u32[]{:S(2)}, u32[]{:S(2)}) collective-permute-start(bf16[4,256,256]{2,1,0:T(8,128)(2,1)S(1)} %collective-permute-done.refs_1_), channel_id=1, source_target_pairs={{0,8},{1,9},{2,10},{3,11},{4,12},{5,13},{6,14},{7,15},{8,0},{9,1},... | collective-permute-start | bytes 1572872 | tf_op jit(solution)/shard_map/ppermute | solution.py:61
  35.4 1.5 %collective-permute-start.5 = (bf16[4,256,256]{2,1,0:T(8,128)(2,1)S(1)}, bf16[4,256,256]{2,1,0:T(8,128)(2,1)}, u32[]{:S(2)}, u32[]{:S(2)}) collective-permute-start(bf16[4,256,256]{2,1,0:T(8,128)(2,1)S(1)} %broadcast_select_fusion.2.refs_1_), channel_id=1, source_target_pairs={{0,16},{1,17},{2,18},{3,19},{4,20},{5,21},{6,22},{7,23},{8,24},{9,... | collective-permute-start | bytes 1572872 | tf_op jit(solution)/shard_map/ppermute | solution.py:61
  36.9 1.3 %collective-permute-start.6 = (bf16[4,256,256]{2,1,0:T(8,128)(2,1)S(1)}, bf16[4,256,256]{2,1,0:T(8,128)(2,1)S(1)}, u32[]{:S(2)}, u32[]{:S(2)}) collective-permute-start(bf16[4,256,256]{2,1,0:T(8,128)(2,1)S(1)} %collective-permute-done.3), channel_id=1, source_target_pairs={{2,0},{3,1},{4,6},{5,7},{10,8},{11,9},{12,14},{13,15},{18,16},{19,... | collective-permute-start | bytes 1572872 | tf_op jit(solution)/shard_map/ppermute | solution.py:61
  38.2 0.8 collective-permute-start.17
  39.0 0.7 collective-permute-start.22
  39.7 11.7 %shard_map.60 = (bf16[10,256,2048]{2,1,0:T(8,128)(2,1)}, f32[4,1024,256]{2,1,0:T(8,128)}, f32[8,128]{1,0:T(8,128)}) custom-call(s32[3]{0:T(128)} %pad_add_fusion.meta, bf16[4,256,1024]{2,1,0:T(8,128)(2,1)} %get-tuple-element.52.sparse, bf16[10,256,2048]{2,1,0:T(8,128)(2,1)} %decoder.7, bf16[4,256,256]{2,1,0:T(8,128)(2,1)} %refs_0_.1, ...), custom_call_target="tpu_custom_call" | custom-call | flops 10737418240 | bytes 20971520 | tf_op jit(solution)/shard_map/pallas_call | solution.py:289
  51.3 3.0 %collective-permute-done.6 = bf16[4,256,256]{2,1,0:T(8,128)(2,1)S(1)} collective-permute-done((bf16[4,256,256]{2,1,0:T(8,128)(2,1)S(1)}, bf16[4,256,256]{2,1,0:T(8,128)(2,1)S(1)}, u32[]{:S(2)}, u32[]{:S(2)}) %collective-permute-start.6) | collective-permute-done | bytes 524320 | tf_op jit(solution)/shard_map/ppermute | solution.py:61
  54.4 0.6 collective-permute-start.20
  55.0 4.5 %collective-permute-done.17.refs_4_ = bf16[4,256,256]{2,1,0:T(8,128)(2,1)} collective-permute-done((bf16[4,256,256]{2,1,0:T(8,128)(2,1)S(1)}, bf16[4,256,256]{2,1,0:T(8,128)(2,1)}, u32[]{:S(2)}, u32[]{:S(2)}) %collective-permute-start.17) | collective-permute-done | bytes 524320 | tf_op jit(solution)/shard_map/ppermute | solution.py:61
  59.6 0.5 collective-permute-start.21
  60.1 1.5 %collective-permute-start.23 = (bf16[4,256,256]{2,1,0:T(8,128)(2,1)S(1)}, bf16[4,256,256]{2,1,0:T(8,128)(2,1)}, u32[]{:S(2)}, u32[]{:S(2)}) collective-permute-start(bf16[4,256,256]{2,1,0:T(8,128)(2,1)S(1)} %broadcast_select_fusion.2.refs_1_), channel_id=1, source_target_pairs={{0,8},{1,9},{2,10},{3,11},{4,12},{5,13},{6,14},{7,15},{8,0},{9,1},... | collective-permute-start | bytes 1572872 | tf_op jit(solution)/shard_map/ppermute | solution.py:61
  61.6 0.5 collective-permute-start.14
  62.1 1.5 %collective-permute-start.15 = (bf16[4,256,256]{2,1,0:T(8,128)(2,1)S(1)}, bf16[4,256,256]{2,1,0:T(8,128)(2,1)S(1)}, u32[]{:S(2)}, u32[]{:S(2)}) collective-permute-start(bf16[4,256,256]{2,1,0:T(8,128)(2,1)S(1)} %broadcast_select_fusion.1.refs_2_), channel_id=1, source_target_pairs={{0,16},{1,17},{2,18},{3,19},{4,20},{5,21},{6,22},{7,23},{8,24},{9,... | collective-permute-start | bytes 1572872 | tf_op jit(solution)/shard_map/ppermute | solution.py:61
  63.6 1.5 %collective-permute-start.24 = (bf16[4,256,256]{2,1,0:T(8,128)(2,1)S(1)}, bf16[4,256,256]{2,1,0:T(8,128)(2,1)S(1)}, u32[]{:S(2)}, u32[]{:S(2)}) collective-permute-start(bf16[4,256,256]{2,1,0:T(8,128)(2,1)S(1)} %collective-permute-done.22), channel_id=1, source_target_pairs={{2,0},{3,1},{4,6},{5,7},{10,8},{11,9},{12,14},{13,15},{18,16},{19,... | collective-permute-start | bytes 1572872 | tf_op jit(solution)/shard_map/ppermute | solution.py:61
  65.1 11.9 %shard_map.61 = (bf16[10,256,2048]{2,1,0:T(8,128)(2,1)}, f32[4,1024,256]{2,1,0:T(8,128)}, f32[8,128]{1,0:T(8,128)}) custom-call(s32[3]{0:T(128)} %pad_add_fusion.meta, bf16[4,256,1024]{2,1,0:T(8,128)(2,1)} %get-tuple-element.52.sparse, bf16[10,256,2048]{2,1,0:T(8,128)(2,1)} %decoder.7, ...), custom_call_target="tpu_custom_call", output_to_operand_aliasing={{0}: (12, {})} | custom-call | flops 10737418240 | bytes 20971520 | tf_op jit(solution)/shard_map/pallas_call | solution.py:289
  77.0 3.3 %collective-permute-done.24 = bf16[4,256,256]{2,1,0:T(8,128)(2,1)S(1)} collective-permute-done((bf16[4,256,256]{2,1,0:T(8,128)(2,1)S(1)}, bf16[4,256,256]{2,1,0:T(8,128)(2,1)S(1)}, u32[]{:S(2)}, u32[]{:S(2)}) %collective-permute-start.24) | collective-permute-done | bytes 524320 | tf_op jit(solution)/shard_map/ppermute | solution.py:61
  80.4 0.1 collective-permute-start.28
  80.5 0.5 collective-permute-start.27
  81.0 0.1 collective-permute-start.26
  81.1 4.1 %collective-permute-done.14.refs_3_ = bf16[4,256,256]{2,1,0:T(8,128)(2,1)S(1)} collective-permute-done((bf16[4,256,256]{2,1,0:T(8,128)(2,1)S(1)}, bf16[4,256,256]{2,1,0:T(8,128)(2,1)S(1)}, u32[]{:S(2)}, u32[]{:S(2)}) %collective-permute-start.14) | collective-permute-done | bytes 524320 | tf_op jit(solution)/shard_map/ppermute | solution.py:61
  85.3 0.5 collective-permute-start.30
  85.8 1.5 %collective-permute-start.29 = (bf16[4,256,256]{2,1,0:T(8,128)(2,1)S(1)}, bf16[4,256,256]{2,1,0:T(8,128)(2,1)S(1)}, u32[]{:S(2)}, u32[]{:S(2)}) collective-permute-start(bf16[4,256,256]{2,1,0:T(8,128)(2,1)S(1)} %collective-permute-done.14.refs_3_), channel_id=1, source_target_pairs={{0,16},{1,17},{2,18},{3,19},{4,20},{5,21},{6,22},{7,23},{8,24},{9,... | collective-permute-start | bytes 1572872 | tf_op jit(solution)/shard_map/ppermute | solution.py:61
  87.3 0.5 collective-permute-start.32
  87.8 0.3 copy-done.11
  88.1 0.2 copy-done.12
  88.3 0.6 copy-done.13
  88.9 11.9 %shard_map.62 = (bf16[10,256,2048]{2,1,0:T(8,128)(2,1)}, f32[4,1024,256]{2,1,0:T(8,128)}, f32[8,128]{1,0:T(8,128)}) custom-call(s32[3]{0:T(128)} %pad_add_fusion.meta, bf16[4,256,1024]{2,1,0:T(8,128)(2,1)} %get-tuple-element.52.sparse, bf16[10,256,2048]{2,1,0:T(8,128)(2,1)} %decoder.7, ...), custom_call_target="tpu_custom_call", output_to_operand_aliasing={{0}: (12, {})} | custom-call | flops 10737418240 | bytes 20971520 | tf_op jit(solution)/shard_map/pallas_call | solution.py:289
  100.8 0.1 collective-permute-start.33
  101.0 1.9 %collective-permute-done.33.refs_9_ = bf16[4,256,256]{2,1,0:T(8,128)(2,1)S(1)} collective-permute-done((bf16[4,256,256]{2,1,0:T(8,128)(2,1)S(1)}, bf16[4,256,256]{2,1,0:T(8,128)(2,1)S(1)}, u32[]{:S(2)}, u32[]{:S(2)}) %collective-permute-start.33) | collective-permute-done | bytes 524320 | tf_op jit(solution)/shard_map/ppermute | solution.py:61
  102.8 0.8 copy-done.14
  103.6 12.3 %shard_map.63 = (bf16[10,256,2048]{2,1,0:T(8,128)(2,1)}, bf16[4,1024,256]{2,1,0:T(8,128)(2,1)}, f32[8,128]{1,0:T(8,128)}) custom-call(s32[3]{0:T(128)} %pad_add_fusion.meta, bf16[4,256,1024]{2,1,0:T(8,128)(2,1)} %get-tuple-element.52.sparse, bf16[10,256,2048]{2,1,0:T(8,128)(2,1)} %decoder.7, ...), custom_call_target="tpu_custom_call", output_to_operand_aliasing={{0}: (13, {})} | custom-call | flops 10737418240 | bytes 20971520 | tf_op jit(solution)/shard_map/pallas_call | solution.py:289
  (59 shorter events, 0.2 us)
Async XLA Ops:
  0.6 14.1 %collective-permute-start.1 = (bf16[4,256,256]{2,1,0:T(8,128)(2,1)}, bf16[4,256,256]{2,1,0:T(8,128)(2,1)S(1)}, u32[]{:S(2)}, u32[]{:S(2)}) collective-permute-start(bf16[4,256,256]{2,1,0:T(8,128)(2,1)} %refs_0_.1), channel_id=1, source_target_pairs={{2,4},{3,5},{4,2},{5,3},{10,12},{11,13},{12,10},{13,11},{18,20},{1... | collective-permute-start | bytes 1572872 | tf_op jit(solution)/shard_map/ppermute | solution.py:61
  1.3 17.7 %collective-permute-start = (bf16[4,256,256]{2,1,0:T(8,128)(2,1)}, bf16[4,256,256]{2,1,0:T(8,128)(2,1)S(1)}, u32[]{:S(2)}, u32[]{:S(2)}) collective-permute-start(bf16[4,256,256]{2,1,0:T(8,128)(2,1)} %refs_0_.1), channel_id=1, source_target_pairs={{0,2},{1,3},{2,0},{3,1},{4,6},{5,7},{6,4},{7,5},{8,10},{9,11},{10,... | collective-permute-start | bytes 1572872 | tf_op jit(solution)/shard_map/ppermute | solution.py:61
  7.2 13.4 %collective-permute-start.8 = (bf16[4,256,256]{2,1,0:T(8,128)(2,1)}, bf16[4,256,256]{2,1,0:T(8,128)(2,1)}, u32[]{:S(2)}, u32[]{:S(2)}) collective-permute-start(bf16[4,256,256]{2,1,0:T(8,128)(2,1)} %refs_0_.1), channel_id=1, source_target_pairs={{0,16},{1,17},{2,18},{3,19},{4,20},{5,21},{6,22},{7,23},{8,24},{9,... | collective-permute-start | bytes 1572872 | tf_op jit(solution)/shard_map/ppermute | solution.py:61
  8.7 14.9 %collective-permute-start.7 = (bf16[4,256,256]{2,1,0:T(8,128)(2,1)}, bf16[4,256,256]{2,1,0:T(8,128)(2,1)}, u32[]{:S(2)}, u32[]{:S(2)}) collective-permute-start(bf16[4,256,256]{2,1,0:T(8,128)(2,1)} %refs_0_.1), channel_id=1, source_target_pairs={{0,8},{1,9},{2,10},{3,11},{4,12},{5,13},{6,14},{7,15},{8,0},{9,1},... | collective-permute-start | bytes 1572872 | tf_op jit(solution)/shard_map/ppermute | solution.py:61
  14.8 17.1 %collective-permute-start.2 = (bf16[4,256,256]{2,1,0:T(8,128)(2,1)S(1)}, bf16[4,256,256]{2,1,0:T(8,128)(2,1)S(1)}, u32[]{:S(2)}, u32[]{:S(2)}) collective-permute-start(bf16[4,256,256]{2,1,0:T(8,128)(2,1)S(1)} %collective-permute-done.1), channel_id=1, source_target_pairs={{2,0},{3,1},{4,6},{5,7},{10,8},{11,9},{12,14},{13,15},{18,16},{19,... | collective-permute-start | bytes 1572872 | tf_op jit(solution)/shard_map/ppermute | solution.py:61
  19.1 35.3 %copy-start.3 = (bf16[4,256,256]{2,1,0:T(8,128)(2,1)}, bf16[4,256,256]{2,1,0:T(8,128)(2,1)S(1)}, u32[]{:S(2)}) copy-start(bf16[4,256,256]{2,1,0:T(8,128)(2,1)S(1)} %collective-permute-done.refs_1_) | copy-start | bytes 1572868
  19.1 12.8 %collective-permute-start.3 = (bf16[4,256,256]{2,1,0:T(8,128)(2,1)S(1)}, bf16[4,256,256]{2,1,0:T(8,128)(2,1)S(1)}, u32[]{:S(2)}, u32[]{:S(2)}) collective-permute-start(bf16[4,256,256]{2,1,0:T(8,128)(2,1)S(1)} %collective-permute-done.refs_1_), channel_id=1, source_target_pairs={{2,4},{3,5},{4,2},{5,3},{10,12},{11,13},{12,10},{13,11},{18,20},{1... | collective-permute-start | bytes 1572872 | tf_op jit(solution)/shard_map/ppermute | solution.py:61
  20.6 12.5 %collective-permute-start.9 = (bf16[4,256,256]{2,1,0:T(8,128)(2,1)}, bf16[4,256,256]{2,1,0:T(8,128)(2,1)}, u32[]{:S(2)}, u32[]{:S(2)}) collective-permute-start(bf16[4,256,256]{2,1,0:T(8,128)(2,1)} %collective-permute-done.8.refs_2_), channel_id=1, source_target_pairs={{0,8},{1,9},{2,10},{3,11},{4,12},{5,13},{6,14},{7,15},{8,0},{9,1},... | collective-permute-start | bytes 1572872 | tf_op jit(solution)/shard_map/ppermute | solution.py:61
  22.1 11.9 %collective-permute-start.4 = (bf16[4,256,256]{2,1,0:T(8,128)(2,1)S(1)}, bf16[4,256,256]{2,1,0:T(8,128)(2,1)S(1)}, u32[]{:S(2)}, u32[]{:S(2)}) collective-permute-start(bf16[4,256,256]{2,1,0:T(8,128)(2,1)S(1)} %collective-permute-done.refs_1_), channel_id=1, source_target_pairs={{0,16},{1,17},{2,18},{3,19},{4,20},{5,21},{6,22},{7,23},{8,24},{9,... | collective-permute-start | bytes 1572872 | tf_op jit(solution)/shard_map/ppermute | solution.py:61
  23.6 11.7 %collective-permute-start.10 = (bf16[4,256,256]{2,1,0:T(8,128)(2,1)}, bf16[4,256,256]{2,1,0:T(8,128)(2,1)}, u32[]{:S(2)}, u32[]{:S(2)}) collective-permute-start(bf16[4,256,256]{2,1,0:T(8,128)(2,1)} %refs_0_.1), channel_id=1, source_target_pairs={{0,1},{1,0},{2,3},{3,2},{4,5},{5,4},{6,7},{7,6},{8,9},{9,8},{10,11... | collective-permute-start | bytes 1572872 | tf_op jit(solution)/shard_map/ppermute | solution.py:61
  31.8 5.1 %collective-permute-start.12 = (bf16[4,256,256]{2,1,0:T(8,128)(2,1)}, bf16[4,256,256]{2,1,0:T(8,128)(2,1)}, u32[]{:S(2)}, u32[]{:S(2)}) collective-permute-start(bf16[4,256,256]{2,1,0:T(8,128)(2,1)} %collective-permute-done.8.refs_2_), channel_id=1, source_target_pairs={{0,1},{1,0},{2,3},{3,2},{4,5},{5,4},{6,7},{7,6},{8,9},{9,8},{10,11... | collective-permute-start | bytes 1572872 | tf_op jit(solution)/shard_map/ppermute | solution.py:61
  31.8 6.3 %collective-permute-start.11 = (bf16[4,256,256]{2,1,0:T(8,128)(2,1)}, bf16[4,256,256]{2,1,0:T(8,128)(2,1)}, u32[]{:S(2)}, u32[]{:S(2)}) collective-permute-start(bf16[4,256,256]{2,1,0:T(8,128)(2,1)} %collective-permute-done.7.refs_1_), channel_id=1, source_target_pairs={{0,1},{1,0},{2,3},{3,2},{4,5},{5,4},{6,7},{7,6},{8,9},{9,8},{10,11... | collective-permute-start | bytes 1572872 | tf_op jit(solution)/shard_map/ppermute | solution.py:61
  33.1 5.8 %collective-permute-start.13 = (bf16[4,256,256]{2,1,0:T(8,128)(2,1)}, bf16[4,256,256]{2,1,0:T(8,128)(2,1)}, u32[]{:S(2)}, u32[]{:S(2)}) collective-permute-start(bf16[4,256,256]{2,1,0:T(8,128)(2,1)} %collective-permute-done.9.refs_3_), channel_id=1, source_target_pairs={{0,1},{1,0},{2,3},{3,2},{4,5},{5,4},{6,7},{7,6},{8,9},{9,8},{10,11... | collective-permute-start | bytes 1572872 | tf_op jit(solution)/shard_map/ppermute | solution.py:61
  33.8 51.4 %copy-start = (bf16[4,256,256]{2,1,0:T(8,128)(2,1)}, bf16[4,256,256]{2,1,0:T(8,128)(2,1)S(1)}, u32[]{:S(2)}) copy-start(bf16[4,256,256]{2,1,0:T(8,128)(2,1)S(1)} %broadcast_select_fusion.2.refs_1_) | copy-start | bytes 1572868
  34.0 20.4 %copy-start.4 = (bf16[4,256,256]{2,1,0:T(8,128)(2,1)}, bf16[4,256,256]{2,1,0:T(8,128)(2,1)S(1)}, u32[]{:S(2)}) copy-start(bf16[4,256,256]{2,1,0:T(8,128)(2,1)S(1)} %collective-permute-done.4.refs_3_) | copy-start | bytes 1572868
  34.0 20.4 %collective-permute-start.16 = (bf16[4,256,256]{2,1,0:T(8,128)(2,1)S(1)}, bf16[4,256,256]{2,1,0:T(8,128)(2,1)}, u32[]{:S(2)}, u32[]{:S(2)}) collective-permute-start(bf16[4,256,256]{2,1,0:T(8,128)(2,1)S(1)} %collective-permute-done.refs_1_), channel_id=1, source_target_pairs={{0,8},{1,9},{2,10},{3,11},{4,12},{5,13},{6,14},{7,15},{8,0},{9,1},... | collective-permute-start | bytes 1572872 | tf_op jit(solution)/shard_map/ppermute | solution.py:61
  35.4 24.7 %collective-permute-start.5 = (bf16[4,256,256]{2,1,0:T(8,128)(2,1)S(1)}, bf16[4,256,256]{2,1,0:T(8,128)(2,1)}, u32[]{:S(2)}, u32[]{:S(2)}) collective-permute-start(bf16[4,256,256]{2,1,0:T(8,128)(2,1)S(1)} %broadcast_select_fusion.2.refs_1_), channel_id=1, source_target_pairs={{0,16},{1,17},{2,18},{3,19},{4,20},{5,21},{6,22},{7,23},{8,24},{9,... | collective-permute-start | bytes 1572872 | tf_op jit(solution)/shard_map/ppermute | solution.py:61
  36.9 17.4 %collective-permute-start.6 = (bf16[4,256,256]{2,1,0:T(8,128)(2,1)S(1)}, bf16[4,256,256]{2,1,0:T(8,128)(2,1)S(1)}, u32[]{:S(2)}, u32[]{:S(2)}) collective-permute-start(bf16[4,256,256]{2,1,0:T(8,128)(2,1)S(1)} %collective-permute-done.3), channel_id=1, source_target_pairs={{2,0},{3,1},{4,6},{5,7},{10,8},{11,9},{12,14},{13,15},{18,16},{19,... | collective-permute-start | bytes 1572872 | tf_op jit(solution)/shard_map/ppermute | solution.py:61
  38.2 21.4 %collective-permute-start.17 = (bf16[4,256,256]{2,1,0:T(8,128)(2,1)S(1)}, bf16[4,256,256]{2,1,0:T(8,128)(2,1)}, u32[]{:S(2)}, u32[]{:S(2)}) collective-permute-start(bf16[4,256,256]{2,1,0:T(8,128)(2,1)S(1)} %collective-permute-done.4.refs_3_), channel_id=1, source_target_pairs={{0,8},{1,9},{2,10},{3,11},{4,12},{5,13},{6,14},{7,15},{8,0},{9,1},... | collective-permute-start | bytes 1572872 | tf_op jit(solution)/shard_map/ppermute | solution.py:61
  39.0 20.6 %collective-permute-start.22 = (bf16[4,256,256]{2,1,0:T(8,128)(2,1)}, bf16[4,256,256]{2,1,0:T(8,128)(2,1)S(1)}, u32[]{:S(2)}, u32[]{:S(2)}) collective-permute-start(bf16[4,256,256]{2,1,0:T(8,128)(2,1)} %collective-permute-done.9.refs_3_), channel_id=1, source_target_pairs={{2,4},{3,5},{4,2},{5,3},{10,12},{11,13},{12,10},{13,11},{18,20},{1... | collective-permute-start | bytes 1572872 | tf_op jit(solution)/shard_map/ppermute | solution.py:61
  54.3 7.2 %collective-permute-start.18 = (bf16[4,256,256]{2,1,0:T(8,128)(2,1)S(1)}, bf16[4,256,256]{2,1,0:T(8,128)(2,1)S(1)}, u32[]{:S(2)}, u32[]{:S(2)}) collective-permute-start(bf16[4,256,256]{2,1,0:T(8,128)(2,1)S(1)} %collective-permute-done.refs_1_), channel_id=1, source_target_pairs={{0,1},{1,0},{2,3},{3,2},{4,5},{5,4},{6,7},{7,6},{8,9},{9,8},{10,11... | collective-permute-start | bytes 1572872 | tf_op jit(solution)/shard_map/ppermute | solution.py:61
  54.4 30.8 %copy-start.1 = (bf16[4,256,256]{2,1,0:T(8,128)(2,1)}, bf16[4,256,256]{2,1,0:T(8,128)(2,1)S(1)}, u32[]{:S(2)}) copy-start(bf16[4,256,256]{2,1,0:T(8,128)(2,1)S(1)} %broadcast_select_fusion.1.refs_2_) | copy-start | bytes 1572868
  54.4 7.7 %collective-permute-start.20 = (bf16[4,256,256]{2,1,0:T(8,128)(2,1)S(1)}, bf16[4,256,256]{2,1,0:T(8,128)(2,1)S(1)}, u32[]{:S(2)}, u32[]{:S(2)}) collective-permute-start(bf16[4,256,256]{2,1,0:T(8,128)(2,1)S(1)} %collective-permute-done.4.refs_3_), channel_id=1, source_target_pairs={{0,1},{1,0},{2,3},{3,2},{4,5},{5,4},{6,7},{7,6},{8,9},{9,8},{10,11... | collective-permute-start | bytes 1572872 | tf_op jit(solution)/shard_map/ppermute | solution.py:61
  59.6 4.1 %collective-permute-start.19 = (bf16[4,256,256]{2,1,0:T(8,128)(2,1)}, bf16[4,256,256]{2,1,0:T(8,128)(2,1)}, u32[]{:S(2)}, u32[]{:S(2)}) collective-permute-start(bf16[4,256,256]{2,1,0:T(8,128)(2,1)} %collective-permute-done.16.refs_2_), channel_id=1, source_target_pairs={{0,1},{1,0},{2,3},{3,2},{4,5},{5,4},{6,7},{7,6},{8,9},{9,8},{10,11... | collective-permute-start | bytes 1572872 | tf_op jit(solution)/shard_map/ppermute | solution.py:61
  59.6 5.5 %collective-permute-start.21 = (bf16[4,256,256]{2,1,0:T(8,128)(2,1)}, bf16[4,256,256]{2,1,0:T(8,128)(2,1)}, u32[]{:S(2)}, u32[]{:S(2)}) collective-permute-start(bf16[4,256,256]{2,1,0:T(8,128)(2,1)} %collective-permute-done.17.refs_4_), channel_id=1, source_target_pairs={{0,1},{1,0},{2,3},{3,2},{4,5},{5,4},{6,7},{7,6},{8,9},{9,8},{10,11... | collective-permute-start | bytes 1572872 | tf_op jit(solution)/shard_map/ppermute | solution.py:61
  60.1 20.9 %collective-permute-start.23 = (bf16[4,256,256]{2,1,0:T(8,128)(2,1)S(1)}, bf16[4,256,256]{2,1,0:T(8,128)(2,1)}, u32[]{:S(2)}, u32[]{:S(2)}) collective-permute-start(bf16[4,256,256]{2,1,0:T(8,128)(2,1)S(1)} %broadcast_select_fusion.2.refs_1_), channel_id=1, source_target_pairs={{0,8},{1,9},{2,10},{3,11},{4,12},{5,13},{6,14},{7,15},{8,0},{9,1},... | collective-permute-start | bytes 1572872 | tf_op jit(solution)/shard_map/ppermute | solution.py:61
  61.6 2.1 %copy-start.8 = (bf16[4,256,256]{2,1,0:T(8,128)(2,1)}, bf16[4,256,256]{2,1,0:T(8,128)(2,1)S(1)}, u32[]{:S(2)}) copy-start(bf16[4,256,256]{2,1,0:T(8,128)(2,1)S(1)} %collective-permute-done.18.refs_5_) | copy-start | bytes 1572868
  61.6 23.6 %collective-permute-start.14 = (bf16[4,256,256]{2,1,0:T(8,128)(2,1)S(1)}, bf16[4,256,256]{2,1,0:T(8,128)(2,1)S(1)}, u32[]{:S(2)}, u32[]{:S(2)}) collective-permute-start(bf16[4,256,256]{2,1,0:T(8,128)(2,1)S(1)} %broadcast_select_fusion.1.refs_2_), channel_id=1, source_target_pairs={{0,8},{1,9},{2,10},{3,11},{4,12},{5,13},{6,14},{7,15},{8,0},{9,1},... | collective-permute-start | bytes 1572872 | tf_op jit(solution)/shard_map/ppermute | solution.py:61
  62.1 3.0 %copy-start.10 = (bf16[4,256,256]{2,1,0:T(8,128)(2,1)}, bf16[4,256,256]{2,1,0:T(8,128)(2,1)S(1)}, u32[]{:S(2)}) copy-start(bf16[4,256,256]{2,1,0:T(8,128)(2,1)S(1)} %collective-permute-done.20.refs_7_) | copy-start | bytes 1572868
  62.1 23.1 %collective-permute-start.15 = (bf16[4,256,256]{2,1,0:T(8,128)(2,1)S(1)}, bf16[4,256,256]{2,1,0:T(8,128)(2,1)S(1)}, u32[]{:S(2)}, u32[]{:S(2)}) collective-permute-start(bf16[4,256,256]{2,1,0:T(8,128)(2,1)S(1)} %broadcast_select_fusion.1.refs_2_), channel_id=1, source_target_pairs={{0,16},{1,17},{2,18},{3,19},{4,20},{5,21},{6,22},{7,23},{8,24},{9,... | collective-permute-start | bytes 1572872 | tf_op jit(solution)/shard_map/ppermute | solution.py:61
  63.6 16.7 %collective-permute-start.24 = (bf16[4,256,256]{2,1,0:T(8,128)(2,1)S(1)}, bf16[4,256,256]{2,1,0:T(8,128)(2,1)S(1)}, u32[]{:S(2)}, u32[]{:S(2)}) collective-permute-start(bf16[4,256,256]{2,1,0:T(8,128)(2,1)S(1)} %collective-permute-done.22), channel_id=1, source_target_pairs={{2,0},{3,1},{4,6},{5,7},{10,8},{11,9},{12,14},{13,15},{18,16},{19,... | collective-permute-start | bytes 1572872 | tf_op jit(solution)/shard_map/ppermute | solution.py:61
  80.4 8.5 %copy-start.2 = (bf16[4,256,256]{2,1,0:T(8,128)(2,1)}, bf16[4,256,256]{2,1,0:T(8,128)(2,1)S(1)}, u32[]{:S(2)}) copy-start(bf16[4,256,256]{2,1,0:T(8,128)(2,1)S(1)} %broadcast_select_fusion.refs_4_) | copy-start | bytes 1572868
  80.4 5.4 %collective-permute-start.28 = (bf16[4,256,256]{2,1,0:T(8,128)(2,1)S(1)}, bf16[4,256,256]{2,1,0:T(8,128)(2,1)}, u32[]{:S(2)}, u32[]{:S(2)}) collective-permute-start(bf16[4,256,256]{2,1,0:T(8,128)(2,1)S(1)} %broadcast_select_fusion.refs_4_), channel_id=1, source_target_pairs={{0,1},{1,0},{2,3},{3,2},{4,5},{5,4},{6,7},{7,6},{8,9},{9,8},{10,11... | collective-permute-start | bytes 1572872 | tf_op jit(solution)/shard_map/ppermute | solution.py:61
  80.5 6.8 %collective-permute-start.27 = (bf16[4,256,256]{2,1,0:T(8,128)(2,1)}, bf16[4,256,256]{2,1,0:T(8,128)(2,1)S(1)}, u32[]{:S(2)}, u32[]{:S(2)}) collective-permute-start(bf16[4,256,256]{2,1,0:T(8,128)(2,1)} %collective-permute-done.5.refs_3_), channel_id=1, source_target_pairs={{0,1},{1,0},{2,3},{3,2},{4,5},{5,4},{6,7},{7,6},{8,9},{9,8},{10,11... | collective-permute-start | bytes 1572872 | tf_op jit(solution)/shard_map/ppermute | solution.py:61
  81.0 6.3 %collective-permute-start.26 = (bf16[4,256,256]{2,1,0:T(8,128)(2,1)}, bf16[4,256,256]{2,1,0:T(8,128)(2,1)S(1)}, u32[]{:S(2)}, u32[]{:S(2)}) collective-permute-start(bf16[4,256,256]{2,1,0:T(8,128)(2,1)} %collective-permute-done.23.refs_2_), channel_id=1, source_target_pairs={{0,1},{1,0},{2,3},{3,2},{4,5},{5,4},{6,7},{7,6},{8,9},{9,8},{10,11... | collective-permute-start | bytes 1572872 | tf_op jit(solution)/shard_map/ppermute | solution.py:61
  85.2 15.6 %copy-start.5 = (bf16[4,256,256]{2,1,0:T(8,128)(2,1)}, bf16[4,256,256]{2,1,0:T(8,128)(2,1)S(1)}, u32[]{:S(2)}) copy-start(bf16[4,256,256]{2,1,0:T(8,128)(2,1)S(1)} %collective-permute-done.14.refs_3_) | copy-start | bytes 1572868
  85.2 2.6 %collective-permute-start.25 = (bf16[4,256,256]{2,1,0:T(8,128)(2,1)S(1)}, bf16[4,256,256]{2,1,0:T(8,128)(2,1)S(1)}, u32[]{:S(2)}, u32[]{:S(2)}) collective-permute-start(bf16[4,256,256]{2,1,0:T(8,128)(2,1)S(1)} %broadcast_select_fusion.2.refs_1_), channel_id=1, source_target_pairs={{0,1},{1,0},{2,3},{3,2},{4,5},{5,4},{6,7},{7,6},{8,9},{9,8},{10,11... | collective-permute-start | bytes 1572872 | tf_op jit(solution)/shard_map/ppermute | solution.py:61
  85.2 15.6 %copy-start.6 = (bf16[4,256,256]{2,1,0:T(8,128)(2,1)}, bf16[4,256,256]{2,1,0:T(8,128)(2,1)S(1)}, u32[]{:S(2)}) copy-start(bf16[4,256,256]{2,1,0:T(8,128)(2,1)S(1)} %collective-permute-done.15.refs_4_) | copy-start | bytes 1572868
  85.3 15.7 %collective-permute-start.30 = (bf16[4,256,256]{2,1,0:T(8,128)(2,1)S(1)}, bf16[4,256,256]{2,1,0:T(8,128)(2,1)S(1)}, u32[]{:S(2)}, u32[]{:S(2)}) collective-permute-start(bf16[4,256,256]{2,1,0:T(8,128)(2,1)S(1)} %broadcast_select_fusion.1.refs_2_), channel_id=1, source_target_pairs={{0,1},{1,0},{2,3},{3,2},{4,5},{5,4},{6,7},{7,6},{8,9},{9,8},{10,11... | collective-permute-start | bytes 1572872 | tf_op jit(solution)/shard_map/ppermute | solution.py:61
  85.8 15.0 %collective-permute-start.29 = (bf16[4,256,256]{2,1,0:T(8,128)(2,1)S(1)}, bf16[4,256,256]{2,1,0:T(8,128)(2,1)S(1)}, u32[]{:S(2)}, u32[]{:S(2)}) collective-permute-start(bf16[4,256,256]{2,1,0:T(8,128)(2,1)S(1)} %collective-permute-done.14.refs_3_), channel_id=1, source_target_pairs={{0,16},{1,17},{2,18},{3,19},{4,20},{5,21},{6,22},{7,23},{8,24},{9,... | collective-permute-start | bytes 1572872 | tf_op jit(solution)/shard_map/ppermute | solution.py:61
  87.3 0.8 copy-start.11
  87.3 13.6 %collective-permute-start.31 = (bf16[4,256,256]{2,1,0:T(8,128)(2,1)S(1)}, bf16[4,256,256]{2,1,0:T(8,128)(2,1)}, u32[]{:S(2)}, u32[]{:S(2)}) collective-permute-start(bf16[4,256,256]{2,1,0:T(8,128)(2,1)S(1)} %collective-permute-done.14.refs_3_), channel_id=1, source_target_pairs={{0,1},{1,0},{2,3},{3,2},{4,5},{5,4},{6,7},{7,6},{8,9},{9,8},{10,11... | collective-permute-start | bytes 1572872 | tf_op jit(solution)/shard_map/ppermute | solution.py:61
  87.3 0.9 copy-start.12
  87.3 13.6 %collective-permute-start.32 = (bf16[4,256,256]{2,1,0:T(8,128)(2,1)S(1)}, bf16[4,256,256]{2,1,0:T(8,128)(2,1)}, u32[]{:S(2)}, u32[]{:S(2)}) collective-permute-start(bf16[4,256,256]{2,1,0:T(8,128)(2,1)S(1)} %collective-permute-done.15.refs_4_), channel_id=1, source_target_pairs={{0,1},{1,0},{2,3},{3,2},{4,5},{5,4},{6,7},{7,6},{8,9},{9,8},{10,11... | collective-permute-start | bytes 1572872 | tf_op jit(solution)/shard_map/ppermute | solution.py:61
  100.8 2.0 %copy-start.9 = (bf16[4,256,256]{2,1,0:T(8,128)(2,1)}, bf16[4,256,256]{2,1,0:T(8,128)(2,1)S(1)}, u32[]{:S(2)}) copy-start(bf16[4,256,256]{2,1,0:T(8,128)(2,1)S(1)} %collective-permute-done.29.refs_5_) | copy-start | bytes 1572868
  100.8 2.0 %collective-permute-start.33 = (bf16[4,256,256]{2,1,0:T(8,128)(2,1)S(1)}, bf16[4,256,256]{2,1,0:T(8,128)(2,1)S(1)}, u32[]{:S(2)}, u32[]{:S(2)}) collective-permute-start(bf16[4,256,256]{2,1,0:T(8,128)(2,1)S(1)} %collective-permute-done.29.refs_5_), channel_id=1, source_target_pairs={{0,1},{1,0},{2,3},{3,2},{4,5},{5,4},{6,7},{7,6},{8,9},{9,8},{10,11... | collective-permute-start | bytes 1572872 | tf_op jit(solution)/shard_map/ppermute | solution.py:61
  100.9 1.9 %copy-start.7 = (bf16[4,256,256]{2,1,0:T(8,128)(2,1)}, bf16[4,256,256]{2,1,0:T(8,128)(2,1)S(1)}, u32[]{:S(2)}) copy-start(bf16[4,256,256]{2,1,0:T(8,128)(2,1)S(1)} %collective-permute-done.30.refs_6_) | copy-start | bytes 1572868
  102.8 0.8 copy-start.14
  (1 other events, 0.8 us)

commit v13 on v12

--- a/solution.py
+++ b/solution.py
@@ -258,9 +258,11 @@
                     feat_v[source, part] = total.astype(jnp.bfloat16)
                 else:
                     acc_v[source, part] = total
-        for source in group:
+            some = pl.ds(low, len(group))
             out = pltpu.make_async_copy(
-                (feat_v if last else acc_v).at[source], acc_out.at[source], out_sem.at[source]
+                (feat_v if last else acc_v).at[some, part],
+                acc_out.at[some, part],
+                out_sem.at[low, at // CHUNK],
             )
             out.start()
             outs.append(out)
@@ -307,7 +309,7 @@
             pltpu.SemaphoreType.DMA((pairs,)),
             pltpu.SemaphoreType.DMA((1 + layers,)),
             pltpu.SemaphoreType.DMA((layers,)),
-            pltpu.SemaphoreType.DMA((layers,)),
+            pltpu.SemaphoreType.DMA((layers, rows // CHUNK)),
         ],
         input_output_aliases=aliases,
         cost_estimate=pl.CostEstimate(

time: 118 us -> 117 us (level)
  Pallas kernels: 52.2 us -> 50.9 us
    pallas_call x4, Pallas kernels: 47.7 us -> 46.3 us  [run_round(): pl.pallas_call(functools.partial(round_kernel, len(mine), len(tokens), la...]
where the time goes in v13:
time: 117 us; the launch traced here: 116 us
  Pallas kernels  50.9 us (44%)
  waiting for transfers between devices  30.8 us (26%)
  starting transfers between devices  30 us (26%)
  local copies, waits for them, and re-layouts  1.92 us (2%)
    pallas_call x4, Pallas kernels, run_round(): pl.pallas_call(functools.partial(round_kernel, len(mine), len(tokens), la...  46.3 us
    ppermute x34, waiting for transfers between devices, permute(): return lax.ppermute(x, ('layer', 'feat'), sorted(flat))  30.8 us
    ppermute x34, starting transfers between devices, permute(): return lax.ppermute(x, ('layer', 'feat'), sorted(flat))  30 us
    pallas_call x1, Pallas kernels, prepare(): pl.pallas_call(prepare_kernel, grid=(layers,), in_specs=[block(rows, widt...  4.55 us
  transfers between devices with their start and end apart: 34, of which 10 were waited for; matrix products, arithmetic and copies ran while one was open for 1% of the time, Pallas kernels for 34%

profile of v13, /device:TPU:0, one launch (start us, length us, event | category | flops | bytes accessed | tf_op | source)
XLA Modules:
  0.0 115.5 jit_solution(6042329487842334656)
XLA Ops:
  0.6 0.7 collective-permute-start.1
  1.3 5.9 %collective-permute-start = (bf16[4,256,256]{2,1,0:T(8,128)(2,1)}, bf16[4,256,256]{2,1,0:T(8,128)(2,1)S(1)}, u32[]{:S(2)}, u32[]{:S(2)}) collective-permute-start(bf16[4,256,256]{2,1,0:T(8,128)(2,1)} %refs_0_.1), channel_id=1, source_target_pairs={{0,2},{1,3},{2,0},{3,1},{4,6},{5,7},{6,4},{7,5},{8,10},{9,11},{10,... | collective-permute-start | bytes 1572872 | tf_op jit(solution)/shard_map/ppermute | solution.py:61
  7.2 1.5 %collective-permute-start.8 = (bf16[4,256,256]{2,1,0:T(8,128)(2,1)}, bf16[4,256,256]{2,1,0:T(8,128)(2,1)}, u32[]{:S(2)}, u32[]{:S(2)}) collective-permute-start(bf16[4,256,256]{2,1,0:T(8,128)(2,1)} %refs_0_.1), channel_id=1, source_target_pairs={{0,16},{1,17},{2,18},{3,19},{4,20},{5,21},{6,22},{7,23},{8,24},{9,... | collective-permute-start | bytes 1572872 | tf_op jit(solution)/shard_map/ppermute | solution.py:61
  8.7 1.5 %collective-permute-start.7 = (bf16[4,256,256]{2,1,0:T(8,128)(2,1)}, bf16[4,256,256]{2,1,0:T(8,128)(2,1)}, u32[]{:S(2)}, u32[]{:S(2)}) collective-permute-start(bf16[4,256,256]{2,1,0:T(8,128)(2,1)} %refs_0_.1), channel_id=1, source_target_pairs={{0,8},{1,9},{2,10},{3,11},{4,12},{5,13},{6,14},{7,15},{8,0},{9,1},... | collective-permute-start | bytes 1572872 | tf_op jit(solution)/shard_map/ppermute | solution.py:61
  10.2 4.5 %shard_map.59 = (bf16[4,256,1024]{2,1,0:T(8,128)(2,1)}, bf16[4,1024,256]{2,1,0:T(8,128)(2,1)}) custom-call(bf16[4,1024,256]{2,1,0:T(8,128)(2,1)} %act.1, s32[4,2,1024]{2,1,0:T(2,128)} %bitcast.4), custom_call_target="tpu_custom_call" | custom-call | bytes 6291456 | tf_op jit(solution)/shard_map/pallas_call | solution.py:121
  14.8 1.3 %collective-permute-start.2 = (bf16[4,256,256]{2,1,0:T(8,128)(2,1)S(1)}, bf16[4,256,256]{2,1,0:T(8,128)(2,1)S(1)}, u32[]{:S(2)}, u32[]{:S(2)}) collective-permute-start(bf16[4,256,256]{2,1,0:T(8,128)(2,1)S(1)} %collective-permute-done.1), channel_id=1, source_target_pairs={{2,0},{3,1},{4,6},{5,7},{10,8},{11,9},{12,14},{13,15},{18,16},{19,... | collective-permute-start | bytes 1572872 | tf_op jit(solution)/shard_map/ppermute | solution.py:61
  16.1 3.0 %collective-permute-done.refs_1_ = bf16[4,256,256]{2,1,0:T(8,128)(2,1)S(1)} collective-permute-done((bf16[4,256,256]{2,1,0:T(8,128)(2,1)}, bf16[4,256,256]{2,1,0:T(8,128)(2,1)S(1)}, u32[]{:S(2)}, u32[]{:S(2)}) %collective-permute-start) | collective-permute-done | bytes 524320 | tf_op jit(solution)/shard_map/ppermute | solution.py:61
  19.1 0.7 collective-permute-start.3
  19.8 0.9 collective-permute-done.8.refs_2_
  20.6 1.5 %collective-permute-start.9 = (bf16[4,256,256]{2,1,0:T(8,128)(2,1)}, bf16[4,256,256]{2,1,0:T(8,128)(2,1)}, u32[]{:S(2)}, u32[]{:S(2)}) collective-permute-start(bf16[4,256,256]{2,1,0:T(8,128)(2,1)} %collective-permute-done.8.refs_2_), channel_id=1, source_target_pairs={{0,8},{1,9},{2,10},{3,11},{4,12},{5,13},{6,14},{7,15},{8,0},{9,1},... | collective-permute-start | bytes 1572872 | tf_op jit(solution)/shard_map/ppermute | solution.py:61
  22.1 1.5 %collective-permute-start.4 = (bf16[4,256,256]{2,1,0:T(8,128)(2,1)S(1)}, bf16[4,256,256]{2,1,0:T(8,128)(2,1)S(1)}, u32[]{:S(2)}, u32[]{:S(2)}) collective-permute-start(bf16[4,256,256]{2,1,0:T(8,128)(2,1)S(1)} %collective-permute-done.refs_1_), channel_id=1, source_target_pairs={{0,16},{1,17},{2,18},{3,19},{4,20},{5,21},{6,22},{7,23},{8,24},{9,... | collective-permute-start | bytes 1572872 | tf_op jit(solution)/shard_map/ppermute | solution.py:61
  23.7 8.2 %collective-permute-done.2 = bf16[4,256,256]{2,1,0:T(8,128)(2,1)S(1)} collective-permute-done((bf16[4,256,256]{2,1,0:T(8,128)(2,1)S(1)}, bf16[4,256,256]{2,1,0:T(8,128)(2,1)S(1)}, u32[]{:S(2)}, u32[]{:S(2)}) %collective-permute-start.2) | collective-permute-done | bytes 524320 | tf_op jit(solution)/shard_map/ppermute | solution.py:61
  31.8 0.5 collective-permute-start.11
  32.4 0.8 collective-permute-done.9.refs_3_
  33.1 0.6 pad_add_fusion.meta
  33.7 0.1 broadcast_select_fusion.2.refs_1_
  33.8 0.2 collective-permute-done.4.refs_3_
  34.0 1.3 %collective-permute-start.16 = (bf16[4,256,256]{2,1,0:T(8,128)(2,1)S(1)}, bf16[4,256,256]{2,1,0:T(8,128)(2,1)}, u32[]{:S(2)}, u32[]{:S(2)}) collective-permute-start(bf16[4,256,256]{2,1,0:T(8,128)(2,1)S(1)} %collective-permute-done.refs_1_), channel_id=1, source_target_pairs={{0,8},{1,9},{2,10},{3,11},{4,12},{5,13},{6,14},{7,15},{8,0},{9,1},... | collective-permute-start | bytes 1572872 | tf_op jit(solution)/shard_map/ppermute | solution.py:61
  35.4 1.5 %collective-permute-start.5 = (bf16[4,256,256]{2,1,0:T(8,128)(2,1)S(1)}, bf16[4,256,256]{2,1,0:T(8,128)(2,1)}, u32[]{:S(2)}, u32[]{:S(2)}) collective-permute-start(bf16[4,256,256]{2,1,0:T(8,128)(2,1)S(1)} %broadcast_select_fusion.2.refs_1_), channel_id=1, source_target_pairs={{0,16},{1,17},{2,18},{3,19},{4,20},{5,21},{6,22},{7,23},{8,24},{9,... | collective-permute-start | bytes 1572872 | tf_op jit(solution)/shard_map/ppermute | solution.py:61
  36.9 1.3 %collective-permute-start.6 = (bf16[4,256,256]{2,1,0:T(8,128)(2,1)S(1)}, bf16[4,256,256]{2,1,0:T(8,128)(2,1)S(1)}, u32[]{:S(2)}, u32[]{:S(2)}) collective-permute-start(bf16[4,256,256]{2,1,0:T(8,128)(2,1)S(1)} %collective-permute-done.3), channel_id=1, source_target_pairs={{2,0},{3,1},{4,6},{5,7},{10,8},{11,9},{12,14},{13,15},{18,16},{19,... | collective-permute-start | bytes 1572872 | tf_op jit(solution)/shard_map/ppermute | solution.py:61
  38.2 0.8 collective-permute-start.17
  39.0 0.7 collective-permute-start.22
  39.7 11.3 %shard_map.60 = (bf16[10,256,2048]{2,1,0:T(8,128)(2,1)}, f32[4,1024,256]{2,1,0:T(8,128)}, f32[8,128]{1,0:T(8,128)}) custom-call(s32[3]{0:T(128)} %pad_add_fusion.meta, bf16[4,256,1024]{2,1,0:T(8,128)(2,1)} %get-tuple-element.52.sparse, bf16[10,256,2048]{2,1,0:T(8,128)(2,1)} %decoder.7, bf16[4,256,256]{2,1,0:T(8,128)(2,1)} %refs_0_.1, ...), custom_call_target="tpu_custom_call" | custom-call | flops 10737418240 | bytes 20971520 | tf_op jit(solution)/shard_map/pallas_call | solution.py:291
  50.9 3.4 %collective-permute-done.6 = bf16[4,256,256]{2,1,0:T(8,128)(2,1)S(1)} collective-permute-done((bf16[4,256,256]{2,1,0:T(8,128)(2,1)S(1)}, bf16[4,256,256]{2,1,0:T(8,128)(2,1)S(1)}, u32[]{:S(2)}, u32[]{:S(2)}) %collective-permute-start.6) | collective-permute-done | bytes 524320 | tf_op jit(solution)/shard_map/ppermute | solution.py:61
  54.4 0.6 collective-permute-start.20
  55.0 4.5 %collective-permute-done.17.refs_4_ = bf16[4,256,256]{2,1,0:T(8,128)(2,1)} collective-permute-done((bf16[4,256,256]{2,1,0:T(8,128)(2,1)S(1)}, bf16[4,256,256]{2,1,0:T(8,128)(2,1)}, u32[]{:S(2)}, u32[]{:S(2)}) %collective-permute-start.17) | collective-permute-done | bytes 524320 | tf_op jit(solution)/shard_map/ppermute | solution.py:61
  59.6 0.5 collective-permute-start.21
  60.1 1.5 %collective-permute-start.23 = (bf16[4,256,256]{2,1,0:T(8,128)(2,1)S(1)}, bf16[4,256,256]{2,1,0:T(8,128)(2,1)}, u32[]{:S(2)}, u32[]{:S(2)}) collective-permute-start(bf16[4,256,256]{2,1,0:T(8,128)(2,1)S(1)} %broadcast_select_fusion.2.refs_1_), channel_id=1, source_target_pairs={{0,8},{1,9},{2,10},{3,11},{4,12},{5,13},{6,14},{7,15},{8,0},{9,1},... | collective-permute-start | bytes 1572872 | tf_op jit(solution)/shard_map/ppermute | solution.py:61
  61.6 0.5 collective-permute-start.14
  62.1 1.5 %collective-permute-start.15 = (bf16[4,256,256]{2,1,0:T(8,128)(2,1)S(1)}, bf16[4,256,256]{2,1,0:T(8,128)(2,1)S(1)}, u32[]{:S(2)}, u32[]{:S(2)}) collective-permute-start(bf16[4,256,256]{2,1,0:T(8,128)(2,1)S(1)} %broadcast_select_fusion.1.refs_2_), channel_id=1, source_target_pairs={{0,16},{1,17},{2,18},{3,19},{4,20},{5,21},{6,22},{7,23},{8,24},{9,... | collective-permute-start | bytes 1572872 | tf_op jit(solution)/shard_map/ppermute | solution.py:61
  63.6 1.5 %collective-permute-start.24 = (bf16[4,256,256]{2,1,0:T(8,128)(2,1)S(1)}, bf16[4,256,256]{2,1,0:T(8,128)(2,1)S(1)}, u32[]{:S(2)}, u32[]{:S(2)}) collective-permute-start(bf16[4,256,256]{2,1,0:T(8,128)(2,1)S(1)} %collective-permute-done.22), channel_id=1, source_target_pairs={{2,0},{3,1},{4,6},{5,7},{10,8},{11,9},{12,14},{13,15},{18,16},{19,... | collective-permute-start | bytes 1572872 | tf_op jit(solution)/shard_map/ppermute | solution.py:61
  65.1 11.5 %shard_map.61 = (bf16[10,256,2048]{2,1,0:T(8,128)(2,1)}, f32[4,1024,256]{2,1,0:T(8,128)}, f32[8,128]{1,0:T(8,128)}) custom-call(s32[3]{0:T(128)} %pad_add_fusion.meta, bf16[4,256,1024]{2,1,0:T(8,128)(2,1)} %get-tuple-element.52.sparse, bf16[10,256,2048]{2,1,0:T(8,128)(2,1)} %decoder.7, ...), custom_call_target="tpu_custom_call", output_to_operand_aliasing={{0}: (12, {})} | custom-call | flops 10737418240 | bytes 20971520 | tf_op jit(solution)/shard_map/pallas_call | solution.py:291
  76.6 3.7 %collective-permute-done.24 = bf16[4,256,256]{2,1,0:T(8,128)(2,1)S(1)} collective-permute-done((bf16[4,256,256]{2,1,0:T(8,128)(2,1)S(1)}, bf16[4,256,256]{2,1,0:T(8,128)(2,1)S(1)}, u32[]{:S(2)}, u32[]{:S(2)}) %collective-permute-start.24) | collective-permute-done | bytes 524320 | tf_op jit(solution)/shard_map/ppermute | solution.py:61
  80.4 0.1 collective-permute-start.28
  80.5 0.5 collective-permute-start.27
  81.0 0.1 collective-permute-start.26
  81.1 4.1 %collective-permute-done.14.refs_3_ = bf16[4,256,256]{2,1,0:T(8,128)(2,1)S(1)} collective-permute-done((bf16[4,256,256]{2,1,0:T(8,128)(2,1)S(1)}, bf16[4,256,256]{2,1,0:T(8,128)(2,1)S(1)}, u32[]{:S(2)}, u32[]{:S(2)}) %collective-permute-start.14) | collective-permute-done | bytes 524320 | tf_op jit(solution)/shard_map/ppermute | solution.py:61
  85.3 0.5 collective-permute-start.30
  85.8 1.5 %collective-permute-start.29 = (bf16[4,256,256]{2,1,0:T(8,128)(2,1)S(1)}, bf16[4,256,256]{2,1,0:T(8,128)(2,1)S(1)}, u32[]{:S(2)}, u32[]{:S(2)}) collective-permute-start(bf16[4,256,256]{2,1,0:T(8,128)(2,1)S(1)} %collective-permute-done.14.refs_3_), channel_id=1, source_target_pairs={{0,16},{1,17},{2,18},{3,19},{4,20},{5,21},{6,22},{7,23},{8,24},{9,... | collective-permute-start | bytes 1572872 | tf_op jit(solution)/shard_map/ppermute | solution.py:61
  87.3 0.5 collective-permute-start.32
  87.8 0.3 copy-done.11
  88.1 0.2 copy-done.12
  88.3 0.6 copy-done.13
  88.9 11.5 %shard_map.62 = (bf16[10,256,2048]{2,1,0:T(8,128)(2,1)}, f32[4,1024,256]{2,1,0:T(8,128)}, f32[8,128]{1,0:T(8,128)}) custom-call(s32[3]{0:T(128)} %pad_add_fusion.meta, bf16[4,256,1024]{2,1,0:T(8,128)(2,1)} %get-tuple-element.52.sparse, bf16[10,256,2048]{2,1,0:T(8,128)(2,1)} %decoder.7, ...), custom_call_target="tpu_custom_call", output_to_operand_aliasing={{0}: (12, {})} | custom-call | flops 10737418240 | bytes 20971520 | tf_op jit(solution)/shard_map/pallas_call | solution.py:291
  100.4 0.1 collective-permute-start.33
  100.5 1.9 %collective-permute-done.33.refs_9_ = bf16[4,256,256]{2,1,0:T(8,128)(2,1)S(1)} collective-permute-done((bf16[4,256,256]{2,1,0:T(8,128)(2,1)S(1)}, bf16[4,256,256]{2,1,0:T(8,128)(2,1)S(1)}, u32[]{:S(2)}, u32[]{:S(2)}) %collective-permute-start.33) | collective-permute-done | bytes 524320 | tf_op jit(solution)/shard_map/ppermute | solution.py:61
  102.4 0.8 copy-done.14
  103.2 12.1 %shard_map.63 = (bf16[10,256,2048]{2,1,0:T(8,128)(2,1)}, bf16[4,1024,256]{2,1,0:T(8,128)(2,1)}, f32[8,128]{1,0:T(8,128)}) custom-call(s32[3]{0:T(128)} %pad_add_fusion.meta, bf16[4,256,1024]{2,1,0:T(8,128)(2,1)} %get-tuple-element.52.sparse, bf16[10,256,2048]{2,1,0:T(8,128)(2,1)} %decoder.7, ...), custom_call_target="tpu_custom_call", output_to_operand_aliasing={{0}: (13, {})} | custom-call | flops 10737418240 | bytes 20971520 | tf_op jit(solution)/shard_map/pallas_call | solution.py:291
  (59 shorter events, 0.2 us)
Async XLA Ops:
  0.6 14.1 %collective-permute-start.1 = (bf16[4,256,256]{2,1,0:T(8,128)(2,1)}, bf16[4,256,256]{2,1,0:T(8,128)(2,1)S(1)}, u32[]{:S(2)}, u32[]{:S(2)}) collective-permute-start(bf16[4,256,256]{2,1,0:T(8,128)(2,1)} %refs_0_.1), channel_id=1, source_target_pairs={{2,4},{3,5},{4,2},{5,3},{10,12},{11,13},{12,10},{13,11},{18,20},{1... | collective-permute-start | bytes 1572872 | tf_op jit(solution)/shard_map/ppermute | solution.py:61
  1.3 17.7 %collective-permute-start = (bf16[4,256,256]{2,1,0:T(8,128)(2,1)}, bf16[4,256,256]{2,1,0:T(8,128)(2,1)S(1)}, u32[]{:S(2)}, u32[]{:S(2)}) collective-permute-start(bf16[4,256,256]{2,1,0:T(8,128)(2,1)} %refs_0_.1), channel_id=1, source_target_pairs={{0,2},{1,3},{2,0},{3,1},{4,6},{5,7},{6,4},{7,5},{8,10},{9,11},{10,... | collective-permute-start | bytes 1572872 | tf_op jit(solution)/shard_map/ppermute | solution.py:61
  7.2 13.4 %collective-permute-start.8 = (bf16[4,256,256]{2,1,0:T(8,128)(2,1)}, bf16[4,256,256]{2,1,0:T(8,128)(2,1)}, u32[]{:S(2)}, u32[]{:S(2)}) collective-permute-start(bf16[4,256,256]{2,1,0:T(8,128)(2,1)} %refs_0_.1), channel_id=1, source_target_pairs={{0,16},{1,17},{2,18},{3,19},{4,20},{5,21},{6,22},{7,23},{8,24},{9,... | collective-permute-start | bytes 1572872 | tf_op jit(solution)/shard_map/ppermute | solution.py:61
  8.7 14.9 %collective-permute-start.7 = (bf16[4,256,256]{2,1,0:T(8,128)(2,1)}, bf16[4,256,256]{2,1,0:T(8,128)(2,1)}, u32[]{:S(2)}, u32[]{:S(2)}) collective-permute-start(bf16[4,256,256]{2,1,0:T(8,128)(2,1)} %refs_0_.1), channel_id=1, source_target_pairs={{0,8},{1,9},{2,10},{3,11},{4,12},{5,13},{6,14},{7,15},{8,0},{9,1},... | collective-permute-start | bytes 1572872 | tf_op jit(solution)/shard_map/ppermute | solution.py:61
  14.8 17.1 %collective-permute-start.2 = (bf16[4,256,256]{2,1,0:T(8,128)(2,1)S(1)}, bf16[4,256,256]{2,1,0:T(8,128)(2,1)S(1)}, u32[]{:S(2)}, u32[]{:S(2)}) collective-permute-start(bf16[4,256,256]{2,1,0:T(8,128)(2,1)S(1)} %collective-permute-done.1), channel_id=1, source_target_pairs={{2,0},{3,1},{4,6},{5,7},{10,8},{11,9},{12,14},{13,15},{18,16},{19,... | collective-permute-start | bytes 1572872 | tf_op jit(solution)/shard_map/ppermute | solution.py:61
  19.1 35.3 %copy-start.3 = (bf16[4,256,256]{2,1,0:T(8,128)(2,1)}, bf16[4,256,256]{2,1,0:T(8,128)(2,1)S(1)}, u32[]{:S(2)}) copy-start(bf16[4,256,256]{2,1,0:T(8,128)(2,1)S(1)} %collective-permute-done.refs_1_) | copy-start | bytes 1572868
  19.1 12.8 %collective-permute-start.3 = (bf16[4,256,256]{2,1,0:T(8,128)(2,1)S(1)}, bf16[4,256,256]{2,1,0:T(8,128)(2,1)S(1)}, u32[]{:S(2)}, u32[]{:S(2)}) collective-permute-start(bf16[4,256,256]{2,1,0:T(8,128)(2,1)S(1)} %collective-permute-done.refs_1_), channel_id=1, source_target_pairs={{2,4},{3,5},{4,2},{5,3},{10,12},{11,13},{12,10},{13,11},{18,20},{1... | collective-permute-start | bytes 1572872 | tf_op jit(solution)/shard_map/ppermute | solution.py:61
  20.6 12.5 %collective-permute-start.9 = (bf16[4,256,256]{2,1,0:T(8,128)(2,1)}, bf16[4,256,256]{2,1,0:T(8,128)(2,1)}, u32[]{:S(2)}, u32[]{:S(2)}) collective-permute-start(bf16[4,256,256]{2,1,0:T(8,128)(2,1)} %collective-permute-done.8.refs_2_), channel_id=1, source_target_pairs={{0,8},{1,9},{2,10},{3,11},{4,12},{5,13},{6,14},{7,15},{8,0},{9,1},... | collective-permute-start | bytes 1572872 | tf_op jit(solution)/shard_map/ppermute | solution.py:61
  22.1 11.9 %collective-permute-start.4 = (bf16[4,256,256]{2,1,0:T(8,128)(2,1)S(1)}, bf16[4,256,256]{2,1,0:T(8,128)(2,1)S(1)}, u32[]{:S(2)}, u32[]{:S(2)}) collective-permute-start(bf16[4,256,256]{2,1,0:T(8,128)(2,1)S(1)} %collective-permute-done.refs_1_), channel_id=1, source_target_pairs={{0,16},{1,17},{2,18},{3,19},{4,20},{5,21},{6,22},{7,23},{8,24},{9,... | collective-permute-start | bytes 1572872 | tf_op jit(solution)/shard_map/ppermute | solution.py:61
  23.6 11.7 %collective-permute-start.10 = (bf16[4,256,256]{2,1,0:T(8,128)(2,1)}, bf16[4,256,256]{2,1,0:T(8,128)(2,1)}, u32[]{:S(2)}, u32[]{:S(2)}) collective-permute-start(bf16[4,256,256]{2,1,0:T(8,128)(2,1)} %refs_0_.1), channel_id=1, source_target_pairs={{0,1},{1,0},{2,3},{3,2},{4,5},{5,4},{6,7},{7,6},{8,9},{9,8},{10,11... | collective-permute-start | bytes 1572872 | tf_op jit(solution)/shard_map/ppermute | solution.py:61
  31.8 5.1 %collective-permute-start.12 = (bf16[4,256,256]{2,1,0:T(8,128)(2,1)}, bf16[4,256,256]{2,1,0:T(8,128)(2,1)}, u32[]{:S(2)}, u32[]{:S(2)}) collective-permute-start(bf16[4,256,256]{2,1,0:T(8,128)(2,1)} %collective-permute-done.8.refs_2_), channel_id=1, source_target_pairs={{0,1},{1,0},{2,3},{3,2},{4,5},{5,4},{6,7},{7,6},{8,9},{9,8},{10,11... | collective-permute-start | bytes 1572872 | tf_op jit(solution)/shard_map/ppermute | solution.py:61
  31.8 6.3 %collective-permute-start.11 = (bf16[4,256,256]{2,1,0:T(8,128)(2,1)}, bf16[4,256,256]{2,1,0:T(8,128)(2,1)}, u32[]{:S(2)}, u32[]{:S(2)}) collective-permute-start(bf16[4,256,256]{2,1,0:T(8,128)(2,1)} %collective-permute-done.7.refs_1_), channel_id=1, source_target_pairs={{0,1},{1,0},{2,3},{3,2},{4,5},{5,4},{6,7},{7,6},{8,9},{9,8},{10,11... | collective-permute-start | bytes 1572872 | tf_op jit(solution)/shard_map/ppermute | solution.py:61
  33.1 5.8 %collective-permute-start.13 = (bf16[4,256,256]{2,1,0:T(8,128)(2,1)}, bf16[4,256,256]{2,1,0:T(8,128)(2,1)}, u32[]{:S(2)}, u32[]{:S(2)}) collective-permute-start(bf16[4,256,256]{2,1,0:T(8,128)(2,1)} %collective-permute-done.9.refs_3_), channel_id=1, source_target_pairs={{0,1},{1,0},{2,3},{3,2},{4,5},{5,4},{6,7},{7,6},{8,9},{9,8},{10,11... | collective-permute-start | bytes 1572872 | tf_op jit(solution)/shard_map/ppermute | solution.py:61
  33.8 51.4 %copy-start = (bf16[4,256,256]{2,1,0:T(8,128)(2,1)}, bf16[4,256,256]{2,1,0:T(8,128)(2,1)S(1)}, u32[]{:S(2)}) copy-start(bf16[4,256,256]{2,1,0:T(8,128)(2,1)S(1)} %broadcast_select_fusion.2.refs_1_) | copy-start | bytes 1572868
  34.0 20.4 %copy-start.4 = (bf16[4,256,256]{2,1,0:T(8,128)(2,1)}, bf16[4,256,256]{2,1,0:T(8,128)(2,1)S(1)}, u32[]{:S(2)}) copy-start(bf16[4,256,256]{2,1,0:T(8,128)(2,1)S(1)} %collective-permute-done.4.refs_3_) | copy-start | bytes 1572868
  34.0 20.4 %collective-permute-start.16 = (bf16[4,256,256]{2,1,0:T(8,128)(2,1)S(1)}, bf16[4,256,256]{2,1,0:T(8,128)(2,1)}, u32[]{:S(2)}, u32[]{:S(2)}) collective-permute-start(bf16[4,256,256]{2,1,0:T(8,128)(2,1)S(1)} %collective-permute-done.refs_1_), channel_id=1, source_target_pairs={{0,8},{1,9},{2,10},{3,11},{4,12},{5,13},{6,14},{7,15},{8,0},{9,1},... | collective-permute-start | bytes 1572872 | tf_op jit(solution)/shard_map/ppermute | solution.py:61
  35.4 24.7 %collective-permute-start.5 = (bf16[4,256,256]{2,1,0:T(8,128)(2,1)S(1)}, bf16[4,256,256]{2,1,0:T(8,128)(2,1)}, u32[]{:S(2)}, u32[]{:S(2)}) collective-permute-start(bf16[4,256,256]{2,1,0:T(8,128)(2,1)S(1)} %broadcast_select_fusion.2.refs_1_), channel_id=1, source_target_pairs={{0,16},{1,17},{2,18},{3,19},{4,20},{5,21},{6,22},{7,23},{8,24},{9,... | collective-permute-start | bytes 1572872 | tf_op jit(solution)/shard_map/ppermute | solution.py:61
  36.9 17.4 %collective-permute-start.6 = (bf16[4,256,256]{2,1,0:T(8,128)(2,1)S(1)}, bf16[4,256,256]{2,1,0:T(8,128)(2,1)S(1)}, u32[]{:S(2)}, u32[]{:S(2)}) collective-permute-start(bf16[4,256,256]{2,1,0:T(8,128)(2,1)S(1)} %collective-permute-done.3), channel_id=1, source_target_pairs={{2,0},{3,1},{4,6},{5,7},{10,8},{11,9},{12,14},{13,15},{18,16},{19,... | collective-permute-start | bytes 1572872 | tf_op jit(solution)/shard_map/ppermute | solution.py:61
  38.2 21.4 %collective-permute-start.17 = (bf16[4,256,256]{2,1,0:T(8,128)(2,1)S(1)}, bf16[4,256,256]{2,1,0:T(8,128)(2,1)}, u32[]{:S(2)}, u32[]{:S(2)}) collective-permute-start(bf16[4,256,256]{2,1,0:T(8,128)(2,1)S(1)} %collective-permute-done.4.refs_3_), channel_id=1, source_target_pairs={{0,8},{1,9},{2,10},{3,11},{4,12},{5,13},{6,14},{7,15},{8,0},{9,1},... | collective-permute-start | bytes 1572872 | tf_op jit(solution)/shard_map/ppermute | solution.py:61
  39.0 20.6 %collective-permute-start.22 = (bf16[4,256,256]{2,1,0:T(8,128)(2,1)}, bf16[4,256,256]{2,1,0:T(8,128)(2,1)S(1)}, u32[]{:S(2)}, u32[]{:S(2)}) collective-permute-start(bf16[4,256,256]{2,1,0:T(8,128)(2,1)} %collective-permute-done.9.refs_3_), channel_id=1, source_target_pairs={{2,4},{3,5},{4,2},{5,3},{10,12},{11,13},{12,10},{13,11},{18,20},{1... | collective-permute-start | bytes 1572872 | tf_op jit(solution)/shard_map/ppermute | solution.py:61
  54.3 7.2 %collective-permute-start.18 = (bf16[4,256,256]{2,1,0:T(8,128)(2,1)S(1)}, bf16[4,256,256]{2,1,0:T(8,128)(2,1)S(1)}, u32[]{:S(2)}, u32[]{:S(2)}) collective-permute-start(bf16[4,256,256]{2,1,0:T(8,128)(2,1)S(1)} %collective-permute-done.refs_1_), channel_id=1, source_target_pairs={{0,1},{1,0},{2,3},{3,2},{4,5},{5,4},{6,7},{7,6},{8,9},{9,8},{10,11... | collective-permute-start | bytes 1572872 | tf_op jit(solution)/shard_map/ppermute | solution.py:61
  54.4 30.8 %copy-start.1 = (bf16[4,256,256]{2,1,0:T(8,128)(2,1)}, bf16[4,256,256]{2,1,0:T(8,128)(2,1)S(1)}, u32[]{:S(2)}) copy-start(bf16[4,256,256]{2,1,0:T(8,128)(2,1)S(1)} %broadcast_select_fusion.1.refs_2_) | copy-start | bytes 1572868
  54.4 7.7 %collective-permute-start.20 = (bf16[4,256,256]{2,1,0:T(8,128)(2,1)S(1)}, bf16[4,256,256]{2,1,0:T(8,128)(2,1)S(1)}, u32[]{:S(2)}, u32[]{:S(2)}) collective-permute-start(bf16[4,256,256]{2,1,0:T(8,128)(2,1)S(1)} %collective-permute-done.4.refs_3_), channel_id=1, source_target_pairs={{0,1},{1,0},{2,3},{3,2},{4,5},{5,4},{6,7},{7,6},{8,9},{9,8},{10,11... | collective-permute-start | bytes 1572872 | tf_op jit(solution)/shard_map/ppermute | solution.py:61
  59.6 4.1 %collective-permute-start.19 = (bf16[4,256,256]{2,1,0:T(8,128)(2,1)}, bf16[4,256,256]{2,1,0:T(8,128)(2,1)}, u32[]{:S(2)}, u32[]{:S(2)}) collective-permute-start(bf16[4,256,256]{2,1,0:T(8,128)(2,1)} %collective-permute-done.16.refs_2_), channel_id=1, source_target_pairs={{0,1},{1,0},{2,3},{3,2},{4,5},{5,4},{6,7},{7,6},{8,9},{9,8},{10,11... | collective-permute-start | bytes 1572872 | tf_op jit(solution)/shard_map/ppermute | solution.py:61
  59.6 5.5 %collective-permute-start.21 = (bf16[4,256,256]{2,1,0:T(8,128)(2,1)}, bf16[4,256,256]{2,1,0:T(8,128)(2,1)}, u32[]{:S(2)}, u32[]{:S(2)}) collective-permute-start(bf16[4,256,256]{2,1,0:T(8,128)(2,1)} %collective-permute-done.17.refs_4_), channel_id=1, source_target_pairs={{0,1},{1,0},{2,3},{3,2},{4,5},{5,4},{6,7},{7,6},{8,9},{9,8},{10,11... | collective-permute-start | bytes 1572872 | tf_op jit(solution)/shard_map/ppermute | solution.py:61
  60.1 20.9 %collective-permute-start.23 = (bf16[4,256,256]{2,1,0:T(8,128)(2,1)S(1)}, bf16[4,256,256]{2,1,0:T(8,128)(2,1)}, u32[]{:S(2)}, u32[]{:S(2)}) collective-permute-start(bf16[4,256,256]{2,1,0:T(8,128)(2,1)S(1)} %broadcast_select_fusion.2.refs_1_), channel_id=1, source_target_pairs={{0,8},{1,9},{2,10},{3,11},{4,12},{5,13},{6,14},{7,15},{8,0},{9,1},... | collective-permute-start | bytes 1572872 | tf_op jit(solution)/shard_map/ppermute | solution.py:61
  61.6 2.1 %copy-start.8 = (bf16[4,256,256]{2,1,0:T(8,128)(2,1)}, bf16[4,256,256]{2,1,0:T(8,128)(2,1)S(1)}, u32[]{:S(2)}) copy-start(bf16[4,256,256]{2,1,0:T(8,128)(2,1)S(1)} %collective-permute-done.18.refs_5_) | copy-start | bytes 1572868
  61.6 23.6 %collective-permute-start.14 = (bf16[4,256,256]{2,1,0:T(8,128)(2,1)S(1)}, bf16[4,256,256]{2,1,0:T(8,128)(2,1)S(1)}, u32[]{:S(2)}, u32[]{:S(2)}) collective-permute-start(bf16[4,256,256]{2,1,0:T(8,128)(2,1)S(1)} %broadcast_select_fusion.1.refs_2_), channel_id=1, source_target_pairs={{0,8},{1,9},{2,10},{3,11},{4,12},{5,13},{6,14},{7,15},{8,0},{9,1},... | collective-permute-start | bytes 1572872 | tf_op jit(solution)/shard_map/ppermute | solution.py:61
  62.1 3.0 %copy-start.10 = (bf16[4,256,256]{2,1,0:T(8,128)(2,1)}, bf16[4,256,256]{2,1,0:T(8,128)(2,1)S(1)}, u32[]{:S(2)}) copy-start(bf16[4,256,256]{2,1,0:T(8,128)(2,1)S(1)} %collective-permute-done.20.refs_7_) | copy-start | bytes 1572868
  62.1 23.1 %collective-permute-start.15 = (bf16[4,256,256]{2,1,0:T(8,128)(2,1)S(1)}, bf16[4,256,256]{2,1,0:T(8,128)(2,1)S(1)}, u32[]{:S(2)}, u32[]{:S(2)}) collective-permute-start(bf16[4,256,256]{2,1,0:T(8,128)(2,1)S(1)} %broadcast_select_fusion.1.refs_2_), channel_id=1, source_target_pairs={{0,16},{1,17},{2,18},{3,19},{4,20},{5,21},{6,22},{7,23},{8,24},{9,... | collective-permute-start | bytes 1572872 | tf_op jit(solution)/shard_map/ppermute | solution.py:61
  63.6 16.7 %collective-permute-start.24 = (bf16[4,256,256]{2,1,0:T(8,128)(2,1)S(1)}, bf16[4,256,256]{2,1,0:T(8,128)(2,1)S(1)}, u32[]{:S(2)}, u32[]{:S(2)}) collective-permute-start(bf16[4,256,256]{2,1,0:T(8,128)(2,1)S(1)} %collective-permute-done.22), channel_id=1, source_target_pairs={{2,0},{3,1},{4,6},{5,7},{10,8},{11,9},{12,14},{13,15},{18,16},{19,... | collective-permute-start | bytes 1572872 | tf_op jit(solution)/shard_map/ppermute | solution.py:61
  80.4 8.5 %copy-start.2 = (bf16[4,256,256]{2,1,0:T(8,128)(2,1)}, bf16[4,256,256]{2,1,0:T(8,128)(2,1)S(1)}, u32[]{:S(2)}) copy-start(bf16[4,256,256]{2,1,0:T(8,128)(2,1)S(1)} %broadcast_select_fusion.refs_4_) | copy-start | bytes 1572868
  80.4 5.4 %collective-permute-start.28 = (bf16[4,256,256]{2,1,0:T(8,128)(2,1)S(1)}, bf16[4,256,256]{2,1,0:T(8,128)(2,1)}, u32[]{:S(2)}, u32[]{:S(2)}) collective-permute-start(bf16[4,256,256]{2,1,0:T(8,128)(2,1)S(1)} %broadcast_select_fusion.refs_4_), channel_id=1, source_target_pairs={{0,1},{1,0},{2,3},{3,2},{4,5},{5,4},{6,7},{7,6},{8,9},{9,8},{10,11... | collective-permute-start | bytes 1572872 | tf_op jit(solution)/shard_map/ppermute | solution.py:61
  80.5 6.8 %collective-permute-start.27 = (bf16[4,256,256]{2,1,0:T(8,128)(2,1)}, bf16[4,256,256]{2,1,0:T(8,128)(2,1)S(1)}, u32[]{:S(2)}, u32[]{:S(2)}) collective-permute-start(bf16[4,256,256]{2,1,0:T(8,128)(2,1)} %collective-permute-done.5.refs_3_), channel_id=1, source_target_pairs={{0,1},{1,0},{2,3},{3,2},{4,5},{5,4},{6,7},{7,6},{8,9},{9,8},{10,11... | collective-permute-start | bytes 1572872 | tf_op jit(solution)/shard_map/ppermute | solution.py:61
  81.0 6.3 %collective-permute-start.26 = (bf16[4,256,256]{2,1,0:T(8,128)(2,1)}, bf16[4,256,256]{2,1,0:T(8,128)(2,1)S(1)}, u32[]{:S(2)}, u32[]{:S(2)}) collective-permute-start(bf16[4,256,256]{2,1,0:T(8,128)(2,1)} %collective-permute-done.23.refs_2_), channel_id=1, source_target_pairs={{0,1},{1,0},{2,3},{3,2},{4,5},{5,4},{6,7},{7,6},{8,9},{9,8},{10,11... | collective-permute-start | bytes 1572872 | tf_op jit(solution)/shard_map/ppermute | solution.py:61
  85.2 15.2 %copy-start.5 = (bf16[4,256,256]{2,1,0:T(8,128)(2,1)}, bf16[4,256,256]{2,1,0:T(8,128)(2,1)S(1)}, u32[]{:S(2)}) copy-start(bf16[4,256,256]{2,1,0:T(8,128)(2,1)S(1)} %collective-permute-done.14.refs_3_) | copy-start | bytes 1572868
  85.2 2.6 %collective-permute-start.25 = (bf16[4,256,256]{2,1,0:T(8,128)(2,1)S(1)}, bf16[4,256,256]{2,1,0:T(8,128)(2,1)S(1)}, u32[]{:S(2)}, u32[]{:S(2)}) collective-permute-start(bf16[4,256,256]{2,1,0:T(8,128)(2,1)S(1)} %broadcast_select_fusion.2.refs_1_), channel_id=1, source_target_pairs={{0,1},{1,0},{2,3},{3,2},{4,5},{5,4},{6,7},{7,6},{8,9},{9,8},{10,11... | collective-permute-start | bytes 1572872 | tf_op jit(solution)/shard_map/ppermute | solution.py:61
  85.2 15.2 %copy-start.6 = (bf16[4,256,256]{2,1,0:T(8,128)(2,1)}, bf16[4,256,256]{2,1,0:T(8,128)(2,1)S(1)}, u32[]{:S(2)}) copy-start(bf16[4,256,256]{2,1,0:T(8,128)(2,1)S(1)} %collective-permute-done.15.refs_4_) | copy-start | bytes 1572868
  85.3 15.3 %collective-permute-start.30 = (bf16[4,256,256]{2,1,0:T(8,128)(2,1)S(1)}, bf16[4,256,256]{2,1,0:T(8,128)(2,1)S(1)}, u32[]{:S(2)}, u32[]{:S(2)}) collective-permute-start(bf16[4,256,256]{2,1,0:T(8,128)(2,1)S(1)} %broadcast_select_fusion.1.refs_2_), channel_id=1, source_target_pairs={{0,1},{1,0},{2,3},{3,2},{4,5},{5,4},{6,7},{7,6},{8,9},{9,8},{10,11... | collective-permute-start | bytes 1572872 | tf_op jit(solution)/shard_map/ppermute | solution.py:61
  85.8 14.6 %collective-permute-start.29 = (bf16[4,256,256]{2,1,0:T(8,128)(2,1)S(1)}, bf16[4,256,256]{2,1,0:T(8,128)(2,1)S(1)}, u32[]{:S(2)}, u32[]{:S(2)}) collective-permute-start(bf16[4,256,256]{2,1,0:T(8,128)(2,1)S(1)} %collective-permute-done.14.refs_3_), channel_id=1, source_target_pairs={{0,16},{1,17},{2,18},{3,19},{4,20},{5,21},{6,22},{7,23},{8,24},{9,... | collective-permute-start | bytes 1572872 | tf_op jit(solution)/shard_map/ppermute | solution.py:61
  87.3 0.8 copy-start.11
  87.3 13.2 %collective-permute-start.31 = (bf16[4,256,256]{2,1,0:T(8,128)(2,1)S(1)}, bf16[4,256,256]{2,1,0:T(8,128)(2,1)}, u32[]{:S(2)}, u32[]{:S(2)}) collective-permute-start(bf16[4,256,256]{2,1,0:T(8,128)(2,1)S(1)} %collective-permute-done.14.refs_3_), channel_id=1, source_target_pairs={{0,1},{1,0},{2,3},{3,2},{4,5},{5,4},{6,7},{7,6},{8,9},{9,8},{10,11... | collective-permute-start | bytes 1572872 | tf_op jit(solution)/shard_map/ppermute | solution.py:61
  87.3 0.9 copy-start.12
  87.3 13.2 %collective-permute-start.32 = (bf16[4,256,256]{2,1,0:T(8,128)(2,1)S(1)}, bf16[4,256,256]{2,1,0:T(8,128)(2,1)}, u32[]{:S(2)}, u32[]{:S(2)}) collective-permute-start(bf16[4,256,256]{2,1,0:T(8,128)(2,1)S(1)} %collective-permute-done.15.refs_4_), channel_id=1, source_target_pairs={{0,1},{1,0},{2,3},{3,2},{4,5},{5,4},{6,7},{7,6},{8,9},{9,8},{10,11... | collective-permute-start | bytes 1572872 | tf_op jit(solution)/shard_map/ppermute | solution.py:61
  100.4 2.0 %copy-start.9 = (bf16[4,256,256]{2,1,0:T(8,128)(2,1)}, bf16[4,256,256]{2,1,0:T(8,128)(2,1)S(1)}, u32[]{:S(2)}) copy-start(bf16[4,256,256]{2,1,0:T(8,128)(2,1)S(1)} %collective-permute-done.29.refs_5_) | copy-start | bytes 1572868
  100.4 2.0 %collective-permute-start.33 = (bf16[4,256,256]{2,1,0:T(8,128)(2,1)S(1)}, bf16[4,256,256]{2,1,0:T(8,128)(2,1)S(1)}, u32[]{:S(2)}, u32[]{:S(2)}) collective-permute-start(bf16[4,256,256]{2,1,0:T(8,128)(2,1)S(1)} %collective-permute-done.29.refs_5_), channel_id=1, source_target_pairs={{0,1},{1,0},{2,3},{3,2},{4,5},{5,4},{6,7},{7,6},{8,9},{9,8},{10,11... | collective-permute-start | bytes 1572872 | tf_op jit(solution)/shard_map/ppermute | solution.py:61
  100.5 1.9 %copy-start.7 = (bf16[4,256,256]{2,1,0:T(8,128)(2,1)}, bf16[4,256,256]{2,1,0:T(8,128)(2,1)S(1)}, u32[]{:S(2)}) copy-start(bf16[4,256,256]{2,1,0:T(8,128)(2,1)S(1)} %collective-permute-done.30.refs_6_) | copy-start | bytes 1572868
  102.4 0.8 copy-start.14
  (1 other events, 0.8 us)

commit v14 on v13

--- a/solution.py
+++ b/solution.py
@@ -352,7 +352,7 @@
             ready = lax.optimization_barrier([blocks.piece(*at) for at in held])
             blocks.pieces.update(zip(held, ready))
             mine = [blocks.piece(r, j) for j in range(n_layer)]
-        free = [0] + blocks.singles if r in (0, 1, end) else []
+        free = [0] + blocks.singles if r in (0, 1, end) else [0]
         theirs = [blocks.swap(x if j in free else blocks.tie(x)) for j, x in enumerate(mine)]
         if r == 0:
             soon = [(far, 0) for far in range(1, planes)] + [(1, j) for j in blocks.singles[1:]]

time: 117 us -> 116 us (level)
  transfers between devices with their start and end apart: 34 -> 34, of which waited for: 10 -> 11; matrix products, arithmetic and copies ran while one was open for 1% -> 1% of each run, Pallas kernels for 34% -> 34%
where the time goes in v14:
time: 116 us; the launch traced here: 115 us
  Pallas kernels  50.9 us (44%)
  waiting for transfers between devices  30.3 us (26%)
  starting transfers between devices  30 us (26%)
  local copies, waits for them, and re-layouts  1.64 us (1%)
    pallas_call x4, Pallas kernels, run_round(): pl.pallas_call(functools.partial(round_kernel, len(mine), len(tokens), la...  46.4 us
    ppermute x34, waiting for transfers between devices, permute(): return lax.ppermute(x, ('layer', 'feat'), sorted(flat))  30.3 us
    ppermute x34, starting transfers between devices, permute(): return lax.ppermute(x, ('layer', 'feat'), sorted(flat))  30 us
    pallas_call x1, Pallas kernels, prepare(): pl.pallas_call(prepare_kernel, grid=(layers,), in_specs=[block(rows, widt...  4.55 us
  transfers between devices with their start and end apart: 34, of which 11 were waited for; matrix products, arithmetic and copies ran while one was open for 1% of the time, Pallas kernels for 34%

profile of v14, /device:TPU:0, one launch (start us, length us, event | category | flops | bytes accessed | tf_op | source)
XLA Modules:
  0.0 114.7 jit_solution(2002593736435718753)
XLA Ops:
  0.6 0.7 collective-permute-start.1
  1.3 5.9 %collective-permute-start = (bf16[4,256,256]{2,1,0:T(8,128)(2,1)}, bf16[4,256,256]{2,1,0:T(8,128)(2,1)S(1)}, u32[]{:S(2)}, u32[]{:S(2)}) collective-permute-start(bf16[4,256,256]{2,1,0:T(8,128)(2,1)} %refs_0_.1), channel_id=1, source_target_pairs={{0,2},{1,3},{2,0},{3,1},{4,6},{5,7},{6,4},{7,5},{8,10},{9,11},{10,... | collective-permute-start | bytes 1572872 | tf_op jit(solution)/shard_map/ppermute | solution.py:61
  7.2 1.5 %collective-permute-start.8 = (bf16[4,256,256]{2,1,0:T(8,128)(2,1)}, bf16[4,256,256]{2,1,0:T(8,128)(2,1)}, u32[]{:S(2)}, u32[]{:S(2)}) collective-permute-start(bf16[4,256,256]{2,1,0:T(8,128)(2,1)} %refs_0_.1), channel_id=1, source_target_pairs={{0,16},{1,17},{2,18},{3,19},{4,20},{5,21},{6,22},{7,23},{8,24},{9,... | collective-permute-start | bytes 1572872 | tf_op jit(solution)/shard_map/ppermute | solution.py:61
  8.7 1.5 %collective-permute-start.7 = (bf16[4,256,256]{2,1,0:T(8,128)(2,1)}, bf16[4,256,256]{2,1,0:T(8,128)(2,1)}, u32[]{:S(2)}, u32[]{:S(2)}) collective-permute-start(bf16[4,256,256]{2,1,0:T(8,128)(2,1)} %refs_0_.1), channel_id=1, source_target_pairs={{0,8},{1,9},{2,10},{3,11},{4,12},{5,13},{6,14},{7,15},{8,0},{9,1},... | collective-permute-start | bytes 1572872 | tf_op jit(solution)/shard_map/ppermute | solution.py:61
  10.2 4.5 %shard_map.59 = (bf16[4,256,1024]{2,1,0:T(8,128)(2,1)}, bf16[4,1024,256]{2,1,0:T(8,128)(2,1)}) custom-call(bf16[4,1024,256]{2,1,0:T(8,128)(2,1)} %act.1, s32[4,2,1024]{2,1,0:T(2,128)} %bitcast.4), custom_call_target="tpu_custom_call" | custom-call | bytes 6291456 | tf_op jit(solution)/shard_map/pallas_call | solution.py:121
  14.8 1.3 %collective-permute-start.2 = (bf16[4,256,256]{2,1,0:T(8,128)(2,1)S(1)}, bf16[4,256,256]{2,1,0:T(8,128)(2,1)S(1)}, u32[]{:S(2)}, u32[]{:S(2)}) collective-permute-start(bf16[4,256,256]{2,1,0:T(8,128)(2,1)S(1)} %collective-permute-done.1), channel_id=1, source_target_pairs={{2,0},{3,1},{4,6},{5,7},{10,8},{11,9},{12,14},{13,15},{18,16},{19,... | collective-permute-start | bytes 1572872 | tf_op jit(solution)/shard_map/ppermute | solution.py:61
  16.1 3.0 %collective-permute-done.refs_1_ = bf16[4,256,256]{2,1,0:T(8,128)(2,1)S(1)} collective-permute-done((bf16[4,256,256]{2,1,0:T(8,128)(2,1)}, bf16[4,256,256]{2,1,0:T(8,128)(2,1)S(1)}, u32[]{:S(2)}, u32[]{:S(2)}) %collective-permute-start) | collective-permute-done | bytes 524320 | tf_op jit(solution)/shard_map/ppermute | solution.py:61
  19.1 0.7 collective-permute-start.3
  19.8 0.9 collective-permute-done.8.refs_2_
  20.6 1.5 %collective-permute-start.9 = (bf16[4,256,256]{2,1,0:T(8,128)(2,1)}, bf16[4,256,256]{2,1,0:T(8,128)(2,1)}, u32[]{:S(2)}, u32[]{:S(2)}) collective-permute-start(bf16[4,256,256]{2,1,0:T(8,128)(2,1)} %collective-permute-done.8.refs_2_), channel_id=1, source_target_pairs={{0,8},{1,9},{2,10},{3,11},{4,12},{5,13},{6,14},{7,15},{8,0},{9,1},... | collective-permute-start | bytes 1572872 | tf_op jit(solution)/shard_map/ppermute | solution.py:61
  22.1 1.5 %collective-permute-start.4 = (bf16[4,256,256]{2,1,0:T(8,128)(2,1)S(1)}, bf16[4,256,256]{2,1,0:T(8,128)(2,1)S(1)}, u32[]{:S(2)}, u32[]{:S(2)}) collective-permute-start(bf16[4,256,256]{2,1,0:T(8,128)(2,1)S(1)} %collective-permute-done.refs_1_), channel_id=1, source_target_pairs={{0,16},{1,17},{2,18},{3,19},{4,20},{5,21},{6,22},{7,23},{8,24},{9,... | collective-permute-start | bytes 1572872 | tf_op jit(solution)/shard_map/ppermute | solution.py:61
  23.7 8.2 %collective-permute-done.2 = bf16[4,256,256]{2,1,0:T(8,128)(2,1)S(1)} collective-permute-done((bf16[4,256,256]{2,1,0:T(8,128)(2,1)S(1)}, bf16[4,256,256]{2,1,0:T(8,128)(2,1)S(1)}, u32[]{:S(2)}, u32[]{:S(2)}) %collective-permute-start.2) | collective-permute-done | bytes 524320 | tf_op jit(solution)/shard_map/ppermute | solution.py:61
  31.8 0.5 collective-permute-start.11
  32.4 0.8 collective-permute-done.9.refs_3_
  33.1 0.6 pad_add_fusion.meta
  33.7 0.1 broadcast_select_fusion.2.refs_1_
  33.8 0.2 collective-permute-done.4.refs_3_
  34.0 1.3 %collective-permute-start.16 = (bf16[4,256,256]{2,1,0:T(8,128)(2,1)S(1)}, bf16[4,256,256]{2,1,0:T(8,128)(2,1)}, u32[]{:S(2)}, u32[]{:S(2)}) collective-permute-start(bf16[4,256,256]{2,1,0:T(8,128)(2,1)S(1)} %collective-permute-done.refs_1_), channel_id=1, source_target_pairs={{0,8},{1,9},{2,10},{3,11},{4,12},{5,13},{6,14},{7,15},{8,0},{9,1},... | collective-permute-start | bytes 1572872 | tf_op jit(solution)/shard_map/ppermute | solution.py:61
  35.4 1.5 %collective-permute-start.5 = (bf16[4,256,256]{2,1,0:T(8,128)(2,1)S(1)}, bf16[4,256,256]{2,1,0:T(8,128)(2,1)}, u32[]{:S(2)}, u32[]{:S(2)}) collective-permute-start(bf16[4,256,256]{2,1,0:T(8,128)(2,1)S(1)} %broadcast_select_fusion.2.refs_1_), channel_id=1, source_target_pairs={{0,16},{1,17},{2,18},{3,19},{4,20},{5,21},{6,22},{7,23},{8,24},{9,... | collective-permute-start | bytes 1572872 | tf_op jit(solution)/shard_map/ppermute | solution.py:61
  36.9 1.3 %collective-permute-start.6 = (bf16[4,256,256]{2,1,0:T(8,128)(2,1)S(1)}, bf16[4,256,256]{2,1,0:T(8,128)(2,1)S(1)}, u32[]{:S(2)}, u32[]{:S(2)}) collective-permute-start(bf16[4,256,256]{2,1,0:T(8,128)(2,1)S(1)} %collective-permute-done.3), channel_id=1, source_target_pairs={{2,0},{3,1},{4,6},{5,7},{10,8},{11,9},{12,14},{13,15},{18,16},{19,... | collective-permute-start | bytes 1572872 | tf_op jit(solution)/shard_map/ppermute | solution.py:61
  38.2 0.8 collective-permute-start.17
  39.0 0.7 collective-permute-start.22
  39.7 11.3 %shard_map.60 = (bf16[10,256,2048]{2,1,0:T(8,128)(2,1)}, f32[4,1024,256]{2,1,0:T(8,128)}, f32[8,128]{1,0:T(8,128)}) custom-call(s32[3]{0:T(128)} %pad_add_fusion.meta, bf16[4,256,1024]{2,1,0:T(8,128)(2,1)} %get-tuple-element.50.sparse, bf16[10,256,2048]{2,1,0:T(8,128)(2,1)} %decoder.7, bf16[4,256,256]{2,1,0:T(8,128)(2,1)} %refs_0_.1, ...), custom_call_target="tpu_custom_call" | custom-call | flops 10737418240 | bytes 20971520 | tf_op jit(solution)/shard_map/pallas_call | solution.py:291
  50.9 3.4 %collective-permute-done.6 = bf16[4,256,256]{2,1,0:T(8,128)(2,1)S(1)} collective-permute-done((bf16[4,256,256]{2,1,0:T(8,128)(2,1)S(1)}, bf16[4,256,256]{2,1,0:T(8,128)(2,1)S(1)}, u32[]{:S(2)}, u32[]{:S(2)}) %collective-permute-start.6) | collective-permute-done | bytes 524320 | tf_op jit(solution)/shard_map/ppermute | solution.py:61
  54.3 0.1 broadcast_select_fusion.1.refs_2_
  54.4 0.6 collective-permute-start.20
  55.0 4.5 %collective-permute-done.17.refs_4_ = bf16[4,256,256]{2,1,0:T(8,128)(2,1)} collective-permute-done((bf16[4,256,256]{2,1,0:T(8,128)(2,1)S(1)}, bf16[4,256,256]{2,1,0:T(8,128)(2,1)}, u32[]{:S(2)}, u32[]{:S(2)}) %collective-permute-start.17) | collective-permute-done | bytes 524320 | tf_op jit(solution)/shard_map/ppermute | solution.py:61
  59.6 0.5 collective-permute-start.21
  60.1 1.5 %collective-permute-start.23 = (bf16[4,256,256]{2,1,0:T(8,128)(2,1)S(1)}, bf16[4,256,256]{2,1,0:T(8,128)(2,1)}, u32[]{:S(2)}, u32[]{:S(2)}) collective-permute-start(bf16[4,256,256]{2,1,0:T(8,128)(2,1)S(1)} %broadcast_select_fusion.2.refs_1_), channel_id=1, source_target_pairs={{0,8},{1,9},{2,10},{3,11},{4,12},{5,13},{6,14},{7,15},{8,0},{9,1},... | collective-permute-start | bytes 1572872 | tf_op jit(solution)/shard_map/ppermute | solution.py:61
  61.6 0.1 collective-permute-start.25
  61.7 0.6 collective-permute-start.14
  62.3 1.5 %collective-permute-start.15 = (bf16[4,256,256]{2,1,0:T(8,128)(2,1)S(1)}, bf16[4,256,256]{2,1,0:T(8,128)(2,1)S(1)}, u32[]{:S(2)}, u32[]{:S(2)}) collective-permute-start(bf16[4,256,256]{2,1,0:T(8,128)(2,1)S(1)} %broadcast_select_fusion.1.refs_2_), channel_id=1, source_target_pairs={{0,16},{1,17},{2,18},{3,19},{4,20},{5,21},{6,22},{7,23},{8,24},{9,... | collective-permute-start | bytes 1572872 | tf_op jit(solution)/shard_map/ppermute | solution.py:61
  63.8 0.8 copy-done.13
  64.6 1.5 %collective-permute-start.24 = (bf16[4,256,256]{2,1,0:T(8,128)(2,1)S(1)}, bf16[4,256,256]{2,1,0:T(8,128)(2,1)S(1)}, u32[]{:S(2)}, u32[]{:S(2)}) collective-permute-start(bf16[4,256,256]{2,1,0:T(8,128)(2,1)S(1)} %collective-permute-done.22), channel_id=1, source_target_pairs={{2,0},{3,1},{4,6},{5,7},{10,8},{11,9},{12,14},{13,15},{18,16},{19,... | collective-permute-start | bytes 1572872 | tf_op jit(solution)/shard_map/ppermute | solution.py:61
  66.1 11.5 %shard_map.61 = (bf16[10,256,2048]{2,1,0:T(8,128)(2,1)}, f32[4,1024,256]{2,1,0:T(8,128)}, f32[8,128]{1,0:T(8,128)}) custom-call(s32[3]{0:T(128)} %pad_add_fusion.meta, bf16[4,256,1024]{2,1,0:T(8,128)(2,1)} %get-tuple-element.50.sparse, bf16[10,256,2048]{2,1,0:T(8,128)(2,1)} %decoder.7, ...), custom_call_target="tpu_custom_call", output_to_operand_aliasing={{0}: (12, {})} | custom-call | flops 10737418240 | bytes 20971520 | tf_op jit(solution)/shard_map/pallas_call | solution.py:291
  77.6 4.4 %collective-permute-done.24 = bf16[4,256,256]{2,1,0:T(8,128)(2,1)S(1)} collective-permute-done((bf16[4,256,256]{2,1,0:T(8,128)(2,1)S(1)}, bf16[4,256,256]{2,1,0:T(8,128)(2,1)S(1)}, u32[]{:S(2)}, u32[]{:S(2)}) %collective-permute-start.24) | collective-permute-done | bytes 524320 | tf_op jit(solution)/shard_map/ppermute | solution.py:61
  82.0 0.1 broadcast_select_fusion.refs_4_
  82.0 0.1 collective-permute-start.28
  82.1 0.5 collective-permute-start.27
  82.6 2.6 %collective-permute-done.14.refs_3_ = bf16[4,256,256]{2,1,0:T(8,128)(2,1)S(1)} collective-permute-done((bf16[4,256,256]{2,1,0:T(8,128)(2,1)S(1)}, bf16[4,256,256]{2,1,0:T(8,128)(2,1)S(1)}, u32[]{:S(2)}, u32[]{:S(2)}) %collective-permute-start.14) | collective-permute-done | bytes 524320 | tf_op jit(solution)/shard_map/ppermute | solution.py:61
  85.2 0.6 collective-permute-start.30
  85.8 1.5 %collective-permute-start.29 = (bf16[4,256,256]{2,1,0:T(8,128)(2,1)S(1)}, bf16[4,256,256]{2,1,0:T(8,128)(2,1)S(1)}, u32[]{:S(2)}, u32[]{:S(2)}) collective-permute-start(bf16[4,256,256]{2,1,0:T(8,128)(2,1)S(1)} %collective-permute-done.14.refs_3_), channel_id=1, source_target_pairs={{0,16},{1,17},{2,18},{3,19},{4,20},{5,21},{6,22},{7,23},{8,24},{9,... | collective-permute-start | bytes 1572872 | tf_op jit(solution)/shard_map/ppermute | solution.py:61
  87.3 0.5 collective-permute-start.32
  87.8 11.5 %shard_map.62 = (bf16[10,256,2048]{2,1,0:T(8,128)(2,1)}, f32[4,1024,256]{2,1,0:T(8,128)}, f32[8,128]{1,0:T(8,128)}) custom-call(s32[3]{0:T(128)} %pad_add_fusion.meta, bf16[4,256,1024]{2,1,0:T(8,128)(2,1)} %get-tuple-element.50.sparse, bf16[10,256,2048]{2,1,0:T(8,128)(2,1)} %decoder.7, ...), custom_call_target="tpu_custom_call", output_to_operand_aliasing={{0}: (12, {})} | custom-call | flops 10737418240 | bytes 20971520 | tf_op jit(solution)/shard_map/pallas_call | solution.py:291
  99.4 0.3 collective-permute-done.29.refs_5_
  99.8 1.9 %collective-permute-done.33.refs_9_ = bf16[4,256,256]{2,1,0:T(8,128)(2,1)S(1)} collective-permute-done((bf16[4,256,256]{2,1,0:T(8,128)(2,1)S(1)}, bf16[4,256,256]{2,1,0:T(8,128)(2,1)S(1)}, u32[]{:S(2)}, u32[]{:S(2)}) %collective-permute-start.33) | collective-permute-done | bytes 524320 | tf_op jit(solution)/shard_map/ppermute | solution.py:61
  101.6 0.8 copy-done.14
  102.4 12.1 %shard_map.63 = (bf16[10,256,2048]{2,1,0:T(8,128)(2,1)}, bf16[4,1024,256]{2,1,0:T(8,128)(2,1)}, f32[8,128]{1,0:T(8,128)}) custom-call(s32[3]{0:T(128)} %pad_add_fusion.meta, bf16[4,256,1024]{2,1,0:T(8,128)(2,1)} %get-tuple-element.50.sparse, bf16[10,256,2048]{2,1,0:T(8,128)(2,1)} %decoder.7, ...), custom_call_target="tpu_custom_call", output_to_operand_aliasing={{0}: (13, {})} | custom-call | flops 10737418240 | bytes 20971520 | tf_op jit(solution)/shard_map/pallas_call | solution.py:291
  (59 shorter events, 0.1 us)
Async XLA Ops:
  0.6 14.1 %collective-permute-start.1 = (bf16[4,256,256]{2,1,0:T(8,128)(2,1)}, bf16[4,256,256]{2,1,0:T(8,128)(2,1)S(1)}, u32[]{:S(2)}, u32[]{:S(2)}) collective-permute-start(bf16[4,256,256]{2,1,0:T(8,128)(2,1)} %refs_0_.1), channel_id=1, source_target_pairs={{2,4},{3,5},{4,2},{5,3},{10,12},{11,13},{12,10},{13,11},{18,20},{1... | collective-permute-start | bytes 1572872 | tf_op jit(solution)/shard_map/ppermute | solution.py:61
  1.3 17.7 %collective-permute-start = (bf16[4,256,256]{2,1,0:T(8,128)(2,1)}, bf16[4,256,256]{2,1,0:T(8,128)(2,1)S(1)}, u32[]{:S(2)}, u32[]{:S(2)}) collective-permute-start(bf16[4,256,256]{2,1,0:T(8,128)(2,1)} %refs_0_.1), channel_id=1, source_target_pairs={{0,2},{1,3},{2,0},{3,1},{4,6},{5,7},{6,4},{7,5},{8,10},{9,11},{10,... | collective-permute-start | bytes 1572872 | tf_op jit(solution)/shard_map/ppermute | solution.py:61
  7.2 13.4 %collective-permute-start.8 = (bf16[4,256,256]{2,1,0:T(8,128)(2,1)}, bf16[4,256,256]{2,1,0:T(8,128)(2,1)}, u32[]{:S(2)}, u32[]{:S(2)}) collective-permute-start(bf16[4,256,256]{2,1,0:T(8,128)(2,1)} %refs_0_.1), channel_id=1, source_target_pairs={{0,16},{1,17},{2,18},{3,19},{4,20},{5,21},{6,22},{7,23},{8,24},{9,... | collective-permute-start | bytes 1572872 | tf_op jit(solution)/shard_map/ppermute | solution.py:61
  8.7 14.9 %collective-permute-start.7 = (bf16[4,256,256]{2,1,0:T(8,128)(2,1)}, bf16[4,256,256]{2,1,0:T(8,128)(2,1)}, u32[]{:S(2)}, u32[]{:S(2)}) collective-permute-start(bf16[4,256,256]{2,1,0:T(8,128)(2,1)} %refs_0_.1), channel_id=1, source_target_pairs={{0,8},{1,9},{2,10},{3,11},{4,12},{5,13},{6,14},{7,15},{8,0},{9,1},... | collective-permute-start | bytes 1572872 | tf_op jit(solution)/shard_map/ppermute | solution.py:61
  14.8 17.1 %collective-permute-start.2 = (bf16[4,256,256]{2,1,0:T(8,128)(2,1)S(1)}, bf16[4,256,256]{2,1,0:T(8,128)(2,1)S(1)}, u32[]{:S(2)}, u32[]{:S(2)}) collective-permute-start(bf16[4,256,256]{2,1,0:T(8,128)(2,1)S(1)} %collective-permute-done.1), channel_id=1, source_target_pairs={{2,0},{3,1},{4,6},{5,7},{10,8},{11,9},{12,14},{13,15},{18,16},{19,... | collective-permute-start | bytes 1572872 | tf_op jit(solution)/shard_map/ppermute | solution.py:61
  19.1 35.3 %copy-start.3 = (bf16[4,256,256]{2,1,0:T(8,128)(2,1)}, bf16[4,256,256]{2,1,0:T(8,128)(2,1)S(1)}, u32[]{:S(2)}) copy-start(bf16[4,256,256]{2,1,0:T(8,128)(2,1)S(1)} %collective-permute-done.refs_1_) | copy-start | bytes 1572868
  19.1 12.8 %collective-permute-start.3 = (bf16[4,256,256]{2,1,0:T(8,128)(2,1)S(1)}, bf16[4,256,256]{2,1,0:T(8,128)(2,1)S(1)}, u32[]{:S(2)}, u32[]{:S(2)}) collective-permute-start(bf16[4,256,256]{2,1,0:T(8,128)(2,1)S(1)} %collective-permute-done.refs_1_), channel_id=1, source_target_pairs={{2,4},{3,5},{4,2},{5,3},{10,12},{11,13},{12,10},{13,11},{18,20},{1... | collective-permute-start | bytes 1572872 | tf_op jit(solution)/shard_map/ppermute | solution.py:61
  20.6 12.5 %collective-permute-start.9 = (bf16[4,256,256]{2,1,0:T(8,128)(2,1)}, bf16[4,256,256]{2,1,0:T(8,128)(2,1)}, u32[]{:S(2)}, u32[]{:S(2)}) collective-permute-start(bf16[4,256,256]{2,1,0:T(8,128)(2,1)} %collective-permute-done.8.refs_2_), channel_id=1, source_target_pairs={{0,8},{1,9},{2,10},{3,11},{4,12},{5,13},{6,14},{7,15},{8,0},{9,1},... | collective-permute-start | bytes 1572872 | tf_op jit(solution)/shard_map/ppermute | solution.py:61
  22.1 11.9 %collective-permute-start.4 = (bf16[4,256,256]{2,1,0:T(8,128)(2,1)S(1)}, bf16[4,256,256]{2,1,0:T(8,128)(2,1)S(1)}, u32[]{:S(2)}, u32[]{:S(2)}) collective-permute-start(bf16[4,256,256]{2,1,0:T(8,128)(2,1)S(1)} %collective-permute-done.refs_1_), channel_id=1, source_target_pairs={{0,16},{1,17},{2,18},{3,19},{4,20},{5,21},{6,22},{7,23},{8,24},{9,... | collective-permute-start | bytes 1572872 | tf_op jit(solution)/shard_map/ppermute | solution.py:61
  23.6 11.7 %collective-permute-start.10 = (bf16[4,256,256]{2,1,0:T(8,128)(2,1)}, bf16[4,256,256]{2,1,0:T(8,128)(2,1)}, u32[]{:S(2)}, u32[]{:S(2)}) collective-permute-start(bf16[4,256,256]{2,1,0:T(8,128)(2,1)} %refs_0_.1), channel_id=1, source_target_pairs={{0,1},{1,0},{2,3},{3,2},{4,5},{5,4},{6,7},{7,6},{8,9},{9,8},{10,11... | collective-permute-start | bytes 1572872 | tf_op jit(solution)/shard_map/ppermute | solution.py:61
  31.8 5.1 %collective-permute-start.12 = (bf16[4,256,256]{2,1,0:T(8,128)(2,1)}, bf16[4,256,256]{2,1,0:T(8,128)(2,1)}, u32[]{:S(2)}, u32[]{:S(2)}) collective-permute-start(bf16[4,256,256]{2,1,0:T(8,128)(2,1)} %collective-permute-done.8.refs_2_), channel_id=1, source_target_pairs={{0,1},{1,0},{2,3},{3,2},{4,5},{5,4},{6,7},{7,6},{8,9},{9,8},{10,11... | collective-permute-start | bytes 1572872 | tf_op jit(solution)/shard_map/ppermute | solution.py:61
  31.8 6.3 %collective-permute-start.11 = (bf16[4,256,256]{2,1,0:T(8,128)(2,1)}, bf16[4,256,256]{2,1,0:T(8,128)(2,1)}, u32[]{:S(2)}, u32[]{:S(2)}) collective-permute-start(bf16[4,256,256]{2,1,0:T(8,128)(2,1)} %collective-permute-done.7.refs_1_), channel_id=1, source_target_pairs={{0,1},{1,0},{2,3},{3,2},{4,5},{5,4},{6,7},{7,6},{8,9},{9,8},{10,11... | collective-permute-start | bytes 1572872 | tf_op jit(solution)/shard_map/ppermute | solution.py:61
  33.1 5.8 %collective-permute-start.13 = (bf16[4,256,256]{2,1,0:T(8,128)(2,1)}, bf16[4,256,256]{2,1,0:T(8,128)(2,1)}, u32[]{:S(2)}, u32[]{:S(2)}) collective-permute-start(bf16[4,256,256]{2,1,0:T(8,128)(2,1)} %collective-permute-done.9.refs_3_), channel_id=1, source_target_pairs={{0,1},{1,0},{2,3},{3,2},{4,5},{5,4},{6,7},{7,6},{8,9},{9,8},{10,11... | collective-permute-start | bytes 1572872 | tf_op jit(solution)/shard_map/ppermute | solution.py:61
  33.8 27.8 %copy-start = (bf16[4,256,256]{2,1,0:T(8,128)(2,1)}, bf16[4,256,256]{2,1,0:T(8,128)(2,1)S(1)}, u32[]{:S(2)}) copy-start(bf16[4,256,256]{2,1,0:T(8,128)(2,1)S(1)} %broadcast_select_fusion.2.refs_1_) | copy-start | bytes 1572868
  34.0 20.4 %copy-start.4 = (bf16[4,256,256]{2,1,0:T(8,128)(2,1)}, bf16[4,256,256]{2,1,0:T(8,128)(2,1)S(1)}, u32[]{:S(2)}) copy-start(bf16[4,256,256]{2,1,0:T(8,128)(2,1)S(1)} %collective-permute-done.4.refs_3_) | copy-start | bytes 1572868
  34.0 20.4 %collective-permute-start.16 = (bf16[4,256,256]{2,1,0:T(8,128)(2,1)S(1)}, bf16[4,256,256]{2,1,0:T(8,128)(2,1)}, u32[]{:S(2)}, u32[]{:S(2)}) collective-permute-start(bf16[4,256,256]{2,1,0:T(8,128)(2,1)S(1)} %collective-permute-done.refs_1_), channel_id=1, source_target_pairs={{0,8},{1,9},{2,10},{3,11},{4,12},{5,13},{6,14},{7,15},{8,0},{9,1},... | collective-permute-start | bytes 1572872 | tf_op jit(solution)/shard_map/ppermute | solution.py:61
  35.4 24.7 %collective-permute-start.5 = (bf16[4,256,256]{2,1,0:T(8,128)(2,1)S(1)}, bf16[4,256,256]{2,1,0:T(8,128)(2,1)}, u32[]{:S(2)}, u32[]{:S(2)}) collective-permute-start(bf16[4,256,256]{2,1,0:T(8,128)(2,1)S(1)} %broadcast_select_fusion.2.refs_1_), channel_id=1, source_target_pairs={{0,16},{1,17},{2,18},{3,19},{4,20},{5,21},{6,22},{7,23},{8,24},{9,... | collective-permute-start | bytes 1572872 | tf_op jit(solution)/shard_map/ppermute | solution.py:61
  36.9 17.4 %collective-permute-start.6 = (bf16[4,256,256]{2,1,0:T(8,128)(2,1)S(1)}, bf16[4,256,256]{2,1,0:T(8,128)(2,1)S(1)}, u32[]{:S(2)}, u32[]{:S(2)}) collective-permute-start(bf16[4,256,256]{2,1,0:T(8,128)(2,1)S(1)} %collective-permute-done.3), channel_id=1, source_target_pairs={{2,0},{3,1},{4,6},{5,7},{10,8},{11,9},{12,14},{13,15},{18,16},{19,... | collective-permute-start | bytes 1572872 | tf_op jit(solution)/shard_map/ppermute | solution.py:61
  38.2 21.4 %collective-permute-start.17 = (bf16[4,256,256]{2,1,0:T(8,128)(2,1)S(1)}, bf16[4,256,256]{2,1,0:T(8,128)(2,1)}, u32[]{:S(2)}, u32[]{:S(2)}) collective-permute-start(bf16[4,256,256]{2,1,0:T(8,128)(2,1)S(1)} %collective-permute-done.4.refs_3_), channel_id=1, source_target_pairs={{0,8},{1,9},{2,10},{3,11},{4,12},{5,13},{6,14},{7,15},{8,0},{9,1},... | collective-permute-start | bytes 1572872 | tf_op jit(solution)/shard_map/ppermute | solution.py:61
  39.0 20.6 %collective-permute-start.22 = (bf16[4,256,256]{2,1,0:T(8,128)(2,1)}, bf16[4,256,256]{2,1,0:T(8,128)(2,1)S(1)}, u32[]{:S(2)}, u32[]{:S(2)}) collective-permute-start(bf16[4,256,256]{2,1,0:T(8,128)(2,1)} %collective-permute-done.9.refs_3_), channel_id=1, source_target_pairs={{2,4},{3,5},{4,2},{5,3},{10,12},{11,13},{12,10},{13,11},{18,20},{1... | collective-permute-start | bytes 1572872 | tf_op jit(solution)/shard_map/ppermute | solution.py:61
  54.3 7.2 %collective-permute-start.18 = (bf16[4,256,256]{2,1,0:T(8,128)(2,1)S(1)}, bf16[4,256,256]{2,1,0:T(8,128)(2,1)S(1)}, u32[]{:S(2)}, u32[]{:S(2)}) collective-permute-start(bf16[4,256,256]{2,1,0:T(8,128)(2,1)S(1)} %collective-permute-done.refs_1_), channel_id=1, source_target_pairs={{0,1},{1,0},{2,3},{3,2},{4,5},{5,4},{6,7},{7,6},{8,9},{9,8},{10,11... | collective-permute-start | bytes 1572872 | tf_op jit(solution)/shard_map/ppermute | solution.py:61
  54.4 30.8 %copy-start.1 = (bf16[4,256,256]{2,1,0:T(8,128)(2,1)}, bf16[4,256,256]{2,1,0:T(8,128)(2,1)S(1)}, u32[]{:S(2)}) copy-start(bf16[4,256,256]{2,1,0:T(8,128)(2,1)S(1)} %broadcast_select_fusion.1.refs_2_) | copy-start | bytes 1572868
  54.4 7.2 %collective-permute-start.20 = (bf16[4,256,256]{2,1,0:T(8,128)(2,1)S(1)}, bf16[4,256,256]{2,1,0:T(8,128)(2,1)S(1)}, u32[]{:S(2)}, u32[]{:S(2)}) collective-permute-start(bf16[4,256,256]{2,1,0:T(8,128)(2,1)S(1)} %collective-permute-done.4.refs_3_), channel_id=1, source_target_pairs={{0,1},{1,0},{2,3},{3,2},{4,5},{5,4},{6,7},{7,6},{8,9},{9,8},{10,11... | collective-permute-start | bytes 1572872 | tf_op jit(solution)/shard_map/ppermute | solution.py:61
  59.6 2.7 %collective-permute-start.19 = (bf16[4,256,256]{2,1,0:T(8,128)(2,1)}, bf16[4,256,256]{2,1,0:T(8,128)(2,1)S(1)}, u32[]{:S(2)}, u32[]{:S(2)}) collective-permute-start(bf16[4,256,256]{2,1,0:T(8,128)(2,1)} %collective-permute-done.16.refs_2_), channel_id=1, source_target_pairs={{0,1},{1,0},{2,3},{3,2},{4,5},{5,4},{6,7},{7,6},{8,9},{9,8},{10,11... | collective-permute-start | bytes 1572872 | tf_op jit(solution)/shard_map/ppermute | solution.py:61
  59.6 4.2 %collective-permute-start.21 = (bf16[4,256,256]{2,1,0:T(8,128)(2,1)}, bf16[4,256,256]{2,1,0:T(8,128)(2,1)S(1)}, u32[]{:S(2)}, u32[]{:S(2)}) collective-permute-start(bf16[4,256,256]{2,1,0:T(8,128)(2,1)} %collective-permute-done.17.refs_4_), channel_id=1, source_target_pairs={{0,1},{1,0},{2,3},{3,2},{4,5},{5,4},{6,7},{7,6},{8,9},{9,8},{10,11... | collective-permute-start | bytes 1572872 | tf_op jit(solution)/shard_map/ppermute | solution.py:61
  60.1 22.0 %collective-permute-start.23 = (bf16[4,256,256]{2,1,0:T(8,128)(2,1)S(1)}, bf16[4,256,256]{2,1,0:T(8,128)(2,1)}, u32[]{:S(2)}, u32[]{:S(2)}) collective-permute-start(bf16[4,256,256]{2,1,0:T(8,128)(2,1)S(1)} %broadcast_select_fusion.2.refs_1_), channel_id=1, source_target_pairs={{0,8},{1,9},{2,10},{3,11},{4,12},{5,13},{6,14},{7,15},{8,0},{9,1},... | collective-permute-start | bytes 1572872 | tf_op jit(solution)/shard_map/ppermute | solution.py:61
  61.6 2.2 %copy-start.7 = (bf16[4,256,256]{2,1,0:T(8,128)(2,1)}, bf16[4,256,256]{2,1,0:T(8,128)(2,1)S(1)}, u32[]{:S(2)}) copy-start(bf16[4,256,256]{2,1,0:T(8,128)(2,1)S(1)} %collective-permute-done.18.refs_5_) | copy-start | bytes 1572868
  61.6 24.2 %collective-permute-start.25 = (bf16[4,256,256]{2,1,0:T(8,128)(2,1)S(1)}, bf16[4,256,256]{2,1,0:T(8,128)(2,1)}, u32[]{:S(2)}, u32[]{:S(2)}) collective-permute-start(bf16[4,256,256]{2,1,0:T(8,128)(2,1)S(1)} %broadcast_select_fusion.2.refs_1_), channel_id=1, source_target_pairs={{0,1},{1,0},{2,3},{3,2},{4,5},{5,4},{6,7},{7,6},{8,9},{9,8},{10,11... | collective-permute-start | bytes 1572872 | tf_op jit(solution)/shard_map/ppermute | solution.py:61
  61.7 4.4 %copy-start.10 = (bf16[4,256,256]{2,1,0:T(8,128)(2,1)}, bf16[4,256,256]{2,1,0:T(8,128)(2,1)S(1)}, u32[]{:S(2)}) copy-start(bf16[4,256,256]{2,1,0:T(8,128)(2,1)S(1)} %collective-permute-done.20.refs_7_) | copy-start | bytes 1572868
  61.7 23.5 %collective-permute-start.14 = (bf16[4,256,256]{2,1,0:T(8,128)(2,1)S(1)}, bf16[4,256,256]{2,1,0:T(8,128)(2,1)S(1)}, u32[]{:S(2)}, u32[]{:S(2)}) collective-permute-start(bf16[4,256,256]{2,1,0:T(8,128)(2,1)S(1)} %broadcast_select_fusion.1.refs_2_), channel_id=1, source_target_pairs={{0,8},{1,9},{2,10},{3,11},{4,12},{5,13},{6,14},{7,15},{8,0},{9,1},... | collective-permute-start | bytes 1572872 | tf_op jit(solution)/shard_map/ppermute | solution.py:61
  62.3 1.5 %copy-start.12 = (bf16[4,256,256]{2,1,0:T(8,128)(2,1)}, bf16[4,256,256]{2,1,0:T(8,128)(2,1)S(1)}, u32[]{:S(2)}) copy-start(bf16[4,256,256]{2,1,0:T(8,128)(2,1)S(1)} %collective-permute-done.19.refs_6_) | copy-start | bytes 1572868
  62.3 22.9 %collective-permute-start.15 = (bf16[4,256,256]{2,1,0:T(8,128)(2,1)S(1)}, bf16[4,256,256]{2,1,0:T(8,128)(2,1)S(1)}, u32[]{:S(2)}, u32[]{:S(2)}) collective-permute-start(bf16[4,256,256]{2,1,0:T(8,128)(2,1)S(1)} %broadcast_select_fusion.1.refs_2_), channel_id=1, source_target_pairs={{0,16},{1,17},{2,18},{3,19},{4,20},{5,21},{6,22},{7,23},{8,24},{9,... | collective-permute-start | bytes 1572872 | tf_op jit(solution)/shard_map/ppermute | solution.py:61
  64.6 17.4 %collective-permute-start.24 = (bf16[4,256,256]{2,1,0:T(8,128)(2,1)S(1)}, bf16[4,256,256]{2,1,0:T(8,128)(2,1)S(1)}, u32[]{:S(2)}, u32[]{:S(2)}) collective-permute-start(bf16[4,256,256]{2,1,0:T(8,128)(2,1)S(1)} %collective-permute-done.22), channel_id=1, source_target_pairs={{2,0},{3,1},{4,6},{5,7},{10,8},{11,9},{12,14},{13,15},{18,16},{19,... | collective-permute-start | bytes 1572872 | tf_op jit(solution)/shard_map/ppermute | solution.py:61
  82.0 5.8 %copy-start.2 = (bf16[4,256,256]{2,1,0:T(8,128)(2,1)}, bf16[4,256,256]{2,1,0:T(8,128)(2,1)S(1)}, u32[]{:S(2)}) copy-start(bf16[4,256,256]{2,1,0:T(8,128)(2,1)S(1)} %broadcast_select_fusion.refs_4_) | copy-start | bytes 1572868
  82.0 5.3 %collective-permute-start.28 = (bf16[4,256,256]{2,1,0:T(8,128)(2,1)S(1)}, bf16[4,256,256]{2,1,0:T(8,128)(2,1)}, u32[]{:S(2)}, u32[]{:S(2)}) collective-permute-start(bf16[4,256,256]{2,1,0:T(8,128)(2,1)S(1)} %broadcast_select_fusion.refs_4_), channel_id=1, source_target_pairs={{0,1},{1,0},{2,3},{3,2},{4,5},{5,4},{6,7},{7,6},{8,9},{9,8},{10,11... | collective-permute-start | bytes 1572872 | tf_op jit(solution)/shard_map/ppermute | solution.py:61
  82.1 5.2 %collective-permute-start.27 = (bf16[4,256,256]{2,1,0:T(8,128)(2,1)}, bf16[4,256,256]{2,1,0:T(8,128)(2,1)}, u32[]{:S(2)}, u32[]{:S(2)}) collective-permute-start(bf16[4,256,256]{2,1,0:T(8,128)(2,1)} %collective-permute-done.5.refs_3_), channel_id=1, source_target_pairs={{0,1},{1,0},{2,3},{3,2},{4,5},{5,4},{6,7},{7,6},{8,9},{9,8},{10,11... | collective-permute-start | bytes 1572872 | tf_op jit(solution)/shard_map/ppermute | solution.py:61
  85.2 14.1 %copy-start.5 = (bf16[4,256,256]{2,1,0:T(8,128)(2,1)}, bf16[4,256,256]{2,1,0:T(8,128)(2,1)S(1)}, u32[]{:S(2)}) copy-start(bf16[4,256,256]{2,1,0:T(8,128)(2,1)S(1)} %collective-permute-done.14.refs_3_) | copy-start | bytes 1572868
  85.2 2.6 %collective-permute-start.26 = (bf16[4,256,256]{2,1,0:T(8,128)(2,1)}, bf16[4,256,256]{2,1,0:T(8,128)(2,1)}, u32[]{:S(2)}, u32[]{:S(2)}) collective-permute-start(bf16[4,256,256]{2,1,0:T(8,128)(2,1)} %collective-permute-done.23.refs_2_), channel_id=1, source_target_pairs={{0,1},{1,0},{2,3},{3,2},{4,5},{5,4},{6,7},{7,6},{8,9},{9,8},{10,11... | collective-permute-start | bytes 1572872 | tf_op jit(solution)/shard_map/ppermute | solution.py:61
  85.2 14.1 %copy-start.6 = (bf16[4,256,256]{2,1,0:T(8,128)(2,1)}, bf16[4,256,256]{2,1,0:T(8,128)(2,1)S(1)}, u32[]{:S(2)}) copy-start(bf16[4,256,256]{2,1,0:T(8,128)(2,1)S(1)} %collective-permute-done.15.refs_4_) | copy-start | bytes 1572868
  85.2 14.5 %collective-permute-start.30 = (bf16[4,256,256]{2,1,0:T(8,128)(2,1)S(1)}, bf16[4,256,256]{2,1,0:T(8,128)(2,1)S(1)}, u32[]{:S(2)}, u32[]{:S(2)}) collective-permute-start(bf16[4,256,256]{2,1,0:T(8,128)(2,1)S(1)} %broadcast_select_fusion.1.refs_2_), channel_id=1, source_target_pairs={{0,1},{1,0},{2,3},{3,2},{4,5},{5,4},{6,7},{7,6},{8,9},{9,8},{10,11... | collective-permute-start | bytes 1572872 | tf_op jit(solution)/shard_map/ppermute | solution.py:61
  85.8 13.9 %collective-permute-start.29 = (bf16[4,256,256]{2,1,0:T(8,128)(2,1)S(1)}, bf16[4,256,256]{2,1,0:T(8,128)(2,1)S(1)}, u32[]{:S(2)}, u32[]{:S(2)}) collective-permute-start(bf16[4,256,256]{2,1,0:T(8,128)(2,1)S(1)} %collective-permute-done.14.refs_3_), channel_id=1, source_target_pairs={{0,16},{1,17},{2,18},{3,19},{4,20},{5,21},{6,22},{7,23},{8,24},{9,... | collective-permute-start | bytes 1572872 | tf_op jit(solution)/shard_map/ppermute | solution.py:61
  87.3 12.4 %collective-permute-start.31 = (bf16[4,256,256]{2,1,0:T(8,128)(2,1)S(1)}, bf16[4,256,256]{2,1,0:T(8,128)(2,1)S(1)}, u32[]{:S(2)}, u32[]{:S(2)}) collective-permute-start(bf16[4,256,256]{2,1,0:T(8,128)(2,1)S(1)} %collective-permute-done.14.refs_3_), channel_id=1, source_target_pairs={{0,1},{1,0},{2,3},{3,2},{4,5},{5,4},{6,7},{7,6},{8,9},{9,8},{10,11... | collective-permute-start | bytes 1572872 | tf_op jit(solution)/shard_map/ppermute | solution.py:61
  87.3 12.4 %collective-permute-start.32 = (bf16[4,256,256]{2,1,0:T(8,128)(2,1)S(1)}, bf16[4,256,256]{2,1,0:T(8,128)(2,1)}, u32[]{:S(2)}, u32[]{:S(2)}) collective-permute-start(bf16[4,256,256]{2,1,0:T(8,128)(2,1)S(1)} %collective-permute-done.15.refs_4_), channel_id=1, source_target_pairs={{0,1},{1,0},{2,3},{3,2},{4,5},{5,4},{6,7},{7,6},{8,9},{9,8},{10,11... | collective-permute-start | bytes 1572872 | tf_op jit(solution)/shard_map/ppermute | solution.py:61
  99.7 1.9 %copy-start.9 = (bf16[4,256,256]{2,1,0:T(8,128)(2,1)}, bf16[4,256,256]{2,1,0:T(8,128)(2,1)S(1)}, u32[]{:S(2)}) copy-start(bf16[4,256,256]{2,1,0:T(8,128)(2,1)S(1)} %collective-permute-done.29.refs_5_) | copy-start | bytes 1572868
  99.7 1.9 %collective-permute-start.33 = (bf16[4,256,256]{2,1,0:T(8,128)(2,1)S(1)}, bf16[4,256,256]{2,1,0:T(8,128)(2,1)S(1)}, u32[]{:S(2)}, u32[]{:S(2)}) collective-permute-start(bf16[4,256,256]{2,1,0:T(8,128)(2,1)S(1)} %collective-permute-done.29.refs_5_), channel_id=1, source_target_pairs={{0,1},{1,0},{2,3},{3,2},{4,5},{5,4},{6,7},{7,6},{8,9},{9,8},{10,11... | collective-permute-start | bytes 1572872 | tf_op jit(solution)/shard_map/ppermute | solution.py:61
  99.7 1.9 %copy-start.8 = (bf16[4,256,256]{2,1,0:T(8,128)(2,1)}, bf16[4,256,256]{2,1,0:T(8,128)(2,1)S(1)}, u32[]{:S(2)}) copy-start(bf16[4,256,256]{2,1,0:T(8,128)(2,1)S(1)} %collective-permute-done.30.refs_6_) | copy-start | bytes 1572868
  99.7 1.9 %copy-start.11 = (bf16[4,256,256]{2,1,0:T(8,128)(2,1)}, bf16[4,256,256]{2,1,0:T(8,128)(2,1)S(1)}, u32[]{:S(2)}) copy-start(bf16[4,256,256]{2,1,0:T(8,128)(2,1)S(1)} %collective-permute-done.31.refs_7_) | copy-start | bytes 1572868
  101.6 0.8 copy-start.14
  (1 other events, 0.8 us)
